TPU v7x, 128 devices: a whole 4x4x4 slice. The times are simulated.
128 devices in a mesh: ctx: 64 (over x, z_lo, y, core), head: 2 (over z_hi).
Axes of the slice: x: 4, y: 4, z: 4 (z_hi: 2, z_lo: 2; z = z_hi * 2 + z_lo), core: 2. Of those that a mesh axis runs over, the one named last changes fastest.
Arguments:
- img_q: bfloat16 [2048, 1536], P('ctx', 'head'), may hold values from -12 to 12
- img_k: bfloat16 [2048, 1536], P('ctx', 'head'), may hold values from -12 to 12
- img_v: bfloat16 [2048, 1536], P('ctx', 'head'), may hold values from -6 to 6
- txt_ids: int32 [512], replicated, may hold values from 0 to 32767
- concept_ids: int32 [1024], replicated, may hold values from 0 to 32767
- step_index: int32 [1], replicated, may hold values from 0 to 27
- token_table: bfloat16 [32768, 3072], P(('ctx', 'head')), may hold values from -6 to 6
- modulation: float32 [28, 2, 3072], replicated, may hold values from -3 to 3
- txt_qkv: bfloat16 [3072, 3, 1536], P(None, None, 'head'), may hold values from -0.109375 to 0.109375
- qk_gain: float32 [2, 128], replicated, may hold values from 0.25 to 1.75
Outputs:
- img_out: bfloat16 [2048, 1536], P('ctx', 'head')
- saliency: float32 [1024, 2048], P(None, 'ctx')
All inputs are finite; a program needn't handle non-finite values.
Results may differ from a plain program's by a relative error of at most 0.013.
Values may be sent and summed in bfloat16 or wider, within the bound.
No kernel may reach another device: no remote copies, remote signals or barrier semaphores. Data moves between devices by JAX's collectives and lax.ppermute only.
A program may use at most 128 MiB of HBM per device.

v0:
```python
import math

import jax
import jax.numpy as jnp
from jax import lax
from jax.experimental import pallas as pl
from jax.experimental.pallas import tpu as pltpu
from jax.sharding import PartitionSpec as P

BF = jnp.bfloat16
F32 = jnp.float32
HD = 128
SLOTS = 32
CON = 96
TXT = 64
ROWS = CON + TXT
MIB = 1 << 20
FACTOR = HD ** (-0.5) * math.log2(math.e)


def modulate(rows, shift_scale):
    values = rows.astype(F32)
    mean = jnp.mean(values, axis=1, keepdims=True)
    centered = values - mean
    var = jnp.mean(centered * centered, axis=1, keepdims=True)
    normed = centered * lax.rsqrt(var + 1e-06)
    return (normed * (1.0 + shift_scale[1]) + shift_scale[0]).astype(BF)


def head_norm(values, gain, head_dim):
    shaped = values.reshape(values.shape[0], -1, head_dim)
    meansq = jnp.mean(shaped * shaped, axis=2, keepdims=True)
    return (shaped * lax.rsqrt(meansq + 1e-06) * gain).reshape(values.shape[0], -1)


def block_stats(queries, keys, values):
    scores = jnp.einsum("rgd,kgd->grk", queries, keys, preferred_element_type=F32)
    scores = scores * queries.shape[-1] ** (-0.5)
    peak = jnp.max(scores, axis=2)
    weights = jnp.exp(scores - peak[:, :, None])
    total = jnp.sum(weights, axis=2)
    summed = jnp.einsum("grk,kgd->grd", weights.astype(BF), values, preferred_element_type=F32)
    return (peak, total, summed)


def combine_stats(first, second):
    peak = jnp.maximum(first[0], second[0])
    left = jnp.exp(first[0] - peak)
    right = jnp.exp(second[0] - peak)
    total = first[1] * left + second[1] * right
    summed = first[2] * left[:, :, None] + second[2] * right[:, :, None]
    return (peak, total, summed)


def scaled_scores(dots, concept_sq, image_sq, width):
    concept_rms = jnp.sqrt(concept_sq / width + 1e-06)
    image_rms = jnp.sqrt(image_sq / width + 1e-06)
    return dots / (jnp.sqrt(F32(width)) * concept_rms[:, None] * image_rms[None, :])


def gather_ctx(block):
    n_ctx = lax.axis_size("ctx")
    spread = jnp.broadcast_to(block[None], (n_ctx,) + block.shape)
    return lax.all_to_all(spread, "ctx", 0, 0, tiled=True)


def general(
    img_q, img_k, img_v, txt_ids, concept_ids, step_index, token_table, modulation, txt_qkv, qk_gain
):
    n_ctx = lax.axis_size("ctx")
    n_head = lax.axis_size("head")
    head_dim = qk_gain.shape[1]
    group = img_q.shape[1] // head_dim
    text_dev = txt_ids.shape[0] // n_ctx
    concept_dev = concept_ids.shape[0] // n_ctx
    vocab_dev = token_table.shape[0]
    combined = jnp.concatenate(
        [txt_ids.reshape(n_ctx, text_dev), concept_ids.reshape(n_ctx, concept_dev)], axis=1
    ).reshape(-1)
    offset = lax.axis_index(("ctx", "head")) * vocab_dev
    wanted = combined - offset
    inside = (wanted >= 0) & (wanted < vocab_dev)
    picked = jnp.take(token_table, jnp.clip(wanted, 0, vocab_dev - 1), axis=0)
    n_all = n_ctx * n_head
    mine = jnp.where(inside[:, None], picked, jnp.zeros((), picked.dtype))
    parts = lax.all_to_all(
        mine.reshape(n_all, -1, mine.shape[1]), ("ctx", "head"), 0, 0, tiled=True
    )
    own_rows = jnp.sum(parts.astype(F32), axis=0)
    prompt_rows = lax.all_gather(own_rows.astype(BF), "head", axis=0, tiled=True)
    shift_scale = lax.dynamic_index_in_dim(modulation, step_index[0], 0, keepdims=False)
    modded = modulate(prompt_rows, shift_scale)
    text_mod = modded[:text_dev]
    concept_mod = modded[text_dev:]
    text_kv = jnp.einsum("rd,dgc->rgc", text_mod, txt_qkv[:, 1:], preferred_element_type=F32)
    concept_qkv = jnp.einsum("rd,dgc->rgc", concept_mod, txt_qkv, preferred_element_type=F32)
    text_keys = head_norm(text_kv[:, 0], qk_gain[1], head_dim).astype(BF)
    text_values = text_kv[:, 1].astype(BF)
    concept_queries = head_norm(concept_qkv[:, 0], qk_gain[0], head_dim).astype(BF)
    concept_keys = head_norm(concept_qkv[:, 1], qk_gain[1], head_dim).astype(BF)
    concept_values = concept_qkv[:, 2].astype(BF)
    local_kv = jnp.stack(
        [
            jnp.concatenate([text_keys, concept_keys], axis=0),
            jnp.concatenate([text_values, concept_values], axis=0),
        ]
    )
    prompt_kv = gather_ctx(local_kv)
    text_part = jnp.swapaxes(prompt_kv[:, :, :text_dev], 0, 1).reshape(2, -1, group, head_dim)
    concept_part = jnp.swapaxes(prompt_kv[:, :, text_dev:], 0, 1).reshape(2, -1, group, head_dim)
    image_queries = img_q.reshape(-1, group, head_dim)
    concept_q3 = concept_queries.reshape(-1, group, head_dim)
    first = block_stats(image_queries, text_part[0], text_part[1])
    second = block_stats(concept_q3, concept_part[0], concept_part[1])
    start_stats = (
        jnp.concatenate([first[0], second[0]], axis=1),
        jnp.concatenate([first[1], second[1]], axis=1),
        jnp.concatenate([first[2], second[2]], axis=1),
    )
    all_queries = jnp.concatenate([image_queries, concept_q3], axis=0)
    image_kv = gather_ctx(jnp.stack([img_k, img_v]))
    keys = image_kv[:, 0].reshape(-1, group, head_dim)
    values = image_kv[:, 1].reshape(-1, group, head_dim)
    peak, total, summed = combine_stats(start_stats, block_stats(all_queries, keys, values))
    attended = (
        jnp.transpose(summed / total[:, :, None], (1, 0, 2))
        .reshape(all_queries.shape[0], -1)
        .astype(BF)
    )
    img_rows = img_q.shape[0]
    img_out = attended[:img_rows]
    concept_out = attended[img_rows:]
    concept_all = gather_ctx(concept_out).reshape(-1, concept_out.shape[1])
    dots = lax.dot_general(
        concept_all, img_out, (((1,), (1,)), ((), ())), preferred_element_type=F32
    )
    image_f = img_out.astype(F32)
    concept_f = concept_all.astype(F32)
    image_sq = jnp.sum(image_f * image_f, axis=1)
    concept_sq = jnp.sum(concept_f * concept_f, axis=1)
    width = group * head_dim * n_head
    sums = jnp.concatenate(
        [
            jnp.concatenate([dots, concept_sq[:, None]], axis=1),
            jnp.concatenate([image_sq, jnp.zeros((1,), F32)])[None],
        ]
    ).astype(BF)
    other = lax.ppermute(sums, "head", [(0, 1), (1, 0)])
    sums = sums.astype(F32) + other.astype(F32)
    concepts = dots.shape[0]
    saliency = scaled_scores(
        sums[:concepts, :img_rows], sums[:concepts, img_rows], sums[concepts, :img_rows], width
    )
    return (img_out, saliency)


def place(x, zl, y, c, g):
    return ((((x * 2 + zl) * 4 + y) * 2 + c) * 2) + g


def pairs(move):
    found = []
    for x in range(4):
        for zl in range(2):
            for y in range(4):
                for c in range(2):
                    for g in range(2):
                        found.append((place(x, zl, y, c, g), place(*move(x, zl, y, c, g))))
    return found


def swap_z(s):
    def move(x, zl, y, c, g):
        z = (2 * g + zl) ^ s
        return x, z & 1, y, c, z >> 1

    return pairs(move)


def swap_u(s):
    return pairs(
        lambda x, zl, y, c, g: (x, zl, y ^ s, c, g) if c else (x ^ s, zl, y, c, g)
    )


def swap_v(s):
    return pairs(
        lambda x, zl, y, c, g: (x ^ s, zl, y, c, g) if c else (x, zl, y ^ s, c, g)
    )


def swap_core(dg):
    return pairs(lambda x, zl, y, c, g: (x, zl, y, c ^ 1, g ^ dg))


def send(array, pairing):
    return lax.ppermute(array, ("ctx", "head"), pairing)


def nt(a, b, **kw):
    return lax.dot_general(a, b, (((1,), (1,)), ((), ())), preferred_element_type=F32, **kw)


def nn(a, b):
    return lax.dot_general(a, b, (((1,), (0,)), ((), ())), preferred_element_type=F32)


def call(kernel, outs, scratch=(), limit=48, flops=0, nbytes=0, smem=1, in_hbm=0):
    def run(*args):
        vm = pl.BlockSpec(memory_space=pltpu.VMEM)
        sm = pl.BlockSpec(memory_space=pltpu.SMEM)
        return pl.pallas_call(
            kernel,
            out_shape=outs,
            in_specs=[sm] * smem
            + [vm] * (len(args) - smem - in_hbm)
            + [pl.BlockSpec(memory_space=pl.ANY)] * in_hbm,
            out_specs=jax.tree.map(lambda _: vm, outs),
            scratch_shapes=list(scratch),
            compiler_params=pltpu.CompilerParams(vmem_limit_bytes=limit * MIB),
            cost_estimate=pl.CostEstimate(flops=flops, bytes_accessed=nbytes, transcendentals=0),
        )(*args)

    return run


def sds(shape, dtype=BF):
    return jax.ShapeDtypeStruct(shape, dtype)


def column_of(owner):
    ctx = owner >> 1
    return ((ctx >> 4) << 2) | ((ctx >> 1) & 3)


def ranks(keys, classes, resets):
    n = keys.shape[1]
    blk = 256
    row = lax.broadcasted_iota(jnp.int32, (blk, blk), 0)
    col = lax.broadcasted_iota(jnp.int32, (blk, blk), 1)
    earlier = (row < col).astype(F32).astype(BF)
    label = lax.broadcasted_iota(jnp.int32, (classes, blk), 0)
    carry = jnp.zeros((classes, 1), F32)
    found, counts = [], []
    for b in range(n // blk):
        if b in resets:
            counts.append(carry)
            carry = jnp.zeros((classes, 1), F32)
        hot = (label == keys[:, b * blk : (b + 1) * blk]).astype(F32)
        before = nn(hot.astype(BF), earlier) + carry
        found.append(jnp.sum(hot * before, axis=0, keepdims=True))
        carry = carry + jnp.sum(hot, axis=1, keepdims=True)
    counts.append(carry)
    return jnp.concatenate(found, axis=1).astype(jnp.int32), counts


def most(counts, n):
    return jnp.broadcast_to(jnp.max(counts, axis=0, keepdims=True).astype(jnp.int32), (1, n))


def plan_kernel(at, con_ref, txt_ref, table_ref, k_ref, v_ref, rows_ref, both_ref, plan_ref):
    ids = jnp.concatenate([con_ref[...], txt_ref[...]], axis=1)
    n = ids.shape[1]
    vocab_dev = table_ref.shape[0]
    owner = ids >> int(math.log2(vocab_dev))
    rank, (counts,) = ranks(owner, 128, ())
    hot_slot = lax.broadcasted_iota(jnp.int32, (SLOTS, n), 0) == rank
    hot_slot = (hot_slot & (owner == at[0])).astype(F32).astype(BF)
    hot_row = lax.broadcasted_iota(jnp.int32, (vocab_dev, n), 0) == (ids & (vocab_dev - 1))
    pick = nt(hot_slot, hot_row.astype(F32).astype(BF)).astype(BF)
    rows = nn(pick, table_ref[...]).astype(BF)
    rows_ref[...] = rows
    both_ref[0:SLOTS, :] = rows
    wide = k_ref.shape[1]
    for j, (ref, row) in enumerate(((k_ref, 0), (k_ref, 16), (v_ref, 0), (v_ref, 16))):
        both_ref[SLOTS:, j * wide : (j + 1) * wide] = ref[row : row + 16, :]
    plan_ref[0:1, :] = rank
    plan_ref[1:2, :] = most(counts, n)
    plan_ref[2:8, :] = jnp.zeros((6, n), jnp.int32)


def empty_bias(at, counts, slots, blocks_lanes):
    lane = lax.broadcasted_iota(jnp.int32, (1, blocks_lanes), 1)
    block = jnp.zeros((1, blocks_lanes), jnp.int32)
    for j in range(1, 16):
        block = block + (lane >= j * slots).astype(jnp.int32)
    item_u = (block & 3) ^ at[4]
    item_v = (block >> 2) ^ at[5]
    column = jnp.where(at[2] == 0, item_u * 4 + item_v, item_v * 4 + item_u)
    hot = lax.broadcasted_iota(jnp.int32, (16, blocks_lanes), 0) == column
    held = jnp.sum(jnp.where(hot, counts, 0.0), axis=0, keepdims=True)
    return jnp.where((lane - block * slots).astype(F32) < held, 0.0, -1e30)


def pack_kernel(at, con_ref, txt_ref, plan_ref, out_ref, spot_ref, con_bias, txt_bias):
    ids = jnp.concatenate([con_ref[...], txt_ref[...]], axis=1)
    n = ids.shape[1]
    n_con = con_ref.shape[1]
    owner = ids >> 8
    column = column_of(owner)
    spot, (con_counts, txt_counts) = ranks(column, 16, (n_con // 256,))
    con_bias[...] = empty_bias(at, con_counts, CON, 16 * CON)
    txt_bias[...] = empty_bias(at, txt_counts, TXT, 16 * TXT)
    spot_ref[0:1, :] = spot
    spot_ref[1:2, :] = most(con_counts, n)
    spot_ref[2:3, :] = most(txt_counts, n)
    spot_ref[3:8, :] = jnp.zeros((5, n), jnp.int32)
    here = column == at[1]
    rank = plan_ref[0:1, :]
    concept = lax.broadcasted_iota(jnp.int32, (1, n), 1) < n_con
    target = jnp.where(
        concept, jnp.where(spot < CON, spot, -1), jnp.where(spot < TXT, spot + CON, -1)
    )
    z = ((owner & 1) << 1) | ((owner >> 4) & 1)
    core = (owner >> 1) & 1
    piece = jnp.where(core == at[2], 0, 4) + (at[3] ^ z)
    source = jnp.where(rank < SLOTS, piece * SLOTS + rank, -1)
    target = jnp.where(here, target, -1)
    source = jnp.where(here, source, -1)
    hot_t = (lax.broadcasted_iota(jnp.int32, (ROWS, n), 0) == target).astype(F32).astype(BF)
    hot_s = (lax.broadcasted_iota(jnp.int32, (8 * SLOTS, n), 0) == source).astype(F32).astype(BF)
    out_ref[...] = nt(hot_t, hot_s).astype(BF)


def project_kernel(at, pack_ref, *refs):
    rows, (mod_ref, gain_ref, w_hbm), outs = refs[:8], refs[8:11], refs[11:15]
    raw_ref, x_ref, w_ref, sems = refs[15:]
    half = w_ref.shape[2]
    lanes = pl.ds(pl.multiple_of(at[2] * half, half), half)
    copies = [
        pltpu.make_async_copy(w_hbm.at[j, :, lanes], w_ref.at[j], sems.at[j]) for j in range(3)
    ]
    for copy in copies:
        copy.start()
    for i, ref in enumerate(rows):
        raw_ref[i * SLOTS : (i + 1) * SLOTS, :] = ref[0:SLOTS, :]
    shift = mod_ref[0:1, :]
    scale = 1.0 + mod_ref[1:2, :]
    for i in range(ROWS // 32):
        block = slice(i * 32, (i + 1) * 32)
        values = nn(pack_ref[block, :], raw_ref[...])
        mean = jnp.mean(values, axis=1, keepdims=True)
        centered = values - mean
        var = jnp.mean(centered * centered, axis=1, keepdims=True)
        x_ref[block, :] = (centered * lax.rsqrt(var + 1e-06) * scale + shift).astype(BF)

    def normed(u, gain):
        meansq = jnp.mean(u * u, axis=1, keepdims=True)
        return u * lax.rsqrt(meansq + 1e-06) * gain

    copies[0].wait()
    q = nn(x_ref[0:CON, :], w_ref[0])
    copies[1].wait()
    k = nn(x_ref[...], w_ref[1])
    copies[2].wait()
    v = nn(x_ref[...], w_ref[2])
    heads = []
    for h in range(3):
        cols = slice(h * HD, (h + 1) * HD)
        heads.append(
            (
                (normed(q[:, cols], gain_ref[0:1, :]) * FACTOR).astype(BF),
                normed(k[:, cols], gain_ref[1:2, :]).astype(BF),
                v[:, cols].astype(BF),
            )
        )
    for s, out in enumerate(outs):
        head = jnp.minimum(at[4] ^ s, 2)
        for h in range(3):

            @pl.when(head == h)
            def _(h=h, out=out):
                out[0:ROWS, 0:HD] = heads[h][1]
                out[0:ROWS, HD:] = heads[h][2]
                out[ROWS:, 0:HD] = heads[h][0][: CON // 2]
                out[ROWS:, HD:] = heads[h][0][CON // 2 :]


def join_kernel(a, b, c, d, q_out, kv_out):
    for i, ref in enumerate((a, b, c, d)):
        kv_out[i * CON : (i + 1) * CON, :] = ref[0:CON, :]
        kv_out[4 * CON + i * TXT : 4 * CON + (i + 1) * TXT, :] = ref[CON:ROWS, :]
        q_out[i * CON : i * CON + CON // 2, :] = ref[ROWS:, 0:HD]
        q_out[i * CON + CON // 2 : (i + 1) * CON, :] = ref[ROWS:, HD:]


def image_heads_kernel(at, q, q_core, own, core, zl, diag, *outs):
    n, wide = q.shape
    for s, out in enumerate(outs):
        head = at[2] * 3 + jnp.minimum(at[4] ^ s, 2)
        lanes = pl.ds(pl.multiple_of(head * HD, HD), HD)
        out[0:n, :] = q[:, lanes]
        out[n : 2 * n, :] = q_core[:, lanes]
        for i in range(2):
            for j, ref in enumerate((own, core, zl, diag)):
                row = (2 + 4 * i + j) * n
                for m in range(2):
                    lanes = pl.ds(pl.multiple_of((2 * i + m) * wide + head * HD, HD), HD)
                    out[row + 16 * m : row + 16 * (m + 1), :] = ref[SLOTS:, lanes]


def image_join_kernel(a, b, c, d, q_out, kv_out):
    n = a.shape[0] // 10
    for i, ref in enumerate((a, b, c, d)):
        q_out[2 * n * i : 2 * n * (i + 1), :] = ref[0 : 2 * n, :]
        kv_out[4 * n * i : 4 * n * (i + 1), :] = ref[2 * n : 6 * n, :]
        kv_out[4 * n * (4 + i) : 4 * n * (5 + i), :] = ref[6 * n :, :]


def weigh(q, parts, factor):
    scores = []
    for keys, _, bias in parts:
        part = nt(q, keys)
        scores.append(part if bias is None else part + bias)
    peak = scores[0].max(axis=1, keepdims=True)
    for part in scores[1:]:
        peak = jnp.maximum(peak, part.max(axis=1, keepdims=True))
    total = None
    for part, (_, values, _) in zip(scores, parts):
        power = part - peak
        weights = jnp.exp2(power if factor is None else power * factor).astype(BF)
        summed = nn(weights, values)
        total = summed if total is None else total + summed
    return (peak if factor is None else peak * factor), total


def merge(first, second):
    peak = jnp.maximum(first[0], second[0])
    summed = first[1] * jnp.exp2(first[0] - peak) + second[1] * jnp.exp2(second[0] - peak)
    return (summed[:, 0:HD] / summed[:, HD:]).astype(BF)


def with_ones(values):
    return jnp.concatenate([values, jnp.ones_like(values)], axis=1)


def image_self_kernel(i0, i1, i2, i3, q, kv, bias, keys, vals, peak, summed):
    part = i0.shape[0] // 2
    for i, ref in enumerate((i0, i1, i2, i3)):
        keys[i * part : (i + 1) * part, :] = ref[0:part, :]
        vals[i * part : (i + 1) * part, :] = with_ones(ref[part:, :])
    text = kv[4 * CON :, :]
    parts = (
        (keys[...], vals[...], None),
        (text[:, 0:HD], with_ones(text[:, HD:]), bias[:, 0 : 4 * TXT]),
    )
    peak[...], summed[...] = weigh(q[...], parts, FACTOR)


def concept_image_kernel(pick, q0, q1, q2, q3, keys, vals, kv, bias, q_out, peak, summed):
    n = 4 * CON
    q_out[...] = sum(
        nn(pick[:, a * n : (a + 1) * n], ref[...]) for a, ref in enumerate((q0, q1, q2, q3))
    ).astype(BF)
    own = (kv[0:n, 0:HD], with_ones(kv[0:n, HD:]), bias[:, 0:n])
    for b in range(q_out.shape[0] // 256):
        rows = slice(b * 256, (b + 1) * 256)
        parts = ((keys[...], vals[...], None), own)
        peak[rows, :], summed[rows, :] = weigh(q_out[rows, :], parts, None)


def prompt_kernel(con_bias, txt_bias, c1, c2, c3, con_q, cm, cs, img_q, im, ims, *refs):
    outs, (con_out,) = refs[:4], refs[4:]
    n, m = 4 * CON, 4 * TXT
    con_parts, txt_parts = [], []
    for a, ref in enumerate((c1, c2, c3)):
        con, txt = ref[0:n, :], ref[n:, :]
        con_parts.append(
            (con[:, 0:HD], with_ones(con[:, HD:]), con_bias[:, (a + 1) * n : (a + 2) * n])
        )
        txt_parts.append(
            (txt[:, 0:HD], with_ones(txt[:, HD:]), txt_bias[:, (a + 1) * m : (a + 2) * m])
        )
    img = merge(weigh(img_q[...], txt_parts, FACTOR), (im[...], ims[...]))
    n_con = con_q.shape[0]
    for b in range(n_con // 256):
        rows = slice(b * 256, (b + 1) * 256)
        part = weigh(con_q[rows, :], con_parts, None)
        con_out[rows, :] = merge(part, (cm[rows, :], cs[rows, :]))
    dots = nt(img, con_out[...]).astype(BF)
    con_f = con_out[...].astype(F32)
    con_sq = nt(jnp.ones((16, HD), F32), con_f * con_f, precision=lax.Precision.HIGHEST).astype(BF)
    for s, out in enumerate(outs):
        rows = slice(s * 64, (s + 1) * 64)
        out[0:64, 0:n_con] = dots[rows]
        out[0:64, n_con:] = img[rows]
        out[64:80, 0:n_con] = con_sq
        out[64:80, n_con:] = jnp.zeros((16, HD), BF)


def head_sum_kernel(at, b0, b1, b2, b3, own, core, diag, out_own):
    n_con = b0.shape[1] - HD
    total = jnp.zeros((80, n_con), F32)
    outs = [jnp.zeros((64, HD), BF) for _ in range(3)]
    for s, ref in enumerate((b0, b1, b2, b3)):
        head = at[4] ^ s
        total = total + jnp.where(head < 3, ref[:, 0:n_con].astype(F32), 0.0)
        for h in range(3):
            outs[h] = jnp.where(head == h, ref[0:64, n_con:], outs[h])
    image_sq = jnp.zeros((64, 1), F32)
    for h in range(3):
        out_f = outs[h].astype(F32)
        image_sq = image_sq + jnp.sum(out_f * out_f, axis=1, keepdims=True)
    image_sq = jnp.broadcast_to(image_sq, (64, HD)).astype(BF)
    total = total.astype(BF)
    for ref, row in ((own, 0), (core, 32), (diag, 32)):
        ref[0:32, 0:n_con] = total[row : row + 32]
        ref[32:48, 0:n_con] = total[64:80]
        ref[0:32, n_con : n_con + HD] = image_sq[row : row + 32]
        ref[32:48, n_con : n_con + HD] = jnp.zeros((16, HD), BF)
    for h in range(3):
        lanes = slice(n_con + (1 + h) * HD, n_con + (2 + h) * HD)
        core[0:32, lanes] = outs[h][32:64]
        core[32:48, lanes] = jnp.zeros((16, HD), BF)
        out_own[:, h * HD : (h + 1) * HD] = outs[h][0:32]


def finish_kernel(at, own, core, head, diag, out_own, img_ref, sal_ref):
    n_con = own.shape[1] - HD
    width = 12 * HD
    cols = n_con + HD
    near = own[...].astype(F32) + core[:, 0:cols].astype(F32)
    far = head[...].astype(F32) + diag[...].astype(F32)
    total = near + far
    con_rms = jnp.sqrt(total[32:33, 0:n_con] / width + 1e-06)
    img_rms = jnp.sqrt(total[0:32, n_con : n_con + 1] / width + 1e-06)
    sal = total[0:32, 0:n_con] / (math.sqrt(width) * con_rms * img_rms)
    sal_ref[...] = jnp.transpose(sal)
    half = 3 * HD
    mine = pl.ds(pl.multiple_of(at[2] * half, half), half)
    theirs = pl.ds(pl.multiple_of((1 - at[2]) * half, half), half)
    img_ref[:, mine] = out_own[...]
    img_ref[:, theirs] = core[0:32, cols:]


def packed(
    img_q, img_k, img_v, txt_ids, concept_ids, step_index, token_table, modulation, txt_qkv, qk_gain
):
    n_con, n_txt = concept_ids.shape[0], txt_ids.shape[0]
    ctx = lax.axis_index("ctx")
    g = lax.axis_index("head")
    c = ctx & 1
    y = (ctx >> 1) & 3
    zl = (ctx >> 3) & 1
    x = ctx >> 4
    u = jnp.where(c == 0, x, y)
    v = jnp.where(c == 0, y, x)
    at = jnp.stack([ctx * 2 + g, x * 4 + y, c, 2 * g + zl, u, v]).astype(jnp.int32)
    con_ids, text_ids = concept_ids[None, :], txt_ids[None, :]
    n = n_con + n_txt
    width = token_table.shape[1]
    half = txt_qkv.shape[2] // 2
    n_img = img_q.shape[0]

    own_rows, own_both, plan = call(
        plan_kernel,
        (sds((SLOTS, width)), sds((SLOTS + 16, width)), sds((8, n), jnp.int32)),
        nbytes=2 * MIB,
        flops=10**9,
    )(at, con_ids, text_ids, token_table, img_k, img_v)
    column_rows = [own_both, send(own_both, swap_z(1))]
    column_rows += [send(own_rows, swap_z(s)) for s in (2, 3)]
    other_rows = [send(r, swap_core(0)) for r in column_rows]
    q_core = send(img_q, swap_core(0))

    pack, spots, con_bias, txt_bias = call(
        pack_kernel,
        (
            sds((ROWS, 8 * SLOTS)),
            sds((8, n), jnp.int32),
            sds((1, 16 * CON), F32),
            sds((1, 16 * TXT), F32),
        ),
        nbytes=MIB,
        flops=10**9,
    )(at, con_ids, text_ids, plan)
    owner = concept_ids >> 8
    item_x = owner >> 5
    item_y = (owner >> 2) & 3
    item_u = jnp.where(c == 0, item_x, item_y)
    item_v = jnp.where(c == 0, item_y, item_x)
    con_slot = ((v ^ item_v) * 4 + (u ^ item_u)) * CON + spots[0, :n_con]
    pick = (con_slot[:, None] == jnp.arange(16 * CON)[None, :]).astype(BF)
    shift_scale = lax.dynamic_index_in_dim(modulation, step_index[0], 0, keepdims=False)

    image_blocks = call(
        image_heads_kernel, tuple(sds((10 * n_img, HD)) for _ in range(4)), nbytes=MIB // 2
    )(at, img_q, q_core, own_both, other_rows[0], column_rows[1], other_rows[1])
    image_blocks = [image_blocks[0]] + [send(image_blocks[s], swap_u(s)) for s in (1, 2, 3)]

    qkv = call(
        project_kernel,
        tuple(sds((ROWS + CON // 2, 2 * HD)) for _ in range(4)),
        scratch=(
            pltpu.VMEM((8 * SLOTS, width), BF),
            pltpu.VMEM((ROWS, width), BF),
            pltpu.VMEM((3, width, half), BF),
            pltpu.SemaphoreType.DMA((3,)),
        ),
        nbytes=10 * MIB,
        flops=10**9,
        in_hbm=1,
    )(at, pack, *column_rows, *other_rows, shift_scale, qk_gain, jnp.transpose(txt_qkv, (1, 0, 2)))

    *image_blocks, first = lax.optimization_barrier((*image_blocks, qkv[0]))
    image_q, image_kv = call(
        image_join_kernel, (sds((8 * n_img, HD)), sds((32 * n_img, HD))), nbytes=MIB // 2, smem=0
    )(*image_blocks)
    image_kvs = [image_kv] + [send(image_kv, swap_v(s)) for s in (1, 2, 3)]

    qkv = [first] + [send(qkv[s], swap_u(s)) for s in (1, 2, 3)]
    q_join, kv_join = call(
        join_kernel, (sds((4 * CON, HD)), sds((4 * ROWS, 2 * HD))), nbytes=MIB, smem=0
    )(*qkv)
    q_chunks = [q_join] + [send(q_join, swap_v(s)) for s in (1, 2, 3)]
    kv_chunks = [send(kv_join, swap_v(s)) for s in (1, 2, 3)]

    all_img = 64 * n_img
    keys, vals, *image_stats = call(
        image_self_kernel,
        (
            sds((all_img, HD)),
            sds((all_img, 2 * HD)),
            sds((8 * n_img, 1), F32),
            sds((8 * n_img, 2 * HD), F32),
        ),
        nbytes=4 * MIB,
        flops=10**9,
        smem=0,
    )(*image_kvs, image_q, kv_join, txt_bias)
    con_q, *con_stats = call(
        concept_image_kernel,
        (sds((n_con, HD)), sds((n_con, 1), F32), sds((n_con, 2 * HD), F32)),
        nbytes=8 * MIB,
        flops=3 * 10**9,
        smem=0,
    )(pick, *q_chunks, keys, vals, kv_join, con_bias)
    blocks = call(
        prompt_kernel,
        tuple(sds((80, n_con + HD)) for _ in range(4)),
        scratch=(pltpu.VMEM((n_con, HD), BF),),
        nbytes=10 * MIB,
        flops=2 * 10**9,
        smem=0,
    )(con_bias, txt_bias, *kv_chunks, con_q, *con_stats, image_q, *image_stats)
    blocks = [blocks[0]] + [send(blocks[s], swap_u(s)) for s in (1, 2, 3)]
    own, core, diag, out_own = call(
        head_sum_kernel,
        (sds((48, n_con + HD)), sds((48, n_con + 4 * HD)), sds((48, n_con + HD)), sds((32, half))),
        nbytes=MIB,
    )(at, *blocks)
    last = (
        at,
        own,
        send(core, swap_core(0)),
        send(own, swap_z(2)),
        send(diag, swap_core(1)),
        out_own,
    )
    finish = call(
        finish_kernel, (sds((n_img, 2 * half)), sds((n_con, n_img), F32)), nbytes=MIB
    )
    fits = (plan[1, 0] <= SLOTS) & (spots[1, 0] <= CON) & (spots[2, 0] <= TXT)
    return fits, lambda: tuple(finish(*last))


def on_device(*args):
    fits, finish = packed(*args)
    return lax.cond(fits, finish, lambda: tuple(general(*args)))


def solution(mesh):
    return jax.shard_map(
        on_device,
        mesh=mesh,
        in_specs=(
            P("ctx", "head"),
            P("ctx", "head"),
            P("ctx", "head"),
            P(),
            P(),
            P(),
            P(("ctx", "head"), None),
            P(),
            P(None, None, "head"),
            P(),
        ),
        out_specs=(P("ctx", "head"), P(None, "ctx")),
        check_vma=False,
    )
```

profile of v0, /device:TPU:1, one launch (start us, length us, event | category | flops | bytes accessed | tf_op | source)
XLA Modules:
  0.0 97.4 jit_solution(16712414428626264556)
XLA Ops:
  0.8 2.7 %shard_map.115 = (bf16[32,3072]{1,0:T(8,128)(2,1)S(1)}, bf16[48,3072]{1,0:T(8,128)(2,1)S(1)}, s32[8,1536]{1,0:T(8,128)S(1)}) custom-call(s32[6]{0:T(128)S(1)} %stack.45.at, s32[1,1024]{1,0:T(1,128)} %bitcast.133, s32[1,512]{1,0:T(1,128)} %bitcast.136, bf16[256,3072]{1,0:T(8,128)(2,1)} %table_ref.1, bf16[32,768]{1,0:T(8,128)(2,1)} %k_ref.1, bf16[32,768]{1,0:T(8,128)(2,1)} %v_ref.1), custom_call_target="tpu_custom_call" | custom-call | flops 1000000000 | bytes 2097152 | tf_op jit(solution)/shard_map/pallas_call | solution.py:212
  3.5 2.5 %collective-permute-start.3 = (bf16[48,3072]{1,0:T(8,128)(2,1)S(1)}, bf16[48,3072]{1,0:T(8,128)(2,1)S(1)}, u32[]{:S(2)}, u32[]{:S(2)}) collective-permute-start(bf16[48,3072]{1,0:T(8,128)(2,1)S(1)} %get-tuple-element.93.own.refs_0_), channel_id=1, source_target_pairs={{0,16},{1,17},{2,18},{3,19},{4,20},{5,21},{6,22},{7,23},{8,24},{9,... | collective-permute-start | bytes 884744 | tf_op jit(solution)/shard_map/ppermute | solution.py:197
  6.0 3.3 %collective-permute-start.8 = (bf16[32,3072]{1,0:T(8,128)(2,1)S(1)}, bf16[32,3072]{1,0:T(8,128)(2,1)S(1)}, u32[]{:S(2)}, u32[]{:S(2)}) collective-permute-start(bf16[32,3072]{1,0:T(8,128)(2,1)S(1)} %get-tuple-element.99), channel_id=1, source_target_pairs={{0,1},{1,0},{2,3},{3,2},{4,5},{5,4},{6,7},{7,6},{8,9},{9,8},{10,11... | collective-permute-start | bytes 589832 | tf_op jit(solution)/shard_map/ppermute | solution.py:197
  9.3 1.2 %collective-permute-start.2 = (bf16[48,3072]{1,0:T(8,128)(2,1)S(1)}, bf16[48,3072]{1,0:T(8,128)(2,1)S(1)}, u32[]{:S(2)}, u32[]{:S(2)}) collective-permute-start(bf16[48,3072]{1,0:T(8,128)(2,1)S(1)} %get-tuple-element.93.own.refs_0_), channel_id=1, source_target_pairs={{0,2},{1,3},{2,0},{3,1},{4,6},{5,7},{6,4},{7,5},{8,10},{9,11},{10,... | collective-permute-start | bytes 884744 | tf_op jit(solution)/shard_map/ppermute | solution.py:197
  11.3 8.7 %collective-permute-done.8.refs_2_ = bf16[32,3072]{1,0:T(8,128)(2,1)S(1)} collective-permute-done((bf16[32,3072]{1,0:T(8,128)(2,1)S(1)}, bf16[32,3072]{1,0:T(8,128)(2,1)S(1)}, u32[]{:S(2)}, u32[]{:S(2)}) %collective-permute-start.8) | collective-permute-done | bytes 196640 | tf_op jit(solution)/shard_map/ppermute | solution.py:197
  20.0 1.6 %collective-permute-start.10 = (bf16[32,3072]{1,0:T(8,128)(2,1)S(1)}, bf16[32,3072]{1,0:T(8,128)(2,1)S(1)}, u32[]{:S(2)}, u32[]{:S(2)}) collective-permute-start(bf16[32,3072]{1,0:T(8,128)(2,1)S(1)} %collective-permute-done.8.refs_2_), channel_id=1, source_target_pairs={{0,2},{1,3},{2,0},{3,1},{4,6},{5,7},{6,4},{7,5},{8,10},{9,11},{10,... | collective-permute-start | bytes 589832 | tf_op jit(solution)/shard_map/ppermute | solution.py:197
  22.9 1.2 %shard_map.116 = (bf16[160,256]{1,0:T(8,128)(2,1)S(1)}, s32[8,1536]{1,0:T(8,128)S(1)}, f32[1,1536]{1,0:T(1,128)S(1)}, f32[1,1024]{1,0:T(1,128)S(1)}) custom-call(s32[6]{0:T(128)S(1)} %stack.45.at, s32[1,1024]{1,0:T(1,128)S(1)} %bitcast.134, s32[1,512]{1,0:T(1,128)S(1)} %bitcast.137, s32[8,1536]{1,0:T(8,128)S(1)} %get-tuple-element.89.plan_ref), custom_call_target="tpu_custom_call" | custom-call | flops 1000000000 | bytes 1048576 | tf_op jit(solution)/shard_map/pallas_call | solution.py:212
  24.7 1.4 %collective-permute-start.5 = (bf16[320,128]{1,0:T(8,128)(2,1)S(1)}, bf16[320,128]{1,0:T(8,128)(2,1)S(1)}, u32[]{:S(2)}, u32[]{:S(2)}) collective-permute-start(bf16[320,128]{1,0:T(8,128)(2,1)S(1)} %get-tuple-element.95), channel_id=1, source_target_pairs={{0,32},{1,33},{2,6},{3,7},{4,36},{5,37},{6,2},{7,3},{8,40},{9,41},... | collective-permute-start | bytes 245768 | tf_op jit(solution)/shard_map/ppermute | solution.py:197
  26.1 4.7 %shard_map.118 = (bf16[208,256]{1,0:T(8,128)(2,1)S(1)}, bf16[208,256]{1,0:T(8,128)(2,1)S(1)}, bf16[208,256]{1,0:T(8,128)(2,1)S(1)}, bf16[208,256]{1,0:T(8,128)(2,1)S(1)}) custom-call(s32[6]{0:T(128)S(1)} %stack.45.at, bf16[160,256]{1,0:T(8,128)(2,1)S(1)} %get-tuple-element.98.pack_ref, bf16[48,3072]{1,0:T(8,128)(2,1)S(1)} %get-tuple-element.93.own.refs_0_, ...), custom_call_target="tpu_custom_call" | custom-call | flops 1000000000 | bytes 10485760 | tf_op jit(solution)/shard_map/pallas_call | solution.py:212
  31.1 2.9 %collective-permute-start.13 = (bf16[208,256]{1,0:T(8,128)(2,1)S(1)}, bf16[208,256]{1,0:T(8,128)(2,1)S(1)}, u32[]{:S(2)}, u32[]{:S(2)}) collective-permute-start(bf16[208,256]{1,0:T(8,128)(2,1)S(1)} %get-tuple-element.103), channel_id=1, source_target_pairs={{0,64},{1,65},{2,10},{3,11},{4,68},{5,69},{6,14},{7,15},{8,72},{9,... | collective-permute-start | bytes 319496 | tf_op jit(solution)/shard_map/ppermute | solution.py:197
  34.8 1.4 %collective-permute-start.6 = (bf16[320,128]{1,0:T(8,128)(2,1)S(1)}, bf16[320,128]{1,0:T(8,128)(2,1)S(1)}, u32[]{:S(2)}, u32[]{:S(2)}) collective-permute-start(bf16[320,128]{1,0:T(8,128)(2,1)S(1)} %get-tuple-element.96), channel_id=1, source_target_pairs={{0,64},{1,65},{2,10},{3,11},{4,68},{5,69},{6,14},{7,15},{8,72},{9,... | collective-permute-start | bytes 245768 | tf_op jit(solution)/shard_map/ppermute | solution.py:197
  36.8 2.8 %collective-permute-done.6.c = bf16[320,128]{1,0:T(8,128)(2,1)S(1)} collective-permute-done((bf16[320,128]{1,0:T(8,128)(2,1)S(1)}, bf16[320,128]{1,0:T(8,128)(2,1)S(1)}, u32[]{:S(2)}, u32[]{:S(2)}) %collective-permute-start.6) | collective-permute-done | bytes 81952 | tf_op jit(solution)/shard_map/ppermute | solution.py:197
  39.6 1.3 %collective-permute-done.7.d = bf16[320,128]{1,0:T(8,128)(2,1)S(1)} collective-permute-done((bf16[320,128]{1,0:T(8,128)(2,1)S(1)}, bf16[320,128]{1,0:T(8,128)(2,1)S(1)}, u32[]{:S(2)}, u32[]{:S(2)}) %collective-permute-start.7) | collective-permute-done | bytes 81952 | tf_op jit(solution)/shard_map/ppermute | solution.py:197
  42.7 2.5 %collective-permute-start.22 = (bf16[1024,128]{1,0:T(8,128)(2,1)S(1)}, bf16[1024,128]{1,0:T(8,128)(2,1)S(1)}, u32[]{:S(2)}, u32[]{:S(2)}) collective-permute-start(bf16[1024,128]{1,0:T(8,128)(2,1)S(1)} %get-tuple-element.111.i0), channel_id=1, source_target_pairs={{0,8},{1,9},{2,66},{3,67},{4,12},{5,13},{6,70},{7,71},{8,0},{9,1},... | collective-permute-start | bytes 786440 | tf_op jit(solution)/shard_map/ppermute | solution.py:197
  46.0 1.5 %collective-permute-start.19 = (bf16[384,128]{1,0:T(8,128)(2,1)S(1)}, bf16[384,128]{1,0:T(8,128)(2,1)S(1)}, u32[]{:S(2)}, u32[]{:S(2)}) collective-permute-start(bf16[384,128]{1,0:T(8,128)(2,1)S(1)} %get-tuple-element.106.q0), channel_id=1, source_target_pairs={{0,8},{1,9},{2,66},{3,67},{4,12},{5,13},{6,70},{7,71},{8,0},{9,1},... | collective-permute-start | bytes 294920 | tf_op jit(solution)/shard_map/ppermute | solution.py:197
  48.2 2.2 %fusion.81.pick = bf16[1024,1536]{1,0:T(8,128)(2,1)} fusion(s32[1024]{0:T(1024)S(1)} %multiply_add_fusion), kind=kLoop, calls=%fused_computation.115 | loop fusion | flops 3145728 | bytes 3149824 | tf_op jit(solution)/shard_map/convert_element_type | solution.py:583
  50.9 1.6 %collective-permute-done.22.i2 = bf16[1024,128]{1,0:T(8,128)(2,1)S(1)} collective-permute-done((bf16[1024,128]{1,0:T(8,128)(2,1)S(1)}, bf16[1024,128]{1,0:T(8,128)(2,1)S(1)}, u32[]{:S(2)}, u32[]{:S(2)}) %collective-permute-start.22) | collective-permute-done | bytes 262176 | tf_op jit(solution)/shard_map/ppermute | solution.py:197
  52.5 1.1 %collective-permute-start.16 = (bf16[640,256]{1,0:T(8,128)(2,1)S(1)}, bf16[640,256]{1,0:T(8,128)(2,1)S(1)}, u32[]{:S(2)}, u32[]{:S(2)}) collective-permute-start(bf16[640,256]{1,0:T(8,128)(2,1)S(1)} %get-tuple-element.105.kv), channel_id=1, source_target_pairs={{0,8},{1,9},{2,66},{3,67},{4,12},{5,13},{6,70},{7,71},{8,0},{9,1},... | collective-permute-start | bytes 983048 | tf_op jit(solution)/shard_map/ppermute | solution.py:197
  53.6 2.1 %collective-permute-done.23.i3 = bf16[1024,128]{1,0:T(8,128)(2,1)S(1)} collective-permute-done((bf16[1024,128]{1,0:T(8,128)(2,1)S(1)}, bf16[1024,128]{1,0:T(8,128)(2,1)S(1)}, u32[]{:S(2)}, u32[]{:S(2)}) %collective-permute-start.23) | collective-permute-done | bytes 262176 | tf_op jit(solution)/shard_map/ppermute | solution.py:197
  56.6 1.6 %shard_map.121 = (bf16[2048,128]{1,0:T(8,128)(2,1)S(1)}, bf16[2048,256]{1,0:T(8,128)(2,1)S(1)}, f32[256,1]{1,0:T(8,128)S(1)}, f32[256,256]{1,0:T(8,128)S(1)}) custom-call(bf16[1024,128]{1,0:T(8,128)(2,1)S(1)} %get-tuple-element.111.i0, bf16[1024,128]{1,0:T(8,128)(2,1)S(1)} %collective-permute-done.21.i1, bf16[1024,128]{1,0:T(8,128)(2,1)S(1)} %collective-permute-done.22.i2, ...), custom_call_target="tpu_custom_call" | custom-call | flops 1000000000 | bytes 4194304 | tf_op jit(solution)/shard_map/pallas_call | solution.py:212
  58.2 6.6 %shard_map.122 = (bf16[1024,128]{1,0:T(8,128)(2,1)S(1)}, f32[1024,1]{1,0:T(8,128)S(1)}, f32[1024,256]{1,0:T(8,128)S(1)}) custom-call(bf16[1024,1536]{1,0:T(8,128)(2,1)} %fusion.81.pick, bf16[384,128]{1,0:T(8,128)(2,1)S(1)} %get-tuple-element.106.q0, bf16[384,128]{1,0:T(8,128)(2,1)S(1)} %collective-permute-done.18.q1, ...), custom_call_target="tpu_custom_call" | custom-call | flops 3000000000 | bytes 8388608 | tf_op jit(solution)/shard_map/pallas_call | solution.py:212
  65.4 3.1 %shard_map.123 = (bf16[80,1152]{1,0:T(8,128)(2,1)S(1)}, bf16[80,1152]{1,0:T(8,128)(2,1)S(1)}, bf16[80,1152]{1,0:T(8,128)(2,1)S(1)}, bf16[80,1152]{1,0:T(8,128)(2,1)S(1)}) custom-call(f32[1,1536]{1,0:T(1,128)S(1)} %get-tuple-element.91.bias.con_bias, f32[1,1024]{1,0:T(1,128)S(1)} %get-tuple-element.92.bias.txt_bias, ...), custom_call_target="tpu_custom_call" | custom-call | flops 2000000000 | bytes 10485760 | tf_op jit(solution)/shard_map/pallas_call | solution.py:212
  68.5 2.4 %collective-permute-start.25 = (bf16[80,1152]{1,0:T(8,128)(2,1)S(1)}, bf16[80,1152]{1,0:T(8,128)(2,1)S(1)}, u32[]{:S(2)}, u32[]{:S(2)}) collective-permute-start(bf16[80,1152]{1,0:T(8,128)(2,1)S(1)} %get-tuple-element.122), channel_id=1, source_target_pairs={{0,64},{1,65},{2,10},{3,11},{4,68},{5,69},{6,14},{7,15},{8,72},{9,... | collective-permute-start | bytes 552968 | tf_op jit(solution)/shard_map/ppermute | solution.py:197
  70.9 1.5 %collective-permute-start.26 = (bf16[80,1152]{1,0:T(8,128)(2,1)S(1)}, bf16[80,1152]{1,0:T(8,128)(2,1)S(1)}, u32[]{:S(2)}, u32[]{:S(2)}) collective-permute-start(bf16[80,1152]{1,0:T(8,128)(2,1)S(1)} %get-tuple-element.123), channel_id=1, source_target_pairs={{0,96},{1,97},{2,14},{3,15},{4,100},{5,101},{6,10},{7,11},{8,104},... | collective-permute-start | bytes 552968 | tf_op jit(solution)/shard_map/ppermute | solution.py:197
  73.0 3.0 %collective-permute-done.25.b2 = bf16[80,1152]{1,0:T(8,128)(2,1)S(1)} collective-permute-done((bf16[80,1152]{1,0:T(8,128)(2,1)S(1)}, bf16[80,1152]{1,0:T(8,128)(2,1)S(1)}, u32[]{:S(2)}, u32[]{:S(2)}) %collective-permute-start.25) | collective-permute-done | bytes 184352 | tf_op jit(solution)/shard_map/ppermute | solution.py:197
  75.9 1.9 %collective-permute-done.26.b3 = bf16[80,1152]{1,0:T(8,128)(2,1)S(1)} collective-permute-done((bf16[80,1152]{1,0:T(8,128)(2,1)S(1)}, bf16[80,1152]{1,0:T(8,128)(2,1)S(1)}, u32[]{:S(2)}, u32[]{:S(2)}) %collective-permute-start.26) | collective-permute-done | bytes 184352 | tf_op jit(solution)/shard_map/ppermute | solution.py:197
  77.8 1.3 %shard_map.124 = (bf16[48,1152]{1,0:T(8,128)(2,1)S(1)}, bf16[48,1536]{1,0:T(8,128)(2,1)S(1)}, bf16[48,1152]{1,0:T(8,128)(2,1)S(1)}, bf16[32,384]{1,0:T(8,128)(2,1)}) custom-call(s32[6]{0:T(128)S(1)} %stack.45.at, bf16[80,1152]{1,0:T(8,128)(2,1)S(1)} %get-tuple-element.120.b0, bf16[80,1152]{1,0:T(8,128)(2,1)S(1)} %collective-permute-done.24.b1, ...), custom_call_target="tpu_custom_call" | custom-call | bytes 1048576 | tf_op jit(solution)/shard_map/pallas_call | solution.py:212
  79.2 6.4 %collective-permute-start.27 = (bf16[48,1536]{1,0:T(8,128)(2,1)S(1)}, bf16[48,1536]{1,0:T(8,128)(2,1)S(1)}, u32[]{:S(2)}, u32[]{:S(2)}) collective-permute-start(bf16[48,1536]{1,0:T(8,128)(2,1)S(1)} %get-tuple-element.125), channel_id=1, source_target_pairs={{0,2},{1,3},{2,0},{3,1},{4,6},{5,7},{6,4},{7,5},{8,10},{9,11},{10,... | collective-permute-start | bytes 442376 | tf_op jit(solution)/shard_map/ppermute | solution.py:197
  86.1 3.1 %collective-permute-start.29 = (bf16[48,1152]{1,0:T(8,128)(2,1)S(1)}, bf16[48,1152]{1,0:T(8,128)(2,1)S(1)}, u32[]{:S(2)}, u32[]{:S(2)}) collective-permute-start(bf16[48,1152]{1,0:T(8,128)(2,1)S(1)} %get-tuple-element.126), channel_id=1, source_target_pairs={{0,3},{1,2},{2,1},{3,0},{4,7},{5,6},{6,5},{7,4},{8,11},{9,10},{10,... | collective-permute-start | bytes 331784 | tf_op jit(solution)/shard_map/ppermute | solution.py:197
  92.3 2.5 %collective-permute-done.29 = bf16[48,1152]{1,0:T(8,128)(2,1)S(1)} collective-permute-done((bf16[48,1152]{1,0:T(8,128)(2,1)S(1)}, bf16[48,1152]{1,0:T(8,128)(2,1)S(1)}, u32[]{:S(2)}, u32[]{:S(2)}) %collective-permute-start.29) | collective-permute-done | bytes 110624 | tf_op jit(solution)/shard_map/ppermute | solution.py:197
  94.8 2.7 %conditional.1 = (bf16[32,768]{1,0:T(8,128)(2,1)}, f32[1024,32]{0,1:T(8,128)}) conditional(s32[]{:T(128)} %bitcast.34, (s32[512]{0:T(512)S(1)}, s32[1024]{0:T(1024)S(1)}, bf16[256,3072]{1,0:T(8,128)(2,1)S(1)}, s32[1]{0:T(128)}, f32[28,2,3072]{2,1,0:T(2,128)}, /*index=5*/bf16[3072,3,768]{2,0,1:T(8,128)(2,1)}, f32[2,128]{1,0:T(2,128)S(1)}, ...), branch_computations={%region_0.15_spmd, %region_15.16_spmd} | conditional | flops 778344960 | bytes 257951312 | solution.py:669
  95.0 1.6 %branch_1_fun.1 = (bf16[32,768]{1,0:T(8,128)(2,1)}, f32[1024,32]{1,0:T(8,128)S(1)}) custom-call(s32[6]{0:T(128)S(1)} %get-tuple-element.42.at, bf16[48,1152]{1,0:T(8,128)(2,1)S(1)} %get-tuple-element.43.own, bf16[48,1536]{1,0:T(8,128)(2,1)S(1)} %get-tuple-element.44.core, bf16[48,1152]{1,0:T(8,128)(2,1)S(1)} %get-tuple-element.45.head, ...), custom_call_target="tpu_custom_call" | custom-call | bytes 1048576 | tf_op jit(solution)/shard_map/cond/branch_1_fun/pallas_call | solution.py:212
  (60 shorter events, 11.8 us)
Async XLA Ops:
  3.5 18.6 %collective-permute-start.3 = (bf16[48,3072]{1,0:T(8,128)(2,1)S(1)}, bf16[48,3072]{1,0:T(8,128)(2,1)S(1)}, u32[]{:S(2)}, u32[]{:S(2)}) collective-permute-start(bf16[48,3072]{1,0:T(8,128)(2,1)S(1)} %get-tuple-element.93.own.refs_0_), channel_id=1, source_target_pairs={{0,16},{1,17},{2,18},{3,19},{4,20},{5,21},{6,22},{7,23},{8,24},{9,... | collective-permute-start | bytes 884744 | tf_op jit(solution)/shard_map/ppermute | solution.py:197
  6.0 14.0 %collective-permute-start.8 = (bf16[32,3072]{1,0:T(8,128)(2,1)S(1)}, bf16[32,3072]{1,0:T(8,128)(2,1)S(1)}, u32[]{:S(2)}, u32[]{:S(2)}) collective-permute-start(bf16[32,3072]{1,0:T(8,128)(2,1)S(1)} %get-tuple-element.99), channel_id=1, source_target_pairs={{0,1},{1,0},{2,3},{3,2},{4,5},{5,4},{6,7},{7,6},{8,9},{9,8},{10,11... | collective-permute-start | bytes 589832 | tf_op jit(solution)/shard_map/ppermute | solution.py:197
  9.3 12.3 %collective-permute-start.9 = (bf16[32,3072]{1,0:T(8,128)(2,1)S(1)}, bf16[32,3072]{1,0:T(8,128)(2,1)S(1)}, u32[]{:S(2)}, u32[]{:S(2)}) collective-permute-start(bf16[32,3072]{1,0:T(8,128)(2,1)S(1)} %get-tuple-element.99), channel_id=1, source_target_pairs={{0,17},{1,16},{2,19},{3,18},{4,21},{5,20},{6,23},{7,22},{8,25},{9,... | collective-permute-start | bytes 589832 | tf_op jit(solution)/shard_map/ppermute | solution.py:197
  9.3 14.7 %collective-permute-start.2 = (bf16[48,3072]{1,0:T(8,128)(2,1)S(1)}, bf16[48,3072]{1,0:T(8,128)(2,1)S(1)}, u32[]{:S(2)}, u32[]{:S(2)}) collective-permute-start(bf16[48,3072]{1,0:T(8,128)(2,1)S(1)} %get-tuple-element.93.own.refs_0_), channel_id=1, source_target_pairs={{0,2},{1,3},{2,0},{3,1},{4,6},{5,7},{6,4},{7,5},{8,10},{9,11},{10,... | collective-permute-start | bytes 884744 | tf_op jit(solution)/shard_map/ppermute | solution.py:197
  10.6 13.5 %collective-permute-start.1 = (bf16[32,768]{1,0:T(8,128)(2,1)S(1)}, bf16[32,768]{1,0:T(8,128)(2,1)S(1)}, u32[]{:S(2)}, u32[]{:S(2)}) collective-permute-start(bf16[32,768]{1,0:T(8,128)(2,1)S(1)} %copy-done.2), channel_id=1, source_target_pairs={{0,2},{1,3},{2,0},{3,1},{4,6},{5,7},{6,4},{7,5},{8,10},{9,11},{10,... | collective-permute-start | bytes 147464 | tf_op jit(solution)/shard_map/ppermute | solution.py:197
  20.0 6.1 %collective-permute-start.10 = (bf16[32,3072]{1,0:T(8,128)(2,1)S(1)}, bf16[32,3072]{1,0:T(8,128)(2,1)S(1)}, u32[]{:S(2)}, u32[]{:S(2)}) collective-permute-start(bf16[32,3072]{1,0:T(8,128)(2,1)S(1)} %collective-permute-done.8.refs_2_), channel_id=1, source_target_pairs={{0,2},{1,3},{2,0},{3,1},{4,6},{5,7},{6,4},{7,5},{8,10},{9,11},{10,... | collective-permute-start | bytes 589832 | tf_op jit(solution)/shard_map/ppermute | solution.py:197
  21.6 4.5 %collective-permute-start.11 = (bf16[32,3072]{1,0:T(8,128)(2,1)S(1)}, bf16[32,3072]{1,0:T(8,128)(2,1)S(1)}, u32[]{:S(2)}, u32[]{:S(2)}) collective-permute-start(bf16[32,3072]{1,0:T(8,128)(2,1)S(1)} %collective-permute-done.9.refs_3_), channel_id=1, source_target_pairs={{0,2},{1,3},{2,0},{3,1},{4,6},{5,7},{6,4},{7,5},{8,10},{9,11},{10,... | collective-permute-start | bytes 589832 | tf_op jit(solution)/shard_map/ppermute | solution.py:197
  22.1 2.0 %collective-permute-start.4 = (bf16[48,3072]{1,0:T(8,128)(2,1)S(1)}, bf16[48,3072]{1,0:T(8,128)(2,1)S(1)}, u32[]{:S(2)}, u32[]{:S(2)}) collective-permute-start(bf16[48,3072]{1,0:T(8,128)(2,1)S(1)} %collective-permute-done.3.zl.refs_1_), channel_id=1, source_target_pairs={{0,2},{1,3},{2,0},{3,1},{4,6},{5,7},{6,4},{7,5},{8,10},{9,11},{10,... | collective-permute-start | bytes 884744 | tf_op jit(solution)/shard_map/ppermute | solution.py:197
  24.7 11.5 %collective-permute-start.5 = (bf16[320,128]{1,0:T(8,128)(2,1)S(1)}, bf16[320,128]{1,0:T(8,128)(2,1)S(1)}, u32[]{:S(2)}, u32[]{:S(2)}) collective-permute-start(bf16[320,128]{1,0:T(8,128)(2,1)S(1)} %get-tuple-element.95), channel_id=1, source_target_pairs={{0,32},{1,33},{2,6},{3,7},{4,36},{5,37},{6,2},{7,3},{8,40},{9,41},... | collective-permute-start | bytes 245768 | tf_op jit(solution)/shard_map/ppermute | solution.py:197
  30.8 10.2 %collective-permute-start.12 = (bf16[208,256]{1,0:T(8,128)(2,1)S(1)}, bf16[208,256]{1,0:T(8,128)(2,1)S(1)}, u32[]{:S(2)}, u32[]{:S(2)}) collective-permute-start(bf16[208,256]{1,0:T(8,128)(2,1)S(1)} %get-tuple-element.102), channel_id=1, source_target_pairs={{0,32},{1,33},{2,6},{3,7},{4,36},{5,37},{6,2},{7,3},{8,40},{9,41},... | collective-permute-start | bytes 319496 | tf_op jit(solution)/shard_map/ppermute | solution.py:197
  31.1 9.9 %collective-permute-start.13 = (bf16[208,256]{1,0:T(8,128)(2,1)S(1)}, bf16[208,256]{1,0:T(8,128)(2,1)S(1)}, u32[]{:S(2)}, u32[]{:S(2)}) collective-permute-start(bf16[208,256]{1,0:T(8,128)(2,1)S(1)} %get-tuple-element.103), channel_id=1, source_target_pairs={{0,64},{1,65},{2,10},{3,11},{4,68},{5,69},{6,14},{7,15},{8,72},{9,... | collective-permute-start | bytes 319496 | tf_op jit(solution)/shard_map/ppermute | solution.py:197
  34.0 7.0 %collective-permute-start.14 = (bf16[208,256]{1,0:T(8,128)(2,1)S(1)}, bf16[208,256]{1,0:T(8,128)(2,1)S(1)}, u32[]{:S(2)}, u32[]{:S(2)}) collective-permute-start(bf16[208,256]{1,0:T(8,128)(2,1)S(1)} %get-tuple-element.104), channel_id=1, source_target_pairs={{0,96},{1,97},{2,14},{3,15},{4,100},{5,101},{6,10},{7,11},{8,104},... | collective-permute-start | bytes 319496 | tf_op jit(solution)/shard_map/ppermute | solution.py:197
  34.8 4.9 %collective-permute-start.6 = (bf16[320,128]{1,0:T(8,128)(2,1)S(1)}, bf16[320,128]{1,0:T(8,128)(2,1)S(1)}, u32[]{:S(2)}, u32[]{:S(2)}) collective-permute-start(bf16[320,128]{1,0:T(8,128)(2,1)S(1)} %get-tuple-element.96), channel_id=1, source_target_pairs={{0,64},{1,65},{2,10},{3,11},{4,68},{5,69},{6,14},{7,15},{8,72},{9,... | collective-permute-start | bytes 245768 | tf_op jit(solution)/shard_map/ppermute | solution.py:197
  36.2 4.8 %collective-permute-start.7 = (bf16[320,128]{1,0:T(8,128)(2,1)S(1)}, bf16[320,128]{1,0:T(8,128)(2,1)S(1)}, u32[]{:S(2)}, u32[]{:S(2)}) collective-permute-start(bf16[320,128]{1,0:T(8,128)(2,1)S(1)} %get-tuple-element.97), channel_id=1, source_target_pairs={{0,96},{1,97},{2,14},{3,15},{4,100},{5,101},{6,10},{7,11},{8,104},... | collective-permute-start | bytes 245768 | tf_op jit(solution)/shard_map/ppermute | solution.py:197
  41.1 6.5 %collective-permute-start.18 = (bf16[384,128]{1,0:T(8,128)(2,1)S(1)}, bf16[384,128]{1,0:T(8,128)(2,1)S(1)}, u32[]{:S(2)}, u32[]{:S(2)}) collective-permute-start(bf16[384,128]{1,0:T(8,128)(2,1)S(1)} %get-tuple-element.106.q0), channel_id=1, source_target_pairs={{0,4},{1,5},{2,34},{3,35},{4,0},{5,1},{6,38},{7,39},{8,12},{9,13},... | collective-permute-start | bytes 294920 | tf_op jit(solution)/shard_map/ppermute | solution.py:197
  42.1 8.3 %collective-permute-start.21 = (bf16[1024,128]{1,0:T(8,128)(2,1)S(1)}, bf16[1024,128]{1,0:T(8,128)(2,1)S(1)}, u32[]{:S(2)}, u32[]{:S(2)}) collective-permute-start(bf16[1024,128]{1,0:T(8,128)(2,1)S(1)} %get-tuple-element.111.i0), channel_id=1, source_target_pairs={{0,4},{1,5},{2,34},{3,35},{4,0},{5,1},{6,38},{7,39},{8,12},{9,13},... | collective-permute-start | bytes 786440 | tf_op jit(solution)/shard_map/ppermute | solution.py:197
  42.7 9.8 %collective-permute-start.22 = (bf16[1024,128]{1,0:T(8,128)(2,1)S(1)}, bf16[1024,128]{1,0:T(8,128)(2,1)S(1)}, u32[]{:S(2)}, u32[]{:S(2)}) collective-permute-start(bf16[1024,128]{1,0:T(8,128)(2,1)S(1)} %get-tuple-element.111.i0), channel_id=1, source_target_pairs={{0,8},{1,9},{2,66},{3,67},{4,12},{5,13},{6,70},{7,71},{8,0},{9,1},... | collective-permute-start | bytes 786440 | tf_op jit(solution)/shard_map/ppermute | solution.py:197
  45.2 10.6 %collective-permute-start.23 = (bf16[1024,128]{1,0:T(8,128)(2,1)S(1)}, bf16[1024,128]{1,0:T(8,128)(2,1)S(1)}, u32[]{:S(2)}, u32[]{:S(2)}) collective-permute-start(bf16[1024,128]{1,0:T(8,128)(2,1)S(1)} %get-tuple-element.111.i0), channel_id=1, source_target_pairs={{0,12},{1,13},{2,98},{3,99},{4,8},{5,9},{6,102},{7,103},{8,4},{9,5... | collective-permute-start | bytes 786440 | tf_op jit(solution)/shard_map/ppermute | solution.py:197
  46.0 12.2 %collective-permute-start.19 = (bf16[384,128]{1,0:T(8,128)(2,1)S(1)}, bf16[384,128]{1,0:T(8,128)(2,1)S(1)}, u32[]{:S(2)}, u32[]{:S(2)}) collective-permute-start(bf16[384,128]{1,0:T(8,128)(2,1)S(1)} %get-tuple-element.106.q0), channel_id=1, source_target_pairs={{0,8},{1,9},{2,66},{3,67},{4,12},{5,13},{6,70},{7,71},{8,0},{9,1},... | collective-permute-start | bytes 294920 | tf_op jit(solution)/shard_map/ppermute | solution.py:197
  47.6 10.6 %collective-permute-start.20 = (bf16[384,128]{1,0:T(8,128)(2,1)S(1)}, bf16[384,128]{1,0:T(8,128)(2,1)S(1)}, u32[]{:S(2)}, u32[]{:S(2)}) collective-permute-start(bf16[384,128]{1,0:T(8,128)(2,1)S(1)} %get-tuple-element.106.q0), channel_id=1, source_target_pairs={{0,12},{1,13},{2,98},{3,99},{4,8},{5,9},{6,102},{7,103},{8,4},{9,5... | collective-permute-start | bytes 294920 | tf_op jit(solution)/shard_map/ppermute | solution.py:197
  50.4 14.4 %collective-permute-start.15 = (bf16[640,256]{1,0:T(8,128)(2,1)S(1)}, bf16[640,256]{1,0:T(8,128)(2,1)S(1)}, u32[]{:S(2)}, u32[]{:S(2)}) collective-permute-start(bf16[640,256]{1,0:T(8,128)(2,1)S(1)} %get-tuple-element.105.kv), channel_id=1, source_target_pairs={{0,4},{1,5},{2,34},{3,35},{4,0},{5,1},{6,38},{7,39},{8,12},{9,13},... | collective-permute-start | bytes 983048 | tf_op jit(solution)/shard_map/ppermute | solution.py:197
  52.5 12.3 %collective-permute-start.16 = (bf16[640,256]{1,0:T(8,128)(2,1)S(1)}, bf16[640,256]{1,0:T(8,128)(2,1)S(1)}, u32[]{:S(2)}, u32[]{:S(2)}) collective-permute-start(bf16[640,256]{1,0:T(8,128)(2,1)S(1)} %get-tuple-element.105.kv), channel_id=1, source_target_pairs={{0,8},{1,9},{2,66},{3,67},{4,12},{5,13},{6,70},{7,71},{8,0},{9,1},... | collective-permute-start | bytes 983048 | tf_op jit(solution)/shard_map/ppermute | solution.py:197
  55.8 9.7 %collective-permute-start.17 = (bf16[640,256]{1,0:T(8,128)(2,1)S(1)}, bf16[640,256]{1,0:T(8,128)(2,1)S(1)}, u32[]{:S(2)}, u32[]{:S(2)}) collective-permute-start(bf16[640,256]{1,0:T(8,128)(2,1)S(1)} %get-tuple-element.105.kv), channel_id=1, source_target_pairs={{0,12},{1,13},{2,98},{3,99},{4,8},{5,9},{6,102},{7,103},{8,4},{9,5... | collective-permute-start | bytes 983048 | tf_op jit(solution)/shard_map/ppermute | solution.py:197
  65.4 29.3 %copy-start = (bf16[256,3072]{1,0:T(8,128)(2,1)S(1)}, bf16[256,3072]{1,0:T(8,128)(2,1)}, u32[]{:S(2)}) copy-start(bf16[256,3072]{1,0:T(8,128)(2,1)} %table_ref.1) | copy-start | bytes 4718596
  65.4 29.3 %copy-start.6 = (bf16[32,768]{1,0:T(8,128)(2,1)S(1)}, bf16[32,768]{1,0:T(8,128)(2,1)}, u32[]{:S(2)}) copy-start(bf16[32,768]{1,0:T(8,128)(2,1)} %k_ref.1) | copy-start | bytes 147460
  65.4 29.3 %copy-start.7 = (bf16[32,768]{1,0:T(8,128)(2,1)S(1)}, bf16[32,768]{1,0:T(8,128)(2,1)}, u32[]{:S(2)}) copy-start(bf16[32,768]{1,0:T(8,128)(2,1)} %v_ref.1) | copy-start | bytes 147460
  68.5 4.4 %collective-permute-start.24 = (bf16[80,1152]{1,0:T(8,128)(2,1)S(1)}, bf16[80,1152]{1,0:T(8,128)(2,1)S(1)}, u32[]{:S(2)}, u32[]{:S(2)}) collective-permute-start(bf16[80,1152]{1,0:T(8,128)(2,1)S(1)} %get-tuple-element.121), channel_id=1, source_target_pairs={{0,32},{1,33},{2,6},{3,7},{4,36},{5,37},{6,2},{7,3},{8,40},{9,41},... | collective-permute-start | bytes 552968 | tf_op jit(solution)/shard_map/ppermute | solution.py:197
  68.5 7.4 %collective-permute-start.25 = (bf16[80,1152]{1,0:T(8,128)(2,1)S(1)}, bf16[80,1152]{1,0:T(8,128)(2,1)S(1)}, u32[]{:S(2)}, u32[]{:S(2)}) collective-permute-start(bf16[80,1152]{1,0:T(8,128)(2,1)S(1)} %get-tuple-element.122), channel_id=1, source_target_pairs={{0,64},{1,65},{2,10},{3,11},{4,68},{5,69},{6,14},{7,15},{8,72},{9,... | collective-permute-start | bytes 552968 | tf_op jit(solution)/shard_map/ppermute | solution.py:197
  70.9 6.9 %collective-permute-start.26 = (bf16[80,1152]{1,0:T(8,128)(2,1)S(1)}, bf16[80,1152]{1,0:T(8,128)(2,1)S(1)}, u32[]{:S(2)}, u32[]{:S(2)}) collective-permute-start(bf16[80,1152]{1,0:T(8,128)(2,1)S(1)} %get-tuple-element.123), channel_id=1, source_target_pairs={{0,96},{1,97},{2,14},{3,15},{4,100},{5,101},{6,10},{7,11},{8,104},... | collective-permute-start | bytes 552968 | tf_op jit(solution)/shard_map/ppermute | solution.py:197
  79.2 15.6 %collective-permute-start.27 = (bf16[48,1536]{1,0:T(8,128)(2,1)S(1)}, bf16[48,1536]{1,0:T(8,128)(2,1)S(1)}, u32[]{:S(2)}, u32[]{:S(2)}) collective-permute-start(bf16[48,1536]{1,0:T(8,128)(2,1)S(1)} %get-tuple-element.125), channel_id=1, source_target_pairs={{0,2},{1,3},{2,0},{3,1},{4,6},{5,7},{6,4},{7,5},{8,10},{9,11},{10,... | collective-permute-start | bytes 442376 | tf_op jit(solution)/shard_map/ppermute | solution.py:197
  86.1 6.2 %collective-permute-start.28 = (bf16[48,1152]{1,0:T(8,128)(2,1)S(1)}, bf16[48,1152]{1,0:T(8,128)(2,1)S(1)}, u32[]{:S(2)}, u32[]{:S(2)}) collective-permute-start(bf16[48,1152]{1,0:T(8,128)(2,1)S(1)} %get-tuple-element.124), channel_id=1, source_target_pairs={{0,1},{1,0},{2,3},{3,2},{4,5},{5,4},{6,7},{7,6},{8,9},{9,8},{10,11... | collective-permute-start | bytes 331784 | tf_op jit(solution)/shard_map/ppermute | solution.py:197
  86.1 8.7 %collective-permute-start.29 = (bf16[48,1152]{1,0:T(8,128)(2,1)S(1)}, bf16[48,1152]{1,0:T(8,128)(2,1)S(1)}, u32[]{:S(2)}, u32[]{:S(2)}) collective-permute-start(bf16[48,1152]{1,0:T(8,128)(2,1)S(1)} %get-tuple-element.126), channel_id=1, source_target_pairs={{0,3},{1,2},{2,1},{3,0},{4,7},{5,6},{6,5},{7,4},{8,11},{9,10},{10,... | collective-permute-start | bytes 331784 | tf_op jit(solution)/shard_map/ppermute | solution.py:197
  (4 other events, 77.0 us)
where the time goes:
time: 97.8 us; the launch traced here: 97.4 us
  starting transfers between devices  39.6 us (40%)
  waiting for transfers between devices  25.6 us (26%)
  Pallas kernels  23.5 us (24%)
  between operations  3.47 us (4%)
  local copies, waits for them, and re-layouts  2.79 us (3%)
  other arithmetic  2.22 us (2%)
    ppermute x29, starting transfers between devices, send(): return lax.ppermute(array, ('ctx', 'head'), pairing)  39.6 us
    ppermute x29, waiting for transfers between devices, send(): return lax.ppermute(array, ('ctx', 'head'), pairing)  25.6 us
    pallas_call x11, Pallas kernels, run(): pl.pallas_call(kernel, out_shape=outs, in_specs=[sm] * smem + [vm] * (len...  23.5 us
    convert_element_type x1, other arithmetic, packed(): pick = (con_slot[:, None] == jnp.arange(16 * CON)[None, :]).astype(BF)  2.2 us
  transfers between devices with their start and end apart: 29, of which 11 were waited for; matrix products, arithmetic and copies ran while one was open for 4% of the time, Pallas kernels for 15%

commit v1 on v0

--- a/solution.py
+++ b/solution.py
@@ -15,6 +15,7 @@
 TXT = 64
 ROWS = CON + TXT
 MIB = 1 << 20
+NEAR_US, FAR_US, PROJ_US, PROMPT_US = 5.0, 4.0, 5.0, 3.0
 FACTOR = HD ** (-0.5) * math.log2(math.e)
 
 
@@ -189,6 +190,10 @@
     )
 
 
+def swap_plane():
+    return pairs(lambda x, zl, y, c, g: (x, zl ^ 1, y, c, g))
+
+
 def swap_core(dg):
     return pairs(lambda x, zl, y, c, g: (x, zl, y, c ^ 1, g ^ dg))
 
@@ -205,7 +210,7 @@
     return lax.dot_general(a, b, (((1,), (0,)), ((), ())), preferred_element_type=F32)
 
 
-def call(kernel, outs, scratch=(), limit=48, flops=0, nbytes=0, smem=1, in_hbm=0):
+def call(kernel, outs, scratch=(), limit=48, us=1.0, smem=1, in_hbm=0):
     def run(*args):
         vm = pl.BlockSpec(memory_space=pltpu.VMEM)
         sm = pl.BlockSpec(memory_space=pltpu.SMEM)
@@ -218,7 +223,9 @@
             out_specs=jax.tree.map(lambda _: vm, outs),
             scratch_shapes=list(scratch),
             compiler_params=pltpu.CompilerParams(vmem_limit_bytes=limit * MIB),
-            cost_estimate=pl.CostEstimate(flops=flops, bytes_accessed=nbytes, transcendentals=0),
+            cost_estimate=pl.CostEstimate(
+                flops=int(us * 1.1e9), bytes_accessed=0, transcendentals=0
+            ),
         )(*args)
 
     return run
@@ -258,7 +265,9 @@
     return jnp.broadcast_to(jnp.max(counts, axis=0, keepdims=True).astype(jnp.int32), (1, n))
 
 
-def plan_kernel(at, con_ref, txt_ref, table_ref, k_ref, v_ref, rows_ref, both_ref, plan_ref):
+def plan_kernel(
+    at, con_ref, txt_ref, table_ref, q_ref, k_ref, v_ref, rows_ref, both_ref, img_ref, plan_ref
+):
     ids = jnp.concatenate([con_ref[...], txt_ref[...]], axis=1)
     n = ids.shape[1]
     vocab_dev = table_ref.shape[0]
@@ -271,9 +280,16 @@
     rows = nn(pick, table_ref[...]).astype(BF)
     rows_ref[...] = rows
     both_ref[0:SLOTS, :] = rows
-    wide = k_ref.shape[1]
-    for j, (ref, row) in enumerate(((k_ref, 0), (k_ref, 16), (v_ref, 0), (v_ref, 16))):
-        both_ref[SLOTS:, j * wide : (j + 1) * wide] = ref[row : row + 16, :]
+    m = q_ref.shape[0]
+    half = q_ref.shape[1] // 2
+    mine = pl.ds(pl.multiple_of(at[2] * half, half), half)
+    theirs = pl.ds(pl.multiple_of((1 - at[2]) * half, half), half)
+    for i, ref in enumerate((q_ref, k_ref, v_ref)):
+        img_ref[i * m : (i + 1) * m, :] = ref[:, mine]
+        for j in range(2):
+            lanes = slice((2 * i + j) * half, (2 * i + j + 1) * half)
+            both_ref[SLOTS:, lanes] = ref[16 * j : 16 * (j + 1), theirs]
+    both_ref[SLOTS:, 6 * half :] = jnp.zeros((16, 2 * half), BF)
     plan_ref[0:1, :] = rank
     plan_ref[1:2, :] = most(counts, n)
     plan_ref[2:8, :] = jnp.zeros((6, n), jnp.int32)
@@ -302,9 +318,11 @@
     con_bias[...] = empty_bias(at, con_counts, CON, 16 * CON)
     txt_bias[...] = empty_bias(at, txt_counts, TXT, 16 * TXT)
     spot_ref[0:1, :] = spot
-    spot_ref[1:2, :] = most(con_counts, n)
-    spot_ref[2:3, :] = most(txt_counts, n)
-    spot_ref[3:8, :] = jnp.zeros((5, n), jnp.int32)
+    spot_ref[1:2, :] = jnp.maximum(
+        jnp.maximum(most(con_counts, n) - CON, most(txt_counts, n) - TXT),
+        plan_ref[1:2, :] - SLOTS,
+    )
+    spot_ref[2:8, :] = jnp.zeros((6, n), jnp.int32)
     here = column == at[1]
     rank = plan_ref[0:1, :]
     concept = lax.broadcasted_iota(jnp.int32, (1, n), 1) < n_con
@@ -384,27 +402,32 @@
         q_out[i * CON + CON // 2 : (i + 1) * CON, :] = ref[ROWS:, HD:]
 
 
-def image_heads_kernel(at, q, q_core, own, core, zl, diag, *outs):
-    n, wide = q.shape
+def image_heads_kernel(at, own, core, *outs):
+    n, half = own.shape[0] // 3, own.shape[1]
     for s, out in enumerate(outs):
-        head = at[2] * 3 + jnp.minimum(at[4] ^ s, 2)
+        head = jnp.minimum(at[4] ^ s, 2)
         lanes = pl.ds(pl.multiple_of(head * HD, HD), HD)
-        out[0:n, :] = q[:, lanes]
-        out[n : 2 * n, :] = q_core[:, lanes]
-        for i in range(2):
-            for j, ref in enumerate((own, core, zl, diag)):
-                row = (2 + 4 * i + j) * n
-                for m in range(2):
-                    lanes = pl.ds(pl.multiple_of((2 * i + m) * wide + head * HD, HD), HD)
-                    out[row + 16 * m : row + 16 * (m + 1), :] = ref[SLOTS:, lanes]
+        for i in range(3):
+            row = 2 * i * n
+            out[row : row + n, :] = own[i * n : (i + 1) * n, lanes]
+            for j in range(2):
+                there = pl.ds(pl.multiple_of((2 * i + j) * half + head * HD, HD), HD)
+                out[row + n + 16 * j : row + n + 16 * (j + 1), :] = core[SLOTS:, there]
 
 
 def image_join_kernel(a, b, c, d, q_out, kv_out):
-    n = a.shape[0] // 10
+    n = a.shape[0] // 3
     for i, ref in enumerate((a, b, c, d)):
-        q_out[2 * n * i : 2 * n * (i + 1), :] = ref[0 : 2 * n, :]
-        kv_out[4 * n * i : 4 * n * (i + 1), :] = ref[2 * n : 6 * n, :]
-        kv_out[4 * n * (4 + i) : 4 * n * (5 + i), :] = ref[6 * n :, :]
+        q_out[n * i : n * (i + 1), :] = ref[0:n, :]
+        kv_out[n * i : n * (i + 1), :] = ref[n : 2 * n, :]
+        kv_out[n * (4 + i) : n * (5 + i), :] = ref[2 * n :, :]
+
+
+def plane_kernel(a, b, c, d, out):
+    n = a.shape[0] // 2
+    for i, ref in enumerate((a, b, c, d)):
+        out[n * i : n * (i + 1), :] = ref[0:n, :]
+        out[n * (4 + i) : n * (5 + i), :] = ref[n:, :]
 
 
 def weigh(q, parts, factor):
@@ -424,9 +447,13 @@
     return (peak if factor is None else peak * factor), total
 
 
+def join(first, second):
+    peak = jnp.maximum(first[0], second[0])
+    return peak, first[1] * jnp.exp2(first[0] - peak) + second[1] * jnp.exp2(second[0] - peak)
+
+
 def merge(first, second):
-    peak = jnp.maximum(first[0], second[0])
-    summed = first[1] * jnp.exp2(first[0] - peak) + second[1] * jnp.exp2(second[0] - peak)
+    _, summed = join(first, second)
     return (summed[:, 0:HD] / summed[:, HD:]).astype(BF)
 
 
@@ -434,29 +461,33 @@
     return jnp.concatenate([values, jnp.ones_like(values)], axis=1)
 
 
-def image_self_kernel(i0, i1, i2, i3, q, kv, bias, keys, vals, peak, summed):
-    part = i0.shape[0] // 2
-    for i, ref in enumerate((i0, i1, i2, i3)):
-        keys[i * part : (i + 1) * part, :] = ref[0:part, :]
-        vals[i * part : (i + 1) * part, :] = with_ones(ref[part:, :])
-    text = kv[4 * CON :, :]
-    parts = (
-        (keys[...], vals[...], None),
-        (text[:, 0:HD], with_ones(text[:, HD:]), bias[:, 0 : 4 * TXT]),
-    )
-    peak[...], summed[...] = weigh(q[...], parts, FACTOR)
-
-
-def concept_image_kernel(pick, q0, q1, q2, q3, keys, vals, kv, bias, q_out, peak, summed):
+def plane_parts(plane):
+    n = plane.shape[0] // 2
+    return (plane[0:n, :], with_ones(plane[n:, :]), None)
+
+
+def near_kernel(pick, q0, q1, q2, q3, plane, kv, con_bias, txt_bias, img_q, q_out, cm, cs, im, ims):
     n = 4 * CON
     q_out[...] = sum(
         nn(pick[:, a * n : (a + 1) * n], ref[...]) for a, ref in enumerate((q0, q1, q2, q3))
     ).astype(BF)
-    own = (kv[0:n, 0:HD], with_ones(kv[0:n, HD:]), bias[:, 0:n])
+    images = plane_parts(plane)
+    own = (kv[0:n, 0:HD], with_ones(kv[0:n, HD:]), con_bias[:, 0:n])
     for b in range(q_out.shape[0] // 256):
         rows = slice(b * 256, (b + 1) * 256)
-        parts = ((keys[...], vals[...], None), own)
-        peak[rows, :], summed[rows, :] = weigh(q_out[rows, :], parts, None)
+        cm[rows, :], cs[rows, :] = weigh(q_out[rows, :], (images, own), None)
+    text = (kv[n:, 0:HD], with_ones(kv[n:, HD:]), txt_bias[:, 0 : 4 * TXT])
+    im[...], ims[...] = weigh(img_q[...], (images, text), FACTOR)
+
+
+def far_kernel(plane, con_q, img_q, cm, cs, im, ims, cm_out, cs_out, im_out, ims_out):
+    images = plane_parts(plane)
+    for b in range(con_q.shape[0] // 256):
+        rows = slice(b * 256, (b + 1) * 256)
+        part = weigh(con_q[rows, :], (images,), None)
+        cm_out[rows, :], cs_out[rows, :] = join(part, (cm[rows, :], cs[rows, :]))
+    part = weigh(img_q[...], (images,), FACTOR)
+    im_out[...], ims_out[...] = join(part, (im[...], ims[...]))
 
 
 def prompt_kernel(con_bias, txt_bias, c1, c2, c3, con_q, cm, cs, img_q, im, ims, *refs):
@@ -525,7 +556,7 @@
     con_rms = jnp.sqrt(total[32:33, 0:n_con] / width + 1e-06)
     img_rms = jnp.sqrt(total[0:32, n_con : n_con + 1] / width + 1e-06)
     sal = total[0:32, 0:n_con] / (math.sqrt(width) * con_rms * img_rms)
-    sal_ref[...] = jnp.transpose(sal)
+    sal_ref[...] = sal
     half = 3 * HD
     mine = pl.ds(pl.multiple_of(at[2] * half, half), half)
     theirs = pl.ds(pl.multiple_of((1 - at[2]) * half, half), half)
@@ -552,16 +583,18 @@
     half = txt_qkv.shape[2] // 2
     n_img = img_q.shape[0]
 
-    own_rows, own_both, plan = call(
+    own_rows, own_both, own_img, plan = call(
         plan_kernel,
-        (sds((SLOTS, width)), sds((SLOTS + 16, width)), sds((8, n), jnp.int32)),
-        nbytes=2 * MIB,
-        flops=10**9,
-    )(at, con_ids, text_ids, token_table, img_k, img_v)
-    column_rows = [own_both, send(own_both, swap_z(1))]
-    column_rows += [send(own_rows, swap_z(s)) for s in (2, 3)]
-    other_rows = [send(r, swap_core(0)) for r in column_rows]
-    q_core = send(img_q, swap_core(0))
+        (
+            sds((SLOTS, width)),
+            sds((SLOTS + 16, width)),
+            sds((3 * n_img, half)),
+            sds((8, n), jnp.int32),
+        ),
+    )(at, con_ids, text_ids, token_table, img_q, img_k, img_v)
+    far_rows = send(own_rows, swap_z(2))
+    column_rows = [own_rows] + [send(own_rows, swap_z(s)) for s in (1, 3)]
+    core_both = send(own_both, swap_core(0))
 
     pack, spots, con_bias, txt_bias = call(
         pack_kernel,
@@ -571,8 +604,6 @@
             sds((1, 16 * CON), F32),
             sds((1, 16 * TXT), F32),
         ),
-        nbytes=MIB,
-        flops=10**9,
     )(at, con_ids, text_ids, plan)
     owner = concept_ids >> 8
     item_x = owner >> 5
@@ -582,11 +613,19 @@
     con_slot = ((v ^ item_v) * 4 + (u ^ item_u)) * CON + spots[0, :n_con]
     pick = (con_slot[:, None] == jnp.arange(16 * CON)[None, :]).astype(BF)
     shift_scale = lax.dynamic_index_in_dim(modulation, step_index[0], 0, keepdims=False)
+    fits = (spots[1, 0] <= 0).astype(jnp.int32)
 
     image_blocks = call(
-        image_heads_kernel, tuple(sds((10 * n_img, HD)) for _ in range(4)), nbytes=MIB // 2
-    )(at, img_q, q_core, own_both, other_rows[0], column_rows[1], other_rows[1])
-    image_blocks = [image_blocks[0]] + [send(image_blocks[s], swap_u(s)) for s in (1, 2, 3)]
+        image_heads_kernel, tuple(sds((6 * n_img, HD)) for _ in range(4))
+    )(at, own_img, core_both)
+    far_rows, pack, shift_scale, pick, fits, *image_blocks = lax.optimization_barrier(
+        (far_rows, pack, shift_scale, pick, fits, *image_blocks)
+    )
+    column_rows.insert(2, far_rows)
+    other_rows = [core_both] + [send(r, swap_core(0)) for r in column_rows[1:]]
+
+    image_blocks = [image_blocks[0]] + [send(image_blocks[s], swap_u(s)) for s in (2, 1, 3)]
+    image_blocks = [image_blocks[0], image_blocks[2], image_blocks[1], image_blocks[3]]
 
     qkv = call(
         project_kernel,
@@ -597,57 +636,51 @@
             pltpu.VMEM((3, width, half), BF),
             pltpu.SemaphoreType.DMA((3,)),
         ),
-        nbytes=10 * MIB,
-        flops=10**9,
+        us=PROJ_US,
         in_hbm=1,
     )(at, pack, *column_rows, *other_rows, shift_scale, qk_gain, jnp.transpose(txt_qkv, (1, 0, 2)))
 
     *image_blocks, first = lax.optimization_barrier((*image_blocks, qkv[0]))
     image_q, image_kv = call(
-        image_join_kernel, (sds((8 * n_img, HD)), sds((32 * n_img, HD))), nbytes=MIB // 2, smem=0
+        image_join_kernel, (sds((8 * n_img, HD)), sds((16 * n_img, HD))), smem=0
     )(*image_blocks)
-    image_kvs = [image_kv] + [send(image_kv, swap_v(s)) for s in (1, 2, 3)]
-
-    qkv = [first] + [send(qkv[s], swap_u(s)) for s in (1, 2, 3)]
+    image_kvs = [image_kv] + [send(image_kv, swap_v(s)) for s in (2, 1, 3)]
+
+    qkv = [first] + [send(qkv[s], swap_u(s)) for s in (2, 1, 3)]
+    qkv = [qkv[0], qkv[2], qkv[1], qkv[3]]
     q_join, kv_join = call(
-        join_kernel, (sds((4 * CON, HD)), sds((4 * ROWS, 2 * HD))), nbytes=MIB, smem=0
+        join_kernel, (sds((4 * CON, HD)), sds((4 * ROWS, 2 * HD))), smem=0
     )(*qkv)
-    q_chunks = [q_join] + [send(q_join, swap_v(s)) for s in (1, 2, 3)]
-    kv_chunks = [send(kv_join, swap_v(s)) for s in (1, 2, 3)]
-
-    all_img = 64 * n_img
-    keys, vals, *image_stats = call(
-        image_self_kernel,
-        (
-            sds((all_img, HD)),
-            sds((all_img, 2 * HD)),
-            sds((8 * n_img, 1), F32),
-            sds((8 * n_img, 2 * HD), F32),
-        ),
-        nbytes=4 * MIB,
-        flops=10**9,
-        smem=0,
-    )(*image_kvs, image_q, kv_join, txt_bias)
-    con_q, *con_stats = call(
-        concept_image_kernel,
-        (sds((n_con, HD)), sds((n_con, 1), F32), sds((n_con, 2 * HD), F32)),
-        nbytes=8 * MIB,
-        flops=3 * 10**9,
-        smem=0,
-    )(pick, *q_chunks, keys, vals, kv_join, con_bias)
+    plane = call(plane_kernel, sds((64 * n_img, HD)), smem=0)(*image_kvs)
+    q_chunks = [q_join] + [send(q_join, swap_v(s)) for s in (2, 1, 3)]
+    q_chunks = [q_chunks[0], q_chunks[2], q_chunks[1], q_chunks[3]]
+    other_plane = send(plane, swap_plane())
+    kv_chunks = [send(kv_join, swap_v(s)) for s in (2, 1, 3)]
+    kv_chunks = [kv_chunks[1], kv_chunks[0], kv_chunks[2]]
+
+    stats = (
+        sds((n_con, 1), F32),
+        sds((n_con, 2 * HD), F32),
+        sds((8 * n_img, 1), F32),
+        sds((8 * n_img, 2 * HD), F32),
+    )
+    con_q, *near = call(near_kernel, (sds((n_con, HD)),) + stats, us=NEAR_US, smem=0)(
+        pick, *q_chunks, plane, kv_join, con_bias, txt_bias, image_q
+    )
+    con_stats = call(far_kernel, stats, us=FAR_US, smem=0)(other_plane, con_q, image_q, *near)
+    con_stats, image_stats = con_stats[:2], con_stats[2:]
     blocks = call(
         prompt_kernel,
         tuple(sds((80, n_con + HD)) for _ in range(4)),
         scratch=(pltpu.VMEM((n_con, HD), BF),),
-        nbytes=10 * MIB,
-        flops=2 * 10**9,
+        us=PROMPT_US,
         smem=0,
     )(con_bias, txt_bias, *kv_chunks, con_q, *con_stats, image_q, *image_stats)
-    blocks = [blocks[0]] + [send(blocks[s], swap_u(s)) for s in (1, 2, 3)]
+    blocks = [blocks[0]] + [send(blocks[s], swap_u(s)) for s in (2, 1, 3)]
+    blocks = [blocks[0], blocks[2], blocks[1], blocks[3]]
     own, core, diag, out_own = call(
         head_sum_kernel,
         (sds((48, n_con + HD)), sds((48, n_con + 4 * HD)), sds((48, n_con + HD)), sds((32, half))),
-        nbytes=MIB,
     )(at, *blocks)
     last = (
         at,
@@ -658,10 +691,14 @@
         out_own,
     )
     finish = call(
-        finish_kernel, (sds((n_img, 2 * half)), sds((n_con, n_img), F32)), nbytes=MIB
-    )
-    fits = (plan[1, 0] <= SLOTS) & (spots[1, 0] <= CON) & (spots[2, 0] <= TXT)
-    return fits, lambda: tuple(finish(*last))
+        finish_kernel, (sds((n_img, 2 * half)), sds((n_img, n_con), F32))
+    )
+
+    def finished():
+        img_out, saliency = finish(*last)
+        return img_out, jnp.transpose(saliency)
+
+    return fits > 0, finished
 
 
 def on_device(*args):

time: 97.8 us -> 88.8 us (0.908)
  waiting for transfers between devices: 25.6 us -> 16.3 us
  starting transfers between devices: 39.6 us -> 43.4 us
  local copies, waits for them, and re-layouts: 2.79 us -> 1.41 us
  between operations: 3.47 us -> 2.2 us
    ppermute x29, waiting for transfers between devices: 25.6 us -> 16.3 us  [send(): return lax.ppermute(array, ('ctx', 'head'), pairing)]
    ppermute x29, starting transfers between devices: 39.6 us -> 43.4 us  [send(): return lax.ppermute(array, ('ctx', 'head'), pairing)]
    pallas_call x11 -> x12, Pallas kernels: 23.5 us -> 22.8 us  [run(): pl.pallas_call(kernel, out_shape=outs, in_specs=[sm] * smem + [vm] * (len...]
  transfers between devices with their start and end apart: 29 -> 29, of which waited for: 11 -> 8; matrix products, arithmetic and copies ran while one was open for 4% -> 4% of each run, Pallas kernels for 15% -> 16%
where the time goes in v1:
time: 88.8 us; the launch traced here: 88.5 us
  starting transfers between devices  43.4 us (49%)
  Pallas kernels  22.8 us (26%)
  waiting for transfers between devices  16.3 us (18%)
  other arithmetic  2.21 us (2%)
  between operations  2.2 us (2%)
  local copies, waits for them, and re-layouts  1.41 us (2%)
    ppermute x29, starting transfers between devices, send(): return lax.ppermute(array, ('ctx', 'head'), pairing)  43.4 us
    pallas_call x12, Pallas kernels, run(): pl.pallas_call(kernel, out_shape=outs, in_specs=[sm] * smem + [vm] * (len...  22.8 us
    ppermute x29, waiting for transfers between devices, send(): return lax.ppermute(array, ('ctx', 'head'), pairing)  16.3 us
    convert_element_type x1, other arithmetic, packed(): pick = (con_slot[:, None] == jnp.arange(16 * CON)[None, :]).astype(BF)  2.2 us
  transfers between devices with their start and end apart: 29, of which 8 were waited for; matrix products, arithmetic and copies ran while one was open for 4% of the time, Pallas kernels for 16%

profile of v1, /device:TPU:1, one launch (start us, length us, event | category | flops | bytes accessed | tf_op | source)
XLA Modules:
  0.0 88.5 jit_solution(12476366719478527519)
XLA Ops:
  0.8 2.7 %shard_map.115 = (bf16[32,3072]{1,0:T(8,128)(2,1)S(1)}, bf16[48,3072]{1,0:T(8,128)(2,1)S(1)}, bf16[96,384]{1,0:T(8,128)(2,1)S(1)}, s32[8,1536]{1,0:T(8,128)S(1)}) custom-call(s32[6]{0:T(128)S(1)} %stack.45.at, s32[1,1024]{1,0:T(1,128)} %bitcast.135, s32[1,512]{1,0:T(1,128)} %bitcast.138, bf16[256,3072]{1,0:T(8,128)(2,1)} %table_ref.1, ...), custom_call_target="tpu_custom_call" | custom-call | flops 1100000000 | tf_op jit(solution)/shard_map/pallas_call | solution.py:217
  3.4 4.5 %collective-permute-start.1 = (bf16[32,3072]{1,0:T(8,128)(2,1)S(1)}, bf16[32,3072]{1,0:T(8,128)(2,1)S(1)}, u32[]{:S(2)}, u32[]{:S(2)}) collective-permute-start(bf16[32,3072]{1,0:T(8,128)(2,1)S(1)} %get-tuple-element.103.refs_0_), channel_id=1, source_target_pairs={{0,1},{1,0},{2,3},{3,2},{4,5},{5,4},{6,7},{7,6},{8,9},{9,8},{10,11... | collective-permute-start | bytes 589832 | tf_op jit(solution)/shard_map/ppermute | solution.py:202
  8.7 1.2 %collective-permute-start.2 = (bf16[48,3072]{1,0:T(8,128)(2,1)S(1)}, bf16[48,3072]{1,0:T(8,128)(2,1)S(1)}, u32[]{:S(2)}, u32[]{:S(2)}) collective-permute-start(bf16[48,3072]{1,0:T(8,128)(2,1)S(1)} %get-tuple-element.108), channel_id=1, source_target_pairs={{0,2},{1,3},{2,0},{3,1},{4,6},{5,7},{6,4},{7,5},{8,10},{9,11},{10,... | collective-permute-start | bytes 884744 | tf_op jit(solution)/shard_map/ppermute | solution.py:202
  9.9 1.1 %shard_map.116 = (bf16[160,256]{1,0:T(8,128)(2,1)S(1)}, s32[8,1536]{1,0:T(8,128)S(1)}, f32[1,1536]{1,0:T(1,128)S(1)}, f32[1,1024]{1,0:T(1,128)S(1)}) custom-call(s32[6]{0:T(128)S(1)} %stack.45.at, s32[1,1024]{1,0:T(1,128)S(1)} %bitcast.136, s32[1,512]{1,0:T(1,128)S(1)} %bitcast.139, s32[8,1536]{1,0:T(8,128)S(1)} %get-tuple-element.104.plan_ref), custom_call_target="tpu_custom_call" | custom-call | flops 1100000000 | tf_op jit(solution)/shard_map/pallas_call | solution.py:217
  11.1 2.2 %fusion.81.pick = bf16[1024,1536]{1,0:T(8,128)(2,1)} fusion(s32[1024]{0:T(1024)S(1)} %multiply_add_fusion), kind=kLoop, calls=%fused_computation.115 | loop fusion | flops 3145728 | bytes 3149824 | tf_op jit(solution)/shard_map/convert_element_type | solution.py:614
  15.9 1.6 %collective-permute-done.7.refs_3_ = bf16[32,3072]{1,0:T(8,128)(2,1)S(1)} collective-permute-done((bf16[32,3072]{1,0:T(8,128)(2,1)S(1)}, bf16[32,3072]{1,0:T(8,128)(2,1)S(1)}, u32[]{:S(2)}, u32[]{:S(2)}) %collective-permute-start.7) | collective-permute-done | bytes 196640 | tf_op jit(solution)/shard_map/ppermute | solution.py:202
  19.5 1.4 %collective-permute-start.3 = (bf16[192,128]{1,0:T(8,128)(2,1)S(1)}, bf16[192,128]{1,0:T(8,128)(2,1)S(1)}, u32[]{:S(2)}, u32[]{:S(2)}) collective-permute-start(bf16[192,128]{1,0:T(8,128)(2,1)S(1)} %get-tuple-element.117), channel_id=1, source_target_pairs={{0,32},{1,33},{2,6},{3,7},{4,36},{5,37},{6,2},{7,3},{8,40},{9,41},... | collective-permute-start | bytes 147464 | tf_op jit(solution)/shard_map/ppermute | solution.py:202
  20.9 2.6 %collective-permute-start.4 = (bf16[192,128]{1,0:T(8,128)(2,1)S(1)}, bf16[192,128]{1,0:T(8,128)(2,1)S(1)}, u32[]{:S(2)}, u32[]{:S(2)}) collective-permute-start(bf16[192,128]{1,0:T(8,128)(2,1)S(1)} %get-tuple-element.118), channel_id=1, source_target_pairs={{0,64},{1,65},{2,10},{3,11},{4,68},{5,69},{6,14},{7,15},{8,72},{9,... | collective-permute-start | bytes 147464 | tf_op jit(solution)/shard_map/ppermute | solution.py:202
  23.5 4.7 %shard_map.118 = (bf16[208,256]{1,0:T(8,128)(2,1)S(1)}, bf16[208,256]{1,0:T(8,128)(2,1)S(1)}, bf16[208,256]{1,0:T(8,128)(2,1)S(1)}, bf16[208,256]{1,0:T(8,128)(2,1)S(1)}) custom-call(s32[6]{0:T(128)S(1)} %stack.45.at, bf16[160,256]{1,0:T(8,128)(2,1)S(1)} %get-tuple-element.120.pack_ref, bf16[32,3072]{1,0:T(8,128)(2,1)S(1)} %get-tuple-element.103.refs_0_, ...), custom_call_target="tpu_custom_call" | custom-call | flops 5500000256 | tf_op jit(solution)/shard_map/pallas_call | solution.py:217
  28.4 3.9 %collective-permute-start.12 = (bf16[208,256]{1,0:T(8,128)(2,1)S(1)}, bf16[208,256]{1,0:T(8,128)(2,1)S(1)}, u32[]{:S(2)}, u32[]{:S(2)}) collective-permute-start(bf16[208,256]{1,0:T(8,128)(2,1)S(1)} %get-tuple-element.126), channel_id=1, source_target_pairs={{0,64},{1,65},{2,10},{3,11},{4,68},{5,69},{6,14},{7,15},{8,72},{9,... | collective-permute-start | bytes 319496 | tf_op jit(solution)/shard_map/ppermute | solution.py:202
  32.3 2.8 %collective-permute-start.20 = (bf16[512,128]{1,0:T(8,128)(2,1)S(1)}, bf16[512,128]{1,0:T(8,128)(2,1)S(1)}, u32[]{:S(2)}, u32[]{:S(2)}) collective-permute-start(bf16[512,128]{1,0:T(8,128)(2,1)S(1)} %get-tuple-element.135.a), channel_id=1, source_target_pairs={{0,8},{1,9},{2,66},{3,67},{4,12},{5,13},{6,70},{7,71},{8,0},{9,1},... | collective-permute-start | bytes 393224 | tf_op jit(solution)/shard_map/ppermute | solution.py:202
  36.0 1.3 %collective-permute-done.13.d = bf16[208,256]{1,0:T(8,128)(2,1)S(1)} collective-permute-done((bf16[208,256]{1,0:T(8,128)(2,1)S(1)}, bf16[208,256]{1,0:T(8,128)(2,1)S(1)}, u32[]{:S(2)}, u32[]{:S(2)}) %collective-permute-start.13) | collective-permute-done | bytes 106528 | tf_op jit(solution)/shard_map/ppermute | solution.py:202
  37.4 2.6 %collective-permute-start.17 = (bf16[384,128]{1,0:T(8,128)(2,1)S(1)}, bf16[384,128]{1,0:T(8,128)(2,1)S(1)}, u32[]{:S(2)}, u32[]{:S(2)}) collective-permute-start(bf16[384,128]{1,0:T(8,128)(2,1)S(1)} %get-tuple-element.130.q0), channel_id=1, source_target_pairs={{0,4},{1,5},{2,34},{3,35},{4,0},{5,1},{6,38},{7,39},{8,12},{9,13},... | collective-permute-start | bytes 294920 | tf_op jit(solution)/shard_map/ppermute | solution.py:202
  40.0 1.5 %collective-permute-start.18 = (bf16[384,128]{1,0:T(8,128)(2,1)S(1)}, bf16[384,128]{1,0:T(8,128)(2,1)S(1)}, u32[]{:S(2)}, u32[]{:S(2)}) collective-permute-start(bf16[384,128]{1,0:T(8,128)(2,1)S(1)} %get-tuple-element.130.q0), channel_id=1, source_target_pairs={{0,8},{1,9},{2,66},{3,67},{4,12},{5,13},{6,70},{7,71},{8,0},{9,1},... | collective-permute-start | bytes 294920 | tf_op jit(solution)/shard_map/ppermute | solution.py:202
  41.5 0.9 %collective-permute-start.19 = (bf16[384,128]{1,0:T(8,128)(2,1)S(1)}, bf16[384,128]{1,0:T(8,128)(2,1)S(1)}, u32[]{:S(2)}, u32[]{:S(2)}) collective-permute-start(bf16[384,128]{1,0:T(8,128)(2,1)S(1)} %get-tuple-element.130.q0), channel_id=1, source_target_pairs={{0,12},{1,13},{2,98},{3,99},{4,8},{5,9},{6,102},{7,103},{8,4},{9,5... | collective-permute-start | bytes 294920 | tf_op jit(solution)/shard_map/ppermute | solution.py:202
  43.5 2.7 %collective-permute-start.15 = (bf16[640,256]{1,0:T(8,128)(2,1)S(1)}, bf16[640,256]{1,0:T(8,128)(2,1)S(1)}, u32[]{:S(2)}, u32[]{:S(2)}) collective-permute-start(bf16[640,256]{1,0:T(8,128)(2,1)S(1)} %get-tuple-element.128.kv), channel_id=1, source_target_pairs={{0,8},{1,9},{2,66},{3,67},{4,12},{5,13},{6,70},{7,71},{8,0},{9,1},... | collective-permute-start | bytes 983048 | tf_op jit(solution)/shard_map/ppermute | solution.py:202
  46.2 0.9 %collective-permute-start.16 = (bf16[640,256]{1,0:T(8,128)(2,1)S(1)}, bf16[640,256]{1,0:T(8,128)(2,1)S(1)}, u32[]{:S(2)}, u32[]{:S(2)}) collective-permute-start(bf16[640,256]{1,0:T(8,128)(2,1)S(1)} %get-tuple-element.128.kv), channel_id=1, source_target_pairs={{0,12},{1,13},{2,98},{3,99},{4,8},{5,9},{6,102},{7,103},{8,4},{9,5... | collective-permute-start | bytes 983048 | tf_op jit(solution)/shard_map/ppermute | solution.py:202
  47.2 5.5 %shard_map.122 = (bf16[1024,128]{1,0:T(8,128)(2,1)S(1)}, f32[1024,1]{1,0:T(8,128)S(1)}, f32[1024,256]{1,0:T(8,128)S(1)}, f32[256,1]{1,0:T(8,128)S(1)}, f32[256,256]{1,0:T(8,128)S(1)}) custom-call(bf16[1024,1536]{1,0:T(8,128)(2,1)} %fusion.81.pick, bf16[384,128]{1,0:T(8,128)(2,1)S(1)} %get-tuple-element.130.q0, ...), custom_call_target="tpu_custom_call" | custom-call | flops 5500000256 | tf_op jit(solution)/shard_map/pallas_call | solution.py:217
  52.7 2.1 %shard_map.123 = (f32[1024,1]{1,0:T(8,128)S(1)}, f32[1024,256]{1,0:T(8,128)S(1)}, f32[256,1]{1,0:T(8,128)S(1)}, f32[256,256]{1,0:T(8,128)S(1)}) custom-call(bf16[2048,128]{1,0:T(8,128)(2,1)S(1)} %collective-permute-done.23.plane, bf16[1024,128]{1,0:T(8,128)(2,1)S(1)} %get-tuple-element.137.con_q, bf16[256,128]{1,0:T(8,128)(2,1)S(1)} %get-tuple-element.136.img_q, ...), custom_call_target="tpu_custom_call" | custom-call | flops 4400000000 | tf_op jit(solution)/shard_map/pallas_call | solution.py:217
  54.9 2.3 %collective-permute-done.16.c3 = bf16[640,256]{1,0:T(8,128)(2,1)S(1)} collective-permute-done((bf16[640,256]{1,0:T(8,128)(2,1)S(1)}, bf16[640,256]{1,0:T(8,128)(2,1)S(1)}, u32[]{:S(2)}, u32[]{:S(2)}) %collective-permute-start.16) | collective-permute-done | bytes 327712 | tf_op jit(solution)/shard_map/ppermute | solution.py:202
  57.2 3.0 %shard_map.124 = (bf16[80,1152]{1,0:T(8,128)(2,1)S(1)}, bf16[80,1152]{1,0:T(8,128)(2,1)S(1)}, bf16[80,1152]{1,0:T(8,128)(2,1)S(1)}, bf16[80,1152]{1,0:T(8,128)(2,1)S(1)}) custom-call(f32[1,1536]{1,0:T(1,128)S(1)} %get-tuple-element.114.con_bias, f32[1,1024]{1,0:T(1,128)S(1)} %get-tuple-element.115.txt_bias, bf16[640,256]{1,0:T(8,128)(2,1)S(1)} %collective-permute-done.14.c1, ...), custom_call_target="tpu_custom_call" | custom-call | flops 3300000000 | tf_op jit(solution)/shard_map/pallas_call | solution.py:217
  60.3 2.1 %collective-permute-start.25 = (bf16[80,1152]{1,0:T(8,128)(2,1)S(1)}, bf16[80,1152]{1,0:T(8,128)(2,1)S(1)}, u32[]{:S(2)}, u32[]{:S(2)}) collective-permute-start(bf16[80,1152]{1,0:T(8,128)(2,1)S(1)} %get-tuple-element.148), channel_id=1, source_target_pairs={{0,64},{1,65},{2,10},{3,11},{4,68},{5,69},{6,14},{7,15},{8,72},{9,... | collective-permute-start | bytes 552968 | tf_op jit(solution)/shard_map/ppermute | solution.py:202
  62.4 1.8 %collective-permute-start.26 = (bf16[80,1152]{1,0:T(8,128)(2,1)S(1)}, bf16[80,1152]{1,0:T(8,128)(2,1)S(1)}, u32[]{:S(2)}, u32[]{:S(2)}) collective-permute-start(bf16[80,1152]{1,0:T(8,128)(2,1)S(1)} %get-tuple-element.149), channel_id=1, source_target_pairs={{0,96},{1,97},{2,14},{3,15},{4,100},{5,101},{6,10},{7,11},{8,104},... | collective-permute-start | bytes 552968 | tf_op jit(solution)/shard_map/ppermute | solution.py:202
  64.7 2.7 %collective-permute-done.25.b2 = bf16[80,1152]{1,0:T(8,128)(2,1)S(1)} collective-permute-done((bf16[80,1152]{1,0:T(8,128)(2,1)S(1)}, bf16[80,1152]{1,0:T(8,128)(2,1)S(1)}, u32[]{:S(2)}, u32[]{:S(2)}) %collective-permute-start.25) | collective-permute-done | bytes 184352 | tf_op jit(solution)/shard_map/ppermute | solution.py:202
  67.4 1.9 %collective-permute-done.26.b3 = bf16[80,1152]{1,0:T(8,128)(2,1)S(1)} collective-permute-done((bf16[80,1152]{1,0:T(8,128)(2,1)S(1)}, bf16[80,1152]{1,0:T(8,128)(2,1)S(1)}, u32[]{:S(2)}, u32[]{:S(2)}) %collective-permute-start.26) | collective-permute-done | bytes 184352 | tf_op jit(solution)/shard_map/ppermute | solution.py:202
  69.3 1.3 %shard_map.125 = (bf16[48,1152]{1,0:T(8,128)(2,1)S(1)}, bf16[48,1536]{1,0:T(8,128)(2,1)S(1)}, bf16[48,1152]{1,0:T(8,128)(2,1)S(1)}, bf16[32,384]{1,0:T(8,128)(2,1)}) custom-call(s32[6]{0:T(128)S(1)} %stack.45.at, bf16[80,1152]{1,0:T(8,128)(2,1)S(1)} %get-tuple-element.146.b0, bf16[80,1152]{1,0:T(8,128)(2,1)S(1)} %collective-permute-done.24.b1, ...), custom_call_target="tpu_custom_call" | custom-call | flops 1100000000 | tf_op jit(solution)/shard_map/pallas_call | solution.py:217
  70.6 7.0 %collective-permute-start.27 = (bf16[48,1536]{1,0:T(8,128)(2,1)S(1)}, bf16[48,1536]{1,0:T(8,128)(2,1)S(1)}, u32[]{:S(2)}, u32[]{:S(2)}) collective-permute-start(bf16[48,1536]{1,0:T(8,128)(2,1)S(1)} %get-tuple-element.151), channel_id=1, source_target_pairs={{0,2},{1,3},{2,0},{3,1},{4,6},{5,7},{6,4},{7,5},{8,10},{9,11},{10,... | collective-permute-start | bytes 442376 | tf_op jit(solution)/shard_map/ppermute | solution.py:202
  77.7 2.5 %collective-permute-start.28 = (bf16[48,1152]{1,0:T(8,128)(2,1)S(1)}, bf16[48,1152]{1,0:T(8,128)(2,1)S(1)}, u32[]{:S(2)}, u32[]{:S(2)}) collective-permute-start(bf16[48,1152]{1,0:T(8,128)(2,1)S(1)} %get-tuple-element.150), channel_id=1, source_target_pairs={{0,1},{1,0},{2,3},{3,2},{4,5},{5,4},{6,7},{7,6},{8,9},{9,8},{10,11... | collective-permute-start | bytes 331784 | tf_op jit(solution)/shard_map/ppermute | solution.py:202
  80.8 3.1 %collective-permute-done.28 = bf16[48,1152]{1,0:T(8,128)(2,1)S(1)} collective-permute-done((bf16[48,1152]{1,0:T(8,128)(2,1)S(1)}, bf16[48,1152]{1,0:T(8,128)(2,1)S(1)}, u32[]{:S(2)}, u32[]{:S(2)}) %collective-permute-start.28) | collective-permute-done | bytes 110624 | tf_op jit(solution)/shard_map/ppermute | solution.py:202
  83.9 2.8 %collective-permute-done.29 = bf16[48,1152]{1,0:T(8,128)(2,1)S(1)} collective-permute-done((bf16[48,1152]{1,0:T(8,128)(2,1)S(1)}, bf16[48,1152]{1,0:T(8,128)(2,1)S(1)}, u32[]{:S(2)}, u32[]{:S(2)}) %collective-permute-start.29) | collective-permute-done | bytes 110624 | tf_op jit(solution)/shard_map/ppermute | solution.py:202
  86.7 1.8 %conditional.1 = (bf16[32,768]{1,0:T(8,128)(2,1)}, f32[1024,32]{0,1:T(8,128)}) conditional(s32[]{:T(128)} %convert_element_type.71, (s32[512]{0:T(512)S(1)}, s32[1024]{0:T(1024)S(1)}, bf16[256,3072]{1,0:T(8,128)(2,1)S(1)}, s32[1]{0:T(128)}, f32[28,2,3072]{2,1,0:T(2,128)}, /*index=5*/bf16[3072,3,768]{2,0,1:T(8,128)(2,1)}, f32[2,128]{1,0:T(2,128)S(1)}, ...), branch_computations={%region_0.15_spmd, %region_15.16_spmd} | conditional | flops 1100000000 | bytes 257951312 | solution.py:706
  87.0 1.5 %branch_1_fun.1 = (bf16[32,768]{1,0:T(8,128)(2,1)}, f32[32,1024]{1,0:T(8,128)}) custom-call(s32[6]{0:T(128)S(1)} %get-tuple-element.42.at, bf16[48,1152]{1,0:T(8,128)(2,1)S(1)} %get-tuple-element.43.own, bf16[48,1536]{1,0:T(8,128)(2,1)S(1)} %get-tuple-element.44.core, bf16[48,1152]{1,0:T(8,128)(2,1)S(1)} %get-tuple-element.45.head, ...), custom_call_target="tpu_custom_call" | custom-call | flops 1100000000 | tf_op jit(solution)/shard_map/cond/branch_1_fun/pallas_call | solution.py:217
  (59 shorter events, 7.4 us)
Async XLA Ops:
  3.4 16.0 %collective-permute-start.1 = (bf16[32,3072]{1,0:T(8,128)(2,1)S(1)}, bf16[32,3072]{1,0:T(8,128)(2,1)S(1)}, u32[]{:S(2)}, u32[]{:S(2)}) collective-permute-start(bf16[32,3072]{1,0:T(8,128)(2,1)S(1)} %get-tuple-element.103.refs_0_), channel_id=1, source_target_pairs={{0,1},{1,0},{2,3},{3,2},{4,5},{5,4},{6,7},{7,6},{8,9},{9,8},{10,11... | collective-permute-start | bytes 589832 | tf_op jit(solution)/shard_map/ppermute | solution.py:202
  8.0 9.6 %collective-permute-start.7 = (bf16[32,3072]{1,0:T(8,128)(2,1)S(1)}, bf16[32,3072]{1,0:T(8,128)(2,1)S(1)}, u32[]{:S(2)}, u32[]{:S(2)}) collective-permute-start(bf16[32,3072]{1,0:T(8,128)(2,1)S(1)} %get-tuple-element.103.refs_0_), channel_id=1, source_target_pairs={{0,17},{1,16},{2,19},{3,18},{4,21},{5,20},{6,23},{7,22},{8,25},{9,... | collective-permute-start | bytes 589832 | tf_op jit(solution)/shard_map/ppermute | solution.py:202
  8.4 9.6 %collective-permute-start.6 = (bf16[32,3072]{1,0:T(8,128)(2,1)S(1)}, bf16[32,3072]{1,0:T(8,128)(2,1)S(1)}, u32[]{:S(2)}, u32[]{:S(2)}) collective-permute-start(bf16[32,3072]{1,0:T(8,128)(2,1)S(1)} %get-tuple-element.103.refs_0_), channel_id=1, source_target_pairs={{0,16},{1,17},{2,18},{3,19},{4,20},{5,21},{6,22},{7,23},{8,24},{9,... | collective-permute-start | bytes 589832 | tf_op jit(solution)/shard_map/ppermute | solution.py:202
  8.7 10.1 %collective-permute-start.2 = (bf16[48,3072]{1,0:T(8,128)(2,1)S(1)}, bf16[48,3072]{1,0:T(8,128)(2,1)S(1)}, u32[]{:S(2)}, u32[]{:S(2)}) collective-permute-start(bf16[48,3072]{1,0:T(8,128)(2,1)S(1)} %get-tuple-element.108), channel_id=1, source_target_pairs={{0,2},{1,3},{2,0},{3,1},{4,6},{5,7},{6,4},{7,5},{8,10},{9,11},{10,... | collective-permute-start | bytes 884744 | tf_op jit(solution)/shard_map/ppermute | solution.py:202
  17.5 6.0 %collective-permute-start.10 = (bf16[32,3072]{1,0:T(8,128)(2,1)S(1)}, bf16[32,3072]{1,0:T(8,128)(2,1)S(1)}, u32[]{:S(2)}, u32[]{:S(2)}) collective-permute-start(bf16[32,3072]{1,0:T(8,128)(2,1)S(1)} %collective-permute-done.7.refs_3_), channel_id=1, source_target_pairs={{0,2},{1,3},{2,0},{3,1},{4,6},{5,7},{6,4},{7,5},{8,10},{9,11},{10,... | collective-permute-start | bytes 589832 | tf_op jit(solution)/shard_map/ppermute | solution.py:202
  18.0 5.5 %collective-permute-start.8 = (bf16[32,3072]{1,0:T(8,128)(2,1)S(1)}, bf16[32,3072]{1,0:T(8,128)(2,1)S(1)}, u32[]{:S(2)}, u32[]{:S(2)}) collective-permute-start(bf16[32,3072]{1,0:T(8,128)(2,1)S(1)} %collective-permute-done.6.refs_1_), channel_id=1, source_target_pairs={{0,2},{1,3},{2,0},{3,1},{4,6},{5,7},{6,4},{7,5},{8,10},{9,11},{10,... | collective-permute-start | bytes 589832 | tf_op jit(solution)/shard_map/ppermute | solution.py:202
  19.4 4.1 %collective-permute-start.9 = (bf16[32,3072]{1,0:T(8,128)(2,1)S(1)}, bf16[32,3072]{1,0:T(8,128)(2,1)S(1)}, u32[]{:S(2)}, u32[]{:S(2)}) collective-permute-start(bf16[32,3072]{1,0:T(8,128)(2,1)S(1)} %collective-permute-done.1.refs_2_), channel_id=1, source_target_pairs={{0,2},{1,3},{2,0},{3,1},{4,6},{5,7},{6,4},{7,5},{8,10},{9,11},{10,... | collective-permute-start | bytes 589832 | tf_op jit(solution)/shard_map/ppermute | solution.py:202
  19.5 8.9 %collective-permute-start.3 = (bf16[192,128]{1,0:T(8,128)(2,1)S(1)}, bf16[192,128]{1,0:T(8,128)(2,1)S(1)}, u32[]{:S(2)}, u32[]{:S(2)}) collective-permute-start(bf16[192,128]{1,0:T(8,128)(2,1)S(1)} %get-tuple-element.117), channel_id=1, source_target_pairs={{0,32},{1,33},{2,6},{3,7},{4,36},{5,37},{6,2},{7,3},{8,40},{9,41},... | collective-permute-start | bytes 147464 | tf_op jit(solution)/shard_map/ppermute | solution.py:202
  20.9 7.5 %collective-permute-start.4 = (bf16[192,128]{1,0:T(8,128)(2,1)S(1)}, bf16[192,128]{1,0:T(8,128)(2,1)S(1)}, u32[]{:S(2)}, u32[]{:S(2)}) collective-permute-start(bf16[192,128]{1,0:T(8,128)(2,1)S(1)} %get-tuple-element.118), channel_id=1, source_target_pairs={{0,64},{1,65},{2,10},{3,11},{4,68},{5,69},{6,14},{7,15},{8,72},{9,... | collective-permute-start | bytes 147464 | tf_op jit(solution)/shard_map/ppermute | solution.py:202
  23.5 4.9 %collective-permute-start.5 = (bf16[192,128]{1,0:T(8,128)(2,1)S(1)}, bf16[192,128]{1,0:T(8,128)(2,1)S(1)}, u32[]{:S(2)}, u32[]{:S(2)}) collective-permute-start(bf16[192,128]{1,0:T(8,128)(2,1)S(1)} %get-tuple-element.119), channel_id=1, source_target_pairs={{0,96},{1,97},{2,14},{3,15},{4,100},{5,101},{6,10},{7,11},{8,104},... | collective-permute-start | bytes 147464 | tf_op jit(solution)/shard_map/ppermute | solution.py:202
  28.3 7.2 %collective-permute-start.11 = (bf16[208,256]{1,0:T(8,128)(2,1)S(1)}, bf16[208,256]{1,0:T(8,128)(2,1)S(1)}, u32[]{:S(2)}, u32[]{:S(2)}) collective-permute-start(bf16[208,256]{1,0:T(8,128)(2,1)S(1)} %get-tuple-element.125), channel_id=1, source_target_pairs={{0,32},{1,33},{2,6},{3,7},{4,36},{5,37},{6,2},{7,3},{8,40},{9,41},... | collective-permute-start | bytes 319496 | tf_op jit(solution)/shard_map/ppermute | solution.py:202
  28.4 7.6 %collective-permute-start.12 = (bf16[208,256]{1,0:T(8,128)(2,1)S(1)}, bf16[208,256]{1,0:T(8,128)(2,1)S(1)}, u32[]{:S(2)}, u32[]{:S(2)}) collective-permute-start(bf16[208,256]{1,0:T(8,128)(2,1)S(1)} %get-tuple-element.126), channel_id=1, source_target_pairs={{0,64},{1,65},{2,10},{3,11},{4,68},{5,69},{6,14},{7,15},{8,72},{9,... | collective-permute-start | bytes 319496 | tf_op jit(solution)/shard_map/ppermute | solution.py:202
  32.3 5.1 %collective-permute-start.13 = (bf16[208,256]{1,0:T(8,128)(2,1)S(1)}, bf16[208,256]{1,0:T(8,128)(2,1)S(1)}, u32[]{:S(2)}, u32[]{:S(2)}) collective-permute-start(bf16[208,256]{1,0:T(8,128)(2,1)S(1)} %get-tuple-element.127), channel_id=1, source_target_pairs={{0,96},{1,97},{2,14},{3,15},{4,100},{5,101},{6,10},{7,11},{8,104},... | collective-permute-start | bytes 319496 | tf_op jit(solution)/shard_map/ppermute | solution.py:202
  32.3 9.2 %collective-permute-start.20 = (bf16[512,128]{1,0:T(8,128)(2,1)S(1)}, bf16[512,128]{1,0:T(8,128)(2,1)S(1)}, u32[]{:S(2)}, u32[]{:S(2)}) collective-permute-start(bf16[512,128]{1,0:T(8,128)(2,1)S(1)} %get-tuple-element.135.a), channel_id=1, source_target_pairs={{0,8},{1,9},{2,66},{3,67},{4,12},{5,13},{6,70},{7,71},{8,0},{9,1},... | collective-permute-start | bytes 393224 | tf_op jit(solution)/shard_map/ppermute | solution.py:202
  35.2 7.3 %collective-permute-start.21 = (bf16[512,128]{1,0:T(8,128)(2,1)S(1)}, bf16[512,128]{1,0:T(8,128)(2,1)S(1)}, u32[]{:S(2)}, u32[]{:S(2)}) collective-permute-start(bf16[512,128]{1,0:T(8,128)(2,1)S(1)} %get-tuple-element.135.a), channel_id=1, source_target_pairs={{0,4},{1,5},{2,34},{3,35},{4,0},{5,1},{6,38},{7,39},{8,12},{9,13},... | collective-permute-start | bytes 393224 | tf_op jit(solution)/shard_map/ppermute | solution.py:202
  35.5 7.0 %collective-permute-start.22 = (bf16[512,128]{1,0:T(8,128)(2,1)S(1)}, bf16[512,128]{1,0:T(8,128)(2,1)S(1)}, u32[]{:S(2)}, u32[]{:S(2)}) collective-permute-start(bf16[512,128]{1,0:T(8,128)(2,1)S(1)} %get-tuple-element.135.a), channel_id=1, source_target_pairs={{0,12},{1,13},{2,98},{3,99},{4,8},{5,9},{6,102},{7,103},{8,4},{9,5... | collective-permute-start | bytes 393224 | tf_op jit(solution)/shard_map/ppermute | solution.py:202
  37.4 6.1 %collective-permute-start.17 = (bf16[384,128]{1,0:T(8,128)(2,1)S(1)}, bf16[384,128]{1,0:T(8,128)(2,1)S(1)}, u32[]{:S(2)}, u32[]{:S(2)}) collective-permute-start(bf16[384,128]{1,0:T(8,128)(2,1)S(1)} %get-tuple-element.130.q0), channel_id=1, source_target_pairs={{0,4},{1,5},{2,34},{3,35},{4,0},{5,1},{6,38},{7,39},{8,12},{9,13},... | collective-permute-start | bytes 294920 | tf_op jit(solution)/shard_map/ppermute | solution.py:202
  40.0 6.3 %collective-permute-start.18 = (bf16[384,128]{1,0:T(8,128)(2,1)S(1)}, bf16[384,128]{1,0:T(8,128)(2,1)S(1)}, u32[]{:S(2)}, u32[]{:S(2)}) collective-permute-start(bf16[384,128]{1,0:T(8,128)(2,1)S(1)} %get-tuple-element.130.q0), channel_id=1, source_target_pairs={{0,8},{1,9},{2,66},{3,67},{4,12},{5,13},{6,70},{7,71},{8,0},{9,1},... | collective-permute-start | bytes 294920 | tf_op jit(solution)/shard_map/ppermute | solution.py:202
  41.5 5.7 %collective-permute-start.19 = (bf16[384,128]{1,0:T(8,128)(2,1)S(1)}, bf16[384,128]{1,0:T(8,128)(2,1)S(1)}, u32[]{:S(2)}, u32[]{:S(2)}) collective-permute-start(bf16[384,128]{1,0:T(8,128)(2,1)S(1)} %get-tuple-element.130.q0), channel_id=1, source_target_pairs={{0,12},{1,13},{2,98},{3,99},{4,8},{5,9},{6,102},{7,103},{8,4},{9,5... | collective-permute-start | bytes 294920 | tf_op jit(solution)/shard_map/ppermute | solution.py:202
  42.5 10.2 %collective-permute-start.23 = (bf16[2048,128]{1,0:T(8,128)(2,1)S(1)}, bf16[2048,128]{1,0:T(8,128)(2,1)S(1)}, u32[]{:S(2)}, u32[]{:S(2)}) collective-permute-start(bf16[2048,128]{1,0:T(8,128)(2,1)S(1)} %shard_map.121.plane), channel_id=1, source_target_pairs={{0,16},{1,17},{2,18},{3,19},{4,20},{5,21},{6,22},{7,23},{8,24},{9,... | collective-permute-start | bytes 1572872 | tf_op jit(solution)/shard_map/ppermute | solution.py:202
  43.3 11.6 %collective-permute-start.14 = (bf16[640,256]{1,0:T(8,128)(2,1)S(1)}, bf16[640,256]{1,0:T(8,128)(2,1)S(1)}, u32[]{:S(2)}, u32[]{:S(2)}) collective-permute-start(bf16[640,256]{1,0:T(8,128)(2,1)S(1)} %get-tuple-element.128.kv), channel_id=1, source_target_pairs={{0,4},{1,5},{2,34},{3,35},{4,0},{5,1},{6,38},{7,39},{8,12},{9,13},... | collective-permute-start | bytes 983048 | tf_op jit(solution)/shard_map/ppermute | solution.py:202
  43.5 11.4 %collective-permute-start.15 = (bf16[640,256]{1,0:T(8,128)(2,1)S(1)}, bf16[640,256]{1,0:T(8,128)(2,1)S(1)}, u32[]{:S(2)}, u32[]{:S(2)}) collective-permute-start(bf16[640,256]{1,0:T(8,128)(2,1)S(1)} %get-tuple-element.128.kv), channel_id=1, source_target_pairs={{0,8},{1,9},{2,66},{3,67},{4,12},{5,13},{6,70},{7,71},{8,0},{9,1},... | collective-permute-start | bytes 983048 | tf_op jit(solution)/shard_map/ppermute | solution.py:202
  46.2 10.9 %collective-permute-start.16 = (bf16[640,256]{1,0:T(8,128)(2,1)S(1)}, bf16[640,256]{1,0:T(8,128)(2,1)S(1)}, u32[]{:S(2)}, u32[]{:S(2)}) collective-permute-start(bf16[640,256]{1,0:T(8,128)(2,1)S(1)} %get-tuple-element.128.kv), channel_id=1, source_target_pairs={{0,12},{1,13},{2,98},{3,99},{4,8},{5,9},{6,102},{7,103},{8,4},{9,5... | collective-permute-start | bytes 983048 | tf_op jit(solution)/shard_map/ppermute | solution.py:202
  60.2 26.5 %copy-start = (bf16[256,3072]{1,0:T(8,128)(2,1)S(1)}, bf16[256,3072]{1,0:T(8,128)(2,1)}, u32[]{:S(2)}) copy-start(bf16[256,3072]{1,0:T(8,128)(2,1)} %table_ref.1) | copy-start | bytes 4718596
  60.2 26.5 %copy-start.3 = (bf16[32,768]{1,0:T(8,128)(2,1)S(1)}, bf16[32,768]{1,0:T(8,128)(2,1)}, u32[]{:S(2)}) copy-start(bf16[32,768]{1,0:T(8,128)(2,1)} %q_ref.1) | copy-start | bytes 147460
  60.2 26.5 %copy-start.6 = (bf16[32,768]{1,0:T(8,128)(2,1)S(1)}, bf16[32,768]{1,0:T(8,128)(2,1)}, u32[]{:S(2)}) copy-start(bf16[32,768]{1,0:T(8,128)(2,1)} %k_ref.1) | copy-start | bytes 147460
  60.2 4.5 %collective-permute-start.24 = (bf16[80,1152]{1,0:T(8,128)(2,1)S(1)}, bf16[80,1152]{1,0:T(8,128)(2,1)S(1)}, u32[]{:S(2)}, u32[]{:S(2)}) collective-permute-start(bf16[80,1152]{1,0:T(8,128)(2,1)S(1)} %get-tuple-element.147), channel_id=1, source_target_pairs={{0,32},{1,33},{2,6},{3,7},{4,36},{5,37},{6,2},{7,3},{8,40},{9,41},... | collective-permute-start | bytes 552968 | tf_op jit(solution)/shard_map/ppermute | solution.py:202
  60.3 7.1 %collective-permute-start.25 = (bf16[80,1152]{1,0:T(8,128)(2,1)S(1)}, bf16[80,1152]{1,0:T(8,128)(2,1)S(1)}, u32[]{:S(2)}, u32[]{:S(2)}) collective-permute-start(bf16[80,1152]{1,0:T(8,128)(2,1)S(1)} %get-tuple-element.148), channel_id=1, source_target_pairs={{0,64},{1,65},{2,10},{3,11},{4,68},{5,69},{6,14},{7,15},{8,72},{9,... | collective-permute-start | bytes 552968 | tf_op jit(solution)/shard_map/ppermute | solution.py:202
  62.4 6.9 %collective-permute-start.26 = (bf16[80,1152]{1,0:T(8,128)(2,1)S(1)}, bf16[80,1152]{1,0:T(8,128)(2,1)S(1)}, u32[]{:S(2)}, u32[]{:S(2)}) collective-permute-start(bf16[80,1152]{1,0:T(8,128)(2,1)S(1)} %get-tuple-element.149), channel_id=1, source_target_pairs={{0,96},{1,97},{2,14},{3,15},{4,100},{5,101},{6,10},{7,11},{8,104},... | collective-permute-start | bytes 552968 | tf_op jit(solution)/shard_map/ppermute | solution.py:202
  70.6 16.1 %collective-permute-start.27 = (bf16[48,1536]{1,0:T(8,128)(2,1)S(1)}, bf16[48,1536]{1,0:T(8,128)(2,1)S(1)}, u32[]{:S(2)}, u32[]{:S(2)}) collective-permute-start(bf16[48,1536]{1,0:T(8,128)(2,1)S(1)} %get-tuple-element.151), channel_id=1, source_target_pairs={{0,2},{1,3},{2,0},{3,1},{4,6},{5,7},{6,4},{7,5},{8,10},{9,11},{10,... | collective-permute-start | bytes 442376 | tf_op jit(solution)/shard_map/ppermute | solution.py:202
  77.7 6.2 %collective-permute-start.28 = (bf16[48,1152]{1,0:T(8,128)(2,1)S(1)}, bf16[48,1152]{1,0:T(8,128)(2,1)S(1)}, u32[]{:S(2)}, u32[]{:S(2)}) collective-permute-start(bf16[48,1152]{1,0:T(8,128)(2,1)S(1)} %get-tuple-element.150), channel_id=1, source_target_pairs={{0,1},{1,0},{2,3},{3,2},{4,5},{5,4},{6,7},{7,6},{8,9},{9,8},{10,11... | collective-permute-start | bytes 331784 | tf_op jit(solution)/shard_map/ppermute | solution.py:202
  80.2 6.5 %collective-permute-start.29 = (bf16[48,1152]{1,0:T(8,128)(2,1)S(1)}, bf16[48,1152]{1,0:T(8,128)(2,1)S(1)}, u32[]{:S(2)}, u32[]{:S(2)}) collective-permute-start(bf16[48,1152]{1,0:T(8,128)(2,1)S(1)} %get-tuple-element.152), channel_id=1, source_target_pairs={{0,3},{1,2},{2,1},{3,0},{4,7},{5,6},{6,5},{7,4},{8,11},{9,10},{10,... | collective-permute-start | bytes 331784 | tf_op jit(solution)/shard_map/ppermute | solution.py:202
  (4 other events, 57.5 us)

commit v2 on v1

--- a/solution.py
+++ b/solution.py
@@ -14,8 +14,11 @@
 CON = 96
 TXT = 64
 ROWS = CON + TXT
+LINE_CON = 320
+LINE_TXT = 176
+LINE = LINE_CON + LINE_TXT
 MIB = 1 << 20
-NEAR_US, FAR_US, PROJ_US, PROMPT_US = 5.0, 4.0, 5.0, 3.0
+PROJ_US, PROMPT_US = 5.0, 9.0
 FACTOR = HD ** (-0.5) * math.log2(math.e)
 
 
@@ -194,8 +197,8 @@
     return pairs(lambda x, zl, y, c, g: (x, zl ^ 1, y, c, g))
 
 
-def swap_core(dg):
-    return pairs(lambda x, zl, y, c, g: (x, zl, y, c ^ 1, g ^ dg))
+def swap_core():
+    return pairs(lambda x, zl, y, c, g: (x, zl, y, c ^ 1, g))
 
 
 def send(array, pairing):
@@ -295,32 +298,89 @@
     plan_ref[2:8, :] = jnp.zeros((6, n), jnp.int32)
 
 
-def empty_bias(at, counts, slots, blocks_lanes):
-    lane = lax.broadcasted_iota(jnp.int32, (1, blocks_lanes), 1)
-    block = jnp.zeros((1, blocks_lanes), jnp.int32)
-    for j in range(1, 16):
-        block = block + (lane >= j * slots).astype(jnp.int32)
-    item_u = (block & 3) ^ at[4]
-    item_v = (block >> 2) ^ at[5]
-    column = jnp.where(at[2] == 0, item_u * 4 + item_v, item_v * 4 + item_u)
-    hot = lax.broadcasted_iota(jnp.int32, (16, blocks_lanes), 0) == column
-    held = jnp.sum(jnp.where(hot, counts, 0.0), axis=0, keepdims=True)
-    return jnp.where((lane - block * slots).astype(F32) < held, 0.0, -1e30)
-
-
-def pack_kernel(at, con_ref, txt_ref, plan_ref, out_ref, spot_ref, con_bias, txt_bias):
+def to_row(column):
+    n = column.shape[0]
+    diagonal = lax.broadcasted_iota(jnp.int32, (n, n), 0) == lax.broadcasted_iota(
+        jnp.int32, (n, n), 1
+    )
+    return jnp.sum(jnp.where(diagonal, column, 0.0), axis=0, keepdims=True)
+
+
+def line_of(at, column):
+    first, second = column >> 2, column & 3
+    return jnp.where(at[2] == 0, first, second), jnp.where(at[2] == 0, second, first)
+
+
+def line_plan(at, counts):
+    u, v = line_of(at, lax.broadcasted_iota(jnp.int32, (16, 16), 0))
+    u2, v2 = line_of(at, lax.broadcasted_iota(jnp.int32, (16, 16), 1))
+    row = to_row(counts)
+    same = v == v2
+    before = same & ((u2 ^ at[4]) < (u ^ at[4]))
+    skipped = jnp.sum(jnp.where(before, row, 0.0), axis=1, keepdims=True)
+    total = jnp.sum(jnp.where(same, row, 0.0), axis=1, keepdims=True)
+    other = jnp.sum(jnp.where(u == u2, row, 0.0), axis=1, keepdims=True)
+    return skipped, total, jnp.max(jnp.maximum(total, other), axis=0, keepdims=True)
+
+
+def per_lane(values, column):
+    hot = lax.broadcasted_iota(jnp.int32, (16, column.shape[1]), 0) == column
+    return jnp.sum(jnp.where(hot, values, 0.0), axis=0, keepdims=True)
+
+
+def blocks_of(lanes, size, blocks):
+    lane = lax.broadcasted_iota(jnp.int32, (1, lanes), 1)
+    block = jnp.zeros((1, lanes), jnp.int32)
+    for j in range(1, blocks):
+        block = block + (lane >= j * size).astype(jnp.int32)
+    return block, (lane - block * size).astype(F32)
+
+
+def column_at(at, u, v):
+    return jnp.where(at[2] == 0, u * 4 + v, v * 4 + u)
+
+
+def line_targets(at, counts, skipped, slots):
+    block, slot = blocks_of(4 * slots, slots, 4)
+    column = column_at(at, block ^ at[4], jnp.zeros_like(block) + at[5])
+    target = per_lane(skipped, column) + slot
+    return jnp.where(slot < per_lane(counts, column), target, -1.0).astype(jnp.int32)
+
+
+def line_bias(at, total, rows):
+    block, slot = blocks_of(4 * rows, rows, 4)
+    column = column_at(at, jnp.zeros_like(block) + at[4], block ^ at[5])
+    return jnp.where(slot < per_lane(total, column), 0.0, -1e30)
+
+
+def pack_kernel(
+    at, con_ref, txt_ref, plan_ref, out_ref, spot_ref, con_bias, txt_bias, con_line, txt_line
+):
     ids = jnp.concatenate([con_ref[...], txt_ref[...]], axis=1)
     n = ids.shape[1]
     n_con = con_ref.shape[1]
     owner = ids >> 8
     column = column_of(owner)
     spot, (con_counts, txt_counts) = ranks(column, 16, (n_con // 256,))
-    con_bias[...] = empty_bias(at, con_counts, CON, 16 * CON)
-    txt_bias[...] = empty_bias(at, txt_counts, TXT, 16 * TXT)
-    spot_ref[0:1, :] = spot
+    con_skip, con_total, con_most = line_plan(at, con_counts)
+    txt_skip, txt_total, txt_most = line_plan(at, txt_counts)
+    con_bias[...] = line_bias(at, con_total, LINE_CON)
+    txt_bias[...] = line_bias(at, txt_total, LINE_TXT)
+    con_line[...] = line_targets(at, con_counts, con_skip, CON)
+    txt_line[...] = line_targets(at, txt_counts, txt_skip, TXT)
+    _, item_v = line_of(at, column)
+    spot_ref[0:1, :] = (
+        (item_v ^ at[5]) * LINE_CON + per_lane(con_skip, column).astype(jnp.int32) + spot
+    )
+    over = jnp.maximum(
+        jnp.maximum(
+            jnp.max(con_counts, axis=0, keepdims=True) - CON,
+            jnp.max(txt_counts, axis=0, keepdims=True) - TXT,
+        ),
+        jnp.maximum(con_most - LINE_CON, txt_most - LINE_TXT),
+    )
     spot_ref[1:2, :] = jnp.maximum(
-        jnp.maximum(most(con_counts, n) - CON, most(txt_counts, n) - TXT),
-        plan_ref[1:2, :] - SLOTS,
+        jnp.broadcast_to(over.astype(jnp.int32), (1, n)), plan_ref[1:2, :] - SLOTS
     )
     spot_ref[2:8, :] = jnp.zeros((6, n), jnp.int32)
     here = column == at[1]
@@ -394,12 +454,19 @@
                 out[ROWS:, HD:] = heads[h][0][CON // 2 :]
 
 
-def join_kernel(a, b, c, d, q_out, kv_out):
+def join_kernel(a, b, c, d, con_line, txt_line, out, con, txt):
     for i, ref in enumerate((a, b, c, d)):
-        kv_out[i * CON : (i + 1) * CON, :] = ref[0:CON, :]
-        kv_out[4 * CON + i * TXT : 4 * CON + (i + 1) * TXT, :] = ref[CON:ROWS, :]
-        q_out[i * CON : i * CON + CON // 2, :] = ref[ROWS:, 0:HD]
-        q_out[i * CON + CON // 2 : (i + 1) * CON, :] = ref[ROWS:, HD:]
+        con[i * CON : (i + 1) * CON, 0 : 2 * HD] = ref[0:CON, :]
+        con[i * CON : i * CON + CON // 2, 2 * HD :] = ref[ROWS:, 0:HD]
+        con[i * CON + CON // 2 : (i + 1) * CON, 2 * HD :] = ref[ROWS:, HD:]
+        txt[i * TXT : (i + 1) * TXT, :] = ref[CON:ROWS, :]
+    hot = lax.broadcasted_iota(jnp.int32, (LINE_CON, 4 * CON), 0) == con_line[...]
+    found = nn(hot.astype(F32).astype(BF), con[...]).astype(BF)
+    out[0:LINE_CON, :] = found[:, 0 : 2 * HD]
+    out[LINE:, 0:HD] = found[: LINE_CON // 2, 2 * HD :]
+    out[LINE:, HD:] = found[LINE_CON // 2 :, 2 * HD :]
+    hot = lax.broadcasted_iota(jnp.int32, (LINE_TXT, 4 * TXT), 0) == txt_line[...]
+    out[LINE_CON:LINE, :] = nn(hot.astype(F32).astype(BF), txt[...]).astype(BF)
 
 
 def image_heads_kernel(at, own, core, *outs):
@@ -423,11 +490,11 @@
         kv_out[n * (4 + i) : n * (5 + i), :] = ref[2 * n :, :]
 
 
-def plane_kernel(a, b, c, d, out):
-    n = a.shape[0] // 2
-    for i, ref in enumerate((a, b, c, d)):
+def planes_kernel(own, other, out):
+    n = own.shape[0] // 2
+    for i, ref in enumerate((own, other)):
         out[n * i : n * (i + 1), :] = ref[0:n, :]
-        out[n * (4 + i) : n * (5 + i), :] = ref[n:, :]
+        out[n * (2 + i) : n * (3 + i), :] = ref[n:, :]
 
 
 def weigh(q, parts, factor):
@@ -461,53 +528,33 @@
     return jnp.concatenate([values, jnp.ones_like(values)], axis=1)
 
 
-def plane_parts(plane):
-    n = plane.shape[0] // 2
-    return (plane[0:n, :], with_ones(plane[n:, :]), None)
-
-
-def near_kernel(pick, q0, q1, q2, q3, plane, kv, con_bias, txt_bias, img_q, q_out, cm, cs, im, ims):
-    n = 4 * CON
-    q_out[...] = sum(
-        nn(pick[:, a * n : (a + 1) * n], ref[...]) for a, ref in enumerate((q0, q1, q2, q3))
-    ).astype(BF)
-    images = plane_parts(plane)
-    own = (kv[0:n, 0:HD], with_ones(kv[0:n, HD:]), con_bias[:, 0:n])
-    for b in range(q_out.shape[0] // 256):
-        rows = slice(b * 256, (b + 1) * 256)
-        cm[rows, :], cs[rows, :] = weigh(q_out[rows, :], (images, own), None)
-    text = (kv[n:, 0:HD], with_ones(kv[n:, HD:]), txt_bias[:, 0 : 4 * TXT])
-    im[...], ims[...] = weigh(img_q[...], (images, text), FACTOR)
-
-
-def far_kernel(plane, con_q, img_q, cm, cs, im, ims, cm_out, cs_out, im_out, ims_out):
-    images = plane_parts(plane)
-    for b in range(con_q.shape[0] // 256):
-        rows = slice(b * 256, (b + 1) * 256)
-        part = weigh(con_q[rows, :], (images,), None)
-        cm_out[rows, :], cs_out[rows, :] = join(part, (cm[rows, :], cs[rows, :]))
-    part = weigh(img_q[...], (images,), FACTOR)
-    im_out[...], ims_out[...] = join(part, (im[...], ims[...]))
-
-
-def prompt_kernel(con_bias, txt_bias, c1, c2, c3, con_q, cm, cs, img_q, im, ims, *refs):
-    outs, (con_out,) = refs[:4], refs[4:]
-    n, m = 4 * CON, 4 * TXT
-    con_parts, txt_parts = [], []
-    for a, ref in enumerate((c1, c2, c3)):
-        con, txt = ref[0:n, :], ref[n:, :]
-        con_parts.append(
-            (con[:, 0:HD], with_ones(con[:, HD:]), con_bias[:, (a + 1) * n : (a + 2) * n])
-        )
-        txt_parts.append(
-            (txt[:, 0:HD], with_ones(txt[:, HD:]), txt_bias[:, (a + 1) * m : (a + 2) * m])
-        )
-    img = merge(weigh(img_q[...], txt_parts, FACTOR), (im[...], ims[...]))
-    n_con = con_q.shape[0]
+def image_self_kernel(i0, i1, i2, i3, q, keys, vals, peak, summed):
+    part = i0.shape[0] // 2
+    for i, ref in enumerate((i0, i1, i2, i3)):
+        keys[i * part : (i + 1) * part, :] = ref[0:part, :]
+        vals[i * part : (i + 1) * part, :] = with_ones(ref[part:, :])
+    peak[...], summed[...] = weigh(q[...], ((keys[...], vals[...], None),), FACTOR)
+
+
+def prompt_kernel(pick, l0, l1, l2, l3, con_bias, txt_bias, keys, vals, img_q, im, ims, *refs):
+    outs, (con_q, con_k, con_v, txt_k, txt_v, con_out) = refs[:4], refs[4:]
+    n, m = LINE_CON, LINE_TXT
+    for a, ref in enumerate((l0, l1, l2, l3)):
+        con_q[a * n : a * n + n // 2, :] = ref[LINE:, 0:HD]
+        con_q[a * n + n // 2 : (a + 1) * n, :] = ref[LINE:, HD:]
+        con_k[a * n : (a + 1) * n, :] = ref[0:n, 0:HD]
+        con_v[a * n : (a + 1) * n, :] = with_ones(ref[0:n, HD:])
+        txt_k[a * m : (a + 1) * m, :] = ref[n:LINE, 0:HD]
+        txt_v[a * m : (a + 1) * m, :] = with_ones(ref[n:LINE, HD:])
+    text = weigh(img_q[...], ((txt_k[...], txt_v[...], txt_bias[...]),), FACTOR)
+    img = merge(text, (im[...], ims[...]))
+    n_con = con_out.shape[0]
     for b in range(n_con // 256):
         rows = slice(b * 256, (b + 1) * 256)
-        part = weigh(con_q[rows, :], con_parts, None)
-        con_out[rows, :] = merge(part, (cm[rows, :], cs[rows, :]))
+        q = nn(pick[rows, :], con_q[...]).astype(BF)
+        parts = ((keys[...], vals[...], None), (con_k[...], con_v[...], con_bias[...]))
+        _, summed = weigh(q, parts, None)
+        con_out[rows, :] = (summed[:, 0:HD] / summed[:, HD:]).astype(BF)
     dots = nt(img, con_out[...]).astype(BF)
     con_f = con_out[...].astype(F32)
     con_sq = nt(jnp.ones((16, HD), F32), con_f * con_f, precision=lax.Precision.HIGHEST).astype(BF)
@@ -519,7 +566,7 @@
         out[64:80, n_con:] = jnp.zeros((16, HD), BF)
 
 
-def head_sum_kernel(at, b0, b1, b2, b3, own, core, diag, out_own):
+def head_sum_kernel(at, b0, b1, b2, b3, own, core, out_own):
     n_con = b0.shape[1] - HD
     total = jnp.zeros((80, n_con), F32)
     outs = [jnp.zeros((64, HD), BF) for _ in range(3)]
@@ -534,7 +581,7 @@
         image_sq = image_sq + jnp.sum(out_f * out_f, axis=1, keepdims=True)
     image_sq = jnp.broadcast_to(image_sq, (64, HD)).astype(BF)
     total = total.astype(BF)
-    for ref, row in ((own, 0), (core, 32), (diag, 32)):
+    for ref, row in ((own, 0), (core, 32)):
         ref[0:32, 0:n_con] = total[row : row + 32]
         ref[32:48, 0:n_con] = total[64:80]
         ref[0:32, n_con : n_con + HD] = image_sq[row : row + 32]
@@ -546,22 +593,23 @@
         out_own[:, h * HD : (h + 1) * HD] = outs[h][0:32]
 
 
-def finish_kernel(at, own, core, head, diag, out_own, img_ref, sal_ref):
+def core_sum_kernel(own, core, out):
+    cols = own.shape[1]
+    out[...] = (own[...].astype(F32) + core[:, 0:cols].astype(F32)).astype(BF)
+
+
+def finish_kernel(at, own, head, core, out_own, img_ref, sal_ref):
     n_con = own.shape[1] - HD
     width = 12 * HD
-    cols = n_con + HD
-    near = own[...].astype(F32) + core[:, 0:cols].astype(F32)
-    far = head[...].astype(F32) + diag[...].astype(F32)
-    total = near + far
+    total = own[...].astype(F32) + head[...].astype(F32)
     con_rms = jnp.sqrt(total[32:33, 0:n_con] / width + 1e-06)
     img_rms = jnp.sqrt(total[0:32, n_con : n_con + 1] / width + 1e-06)
-    sal = total[0:32, 0:n_con] / (math.sqrt(width) * con_rms * img_rms)
-    sal_ref[...] = sal
+    sal_ref[...] = total[0:32, 0:n_con] / (math.sqrt(width) * con_rms * img_rms)
     half = 3 * HD
     mine = pl.ds(pl.multiple_of(at[2] * half, half), half)
     theirs = pl.ds(pl.multiple_of((1 - at[2]) * half, half), half)
     img_ref[:, mine] = out_own[...]
-    img_ref[:, theirs] = core[0:32, cols:]
+    img_ref[:, theirs] = core[0:32, n_con + HD :]
 
 
 def packed(
@@ -594,38 +642,35 @@
     )(at, con_ids, text_ids, token_table, img_q, img_k, img_v)
     far_rows = send(own_rows, swap_z(2))
     column_rows = [own_rows] + [send(own_rows, swap_z(s)) for s in (1, 3)]
-    core_both = send(own_both, swap_core(0))
-
-    pack, spots, con_bias, txt_bias = call(
+    core_both = send(own_both, swap_core())
+
+    pack, spots, con_bias, txt_bias, con_line, txt_line = call(
         pack_kernel,
         (
             sds((ROWS, 8 * SLOTS)),
             sds((8, n), jnp.int32),
-            sds((1, 16 * CON), F32),
-            sds((1, 16 * TXT), F32),
+            sds((1, 4 * LINE_CON), F32),
+            sds((1, 4 * LINE_TXT), F32),
+            sds((1, 4 * CON), jnp.int32),
+            sds((1, 4 * TXT), jnp.int32),
         ),
     )(at, con_ids, text_ids, plan)
-    owner = concept_ids >> 8
-    item_x = owner >> 5
-    item_y = (owner >> 2) & 3
-    item_u = jnp.where(c == 0, item_x, item_y)
-    item_v = jnp.where(c == 0, item_y, item_x)
-    con_slot = ((v ^ item_v) * 4 + (u ^ item_u)) * CON + spots[0, :n_con]
-    pick = (con_slot[:, None] == jnp.arange(16 * CON)[None, :]).astype(BF)
+    con_slot = spots[0, :n_con]
+    pick = (con_slot[:, None] == jnp.arange(4 * LINE_CON)[None, :]).astype(BF)
     shift_scale = lax.dynamic_index_in_dim(modulation, step_index[0], 0, keepdims=False)
     fits = (spots[1, 0] <= 0).astype(jnp.int32)
 
     image_blocks = call(
         image_heads_kernel, tuple(sds((6 * n_img, HD)) for _ in range(4))
     )(at, own_img, core_both)
-    far_rows, pack, shift_scale, pick, fits, *image_blocks = lax.optimization_barrier(
-        (far_rows, pack, shift_scale, pick, fits, *image_blocks)
-    )
-    column_rows.insert(2, far_rows)
-    other_rows = [core_both] + [send(r, swap_core(0)) for r in column_rows[1:]]
-
     image_blocks = [image_blocks[0]] + [send(image_blocks[s], swap_u(s)) for s in (2, 1, 3)]
     image_blocks = [image_blocks[0], image_blocks[2], image_blocks[1], image_blocks[3]]
+    column_rows[1], image_blocks[2] = lax.optimization_barrier((column_rows[1], image_blocks[2]))
+    far_rows, pack, shift_scale, fits, image_blocks[1] = lax.optimization_barrier(
+        (far_rows, pack, shift_scale, fits, image_blocks[1])
+    )
+    column_rows.insert(2, far_rows)
+    other_rows = [core_both] + [send(r, swap_core()) for r in column_rows[1:]]
 
     qkv = call(
         project_kernel,
@@ -644,55 +689,58 @@
     image_q, image_kv = call(
         image_join_kernel, (sds((8 * n_img, HD)), sds((16 * n_img, HD))), smem=0
     )(*image_blocks)
-    image_kvs = [image_kv] + [send(image_kv, swap_v(s)) for s in (2, 1, 3)]
-
+    other_kv = send(image_kv, swap_plane())
     qkv = [first] + [send(qkv[s], swap_u(s)) for s in (2, 1, 3)]
     qkv = [qkv[0], qkv[2], qkv[1], qkv[3]]
-    q_join, kv_join = call(
-        join_kernel, (sds((4 * CON, HD)), sds((4 * ROWS, 2 * HD))), smem=0
-    )(*qkv)
-    plane = call(plane_kernel, sds((64 * n_img, HD)), smem=0)(*image_kvs)
-    q_chunks = [q_join] + [send(q_join, swap_v(s)) for s in (2, 1, 3)]
-    q_chunks = [q_chunks[0], q_chunks[2], q_chunks[1], q_chunks[3]]
-    other_plane = send(plane, swap_plane())
-    kv_chunks = [send(kv_join, swap_v(s)) for s in (2, 1, 3)]
-    kv_chunks = [kv_chunks[1], kv_chunks[0], kv_chunks[2]]
-
-    stats = (
-        sds((n_con, 1), F32),
-        sds((n_con, 2 * HD), F32),
-        sds((8 * n_img, 1), F32),
-        sds((8 * n_img, 2 * HD), F32),
-    )
-    con_q, *near = call(near_kernel, (sds((n_con, HD)),) + stats, us=NEAR_US, smem=0)(
-        pick, *q_chunks, plane, kv_join, con_bias, txt_bias, image_q
-    )
-    con_stats = call(far_kernel, stats, us=FAR_US, smem=0)(other_plane, con_q, image_q, *near)
-    con_stats, image_stats = con_stats[:2], con_stats[2:]
+    other_kv, *qkv = lax.optimization_barrier((other_kv, *qkv))
+    planes = call(planes_kernel, sds((32 * n_img, HD)), smem=0)(image_kv, other_kv)
+    image_kvs = [planes] + [send(planes, swap_v(s)) for s in (2, 1, 3)]
+    line = call(
+        join_kernel,
+        sds((LINE + LINE_CON // 2, 2 * HD)),
+        scratch=(pltpu.VMEM((4 * CON, 3 * HD), BF), pltpu.VMEM((4 * TXT, 2 * HD), BF)),
+        smem=0,
+    )(*qkv, con_line, txt_line)
+    lines = [line] + [send(line, swap_v(s)) for s in (2, 1, 3)]
+    lines = [lines[0], lines[2], lines[1], lines[3]]
+
+    all_img = 64 * n_img
+    image_self = call(
+        image_self_kernel,
+        (
+            sds((all_img, HD)),
+            sds((all_img, 2 * HD)),
+            sds((8 * n_img, 1), F32),
+            sds((8 * n_img, 2 * HD), F32),
+        ),
+        us=2.0,
+        smem=0,
+    )
+    keys, vals, *image_stats = image_self(*image_kvs, image_q)
     blocks = call(
         prompt_kernel,
         tuple(sds((80, n_con + HD)) for _ in range(4)),
-        scratch=(pltpu.VMEM((n_con, HD), BF),),
+        scratch=(
+            pltpu.VMEM((4 * LINE_CON, HD), BF),
+            pltpu.VMEM((4 * LINE_CON, HD), BF),
+            pltpu.VMEM((4 * LINE_CON, 2 * HD), BF),
+            pltpu.VMEM((4 * LINE_TXT, HD), BF),
+            pltpu.VMEM((4 * LINE_TXT, 2 * HD), BF),
+            pltpu.VMEM((n_con, HD), BF),
+        ),
         us=PROMPT_US,
         smem=0,
-    )(con_bias, txt_bias, *kv_chunks, con_q, *con_stats, image_q, *image_stats)
+    )(pick, *lines, con_bias, txt_bias, keys, vals, image_q, *image_stats)
     blocks = [blocks[0]] + [send(blocks[s], swap_u(s)) for s in (2, 1, 3)]
     blocks = [blocks[0], blocks[2], blocks[1], blocks[3]]
-    own, core, diag, out_own = call(
+    own, core, out_own = call(
         head_sum_kernel,
-        (sds((48, n_con + HD)), sds((48, n_con + 4 * HD)), sds((48, n_con + HD)), sds((32, half))),
+        (sds((48, n_con + HD)), sds((48, n_con + 4 * HD)), sds((32, half))),
     )(at, *blocks)
-    last = (
-        at,
-        own,
-        send(core, swap_core(0)),
-        send(own, swap_z(2)),
-        send(diag, swap_core(1)),
-        out_own,
-    )
-    finish = call(
-        finish_kernel, (sds((n_img, 2 * half)), sds((n_img, n_con), F32))
-    )
+    core = send(core, swap_core())
+    own = call(core_sum_kernel, sds((48, n_con + HD)), smem=0)(own, core)
+    last = (at, own, send(own, swap_z(2)), core, out_own)
+    finish = call(finish_kernel, (sds((n_img, 2 * half)), sds((n_img, n_con), F32)))
 
     def finished():
         img_out, saliency = finish(*last)

time: 88.8 us -> 91.2 us (1.027)
  waiting for transfers between devices: 16.3 us -> 22.3 us
  starting transfers between devices: 43.4 us -> 39.1 us
    ppermute x29 -> x25, waiting for transfers between devices: 16.3 us -> 22.3 us  [send(): return lax.ppermute(array, ('ctx', 'head'), pairing)]
    ppermute x29 -> x25, starting transfers between devices: 43.4 us -> 39.1 us  [send(): return lax.ppermute(array, ('ctx', 'head'), pairing)]
  transfers between devices with their start and end apart: 29 -> 25, of which waited for: 8 -> 11; matrix products, arithmetic and copies ran while one was open for 4% -> 4% of each run, Pallas kernels for 16% -> 9%
where the time goes in v2:
time: 91.2 us; the launch traced here: 90.9 us
  starting transfers between devices  39.1 us (43%)
  Pallas kernels  23.1 us (25%)
  waiting for transfers between devices  22.3 us (24%)
  between operations  2.09 us (2%)
  local copies, waits for them, and re-layouts  1.99 us (2%)
  other arithmetic  1.99 us (2%)
    ppermute x25, starting transfers between devices, send(): return lax.ppermute(array, ('ctx', 'head'), pairing)  39.1 us
    pallas_call x12, Pallas kernels, run(): pl.pallas_call(kernel, out_shape=outs, in_specs=[sm] * smem + [vm] * (len...  23.1 us
    ppermute x25, waiting for transfers between devices, send(): return lax.ppermute(array, ('ctx', 'head'), pairing)  22.3 us
    convert_element_type x1, other arithmetic, packed(): pick = (con_slot[:, None] == jnp.arange(4 * LINE_CON)[None, :]).astype(BF)  1.99 us
  transfers between devices with their start and end apart: 25, of which 11 were waited for; matrix products, arithmetic and copies ran while one was open for 4% of the time, Pallas kernels for 9%

profile of v2, /device:TPU:1, one launch (start us, length us, event | category | flops | bytes accessed | tf_op | source)
XLA Modules:
  0.0 90.9 jit_solution(6752120198036056208)
XLA Ops:
  0.7 2.7 %shard_map.115 = (bf16[32,3072]{1,0:T(8,128)(2,1)S(1)}, bf16[48,3072]{1,0:T(8,128)(2,1)S(1)}, bf16[96,384]{1,0:T(8,128)(2,1)S(1)}, s32[8,1536]{1,0:T(8,128)S(1)}) custom-call(s32[6]{0:T(128)S(1)} %stack.45.at, s32[1,1024]{1,0:T(1,128)} %bitcast.136, s32[1,512]{1,0:T(1,128)} %bitcast.138, bf16[256,3072]{1,0:T(8,128)(2,1)} %table_ref.1, ...), custom_call_target="tpu_custom_call" | custom-call | flops 1100000000 | tf_op jit(solution)/shard_map/pallas_call | solution.py:220
  3.5 2.5 %collective-permute-start.4 = (bf16[32,3072]{1,0:T(8,128)(2,1)S(1)}, bf16[32,3072]{1,0:T(8,128)(2,1)S(1)}, u32[]{:S(2)}, u32[]{:S(2)}) collective-permute-start(bf16[32,3072]{1,0:T(8,128)(2,1)S(1)} %get-tuple-element.97.refs_0_), channel_id=1, source_target_pairs={{0,16},{1,17},{2,18},{3,19},{4,20},{5,21},{6,22},{7,23},{8,24},{9,... | collective-permute-start | bytes 589832 | tf_op jit(solution)/shard_map/ppermute | solution.py:205
  6.0 3.3 %collective-permute-start.1 = (bf16[32,3072]{1,0:T(8,128)(2,1)S(1)}, bf16[32,3072]{1,0:T(8,128)(2,1)S(1)}, u32[]{:S(2)}, u32[]{:S(2)}) collective-permute-start(bf16[32,3072]{1,0:T(8,128)(2,1)S(1)} %get-tuple-element.97.refs_0_), channel_id=1, source_target_pairs={{0,1},{1,0},{2,3},{3,2},{4,5},{5,4},{6,7},{7,6},{8,9},{9,8},{10,11... | collective-permute-start | bytes 589832 | tf_op jit(solution)/shard_map/ppermute | solution.py:205
  9.3 1.2 %collective-permute-start.2 = (bf16[48,3072]{1,0:T(8,128)(2,1)S(1)}, bf16[48,3072]{1,0:T(8,128)(2,1)S(1)}, u32[]{:S(2)}, u32[]{:S(2)}) collective-permute-start(bf16[48,3072]{1,0:T(8,128)(2,1)S(1)} %get-tuple-element.102), channel_id=1, source_target_pairs={{0,2},{1,3},{2,0},{3,1},{4,6},{5,7},{6,4},{7,5},{8,10},{9,11},{10,... | collective-permute-start | bytes 884744 | tf_op jit(solution)/shard_map/ppermute | solution.py:205
  12.5 3.0 %collective-permute-start.5 = (bf16[192,128]{1,0:T(8,128)(2,1)S(1)}, bf16[192,128]{1,0:T(8,128)(2,1)S(1)}, u32[]{:S(2)}, u32[]{:S(2)}) collective-permute-start(bf16[192,128]{1,0:T(8,128)(2,1)S(1)} %get-tuple-element.107), channel_id=1, source_target_pairs={{0,64},{1,65},{2,10},{3,11},{4,68},{5,69},{6,14},{7,15},{8,72},{9,... | collective-permute-start | bytes 147464 | tf_op jit(solution)/shard_map/ppermute | solution.py:205
  15.9 1.2 %shard_map.116 = (bf16[160,256]{1,0:T(8,128)(2,1)S(1)}, s32[8,1536]{1,0:T(8,128)S(1)}, f32[1,1280]{1,0:T(1,128)S(1)}, f32[1,704]{1,0:T(1,128)S(1)}, s32[1,384]{1,0:T(1,128)S(1)}, /*index=5*/s32[1,256]{1,0:T(1,128)S(1)}) custom-call(s32[6]{0:T(128)S(1)} %stack.45.at, s32[1,1024]{1,0:T(1,128)S(1)} %bitcast.137, s32[1,512]{1,0:T(1,128)S(1)} %bitcast.139, ...), custom_call_target="tpu_custom_call" | custom-call | flops 1100000000 | tf_op jit(solution)/shard_map/pallas_call | solution.py:220
  18.3 2.2 %collective-permute-done.7.refs_3_ = bf16[32,3072]{1,0:T(8,128)(2,1)S(1)} collective-permute-done((bf16[32,3072]{1,0:T(8,128)(2,1)S(1)}, bf16[32,3072]{1,0:T(8,128)(2,1)S(1)}, u32[]{:S(2)}, u32[]{:S(2)}) %collective-permute-start.7) | collective-permute-done | bytes 196640 | tf_op jit(solution)/shard_map/ppermute | solution.py:205
  20.5 1.5 %collective-permute-start.10 = (bf16[32,3072]{1,0:T(8,128)(2,1)S(1)}, bf16[32,3072]{1,0:T(8,128)(2,1)S(1)}, u32[]{:S(2)}, u32[]{:S(2)}) collective-permute-start(bf16[32,3072]{1,0:T(8,128)(2,1)S(1)} %collective-permute-done.7.refs_3_), channel_id=1, source_target_pairs={{0,2},{1,3},{2,0},{3,1},{4,6},{5,7},{6,4},{7,5},{8,10},{9,11},{10,... | collective-permute-start | bytes 589832 | tf_op jit(solution)/shard_map/ppermute | solution.py:205
  22.6 2.7 %collective-permute-start.6 = (bf16[192,128]{1,0:T(8,128)(2,1)S(1)}, bf16[192,128]{1,0:T(8,128)(2,1)S(1)}, u32[]{:S(2)}, u32[]{:S(2)}) collective-permute-start(bf16[192,128]{1,0:T(8,128)(2,1)S(1)} %get-tuple-element.109), channel_id=1, source_target_pairs={{0,96},{1,97},{2,14},{3,15},{4,100},{5,101},{6,10},{7,11},{8,104},... | collective-permute-start | bytes 147464 | tf_op jit(solution)/shard_map/ppermute | solution.py:205
  25.3 4.7 %shard_map.118 = (bf16[208,256]{1,0:T(8,128)(2,1)S(1)}, bf16[208,256]{1,0:T(8,128)(2,1)S(1)}, bf16[208,256]{1,0:T(8,128)(2,1)S(1)}, bf16[208,256]{1,0:T(8,128)(2,1)S(1)}) custom-call(s32[6]{0:T(128)S(1)} %stack.45.at, bf16[160,256]{1,0:T(8,128)(2,1)S(1)} %get-tuple-element.110.pack_ref, bf16[32,3072]{1,0:T(8,128)(2,1)S(1)} %get-tuple-element.97.refs_0_, ...), custom_call_target="tpu_custom_call" | custom-call | flops 5500000256 | tf_op jit(solution)/shard_map/pallas_call | solution.py:220
  30.3 2.3 %collective-permute-start.13 = (bf16[208,256]{1,0:T(8,128)(2,1)S(1)}, bf16[208,256]{1,0:T(8,128)(2,1)S(1)}, u32[]{:S(2)}, u32[]{:S(2)}) collective-permute-start(bf16[208,256]{1,0:T(8,128)(2,1)S(1)} %get-tuple-element.122), channel_id=1, source_target_pairs={{0,64},{1,65},{2,10},{3,11},{4,68},{5,69},{6,14},{7,15},{8,72},{9,... | collective-permute-start | bytes 319496 | tf_op jit(solution)/shard_map/ppermute | solution.py:205
  32.6 1.5 %collective-permute-start.14 = (bf16[208,256]{1,0:T(8,128)(2,1)S(1)}, bf16[208,256]{1,0:T(8,128)(2,1)S(1)}, u32[]{:S(2)}, u32[]{:S(2)}) collective-permute-start(bf16[208,256]{1,0:T(8,128)(2,1)S(1)} %get-tuple-element.123), channel_id=1, source_target_pairs={{0,96},{1,97},{2,14},{3,15},{4,100},{5,101},{6,10},{7,11},{8,104},... | collective-permute-start | bytes 319496 | tf_op jit(solution)/shard_map/ppermute | solution.py:205
  34.2 2.0 %collective-permute-done.13.c = bf16[208,256]{1,0:T(8,128)(2,1)S(1)} collective-permute-done((bf16[208,256]{1,0:T(8,128)(2,1)S(1)}, bf16[208,256]{1,0:T(8,128)(2,1)S(1)}, u32[]{:S(2)}, u32[]{:S(2)}) %collective-permute-start.13) | collective-permute-done | bytes 106528 | tf_op jit(solution)/shard_map/ppermute | solution.py:205
  36.2 1.5 %collective-permute-done.14.d = bf16[208,256]{1,0:T(8,128)(2,1)S(1)} collective-permute-done((bf16[208,256]{1,0:T(8,128)(2,1)S(1)}, bf16[208,256]{1,0:T(8,128)(2,1)S(1)}, u32[]{:S(2)}, u32[]{:S(2)}) %collective-permute-start.14) | collective-permute-done | bytes 106528 | tf_op jit(solution)/shard_map/ppermute | solution.py:205
  37.7 2.5 %collective-permute-start.18 = (bf16[1024,128]{1,0:T(8,128)(2,1)S(1)}, bf16[1024,128]{1,0:T(8,128)(2,1)S(1)}, u32[]{:S(2)}, u32[]{:S(2)}) collective-permute-start(bf16[1024,128]{1,0:T(8,128)(2,1)S(1)} %shard_map.121.i0), channel_id=1, source_target_pairs={{0,8},{1,9},{2,66},{3,67},{4,12},{5,13},{6,70},{7,71},{8,0},{9,1},... | collective-permute-start | bytes 786440 | tf_op jit(solution)/shard_map/ppermute | solution.py:205
  42.4 2.7 %collective-permute-start.16 = (bf16[656,256]{1,0:T(8,128)(2,1)S(1)}, bf16[656,256]{1,0:T(8,128)(2,1)S(1)}, u32[]{:S(2)}, u32[]{:S(2)}) collective-permute-start(bf16[656,256]{1,0:T(8,128)(2,1)S(1)} %shard_map.120.l0), channel_id=1, source_target_pairs={{0,8},{1,9},{2,66},{3,67},{4,12},{5,13},{6,70},{7,71},{8,0},{9,1},... | collective-permute-start | bytes 1007624 | tf_op jit(solution)/shard_map/ppermute | solution.py:205
  45.2 2.2 %collective-permute-start.17 = (bf16[656,256]{1,0:T(8,128)(2,1)S(1)}, bf16[656,256]{1,0:T(8,128)(2,1)S(1)}, u32[]{:S(2)}, u32[]{:S(2)}) collective-permute-start(bf16[656,256]{1,0:T(8,128)(2,1)S(1)} %shard_map.120.l0), channel_id=1, source_target_pairs={{0,12},{1,13},{2,98},{3,99},{4,8},{5,9},{6,102},{7,103},{8,4},{9,5... | collective-permute-start | bytes 1007624 | tf_op jit(solution)/shard_map/ppermute | solution.py:205
  47.4 2.0 %fusion.81.pick = bf16[1024,1280]{1,0:T(8,128)(2,1)} fusion(s32[1024]{0:T(1024)S(1)} %bitcast.134), kind=kLoop, calls=%fused_computation.115 | loop fusion | flops 2621440 | bytes 2625536 | tf_op jit(solution)/shard_map/convert_element_type | solution.py:659
  49.3 1.4 %shard_map.122 = (bf16[2048,128]{1,0:T(8,128)(2,1)S(1)}, bf16[2048,256]{1,0:T(8,128)(2,1)S(1)}, f32[256,1]{1,0:T(8,128)S(1)}, f32[256,256]{1,0:T(8,128)S(1)}) custom-call(bf16[1024,128]{1,0:T(8,128)(2,1)S(1)} %shard_map.121.i0, bf16[1024,128]{1,0:T(8,128)(2,1)S(1)} %collective-permute-done.18.i1, bf16[1024,128]{1,0:T(8,128)(2,1)S(1)} %collective-permute-done.19.i2, ...), custom_call_target="tpu_custom_call" | custom-call | flops 2200000000 | tf_op jit(solution)/shard_map/pallas_call | solution.py:220
  51.4 3.5 %collective-permute-done.16.l2 = bf16[656,256]{1,0:T(8,128)(2,1)S(1)} collective-permute-done((bf16[656,256]{1,0:T(8,128)(2,1)S(1)}, bf16[656,256]{1,0:T(8,128)(2,1)S(1)}, u32[]{:S(2)}, u32[]{:S(2)}) %collective-permute-start.16) | collective-permute-done | bytes 335904 | tf_op jit(solution)/shard_map/ppermute | solution.py:205
  54.9 1.4 %collective-permute-done.17.l3 = bf16[656,256]{1,0:T(8,128)(2,1)S(1)} collective-permute-done((bf16[656,256]{1,0:T(8,128)(2,1)S(1)}, bf16[656,256]{1,0:T(8,128)(2,1)S(1)}, u32[]{:S(2)}, u32[]{:S(2)}) %collective-permute-start.17) | collective-permute-done | bytes 335904 | tf_op jit(solution)/shard_map/ppermute | solution.py:205
  56.3 9.0 %shard_map.123 = (bf16[80,1152]{1,0:T(8,128)(2,1)S(1)}, bf16[80,1152]{1,0:T(8,128)(2,1)S(1)}, bf16[80,1152]{1,0:T(8,128)(2,1)S(1)}, bf16[80,1152]{1,0:T(8,128)(2,1)S(1)}) custom-call(bf16[1024,1280]{1,0:T(8,128)(2,1)} %fusion.81.pick, bf16[656,256]{1,0:T(8,128)(2,1)S(1)} %shard_map.120.l0, bf16[656,256]{1,0:T(8,128)(2,1)S(1)} %collective-permute-done.15.l1, ...), custom_call_target="tpu_custom_call" | custom-call | flops 9900000256 | tf_op jit(solution)/shard_map/pallas_call | solution.py:220
  65.3 2.4 %collective-permute-start.22 = (bf16[80,1152]{1,0:T(8,128)(2,1)S(1)}, bf16[80,1152]{1,0:T(8,128)(2,1)S(1)}, u32[]{:S(2)}, u32[]{:S(2)}) collective-permute-start(bf16[80,1152]{1,0:T(8,128)(2,1)S(1)} %get-tuple-element.140), channel_id=1, source_target_pairs={{0,64},{1,65},{2,10},{3,11},{4,68},{5,69},{6,14},{7,15},{8,72},{9,... | collective-permute-start | bytes 552968 | tf_op jit(solution)/shard_map/ppermute | solution.py:205
  67.7 1.5 %collective-permute-start.23 = (bf16[80,1152]{1,0:T(8,128)(2,1)S(1)}, bf16[80,1152]{1,0:T(8,128)(2,1)S(1)}, u32[]{:S(2)}, u32[]{:S(2)}) collective-permute-start(bf16[80,1152]{1,0:T(8,128)(2,1)S(1)} %get-tuple-element.141), channel_id=1, source_target_pairs={{0,96},{1,97},{2,14},{3,15},{4,100},{5,101},{6,10},{7,11},{8,104},... | collective-permute-start | bytes 552968 | tf_op jit(solution)/shard_map/ppermute | solution.py:205
  69.7 3.0 %collective-permute-done.22.b2 = bf16[80,1152]{1,0:T(8,128)(2,1)S(1)} collective-permute-done((bf16[80,1152]{1,0:T(8,128)(2,1)S(1)}, bf16[80,1152]{1,0:T(8,128)(2,1)S(1)}, u32[]{:S(2)}, u32[]{:S(2)}) %collective-permute-start.22) | collective-permute-done | bytes 184352 | tf_op jit(solution)/shard_map/ppermute | solution.py:205
  72.7 1.9 %collective-permute-done.23.b3 = bf16[80,1152]{1,0:T(8,128)(2,1)S(1)} collective-permute-done((bf16[80,1152]{1,0:T(8,128)(2,1)S(1)}, bf16[80,1152]{1,0:T(8,128)(2,1)S(1)}, u32[]{:S(2)}, u32[]{:S(2)}) %collective-permute-start.23) | collective-permute-done | bytes 184352 | tf_op jit(solution)/shard_map/ppermute | solution.py:205
  74.6 1.4 %shard_map.124 = (bf16[48,1152]{1,0:T(8,128)(2,1)S(1)}, bf16[48,1536]{1,0:T(8,128)(2,1)S(1)}, bf16[32,384]{1,0:T(8,128)(2,1)}) custom-call(s32[6]{0:T(128)S(1)} %stack.45.at, bf16[80,1152]{1,0:T(8,128)(2,1)S(1)} %get-tuple-element.138.b0, bf16[80,1152]{1,0:T(8,128)(2,1)S(1)} %collective-permute-done.21.b1, bf16[80,1152]{1,0:T(8,128)(2,1)S(1)} %collective-permute-done.22.b2, ...), custom_call_target="tpu_custom_call" | custom-call | flops 1100000000 | tf_op jit(solution)/shard_map/pallas_call | solution.py:220
  76.0 5.5 %collective-permute-start.24 = (bf16[48,1536]{1,0:T(8,128)(2,1)S(1)}, bf16[48,1536]{1,0:T(8,128)(2,1)S(1)}, u32[]{:S(2)}, u32[]{:S(2)}) collective-permute-start(bf16[48,1536]{1,0:T(8,128)(2,1)S(1)} %get-tuple-element.143), channel_id=1, source_target_pairs={{0,2},{1,3},{2,0},{3,1},{4,6},{5,7},{6,4},{7,5},{8,10},{9,11},{10,... | collective-permute-start | bytes 442376 | tf_op jit(solution)/shard_map/ppermute | solution.py:205
  83.1 1.2 %collective-permute-start.25 = (bf16[48,1152]{1,0:T(8,128)(2,1)S(1)}, bf16[48,1152]{1,0:T(8,128)(2,1)S(1)}, u32[]{:S(2)}, u32[]{:S(2)}) collective-permute-start(bf16[48,1152]{1,0:T(8,128)(2,1)S(1)} %shard_map.125), channel_id=1, source_target_pairs={{0,1},{1,0},{2,3},{3,2},{4,5},{5,4},{6,7},{7,6},{8,9},{9,8},{10,11... | collective-permute-start | bytes 331784 | tf_op jit(solution)/shard_map/ppermute | solution.py:205
  84.4 4.6 %collective-permute-done.25 = bf16[48,1152]{1,0:T(8,128)(2,1)S(1)} collective-permute-done((bf16[48,1152]{1,0:T(8,128)(2,1)S(1)}, bf16[48,1152]{1,0:T(8,128)(2,1)S(1)}, u32[]{:S(2)}, u32[]{:S(2)}) %collective-permute-start.25) | collective-permute-done | bytes 110624 | tf_op jit(solution)/shard_map/ppermute | solution.py:205
  88.9 2.0 %conditional.1 = (bf16[32,768]{1,0:T(8,128)(2,1)}, f32[1024,32]{0,1:T(8,128)}) conditional(s32[]{:T(128)} %convert_element_type.70, (s32[512]{0:T(512)S(1)}, s32[1024]{0:T(1024)S(1)}, bf16[256,3072]{1,0:T(8,128)(2,1)S(1)}, s32[1]{0:T(128)}, f32[28,2,3072]{2,1,0:T(2,128)}, /*index=5*/bf16[3072,3,768]{2,0,1:T(8,128)(2,1)}, f32[2,128]{1,0:T(2,128)S(1)}, ...), branch_computations={%region_0.15_spmd, %region_15.16_spmd} | conditional | flops 1100000000 | bytes 257951312 | solution.py:754
  89.2 1.7 %branch_1_fun.1 = (bf16[32,768]{1,0:T(8,128)(2,1)}, f32[32,1024]{1,0:T(8,128)}) custom-call(s32[6]{0:T(128)S(1)} %get-tuple-element.40.at, bf16[48,1152]{1,0:T(8,128)(2,1)S(1)} %get-tuple-element.41.own, bf16[48,1152]{1,0:T(8,128)(2,1)S(1)} %get-tuple-element.42.head, bf16[48,1536]{1,0:T(8,128)(2,1)} %get-tuple-element.43.core, ...), custom_call_target="tpu_custom_call" | custom-call | flops 1100000000 | tf_op jit(solution)/shard_map/cond/branch_1_fun/pallas_call | solution.py:220
  (52 shorter events, 8.1 us)
Async XLA Ops:
  0.7 15.2 %copy-start.8 = (s32[1024]{0:T(1024)S(1)}, s32[1024]{0:T(1024)}, u32[]{:S(2)}) copy-start(s32[1024]{0:T(1024)} %param.16) | copy-start | bytes 12292
  0.7 15.2 %copy-start.9 = (s32[512]{0:T(512)S(1)}, s32[512]{0:T(512)}, u32[]{:S(2)}) copy-start(s32[512]{0:T(512)} %param.15) | copy-start | bytes 6148
  3.5 18.6 %collective-permute-start.4 = (bf16[32,3072]{1,0:T(8,128)(2,1)S(1)}, bf16[32,3072]{1,0:T(8,128)(2,1)S(1)}, u32[]{:S(2)}, u32[]{:S(2)}) collective-permute-start(bf16[32,3072]{1,0:T(8,128)(2,1)S(1)} %get-tuple-element.97.refs_0_), channel_id=1, source_target_pairs={{0,16},{1,17},{2,18},{3,19},{4,20},{5,21},{6,22},{7,23},{8,24},{9,... | collective-permute-start | bytes 589832 | tf_op jit(solution)/shard_map/ppermute | solution.py:205
  6.0 16.1 %collective-permute-start.1 = (bf16[32,3072]{1,0:T(8,128)(2,1)S(1)}, bf16[32,3072]{1,0:T(8,128)(2,1)S(1)}, u32[]{:S(2)}, u32[]{:S(2)}) collective-permute-start(bf16[32,3072]{1,0:T(8,128)(2,1)S(1)} %get-tuple-element.97.refs_0_), channel_id=1, source_target_pairs={{0,1},{1,0},{2,3},{3,2},{4,5},{5,4},{6,7},{7,6},{8,9},{9,8},{10,11... | collective-permute-start | bytes 589832 | tf_op jit(solution)/shard_map/ppermute | solution.py:205
  9.3 11.2 %collective-permute-start.7 = (bf16[32,3072]{1,0:T(8,128)(2,1)S(1)}, bf16[32,3072]{1,0:T(8,128)(2,1)S(1)}, u32[]{:S(2)}, u32[]{:S(2)}) collective-permute-start(bf16[32,3072]{1,0:T(8,128)(2,1)S(1)} %get-tuple-element.97.refs_0_), channel_id=1, source_target_pairs={{0,17},{1,16},{2,19},{3,18},{4,21},{5,20},{6,23},{7,22},{8,25},{9,... | collective-permute-start | bytes 589832 | tf_op jit(solution)/shard_map/ppermute | solution.py:205
  9.3 2.6 %collective-permute-start.2 = (bf16[48,3072]{1,0:T(8,128)(2,1)S(1)}, bf16[48,3072]{1,0:T(8,128)(2,1)S(1)}, u32[]{:S(2)}, u32[]{:S(2)}) collective-permute-start(bf16[48,3072]{1,0:T(8,128)(2,1)S(1)} %get-tuple-element.102), channel_id=1, source_target_pairs={{0,2},{1,3},{2,0},{3,1},{4,6},{5,7},{6,4},{7,5},{8,10},{9,11},{10,... | collective-permute-start | bytes 884744 | tf_op jit(solution)/shard_map/ppermute | solution.py:205
  11.9 13.4 %copy-start.10 = (f32[2,128]{1,0:T(2,128)S(1)}, f32[2,128]{1,0:T(2,128)}, u32[]{:S(2)}) copy-start(f32[2,128]{1,0:T(2,128)} %refs_9_.1) | copy-start | bytes 3076
  12.5 9.5 %collective-permute-start.5 = (bf16[192,128]{1,0:T(8,128)(2,1)S(1)}, bf16[192,128]{1,0:T(8,128)(2,1)S(1)}, u32[]{:S(2)}, u32[]{:S(2)}) collective-permute-start(bf16[192,128]{1,0:T(8,128)(2,1)S(1)} %get-tuple-element.107), channel_id=1, source_target_pairs={{0,64},{1,65},{2,10},{3,11},{4,68},{5,69},{6,14},{7,15},{8,72},{9,... | collective-permute-start | bytes 147464 | tf_op jit(solution)/shard_map/ppermute | solution.py:205
  15.5 6.6 %collective-permute-start.3 = (bf16[192,128]{1,0:T(8,128)(2,1)S(1)}, bf16[192,128]{1,0:T(8,128)(2,1)S(1)}, u32[]{:S(2)}, u32[]{:S(2)}) collective-permute-start(bf16[192,128]{1,0:T(8,128)(2,1)S(1)} %get-tuple-element.103), channel_id=1, source_target_pairs={{0,32},{1,33},{2,6},{3,7},{4,36},{5,37},{6,2},{7,3},{8,40},{9,41},... | collective-permute-start | bytes 147464 | tf_op jit(solution)/shard_map/ppermute | solution.py:205
  20.5 4.8 %collective-permute-start.10 = (bf16[32,3072]{1,0:T(8,128)(2,1)S(1)}, bf16[32,3072]{1,0:T(8,128)(2,1)S(1)}, u32[]{:S(2)}, u32[]{:S(2)}) collective-permute-start(bf16[32,3072]{1,0:T(8,128)(2,1)S(1)} %collective-permute-done.7.refs_3_), channel_id=1, source_target_pairs={{0,2},{1,3},{2,0},{3,1},{4,6},{5,7},{6,4},{7,5},{8,10},{9,11},{10,... | collective-permute-start | bytes 589832 | tf_op jit(solution)/shard_map/ppermute | solution.py:205
  22.1 3.3 %collective-permute-start.8 = (bf16[32,3072]{1,0:T(8,128)(2,1)S(1)}, bf16[32,3072]{1,0:T(8,128)(2,1)S(1)}, u32[]{:S(2)}, u32[]{:S(2)}) collective-permute-start(bf16[32,3072]{1,0:T(8,128)(2,1)S(1)} %collective-permute-done.4.refs_1_), channel_id=1, source_target_pairs={{0,2},{1,3},{2,0},{3,1},{4,6},{5,7},{6,4},{7,5},{8,10},{9,11},{10,... | collective-permute-start | bytes 589832 | tf_op jit(solution)/shard_map/ppermute | solution.py:205
  22.1 3.2 %collective-permute-start.9 = (bf16[32,3072]{1,0:T(8,128)(2,1)S(1)}, bf16[32,3072]{1,0:T(8,128)(2,1)S(1)}, u32[]{:S(2)}, u32[]{:S(2)}) collective-permute-start(bf16[32,3072]{1,0:T(8,128)(2,1)S(1)} %collective-permute-done.1.refs_2_), channel_id=1, source_target_pairs={{0,2},{1,3},{2,0},{3,1},{4,6},{5,7},{6,4},{7,5},{8,10},{9,11},{10,... | collective-permute-start | bytes 589832 | tf_op jit(solution)/shard_map/ppermute | solution.py:205
  22.6 7.5 %collective-permute-start.6 = (bf16[192,128]{1,0:T(8,128)(2,1)S(1)}, bf16[192,128]{1,0:T(8,128)(2,1)S(1)}, u32[]{:S(2)}, u32[]{:S(2)}) collective-permute-start(bf16[192,128]{1,0:T(8,128)(2,1)S(1)} %get-tuple-element.109), channel_id=1, source_target_pairs={{0,96},{1,97},{2,14},{3,15},{4,100},{5,101},{6,10},{7,11},{8,104},... | collective-permute-start | bytes 147464 | tf_op jit(solution)/shard_map/ppermute | solution.py:205
  30.1 7.6 %collective-permute-start.11 = (bf16[512,128]{1,0:T(8,128)(2,1)S(1)}, bf16[512,128]{1,0:T(8,128)(2,1)S(1)}, u32[]{:S(2)}, u32[]{:S(2)}) collective-permute-start(bf16[512,128]{1,0:T(8,128)(2,1)S(1)} %get-tuple-element.119.own), channel_id=1, source_target_pairs={{0,16},{1,17},{2,18},{3,19},{4,20},{5,21},{6,22},{7,23},{8,24},{9,... | collective-permute-start | bytes 393224 | tf_op jit(solution)/shard_map/ppermute | solution.py:205
  30.2 3.9 %collective-permute-start.12 = (bf16[208,256]{1,0:T(8,128)(2,1)S(1)}, bf16[208,256]{1,0:T(8,128)(2,1)S(1)}, u32[]{:S(2)}, u32[]{:S(2)}) collective-permute-start(bf16[208,256]{1,0:T(8,128)(2,1)S(1)} %get-tuple-element.121), channel_id=1, source_target_pairs={{0,32},{1,33},{2,6},{3,7},{4,36},{5,37},{6,2},{7,3},{8,40},{9,41},... | collective-permute-start | bytes 319496 | tf_op jit(solution)/shard_map/ppermute | solution.py:205
  30.3 5.9 %collective-permute-start.13 = (bf16[208,256]{1,0:T(8,128)(2,1)S(1)}, bf16[208,256]{1,0:T(8,128)(2,1)S(1)}, u32[]{:S(2)}, u32[]{:S(2)}) collective-permute-start(bf16[208,256]{1,0:T(8,128)(2,1)S(1)} %get-tuple-element.122), channel_id=1, source_target_pairs={{0,64},{1,65},{2,10},{3,11},{4,68},{5,69},{6,14},{7,15},{8,72},{9,... | collective-permute-start | bytes 319496 | tf_op jit(solution)/shard_map/ppermute | solution.py:205
  32.6 5.1 %collective-permute-start.14 = (bf16[208,256]{1,0:T(8,128)(2,1)S(1)}, bf16[208,256]{1,0:T(8,128)(2,1)S(1)}, u32[]{:S(2)}, u32[]{:S(2)}) collective-permute-start(bf16[208,256]{1,0:T(8,128)(2,1)S(1)} %get-tuple-element.123), channel_id=1, source_target_pairs={{0,96},{1,97},{2,14},{3,15},{4,100},{5,101},{6,10},{7,11},{8,104},... | collective-permute-start | bytes 319496 | tf_op jit(solution)/shard_map/ppermute | solution.py:205
  37.7 7.4 %collective-permute-start.18 = (bf16[1024,128]{1,0:T(8,128)(2,1)S(1)}, bf16[1024,128]{1,0:T(8,128)(2,1)S(1)}, u32[]{:S(2)}, u32[]{:S(2)}) collective-permute-start(bf16[1024,128]{1,0:T(8,128)(2,1)S(1)} %shard_map.121.i0), channel_id=1, source_target_pairs={{0,8},{1,9},{2,66},{3,67},{4,12},{5,13},{6,70},{7,71},{8,0},{9,1},... | collective-permute-start | bytes 786440 | tf_op jit(solution)/shard_map/ppermute | solution.py:205
  40.3 9.1 %collective-permute-start.19 = (bf16[1024,128]{1,0:T(8,128)(2,1)S(1)}, bf16[1024,128]{1,0:T(8,128)(2,1)S(1)}, u32[]{:S(2)}, u32[]{:S(2)}) collective-permute-start(bf16[1024,128]{1,0:T(8,128)(2,1)S(1)} %shard_map.121.i0), channel_id=1, source_target_pairs={{0,4},{1,5},{2,34},{3,35},{4,0},{5,1},{6,38},{7,39},{8,12},{9,13},... | collective-permute-start | bytes 786440 | tf_op jit(solution)/shard_map/ppermute | solution.py:205
  40.9 8.5 %collective-permute-start.20 = (bf16[1024,128]{1,0:T(8,128)(2,1)S(1)}, bf16[1024,128]{1,0:T(8,128)(2,1)S(1)}, u32[]{:S(2)}, u32[]{:S(2)}) collective-permute-start(bf16[1024,128]{1,0:T(8,128)(2,1)S(1)} %shard_map.121.i0), channel_id=1, source_target_pairs={{0,12},{1,13},{2,98},{3,99},{4,8},{5,9},{6,102},{7,103},{8,4},{9,5... | collective-permute-start | bytes 786440 | tf_op jit(solution)/shard_map/ppermute | solution.py:205
  41.5 9.9 %collective-permute-start.15 = (bf16[656,256]{1,0:T(8,128)(2,1)S(1)}, bf16[656,256]{1,0:T(8,128)(2,1)S(1)}, u32[]{:S(2)}, u32[]{:S(2)}) collective-permute-start(bf16[656,256]{1,0:T(8,128)(2,1)S(1)} %shard_map.120.l0), channel_id=1, source_target_pairs={{0,4},{1,5},{2,34},{3,35},{4,0},{5,1},{6,38},{7,39},{8,12},{9,13},... | collective-permute-start | bytes 1007624 | tf_op jit(solution)/shard_map/ppermute | solution.py:205
  42.4 12.5 %collective-permute-start.16 = (bf16[656,256]{1,0:T(8,128)(2,1)S(1)}, bf16[656,256]{1,0:T(8,128)(2,1)S(1)}, u32[]{:S(2)}, u32[]{:S(2)}) collective-permute-start(bf16[656,256]{1,0:T(8,128)(2,1)S(1)} %shard_map.120.l0), channel_id=1, source_target_pairs={{0,8},{1,9},{2,66},{3,67},{4,12},{5,13},{6,70},{7,71},{8,0},{9,1},... | collective-permute-start | bytes 1007624 | tf_op jit(solution)/shard_map/ppermute | solution.py:205
  45.2 11.1 %collective-permute-start.17 = (bf16[656,256]{1,0:T(8,128)(2,1)S(1)}, bf16[656,256]{1,0:T(8,128)(2,1)S(1)}, u32[]{:S(2)}, u32[]{:S(2)}) collective-permute-start(bf16[656,256]{1,0:T(8,128)(2,1)S(1)} %shard_map.120.l0), channel_id=1, source_target_pairs={{0,12},{1,13},{2,98},{3,99},{4,8},{5,9},{6,102},{7,103},{8,4},{9,5... | collective-permute-start | bytes 1007624 | tf_op jit(solution)/shard_map/ppermute | solution.py:205
  65.3 4.4 %collective-permute-start.21 = (bf16[80,1152]{1,0:T(8,128)(2,1)S(1)}, bf16[80,1152]{1,0:T(8,128)(2,1)S(1)}, u32[]{:S(2)}, u32[]{:S(2)}) collective-permute-start(bf16[80,1152]{1,0:T(8,128)(2,1)S(1)} %get-tuple-element.139), channel_id=1, source_target_pairs={{0,32},{1,33},{2,6},{3,7},{4,36},{5,37},{6,2},{7,3},{8,40},{9,41},... | collective-permute-start | bytes 552968 | tf_op jit(solution)/shard_map/ppermute | solution.py:205
  65.3 7.4 %collective-permute-start.22 = (bf16[80,1152]{1,0:T(8,128)(2,1)S(1)}, bf16[80,1152]{1,0:T(8,128)(2,1)S(1)}, u32[]{:S(2)}, u32[]{:S(2)}) collective-permute-start(bf16[80,1152]{1,0:T(8,128)(2,1)S(1)} %get-tuple-element.140), channel_id=1, source_target_pairs={{0,64},{1,65},{2,10},{3,11},{4,68},{5,69},{6,14},{7,15},{8,72},{9,... | collective-permute-start | bytes 552968 | tf_op jit(solution)/shard_map/ppermute | solution.py:205
  67.7 6.9 %collective-permute-start.23 = (bf16[80,1152]{1,0:T(8,128)(2,1)S(1)}, bf16[80,1152]{1,0:T(8,128)(2,1)S(1)}, u32[]{:S(2)}, u32[]{:S(2)}) collective-permute-start(bf16[80,1152]{1,0:T(8,128)(2,1)S(1)} %get-tuple-element.141), channel_id=1, source_target_pairs={{0,96},{1,97},{2,14},{3,15},{4,100},{5,101},{6,10},{7,11},{8,104},... | collective-permute-start | bytes 552968 | tf_op jit(solution)/shard_map/ppermute | solution.py:205
  74.6 14.3 %copy-start = (bf16[256,3072]{1,0:T(8,128)(2,1)S(1)}, bf16[256,3072]{1,0:T(8,128)(2,1)}, u32[]{:S(2)}) copy-start(bf16[256,3072]{1,0:T(8,128)(2,1)} %table_ref.1) | copy-start | bytes 4718596
  74.6 14.3 %copy-start.3 = (bf16[32,768]{1,0:T(8,128)(2,1)S(1)}, bf16[32,768]{1,0:T(8,128)(2,1)}, u32[]{:S(2)}) copy-start(bf16[32,768]{1,0:T(8,128)(2,1)} %q_ref.1) | copy-start | bytes 147460
  74.6 14.3 %copy-start.6 = (bf16[32,768]{1,0:T(8,128)(2,1)S(1)}, bf16[32,768]{1,0:T(8,128)(2,1)}, u32[]{:S(2)}) copy-start(bf16[32,768]{1,0:T(8,128)(2,1)} %k_ref.1) | copy-start | bytes 147460
  74.6 14.3 %copy-start.7 = (bf16[32,768]{1,0:T(8,128)(2,1)S(1)}, bf16[32,768]{1,0:T(8,128)(2,1)}, u32[]{:S(2)}) copy-start(bf16[32,768]{1,0:T(8,128)(2,1)} %v_ref.1) | copy-start | bytes 147460
  76.0 6.5 %collective-permute-start.24 = (bf16[48,1536]{1,0:T(8,128)(2,1)S(1)}, bf16[48,1536]{1,0:T(8,128)(2,1)S(1)}, u32[]{:S(2)}, u32[]{:S(2)}) collective-permute-start(bf16[48,1536]{1,0:T(8,128)(2,1)S(1)} %get-tuple-element.143), channel_id=1, source_target_pairs={{0,2},{1,3},{2,0},{3,1},{4,6},{5,7},{6,4},{7,5},{8,10},{9,11},{10,... | collective-permute-start | bytes 442376 | tf_op jit(solution)/shard_map/ppermute | solution.py:205
  83.1 5.8 %collective-permute-start.25 = (bf16[48,1152]{1,0:T(8,128)(2,1)S(1)}, bf16[48,1152]{1,0:T(8,128)(2,1)S(1)}, u32[]{:S(2)}, u32[]{:S(2)}) collective-permute-start(bf16[48,1152]{1,0:T(8,128)(2,1)S(1)} %shard_map.125), channel_id=1, source_target_pairs={{0,1},{1,0},{2,3},{3,2},{4,5},{5,4},{6,7},{7,6},{8,9},{9,8},{10,11... | collective-permute-start | bytes 331784 | tf_op jit(solution)/shard_map/ppermute | solution.py:205
  (1 other events, 0.7 us)

commit v3 on v2

--- a/solution.py
+++ b/solution.py
@@ -18,7 +18,7 @@
 LINE_TXT = 176
 LINE = LINE_CON + LINE_TXT
 MIB = 1 << 20
-PROJ_US, PROMPT_US = 5.0, 9.0
+PROJ_US, NEAR_US, FAR_US = 5.0, 6.0, 3.0
 FACTOR = HD ** (-0.5) * math.log2(math.e)
 
 
@@ -490,11 +490,11 @@
         kv_out[n * (4 + i) : n * (5 + i), :] = ref[2 * n :, :]
 
 
-def planes_kernel(own, other, out):
-    n = own.shape[0] // 2
-    for i, ref in enumerate((own, other)):
+def plane_kernel(a, b, c, d, out):
+    n = a.shape[0] // 2
+    for i, ref in enumerate((a, b, c, d)):
         out[n * i : n * (i + 1), :] = ref[0:n, :]
-        out[n * (2 + i) : n * (3 + i), :] = ref[n:, :]
+        out[n * (4 + i) : n * (5 + i), :] = ref[n:, :]
 
 
 def weigh(q, parts, factor):
@@ -528,16 +528,17 @@
     return jnp.concatenate([values, jnp.ones_like(values)], axis=1)
 
 
-def image_self_kernel(i0, i1, i2, i3, q, keys, vals, peak, summed):
-    part = i0.shape[0] // 2
-    for i, ref in enumerate((i0, i1, i2, i3)):
-        keys[i * part : (i + 1) * part, :] = ref[0:part, :]
-        vals[i * part : (i + 1) * part, :] = with_ones(ref[part:, :])
-    peak[...], summed[...] = weigh(q[...], ((keys[...], vals[...], None),), FACTOR)
-
-
-def prompt_kernel(pick, l0, l1, l2, l3, con_bias, txt_bias, keys, vals, img_q, im, ims, *refs):
-    outs, (con_q, con_k, con_v, txt_k, txt_v, con_out) = refs[:4], refs[4:]
+def plane_part(plane):
+    n = plane.shape[0] // 2
+    return (plane[0:n, :], with_ones(plane[n:, :]), None)
+
+
+def image_near_kernel(plane, q, peak, summed):
+    peak[...], summed[...] = weigh(q[...], (plane_part(plane),), FACTOR)
+
+
+def near_kernel(pick, l0, l1, l2, l3, con_bias, txt_bias, plane, img_q, im, ims, *refs):
+    (q_out, cm_out, cs_out, im_out, ims_out), (con_q, con_k, con_v, txt_k, txt_v) = refs[:5], refs[5:]
     n, m = LINE_CON, LINE_TXT
     for a, ref in enumerate((l0, l1, l2, l3)):
         con_q[a * n : a * n + n // 2, :] = ref[LINE:, 0:HD]
@@ -546,15 +547,25 @@
         con_v[a * n : (a + 1) * n, :] = with_ones(ref[0:n, HD:])
         txt_k[a * m : (a + 1) * m, :] = ref[n:LINE, 0:HD]
         txt_v[a * m : (a + 1) * m, :] = with_ones(ref[n:LINE, HD:])
+    images = plane_part(plane)
+    q_out[...] = nn(pick[...], con_q[...]).astype(BF)
+    for b in range(q_out.shape[0] // 256):
+        rows = slice(b * 256, (b + 1) * 256)
+        parts = (images, (con_k[...], con_v[...], con_bias[...]))
+        cm_out[rows, :], cs_out[rows, :] = weigh(q_out[rows, :], parts, None)
     text = weigh(img_q[...], ((txt_k[...], txt_v[...], txt_bias[...]),), FACTOR)
-    img = merge(text, (im[...], ims[...]))
+    im_out[...], ims_out[...] = join(text, (im[...], ims[...]))
+
+
+def far_kernel(plane, con_q, img_q, cm, cs, im, ims, *refs):
+    outs, (con_out,) = refs[:4], refs[4:]
+    images = plane_part(plane)
+    img = merge(weigh(img_q[...], (images,), FACTOR), (im[...], ims[...]))
     n_con = con_out.shape[0]
     for b in range(n_con // 256):
         rows = slice(b * 256, (b + 1) * 256)
-        q = nn(pick[rows, :], con_q[...]).astype(BF)
-        parts = ((keys[...], vals[...], None), (con_k[...], con_v[...], con_bias[...]))
-        _, summed = weigh(q, parts, None)
-        con_out[rows, :] = (summed[:, 0:HD] / summed[:, HD:]).astype(BF)
+        part = weigh(con_q[rows, :], (images,), None)
+        con_out[rows, :] = merge(part, (cm[rows, :], cs[rows, :]))
     dots = nt(img, con_out[...]).astype(BF)
     con_f = con_out[...].astype(F32)
     con_sq = nt(jnp.ones((16, HD), F32), con_f * con_f, precision=lax.Precision.HIGHEST).astype(BF)
@@ -655,8 +666,6 @@
             sds((1, 4 * TXT), jnp.int32),
         ),
     )(at, con_ids, text_ids, plan)
-    con_slot = spots[0, :n_con]
-    pick = (con_slot[:, None] == jnp.arange(4 * LINE_CON)[None, :]).astype(BF)
     shift_scale = lax.dynamic_index_in_dim(modulation, step_index[0], 0, keepdims=False)
     fits = (spots[1, 0] <= 0).astype(jnp.int32)
 
@@ -689,12 +698,10 @@
     image_q, image_kv = call(
         image_join_kernel, (sds((8 * n_img, HD)), sds((16 * n_img, HD))), smem=0
     )(*image_blocks)
-    other_kv = send(image_kv, swap_plane())
+    image_kvs = [image_kv] + [send(image_kv, swap_v(s)) for s in (2, 1, 3)]
+
     qkv = [first] + [send(qkv[s], swap_u(s)) for s in (2, 1, 3)]
     qkv = [qkv[0], qkv[2], qkv[1], qkv[3]]
-    other_kv, *qkv = lax.optimization_barrier((other_kv, *qkv))
-    planes = call(planes_kernel, sds((32 * n_img, HD)), smem=0)(image_kv, other_kv)
-    image_kvs = [planes] + [send(planes, swap_v(s)) for s in (2, 1, 3)]
     line = call(
         join_kernel,
         sds((LINE + LINE_CON // 2, 2 * HD)),
@@ -703,34 +710,34 @@
     )(*qkv, con_line, txt_line)
     lines = [line] + [send(line, swap_v(s)) for s in (2, 1, 3)]
     lines = [lines[0], lines[2], lines[1], lines[3]]
-
-    all_img = 64 * n_img
-    image_self = call(
-        image_self_kernel,
-        (
-            sds((all_img, HD)),
-            sds((all_img, 2 * HD)),
-            sds((8 * n_img, 1), F32),
-            sds((8 * n_img, 2 * HD), F32),
-        ),
-        us=2.0,
-        smem=0,
-    )
-    keys, vals, *image_stats = image_self(*image_kvs, image_q)
-    blocks = call(
-        prompt_kernel,
-        tuple(sds((80, n_con + HD)) for _ in range(4)),
+    plane = call(plane_kernel, sds((64 * n_img, HD)), smem=0)(*image_kvs)
+    con_slot, plane = lax.optimization_barrier((spots[0, :n_con], plane))
+    other_plane = send(plane, swap_plane())
+    pick = (con_slot[:, None] == jnp.arange(4 * LINE_CON)[None, :]).astype(BF)
+
+    image_stats = (sds((8 * n_img, 1), F32), sds((8 * n_img, 2 * HD), F32))
+    stats = (sds((n_con, 1), F32), sds((n_con, 2 * HD), F32)) + image_stats
+    image_near = call(image_near_kernel, image_stats, smem=0)(plane, image_q)
+    con_q, *near = call(
+        near_kernel,
+        (sds((n_con, HD)),) + stats,
         scratch=(
             pltpu.VMEM((4 * LINE_CON, HD), BF),
             pltpu.VMEM((4 * LINE_CON, HD), BF),
             pltpu.VMEM((4 * LINE_CON, 2 * HD), BF),
             pltpu.VMEM((4 * LINE_TXT, HD), BF),
             pltpu.VMEM((4 * LINE_TXT, 2 * HD), BF),
-            pltpu.VMEM((n_con, HD), BF),
         ),
-        us=PROMPT_US,
+        us=NEAR_US,
         smem=0,
-    )(pick, *lines, con_bias, txt_bias, keys, vals, image_q, *image_stats)
+    )(pick, *lines, con_bias, txt_bias, plane, image_q, *image_near)
+    blocks = call(
+        far_kernel,
+        tuple(sds((80, n_con + HD)) for _ in range(4)),
+        scratch=(pltpu.VMEM((n_con, HD), BF),),
+        us=FAR_US,
+        smem=0,
+    )(other_plane, con_q, image_q, *near)
     blocks = [blocks[0]] + [send(blocks[s], swap_u(s)) for s in (2, 1, 3)]
     blocks = [blocks[0], blocks[2], blocks[1], blocks[3]]
     own, core, out_own = call(

time: 91.2 us -> 90.1 us (0.988)
  waiting for transfers between devices: 22.3 us -> 21.2 us
    ppermute x25, waiting for transfers between devices: 22.3 us -> 21.2 us  [send(): return lax.ppermute(array, ('ctx', 'head'), pairing)]
    pallas_call x12 -> x13, Pallas kernels: 23.1 us -> 23.5 us  [run(): pl.pallas_call(kernel, out_shape=outs, in_specs=[sm] * smem + [vm] * (len...]
  transfers between devices with their start and end apart: 25 -> 25, of which waited for: 11 -> 8; matrix products, arithmetic and copies ran while one was open for 4% -> 4% of each run, Pallas kernels for 9% -> 17%
where the time goes in v3:
time: 90.1 us; the launch traced here: 89.8 us
  starting transfers between devices  38.7 us (43%)
  Pallas kernels  23.5 us (26%)
  waiting for transfers between devices  21.2 us (24%)
  between operations  2.1 us (2%)
  other arithmetic  1.99 us (2%)
  local copies, waits for them, and re-layouts  1.98 us (2%)
    ppermute x25, starting transfers between devices, send(): return lax.ppermute(array, ('ctx', 'head'), pairing)  38.7 us
    pallas_call x13, Pallas kernels, run(): pl.pallas_call(kernel, out_shape=outs, in_specs=[sm] * smem + [vm] * (len...  23.5 us
    ppermute x25, waiting for transfers between devices, send(): return lax.ppermute(array, ('ctx', 'head'), pairing)  21.2 us
    convert_element_type x1, other arithmetic, packed(): pick = (con_slot[:, None] == jnp.arange(4 * LINE_CON)[None, :]).astype(BF)  1.99 us
  transfers between devices with their start and end apart: 25, of which 8 were waited for; matrix products, arithmetic and copies ran while one was open for 4% of the time, Pallas kernels for 17%

profile of v3, /device:TPU:1, one launch (start us, length us, event | category | flops | bytes accessed | tf_op | source)
XLA Modules:
  0.0 89.8 jit_solution(8128169362456812608)
XLA Ops:
  0.7 2.7 %shard_map.115 = (bf16[32,3072]{1,0:T(8,128)(2,1)S(1)}, bf16[48,3072]{1,0:T(8,128)(2,1)S(1)}, bf16[96,384]{1,0:T(8,128)(2,1)S(1)}, s32[8,1536]{1,0:T(8,128)S(1)}) custom-call(s32[6]{0:T(128)S(1)} %stack.45.at, s32[1,1024]{1,0:T(1,128)} %bitcast.136, s32[1,512]{1,0:T(1,128)} %bitcast.138, bf16[256,3072]{1,0:T(8,128)(2,1)} %table_ref.1, ...), custom_call_target="tpu_custom_call" | custom-call | flops 1100000000 | tf_op jit(solution)/shard_map/pallas_call | solution.py:220
  3.5 2.5 %collective-permute-start.4 = (bf16[32,3072]{1,0:T(8,128)(2,1)S(1)}, bf16[32,3072]{1,0:T(8,128)(2,1)S(1)}, u32[]{:S(2)}, u32[]{:S(2)}) collective-permute-start(bf16[32,3072]{1,0:T(8,128)(2,1)S(1)} %get-tuple-element.97.refs_0_), channel_id=1, source_target_pairs={{0,16},{1,17},{2,18},{3,19},{4,20},{5,21},{6,22},{7,23},{8,24},{9,... | collective-permute-start | bytes 589832 | tf_op jit(solution)/shard_map/ppermute | solution.py:205
  6.0 3.3 %collective-permute-start.1 = (bf16[32,3072]{1,0:T(8,128)(2,1)S(1)}, bf16[32,3072]{1,0:T(8,128)(2,1)S(1)}, u32[]{:S(2)}, u32[]{:S(2)}) collective-permute-start(bf16[32,3072]{1,0:T(8,128)(2,1)S(1)} %get-tuple-element.97.refs_0_), channel_id=1, source_target_pairs={{0,1},{1,0},{2,3},{3,2},{4,5},{5,4},{6,7},{7,6},{8,9},{9,8},{10,11... | collective-permute-start | bytes 589832 | tf_op jit(solution)/shard_map/ppermute | solution.py:205
  9.3 1.2 %collective-permute-start.2 = (bf16[48,3072]{1,0:T(8,128)(2,1)S(1)}, bf16[48,3072]{1,0:T(8,128)(2,1)S(1)}, u32[]{:S(2)}, u32[]{:S(2)}) collective-permute-start(bf16[48,3072]{1,0:T(8,128)(2,1)S(1)} %get-tuple-element.102), channel_id=1, source_target_pairs={{0,2},{1,3},{2,0},{3,1},{4,6},{5,7},{6,4},{7,5},{8,10},{9,11},{10,... | collective-permute-start | bytes 884744 | tf_op jit(solution)/shard_map/ppermute | solution.py:205
  12.5 3.0 %collective-permute-start.5 = (bf16[192,128]{1,0:T(8,128)(2,1)S(1)}, bf16[192,128]{1,0:T(8,128)(2,1)S(1)}, u32[]{:S(2)}, u32[]{:S(2)}) collective-permute-start(bf16[192,128]{1,0:T(8,128)(2,1)S(1)} %get-tuple-element.107), channel_id=1, source_target_pairs={{0,64},{1,65},{2,10},{3,11},{4,68},{5,69},{6,14},{7,15},{8,72},{9,... | collective-permute-start | bytes 147464 | tf_op jit(solution)/shard_map/ppermute | solution.py:205
  15.9 1.2 %shard_map.116 = (bf16[160,256]{1,0:T(8,128)(2,1)S(1)}, s32[8,1536]{1,0:T(8,128)S(1)}, f32[1,1280]{1,0:T(1,128)S(1)}, f32[1,704]{1,0:T(1,128)S(1)}, s32[1,384]{1,0:T(1,128)S(1)}, /*index=5*/s32[1,256]{1,0:T(1,128)S(1)}) custom-call(s32[6]{0:T(128)S(1)} %stack.45.at, s32[1,1024]{1,0:T(1,128)S(1)} %bitcast.137, s32[1,512]{1,0:T(1,128)S(1)} %bitcast.139, ...), custom_call_target="tpu_custom_call" | custom-call | flops 1100000000 | tf_op jit(solution)/shard_map/pallas_call | solution.py:220
  18.3 2.2 %collective-permute-done.7.refs_3_ = bf16[32,3072]{1,0:T(8,128)(2,1)S(1)} collective-permute-done((bf16[32,3072]{1,0:T(8,128)(2,1)S(1)}, bf16[32,3072]{1,0:T(8,128)(2,1)S(1)}, u32[]{:S(2)}, u32[]{:S(2)}) %collective-permute-start.7) | collective-permute-done | bytes 196640 | tf_op jit(solution)/shard_map/ppermute | solution.py:205
  20.5 1.5 %collective-permute-start.10 = (bf16[32,3072]{1,0:T(8,128)(2,1)S(1)}, bf16[32,3072]{1,0:T(8,128)(2,1)S(1)}, u32[]{:S(2)}, u32[]{:S(2)}) collective-permute-start(bf16[32,3072]{1,0:T(8,128)(2,1)S(1)} %collective-permute-done.7.refs_3_), channel_id=1, source_target_pairs={{0,2},{1,3},{2,0},{3,1},{4,6},{5,7},{6,4},{7,5},{8,10},{9,11},{10,... | collective-permute-start | bytes 589832 | tf_op jit(solution)/shard_map/ppermute | solution.py:205
  22.6 2.7 %collective-permute-start.6 = (bf16[192,128]{1,0:T(8,128)(2,1)S(1)}, bf16[192,128]{1,0:T(8,128)(2,1)S(1)}, u32[]{:S(2)}, u32[]{:S(2)}) collective-permute-start(bf16[192,128]{1,0:T(8,128)(2,1)S(1)} %get-tuple-element.109), channel_id=1, source_target_pairs={{0,96},{1,97},{2,14},{3,15},{4,100},{5,101},{6,10},{7,11},{8,104},... | collective-permute-start | bytes 147464 | tf_op jit(solution)/shard_map/ppermute | solution.py:205
  25.3 4.7 %shard_map.118 = (bf16[208,256]{1,0:T(8,128)(2,1)S(1)}, bf16[208,256]{1,0:T(8,128)(2,1)S(1)}, bf16[208,256]{1,0:T(8,128)(2,1)S(1)}, bf16[208,256]{1,0:T(8,128)(2,1)S(1)}) custom-call(s32[6]{0:T(128)S(1)} %stack.45.at, bf16[160,256]{1,0:T(8,128)(2,1)S(1)} %get-tuple-element.110.pack_ref, bf16[32,3072]{1,0:T(8,128)(2,1)S(1)} %get-tuple-element.97.refs_0_, ...), custom_call_target="tpu_custom_call" | custom-call | flops 5500000256 | tf_op jit(solution)/shard_map/pallas_call | solution.py:220
  30.2 2.4 %collective-permute-start.16 = (bf16[208,256]{1,0:T(8,128)(2,1)S(1)}, bf16[208,256]{1,0:T(8,128)(2,1)S(1)}, u32[]{:S(2)}, u32[]{:S(2)}) collective-permute-start(bf16[208,256]{1,0:T(8,128)(2,1)S(1)} %get-tuple-element.124), channel_id=1, source_target_pairs={{0,64},{1,65},{2,10},{3,11},{4,68},{5,69},{6,14},{7,15},{8,72},{9,... | collective-permute-start | bytes 319496 | tf_op jit(solution)/shard_map/ppermute | solution.py:205
  32.5 1.5 %collective-permute-start.17 = (bf16[208,256]{1,0:T(8,128)(2,1)S(1)}, bf16[208,256]{1,0:T(8,128)(2,1)S(1)}, u32[]{:S(2)}, u32[]{:S(2)}) collective-permute-start(bf16[208,256]{1,0:T(8,128)(2,1)S(1)} %get-tuple-element.125), channel_id=1, source_target_pairs={{0,96},{1,97},{2,14},{3,15},{4,100},{5,101},{6,10},{7,11},{8,104},... | collective-permute-start | bytes 319496 | tf_op jit(solution)/shard_map/ppermute | solution.py:205
  34.0 2.8 %collective-permute-start.11 = (bf16[512,128]{1,0:T(8,128)(2,1)S(1)}, bf16[512,128]{1,0:T(8,128)(2,1)S(1)}, u32[]{:S(2)}, u32[]{:S(2)}) collective-permute-start(bf16[512,128]{1,0:T(8,128)(2,1)S(1)} %get-tuple-element.119.a), channel_id=1, source_target_pairs={{0,8},{1,9},{2,66},{3,67},{4,12},{5,13},{6,70},{7,71},{8,0},{9,1},... | collective-permute-start | bytes 393224 | tf_op jit(solution)/shard_map/ppermute | solution.py:205
  38.1 2.3 %collective-permute-start.18 = (bf16[656,256]{1,0:T(8,128)(2,1)S(1)}, bf16[656,256]{1,0:T(8,128)(2,1)S(1)}, u32[]{:S(2)}, u32[]{:S(2)}) collective-permute-start(bf16[656,256]{1,0:T(8,128)(2,1)S(1)} %shard_map.121.l0), channel_id=1, source_target_pairs={{0,4},{1,5},{2,34},{3,35},{4,0},{5,1},{6,38},{7,39},{8,12},{9,13},... | collective-permute-start | bytes 1007624 | tf_op jit(solution)/shard_map/ppermute | solution.py:205
  40.4 1.6 %collective-permute-start.19 = (bf16[656,256]{1,0:T(8,128)(2,1)S(1)}, bf16[656,256]{1,0:T(8,128)(2,1)S(1)}, u32[]{:S(2)}, u32[]{:S(2)}) collective-permute-start(bf16[656,256]{1,0:T(8,128)(2,1)S(1)} %shard_map.121.l0), channel_id=1, source_target_pairs={{0,8},{1,9},{2,66},{3,67},{4,12},{5,13},{6,70},{7,71},{8,0},{9,1},... | collective-permute-start | bytes 1007624 | tf_op jit(solution)/shard_map/ppermute | solution.py:205
  42.0 0.9 %collective-permute-start.20 = (bf16[656,256]{1,0:T(8,128)(2,1)S(1)}, bf16[656,256]{1,0:T(8,128)(2,1)S(1)}, u32[]{:S(2)}, u32[]{:S(2)}) collective-permute-start(bf16[656,256]{1,0:T(8,128)(2,1)S(1)} %shard_map.121.l0), channel_id=1, source_target_pairs={{0,12},{1,13},{2,98},{3,99},{4,8},{5,9},{6,102},{7,103},{8,4},{9,5... | collective-permute-start | bytes 1007624 | tf_op jit(solution)/shard_map/ppermute | solution.py:205
  43.2 0.8 shard_map.122
  44.0 2.0 %fusion.81.pick = bf16[1024,1280]{1,0:T(8,128)(2,1)} fusion(s32[1024]{0:T(1024)S(1)} %bitcast.134), kind=kLoop, calls=%fused_computation.115 | loop fusion | flops 2621440 | bytes 2625536 | tf_op jit(solution)/shard_map/convert_element_type | solution.py:716
  46.0 4.3 %collective-permute-done.19.l2 = bf16[656,256]{1,0:T(8,128)(2,1)S(1)} collective-permute-done((bf16[656,256]{1,0:T(8,128)(2,1)S(1)}, bf16[656,256]{1,0:T(8,128)(2,1)S(1)}, u32[]{:S(2)}, u32[]{:S(2)}) %collective-permute-start.19) | collective-permute-done | bytes 335904 | tf_op jit(solution)/shard_map/ppermute | solution.py:205
  50.4 2.7 %collective-permute-done.20.l3 = bf16[656,256]{1,0:T(8,128)(2,1)S(1)} collective-permute-done((bf16[656,256]{1,0:T(8,128)(2,1)S(1)}, bf16[656,256]{1,0:T(8,128)(2,1)S(1)}, u32[]{:S(2)}, u32[]{:S(2)}) %collective-permute-start.20) | collective-permute-done | bytes 335904 | tf_op jit(solution)/shard_map/ppermute | solution.py:205
  53.1 7.3 %shard_map.123 = (bf16[1024,128]{1,0:T(8,128)(2,1)S(1)}, f32[1024,1]{1,0:T(8,128)S(1)}, f32[1024,256]{1,0:T(8,128)S(1)}, f32[256,1]{1,0:T(8,128)S(1)}, f32[256,256]{1,0:T(8,128)S(1)}) custom-call(bf16[1024,1280]{1,0:T(8,128)(2,1)} %fusion.81.pick, bf16[656,256]{1,0:T(8,128)(2,1)S(1)} %shard_map.121.l0, bf16[656,256]{1,0:T(8,128)(2,1)S(1)} %collective-permute-done.18.l1, ...), custom_call_target="tpu_custom_call" | custom-call | flops 6600000000 | tf_op jit(solution)/shard_map/pallas_call | solution.py:220
  60.4 2.7 %shard_map.124 = (bf16[80,1152]{1,0:T(8,128)(2,1)S(1)}, bf16[80,1152]{1,0:T(8,128)(2,1)S(1)}, bf16[80,1152]{1,0:T(8,128)(2,1)S(1)}, bf16[80,1152]{1,0:T(8,128)(2,1)S(1)}) custom-call(bf16[2048,128]{1,0:T(8,128)(2,1)S(1)} %collective-permute-done.14.plane, bf16[1024,128]{1,0:T(8,128)(2,1)S(1)} %get-tuple-element.133.con_q, ...), custom_call_target="tpu_custom_call" | custom-call | flops 3300000000 | tf_op jit(solution)/shard_map/pallas_call | solution.py:220
  63.1 2.1 %collective-permute-start.22 = (bf16[80,1152]{1,0:T(8,128)(2,1)S(1)}, bf16[80,1152]{1,0:T(8,128)(2,1)S(1)}, u32[]{:S(2)}, u32[]{:S(2)}) collective-permute-start(bf16[80,1152]{1,0:T(8,128)(2,1)S(1)} %get-tuple-element.140), channel_id=1, source_target_pairs={{0,64},{1,65},{2,10},{3,11},{4,68},{5,69},{6,14},{7,15},{8,72},{9,... | collective-permute-start | bytes 552968 | tf_op jit(solution)/shard_map/ppermute | solution.py:205
  65.2 1.7 %collective-permute-start.23 = (bf16[80,1152]{1,0:T(8,128)(2,1)S(1)}, bf16[80,1152]{1,0:T(8,128)(2,1)S(1)}, u32[]{:S(2)}, u32[]{:S(2)}) collective-permute-start(bf16[80,1152]{1,0:T(8,128)(2,1)S(1)} %get-tuple-element.141), channel_id=1, source_target_pairs={{0,96},{1,97},{2,14},{3,15},{4,100},{5,101},{6,10},{7,11},{8,104},... | collective-permute-start | bytes 552968 | tf_op jit(solution)/shard_map/ppermute | solution.py:205
  67.5 2.7 %collective-permute-done.22.b2 = bf16[80,1152]{1,0:T(8,128)(2,1)S(1)} collective-permute-done((bf16[80,1152]{1,0:T(8,128)(2,1)S(1)}, bf16[80,1152]{1,0:T(8,128)(2,1)S(1)}, u32[]{:S(2)}, u32[]{:S(2)}) %collective-permute-start.22) | collective-permute-done | bytes 184352 | tf_op jit(solution)/shard_map/ppermute | solution.py:205
  70.2 1.9 %collective-permute-done.23.b3 = bf16[80,1152]{1,0:T(8,128)(2,1)S(1)} collective-permute-done((bf16[80,1152]{1,0:T(8,128)(2,1)S(1)}, bf16[80,1152]{1,0:T(8,128)(2,1)S(1)}, u32[]{:S(2)}, u32[]{:S(2)}) %collective-permute-start.23) | collective-permute-done | bytes 184352 | tf_op jit(solution)/shard_map/ppermute | solution.py:205
  72.1 1.3 %shard_map.125 = (bf16[48,1152]{1,0:T(8,128)(2,1)S(1)}, bf16[48,1536]{1,0:T(8,128)(2,1)S(1)}, bf16[32,384]{1,0:T(8,128)(2,1)}) custom-call(s32[6]{0:T(128)S(1)} %stack.45.at, bf16[80,1152]{1,0:T(8,128)(2,1)S(1)} %get-tuple-element.138.b0, bf16[80,1152]{1,0:T(8,128)(2,1)S(1)} %collective-permute-done.21.b1, bf16[80,1152]{1,0:T(8,128)(2,1)S(1)} %collective-permute-done.22.b2, ...), custom_call_target="tpu_custom_call" | custom-call | flops 1100000000 | tf_op jit(solution)/shard_map/pallas_call | solution.py:220
  73.4 6.9 %collective-permute-start.24 = (bf16[48,1536]{1,0:T(8,128)(2,1)S(1)}, bf16[48,1536]{1,0:T(8,128)(2,1)S(1)}, u32[]{:S(2)}, u32[]{:S(2)}) collective-permute-start(bf16[48,1536]{1,0:T(8,128)(2,1)S(1)} %get-tuple-element.143), channel_id=1, source_target_pairs={{0,2},{1,3},{2,0},{3,1},{4,6},{5,7},{6,4},{7,5},{8,10},{9,11},{10,... | collective-permute-start | bytes 442376 | tf_op jit(solution)/shard_map/ppermute | solution.py:205
  80.4 1.0 %collective-permute-done.24.core = bf16[48,1536]{1,0:T(8,128)(2,1)S(1)} collective-permute-done((bf16[48,1536]{1,0:T(8,128)(2,1)S(1)}, bf16[48,1536]{1,0:T(8,128)(2,1)S(1)}, u32[]{:S(2)}, u32[]{:S(2)}) %collective-permute-start.24) | collective-permute-done | bytes 147488 | tf_op jit(solution)/shard_map/ppermute | solution.py:205
  82.0 5.8 %collective-permute-done.25 = bf16[48,1152]{1,0:T(8,128)(2,1)S(1)} collective-permute-done((bf16[48,1152]{1,0:T(8,128)(2,1)S(1)}, bf16[48,1152]{1,0:T(8,128)(2,1)S(1)}, u32[]{:S(2)}, u32[]{:S(2)}) %collective-permute-start.25) | collective-permute-done | bytes 110624 | tf_op jit(solution)/shard_map/ppermute | solution.py:205
  87.8 2.0 %conditional.1 = (bf16[32,768]{1,0:T(8,128)(2,1)}, f32[1024,32]{0,1:T(8,128)}) conditional(s32[]{:T(128)} %convert_element_type.70, (s32[512]{0:T(512)S(1)}, s32[1024]{0:T(1024)S(1)}, bf16[256,3072]{1,0:T(8,128)(2,1)S(1)}, s32[1]{0:T(128)}, f32[28,2,3072]{2,1,0:T(2,128)}, /*index=5*/bf16[3072,3,768]{2,0,1:T(8,128)(2,1)}, f32[2,128]{1,0:T(2,128)S(1)}, ...), branch_computations={%region_0.15_spmd, %region_15.16_spmd} | conditional | flops 1100000000 | bytes 257951312 | solution.py:761
  88.1 1.7 %branch_1_fun.1 = (bf16[32,768]{1,0:T(8,128)(2,1)}, f32[32,1024]{1,0:T(8,128)}) custom-call(s32[6]{0:T(128)S(1)} %get-tuple-element.40.at, bf16[48,1152]{1,0:T(8,128)(2,1)S(1)} %get-tuple-element.41.own, bf16[48,1152]{1,0:T(8,128)(2,1)S(1)} %get-tuple-element.42.head, bf16[48,1536]{1,0:T(8,128)(2,1)} %get-tuple-element.43.core, ...), custom_call_target="tpu_custom_call" | custom-call | flops 1100000000 | tf_op jit(solution)/shard_map/cond/branch_1_fun/pallas_call | solution.py:220
  (53 shorter events, 5.7 us)
Async XLA Ops:
  0.7 15.2 %copy-start.8 = (s32[1024]{0:T(1024)S(1)}, s32[1024]{0:T(1024)}, u32[]{:S(2)}) copy-start(s32[1024]{0:T(1024)} %param.16) | copy-start | bytes 12292
  0.7 15.2 %copy-start.9 = (s32[512]{0:T(512)S(1)}, s32[512]{0:T(512)}, u32[]{:S(2)}) copy-start(s32[512]{0:T(512)} %param.15) | copy-start | bytes 6148
  3.5 18.6 %collective-permute-start.4 = (bf16[32,3072]{1,0:T(8,128)(2,1)S(1)}, bf16[32,3072]{1,0:T(8,128)(2,1)S(1)}, u32[]{:S(2)}, u32[]{:S(2)}) collective-permute-start(bf16[32,3072]{1,0:T(8,128)(2,1)S(1)} %get-tuple-element.97.refs_0_), channel_id=1, source_target_pairs={{0,16},{1,17},{2,18},{3,19},{4,20},{5,21},{6,22},{7,23},{8,24},{9,... | collective-permute-start | bytes 589832 | tf_op jit(solution)/shard_map/ppermute | solution.py:205
  6.0 16.1 %collective-permute-start.1 = (bf16[32,3072]{1,0:T(8,128)(2,1)S(1)}, bf16[32,3072]{1,0:T(8,128)(2,1)S(1)}, u32[]{:S(2)}, u32[]{:S(2)}) collective-permute-start(bf16[32,3072]{1,0:T(8,128)(2,1)S(1)} %get-tuple-element.97.refs_0_), channel_id=1, source_target_pairs={{0,1},{1,0},{2,3},{3,2},{4,5},{5,4},{6,7},{7,6},{8,9},{9,8},{10,11... | collective-permute-start | bytes 589832 | tf_op jit(solution)/shard_map/ppermute | solution.py:205
  9.3 11.2 %collective-permute-start.7 = (bf16[32,3072]{1,0:T(8,128)(2,1)S(1)}, bf16[32,3072]{1,0:T(8,128)(2,1)S(1)}, u32[]{:S(2)}, u32[]{:S(2)}) collective-permute-start(bf16[32,3072]{1,0:T(8,128)(2,1)S(1)} %get-tuple-element.97.refs_0_), channel_id=1, source_target_pairs={{0,17},{1,16},{2,19},{3,18},{4,21},{5,20},{6,23},{7,22},{8,25},{9,... | collective-permute-start | bytes 589832 | tf_op jit(solution)/shard_map/ppermute | solution.py:205
  9.3 2.6 %collective-permute-start.2 = (bf16[48,3072]{1,0:T(8,128)(2,1)S(1)}, bf16[48,3072]{1,0:T(8,128)(2,1)S(1)}, u32[]{:S(2)}, u32[]{:S(2)}) collective-permute-start(bf16[48,3072]{1,0:T(8,128)(2,1)S(1)} %get-tuple-element.102), channel_id=1, source_target_pairs={{0,2},{1,3},{2,0},{3,1},{4,6},{5,7},{6,4},{7,5},{8,10},{9,11},{10,... | collective-permute-start | bytes 884744 | tf_op jit(solution)/shard_map/ppermute | solution.py:205
  11.9 13.4 %copy-start.10 = (f32[2,128]{1,0:T(2,128)S(1)}, f32[2,128]{1,0:T(2,128)}, u32[]{:S(2)}) copy-start(f32[2,128]{1,0:T(2,128)} %refs_9_.1) | copy-start | bytes 3076
  12.5 9.5 %collective-permute-start.5 = (bf16[192,128]{1,0:T(8,128)(2,1)S(1)}, bf16[192,128]{1,0:T(8,128)(2,1)S(1)}, u32[]{:S(2)}, u32[]{:S(2)}) collective-permute-start(bf16[192,128]{1,0:T(8,128)(2,1)S(1)} %get-tuple-element.107), channel_id=1, source_target_pairs={{0,64},{1,65},{2,10},{3,11},{4,68},{5,69},{6,14},{7,15},{8,72},{9,... | collective-permute-start | bytes 147464 | tf_op jit(solution)/shard_map/ppermute | solution.py:205
  15.5 6.6 %collective-permute-start.3 = (bf16[192,128]{1,0:T(8,128)(2,1)S(1)}, bf16[192,128]{1,0:T(8,128)(2,1)S(1)}, u32[]{:S(2)}, u32[]{:S(2)}) collective-permute-start(bf16[192,128]{1,0:T(8,128)(2,1)S(1)} %get-tuple-element.103), channel_id=1, source_target_pairs={{0,32},{1,33},{2,6},{3,7},{4,36},{5,37},{6,2},{7,3},{8,40},{9,41},... | collective-permute-start | bytes 147464 | tf_op jit(solution)/shard_map/ppermute | solution.py:205
  20.5 4.8 %collective-permute-start.10 = (bf16[32,3072]{1,0:T(8,128)(2,1)S(1)}, bf16[32,3072]{1,0:T(8,128)(2,1)S(1)}, u32[]{:S(2)}, u32[]{:S(2)}) collective-permute-start(bf16[32,3072]{1,0:T(8,128)(2,1)S(1)} %collective-permute-done.7.refs_3_), channel_id=1, source_target_pairs={{0,2},{1,3},{2,0},{3,1},{4,6},{5,7},{6,4},{7,5},{8,10},{9,11},{10,... | collective-permute-start | bytes 589832 | tf_op jit(solution)/shard_map/ppermute | solution.py:205
  22.1 3.3 %collective-permute-start.8 = (bf16[32,3072]{1,0:T(8,128)(2,1)S(1)}, bf16[32,3072]{1,0:T(8,128)(2,1)S(1)}, u32[]{:S(2)}, u32[]{:S(2)}) collective-permute-start(bf16[32,3072]{1,0:T(8,128)(2,1)S(1)} %collective-permute-done.4.refs_1_), channel_id=1, source_target_pairs={{0,2},{1,3},{2,0},{3,1},{4,6},{5,7},{6,4},{7,5},{8,10},{9,11},{10,... | collective-permute-start | bytes 589832 | tf_op jit(solution)/shard_map/ppermute | solution.py:205
  22.1 3.2 %collective-permute-start.9 = (bf16[32,3072]{1,0:T(8,128)(2,1)S(1)}, bf16[32,3072]{1,0:T(8,128)(2,1)S(1)}, u32[]{:S(2)}, u32[]{:S(2)}) collective-permute-start(bf16[32,3072]{1,0:T(8,128)(2,1)S(1)} %collective-permute-done.1.refs_2_), channel_id=1, source_target_pairs={{0,2},{1,3},{2,0},{3,1},{4,6},{5,7},{6,4},{7,5},{8,10},{9,11},{10,... | collective-permute-start | bytes 589832 | tf_op jit(solution)/shard_map/ppermute | solution.py:205
  22.6 11.5 %collective-permute-start.6 = (bf16[192,128]{1,0:T(8,128)(2,1)S(1)}, bf16[192,128]{1,0:T(8,128)(2,1)S(1)}, u32[]{:S(2)}, u32[]{:S(2)}) collective-permute-start(bf16[192,128]{1,0:T(8,128)(2,1)S(1)} %get-tuple-element.109), channel_id=1, source_target_pairs={{0,96},{1,97},{2,14},{3,15},{4,100},{5,101},{6,10},{7,11},{8,104},... | collective-permute-start | bytes 147464 | tf_op jit(solution)/shard_map/ppermute | solution.py:205
  30.1 7.1 %collective-permute-start.15 = (bf16[208,256]{1,0:T(8,128)(2,1)S(1)}, bf16[208,256]{1,0:T(8,128)(2,1)S(1)}, u32[]{:S(2)}, u32[]{:S(2)}) collective-permute-start(bf16[208,256]{1,0:T(8,128)(2,1)S(1)} %get-tuple-element.123), channel_id=1, source_target_pairs={{0,32},{1,33},{2,6},{3,7},{4,36},{5,37},{6,2},{7,3},{8,40},{9,41},... | collective-permute-start | bytes 319496 | tf_op jit(solution)/shard_map/ppermute | solution.py:205
  30.2 7.6 %collective-permute-start.16 = (bf16[208,256]{1,0:T(8,128)(2,1)S(1)}, bf16[208,256]{1,0:T(8,128)(2,1)S(1)}, u32[]{:S(2)}, u32[]{:S(2)}) collective-permute-start(bf16[208,256]{1,0:T(8,128)(2,1)S(1)} %get-tuple-element.124), channel_id=1, source_target_pairs={{0,64},{1,65},{2,10},{3,11},{4,68},{5,69},{6,14},{7,15},{8,72},{9,... | collective-permute-start | bytes 319496 | tf_op jit(solution)/shard_map/ppermute | solution.py:205
  32.5 5.2 %collective-permute-start.17 = (bf16[208,256]{1,0:T(8,128)(2,1)S(1)}, bf16[208,256]{1,0:T(8,128)(2,1)S(1)}, u32[]{:S(2)}, u32[]{:S(2)}) collective-permute-start(bf16[208,256]{1,0:T(8,128)(2,1)S(1)} %get-tuple-element.125), channel_id=1, source_target_pairs={{0,96},{1,97},{2,14},{3,15},{4,100},{5,101},{6,10},{7,11},{8,104},... | collective-permute-start | bytes 319496 | tf_op jit(solution)/shard_map/ppermute | solution.py:205
  34.0 7.9 %collective-permute-start.11 = (bf16[512,128]{1,0:T(8,128)(2,1)S(1)}, bf16[512,128]{1,0:T(8,128)(2,1)S(1)}, u32[]{:S(2)}, u32[]{:S(2)}) collective-permute-start(bf16[512,128]{1,0:T(8,128)(2,1)S(1)} %get-tuple-element.119.a), channel_id=1, source_target_pairs={{0,8},{1,9},{2,66},{3,67},{4,12},{5,13},{6,70},{7,71},{8,0},{9,1},... | collective-permute-start | bytes 393224 | tf_op jit(solution)/shard_map/ppermute | solution.py:205
  36.9 6.0 %collective-permute-start.12 = (bf16[512,128]{1,0:T(8,128)(2,1)S(1)}, bf16[512,128]{1,0:T(8,128)(2,1)S(1)}, u32[]{:S(2)}, u32[]{:S(2)}) collective-permute-start(bf16[512,128]{1,0:T(8,128)(2,1)S(1)} %get-tuple-element.119.a), channel_id=1, source_target_pairs={{0,4},{1,5},{2,34},{3,35},{4,0},{5,1},{6,38},{7,39},{8,12},{9,13},... | collective-permute-start | bytes 393224 | tf_op jit(solution)/shard_map/ppermute | solution.py:205
  37.2 5.7 %collective-permute-start.13 = (bf16[512,128]{1,0:T(8,128)(2,1)S(1)}, bf16[512,128]{1,0:T(8,128)(2,1)S(1)}, u32[]{:S(2)}, u32[]{:S(2)}) collective-permute-start(bf16[512,128]{1,0:T(8,128)(2,1)S(1)} %get-tuple-element.119.a), channel_id=1, source_target_pairs={{0,12},{1,13},{2,98},{3,99},{4,8},{5,9},{6,102},{7,103},{8,4},{9,5... | collective-permute-start | bytes 393224 | tf_op jit(solution)/shard_map/ppermute | solution.py:205
  38.1 7.9 %collective-permute-start.18 = (bf16[656,256]{1,0:T(8,128)(2,1)S(1)}, bf16[656,256]{1,0:T(8,128)(2,1)S(1)}, u32[]{:S(2)}, u32[]{:S(2)}) collective-permute-start(bf16[656,256]{1,0:T(8,128)(2,1)S(1)} %shard_map.121.l0), channel_id=1, source_target_pairs={{0,4},{1,5},{2,34},{3,35},{4,0},{5,1},{6,38},{7,39},{8,12},{9,13},... | collective-permute-start | bytes 1007624 | tf_op jit(solution)/shard_map/ppermute | solution.py:205
  40.4 10.0 %collective-permute-start.19 = (bf16[656,256]{1,0:T(8,128)(2,1)S(1)}, bf16[656,256]{1,0:T(8,128)(2,1)S(1)}, u32[]{:S(2)}, u32[]{:S(2)}) collective-permute-start(bf16[656,256]{1,0:T(8,128)(2,1)S(1)} %shard_map.121.l0), channel_id=1, source_target_pairs={{0,8},{1,9},{2,66},{3,67},{4,12},{5,13},{6,70},{7,71},{8,0},{9,1},... | collective-permute-start | bytes 1007624 | tf_op jit(solution)/shard_map/ppermute | solution.py:205
  42.0 11.1 %collective-permute-start.20 = (bf16[656,256]{1,0:T(8,128)(2,1)S(1)}, bf16[656,256]{1,0:T(8,128)(2,1)S(1)}, u32[]{:S(2)}, u32[]{:S(2)}) collective-permute-start(bf16[656,256]{1,0:T(8,128)(2,1)S(1)} %shard_map.121.l0), channel_id=1, source_target_pairs={{0,12},{1,13},{2,98},{3,99},{4,8},{5,9},{6,102},{7,103},{8,4},{9,5... | collective-permute-start | bytes 1007624 | tf_op jit(solution)/shard_map/ppermute | solution.py:205
  42.9 17.4 %collective-permute-start.14 = (bf16[2048,128]{1,0:T(8,128)(2,1)S(1)}, bf16[2048,128]{1,0:T(8,128)(2,1)S(1)}, u32[]{:S(2)}, u32[]{:S(2)}) collective-permute-start(bf16[2048,128]{1,0:T(8,128)(2,1)S(1)} %shard_map.120.plane), channel_id=1, source_target_pairs={{0,16},{1,17},{2,18},{3,19},{4,20},{5,21},{6,22},{7,23},{8,24},{9,... | collective-permute-start | bytes 1572872 | tf_op jit(solution)/shard_map/ppermute | solution.py:205
  63.1 4.4 %collective-permute-start.21 = (bf16[80,1152]{1,0:T(8,128)(2,1)S(1)}, bf16[80,1152]{1,0:T(8,128)(2,1)S(1)}, u32[]{:S(2)}, u32[]{:S(2)}) collective-permute-start(bf16[80,1152]{1,0:T(8,128)(2,1)S(1)} %get-tuple-element.139), channel_id=1, source_target_pairs={{0,32},{1,33},{2,6},{3,7},{4,36},{5,37},{6,2},{7,3},{8,40},{9,41},... | collective-permute-start | bytes 552968 | tf_op jit(solution)/shard_map/ppermute | solution.py:205
  63.1 7.1 %collective-permute-start.22 = (bf16[80,1152]{1,0:T(8,128)(2,1)S(1)}, bf16[80,1152]{1,0:T(8,128)(2,1)S(1)}, u32[]{:S(2)}, u32[]{:S(2)}) collective-permute-start(bf16[80,1152]{1,0:T(8,128)(2,1)S(1)} %get-tuple-element.140), channel_id=1, source_target_pairs={{0,64},{1,65},{2,10},{3,11},{4,68},{5,69},{6,14},{7,15},{8,72},{9,... | collective-permute-start | bytes 552968 | tf_op jit(solution)/shard_map/ppermute | solution.py:205
  65.2 6.9 %collective-permute-start.23 = (bf16[80,1152]{1,0:T(8,128)(2,1)S(1)}, bf16[80,1152]{1,0:T(8,128)(2,1)S(1)}, u32[]{:S(2)}, u32[]{:S(2)}) collective-permute-start(bf16[80,1152]{1,0:T(8,128)(2,1)S(1)} %get-tuple-element.141), channel_id=1, source_target_pairs={{0,96},{1,97},{2,14},{3,15},{4,100},{5,101},{6,10},{7,11},{8,104},... | collective-permute-start | bytes 552968 | tf_op jit(solution)/shard_map/ppermute | solution.py:205
  72.1 15.7 %copy-start = (bf16[256,3072]{1,0:T(8,128)(2,1)S(1)}, bf16[256,3072]{1,0:T(8,128)(2,1)}, u32[]{:S(2)}) copy-start(bf16[256,3072]{1,0:T(8,128)(2,1)} %table_ref.1) | copy-start | bytes 4718596
  72.1 15.7 %copy-start.3 = (bf16[32,768]{1,0:T(8,128)(2,1)S(1)}, bf16[32,768]{1,0:T(8,128)(2,1)}, u32[]{:S(2)}) copy-start(bf16[32,768]{1,0:T(8,128)(2,1)} %q_ref.1) | copy-start | bytes 147460
  72.1 15.7 %copy-start.6 = (bf16[32,768]{1,0:T(8,128)(2,1)S(1)}, bf16[32,768]{1,0:T(8,128)(2,1)}, u32[]{:S(2)}) copy-start(bf16[32,768]{1,0:T(8,128)(2,1)} %k_ref.1) | copy-start | bytes 147460
  72.1 15.7 %copy-start.7 = (bf16[32,768]{1,0:T(8,128)(2,1)S(1)}, bf16[32,768]{1,0:T(8,128)(2,1)}, u32[]{:S(2)}) copy-start(bf16[32,768]{1,0:T(8,128)(2,1)} %v_ref.1) | copy-start | bytes 147460
  73.4 8.0 %collective-permute-start.24 = (bf16[48,1536]{1,0:T(8,128)(2,1)S(1)}, bf16[48,1536]{1,0:T(8,128)(2,1)S(1)}, u32[]{:S(2)}, u32[]{:S(2)}) collective-permute-start(bf16[48,1536]{1,0:T(8,128)(2,1)S(1)} %get-tuple-element.143), channel_id=1, source_target_pairs={{0,2},{1,3},{2,0},{3,1},{4,6},{5,7},{6,4},{7,5},{8,10},{9,11},{10,... | collective-permute-start | bytes 442376 | tf_op jit(solution)/shard_map/ppermute | solution.py:205
  82.0 5.8 %collective-permute-start.25 = (bf16[48,1152]{1,0:T(8,128)(2,1)S(1)}, bf16[48,1152]{1,0:T(8,128)(2,1)S(1)}, u32[]{:S(2)}, u32[]{:S(2)}) collective-permute-start(bf16[48,1152]{1,0:T(8,128)(2,1)S(1)} %shard_map.126), channel_id=1, source_target_pairs={{0,1},{1,0},{2,3},{3,2},{4,5},{5,4},{6,7},{7,6},{8,9},{9,8},{10,11... | collective-permute-start | bytes 331784 | tf_op jit(solution)/shard_map/ppermute | solution.py:205
  (1 other events, 0.6 us)

commit v4 on v3

--- a/solution.py
+++ b/solution.py
@@ -18,7 +18,7 @@
 LINE_TXT = 176
 LINE = LINE_CON + LINE_TXT
 MIB = 1 << 20
-PROJ_US, NEAR_US, FAR_US = 5.0, 6.0, 3.0
+PROJ_US, NEAR_US, FAR_US = 5.0, 2.0, 3.0
 FACTOR = HD ** (-0.5) * math.log2(math.e)
 
 
@@ -213,7 +213,7 @@
     return lax.dot_general(a, b, (((1,), (0,)), ((), ())), preferred_element_type=F32)
 
 
-def call(kernel, outs, scratch=(), limit=48, us=1.0, smem=1, in_hbm=0):
+def call(kernel, outs, scratch=(), limit=16, us=1.0, smem=1, in_hbm=0):
     def run(*args):
         vm = pl.BlockSpec(memory_space=pltpu.VMEM)
         sm = pl.BlockSpec(memory_space=pltpu.SMEM)
@@ -264,38 +264,45 @@
     return jnp.concatenate(found, axis=1).astype(jnp.int32), counts
 
 
-def most(counts, n):
-    return jnp.broadcast_to(jnp.max(counts, axis=0, keepdims=True).astype(jnp.int32), (1, n))
-
-
 def plan_kernel(
-    at, con_ref, txt_ref, table_ref, q_ref, k_ref, v_ref, rows_ref, both_ref, img_ref, plan_ref
+    at, con_ref, txt_ref, table_ref, q_ref, k_ref, v_ref, rows_ref, both_ref, img_ref
 ):
     ids = jnp.concatenate([con_ref[...], txt_ref[...]], axis=1)
     n = ids.shape[1]
+    blk = 256
+    blocks = n // blk
     vocab_dev = table_ref.shape[0]
-    owner = ids >> int(math.log2(vocab_dev))
-    rank, (counts,) = ranks(owner, 128, ())
-    hot_slot = lax.broadcasted_iota(jnp.int32, (SLOTS, n), 0) == rank
-    hot_slot = (hot_slot & (owner == at[0])).astype(F32).astype(BF)
-    hot_row = lax.broadcasted_iota(jnp.int32, (vocab_dev, n), 0) == (ids & (vocab_dev - 1))
-    pick = nt(hot_slot, hot_row.astype(F32).astype(BF)).astype(BF)
-    rows = nn(pick, table_ref[...]).astype(BF)
+    mine = ((ids >> int(math.log2(vocab_dev))) == at[0]).astype(F32)
+    pieces = [slice(b * blk, (b + 1) * blk) for b in range(blocks)]
+    folded = jnp.concatenate(
+        [mine[:, p] for p in pieces] + [jnp.zeros((8 - blocks, blk), F32)], axis=0
+    )
+    row = lax.broadcasted_iota(jnp.int32, (blk, blk), 0)
+    col = lax.broadcasted_iota(jnp.int32, (blk, blk), 1)
+    before = nn(folded.astype(BF), (row < col).astype(F32).astype(BF))
+    label = lax.broadcasted_iota(jnp.int32, (SLOTS, blk), 0).astype(F32)
+    found = jnp.zeros((SLOTS, blk), F32)
+    skipped = jnp.zeros((1, 1), F32)
+    for b, p in enumerate(pieces):
+        rank = before[b : b + 1, :] + skipped
+        row_in_table = ((ids[:, p] & (vocab_dev - 1)) + 1).astype(F32) * mine[:, p]
+        found = found + jnp.where(label == rank, row_in_table, 0.0)
+        skipped = skipped + jnp.sum(mine[:, p], axis=1, keepdims=True)
+    found = jnp.sum(found, axis=1, keepdims=True).astype(jnp.int32) - 1
+    pick = lax.broadcasted_iota(jnp.int32, (SLOTS, vocab_dev), 1) == found
+    rows = nn(pick.astype(F32).astype(BF), table_ref[...]).astype(BF)
     rows_ref[...] = rows
     both_ref[0:SLOTS, :] = rows
     m = q_ref.shape[0]
     half = q_ref.shape[1] // 2
-    mine = pl.ds(pl.multiple_of(at[2] * half, half), half)
-    theirs = pl.ds(pl.multiple_of((1 - at[2]) * half, half), half)
+    lanes_own = pl.ds(pl.multiple_of(at[2] * half, half), half)
+    lanes_other = pl.ds(pl.multiple_of((1 - at[2]) * half, half), half)
     for i, ref in enumerate((q_ref, k_ref, v_ref)):
-        img_ref[i * m : (i + 1) * m, :] = ref[:, mine]
+        img_ref[i * m : (i + 1) * m, :] = ref[:, lanes_own]
         for j in range(2):
             lanes = slice((2 * i + j) * half, (2 * i + j + 1) * half)
-            both_ref[SLOTS:, lanes] = ref[16 * j : 16 * (j + 1), theirs]
+            both_ref[SLOTS:, lanes] = ref[16 * j : 16 * (j + 1), lanes_other]
     both_ref[SLOTS:, 6 * half :] = jnp.zeros((16, 2 * half), BF)
-    plan_ref[0:1, :] = rank
-    plan_ref[1:2, :] = most(counts, n)
-    plan_ref[2:8, :] = jnp.zeros((6, n), jnp.int32)
 
 
 def to_row(column):
@@ -354,13 +361,22 @@
 
 
 def pack_kernel(
-    at, con_ref, txt_ref, plan_ref, out_ref, spot_ref, con_bias, txt_bias, con_line, txt_line
+    at, con_ref, txt_ref, w_hbm, out_ref, spot_ref, con_bias, txt_bias, con_line, txt_line, w_ref, sem
 ):
+    half = w_ref.shape[2]
+    lanes = pl.ds(pl.multiple_of(at[2] * half, half), half)
+    weights = pltpu.make_async_copy(w_hbm.at[:, :, lanes], w_ref, sem)
+    weights.start()
     ids = jnp.concatenate([con_ref[...], txt_ref[...]], axis=1)
     n = ids.shape[1]
     n_con = con_ref.shape[1]
     owner = ids >> 8
     column = column_of(owner)
+    here = column == at[1]
+    z = ((owner & 1) << 1) | ((owner >> 4) & 1)
+    core = (owner >> 1) & 1
+    piece = jnp.where(here, jnp.where(core == at[2], 0, 4) + (at[3] ^ z), -1)
+    rank, _ = ranks(piece, 8, ())
     spot, (con_counts, txt_counts) = ranks(column, 16, (n_con // 256,))
     con_skip, con_total, con_most = line_plan(at, con_counts)
     txt_skip, txt_total, txt_most = line_plan(at, txt_counts)
@@ -372,6 +388,7 @@
     spot_ref[0:1, :] = (
         (item_v ^ at[5]) * LINE_CON + per_lane(con_skip, column).astype(jnp.int32) + spot
     )
+    wanted = (lax.broadcasted_iota(jnp.int32, (128, n), 0) == owner).astype(F32)
     over = jnp.maximum(
         jnp.maximum(
             jnp.max(con_counts, axis=0, keepdims=True) - CON,
@@ -379,37 +396,26 @@
         ),
         jnp.maximum(con_most - LINE_CON, txt_most - LINE_TXT),
     )
-    spot_ref[1:2, :] = jnp.maximum(
-        jnp.broadcast_to(over.astype(jnp.int32), (1, n)), plan_ref[1:2, :] - SLOTS
-    )
+    most = jnp.max(jnp.sum(wanted, axis=1, keepdims=True), axis=0, keepdims=True)
+    over = jnp.maximum(over, most - SLOTS)
+    spot_ref[1:2, :] = jnp.broadcast_to(over.astype(jnp.int32), (1, n))
     spot_ref[2:8, :] = jnp.zeros((6, n), jnp.int32)
-    here = column == at[1]
-    rank = plan_ref[0:1, :]
     concept = lax.broadcasted_iota(jnp.int32, (1, n), 1) < n_con
     target = jnp.where(
         concept, jnp.where(spot < CON, spot, -1), jnp.where(spot < TXT, spot + CON, -1)
     )
-    z = ((owner & 1) << 1) | ((owner >> 4) & 1)
-    core = (owner >> 1) & 1
-    piece = jnp.where(core == at[2], 0, 4) + (at[3] ^ z)
-    source = jnp.where(rank < SLOTS, piece * SLOTS + rank, -1)
+    source = jnp.where(here & (rank < SLOTS), piece * SLOTS + rank, -1)
     target = jnp.where(here, target, -1)
-    source = jnp.where(here, source, -1)
     hot_t = (lax.broadcasted_iota(jnp.int32, (ROWS, n), 0) == target).astype(F32).astype(BF)
     hot_s = (lax.broadcasted_iota(jnp.int32, (8 * SLOTS, n), 0) == source).astype(F32).astype(BF)
     out_ref[...] = nt(hot_t, hot_s).astype(BF)
+    weights.wait()
 
 
 def project_kernel(at, pack_ref, *refs):
-    rows, (mod_ref, gain_ref, w_hbm), outs = refs[:8], refs[8:11], refs[11:15]
-    raw_ref, x_ref, w_ref, sems = refs[15:]
-    half = w_ref.shape[2]
-    lanes = pl.ds(pl.multiple_of(at[2] * half, half), half)
-    copies = [
-        pltpu.make_async_copy(w_hbm.at[j, :, lanes], w_ref.at[j], sems.at[j]) for j in range(3)
-    ]
-    for copy in copies:
-        copy.start()
+    rows, (mod_ref, gain_ref, w_ref), outs, (raw_ref, x_ref) = (
+        refs[:8], refs[8:11], refs[11:15], refs[15:]
+    )
     for i, ref in enumerate(rows):
         raw_ref[i * SLOTS : (i + 1) * SLOTS, :] = ref[0:SLOTS, :]
     shift = mod_ref[0:1, :]
@@ -426,11 +432,8 @@
         meansq = jnp.mean(u * u, axis=1, keepdims=True)
         return u * lax.rsqrt(meansq + 1e-06) * gain
 
-    copies[0].wait()
     q = nn(x_ref[0:CON, :], w_ref[0])
-    copies[1].wait()
     k = nn(x_ref[...], w_ref[1])
-    copies[2].wait()
     v = nn(x_ref[...], w_ref[2])
     heads = []
     for h in range(3):
@@ -528,58 +531,101 @@
     return jnp.concatenate([values, jnp.ones_like(values)], axis=1)
 
 
-def plane_part(plane):
+def image_near_kernel(plane, q, peak, summed):
     n = plane.shape[0] // 2
-    return (plane[0:n, :], with_ones(plane[n:, :]), None)
-
-
-def image_near_kernel(plane, q, peak, summed):
-    peak[...], summed[...] = weigh(q[...], (plane_part(plane),), FACTOR)
-
-
-def near_kernel(pick, l0, l1, l2, l3, con_bias, txt_bias, plane, img_q, im, ims, *refs):
-    (q_out, cm_out, cs_out, im_out, ims_out), (con_q, con_k, con_v, txt_k, txt_v) = refs[:5], refs[5:]
-    n, m = LINE_CON, LINE_TXT
-    for a, ref in enumerate((l0, l1, l2, l3)):
+    part = (plane[0:n, :], with_ones(plane[n:, :]), None)
+    peak[...], summed[...] = weigh(q[...], (part,), FACTOR)
+
+
+def line_queries(con_q, refs):
+    n = LINE_CON
+    for a, ref in enumerate(refs):
         con_q[a * n : a * n + n // 2, :] = ref[LINE:, 0:HD]
         con_q[a * n + n // 2 : (a + 1) * n, :] = ref[LINE:, HD:]
+
+
+def order_kernel(pick, l0, l1, q_out, con_q):
+    line_queries(con_q, (l0, l1))
+    q_out[...] = nn(pick[:, : 2 * LINE_CON], con_q[...]).astype(BF)
+
+
+def weigh_blocks(q, parts, store):
+    blk = 256
+    blocks = [slice(b, b + blk) for b in range(0, q.shape[0], blk)]
+
+    def scores(rows):
+        found = []
+        for keys, _, bias in parts:
+            part = nt(q[rows, :], keys[...])
+            found.append(part if bias is None else part + bias[...])
+        return found
+
+    ready = scores(blocks[0])
+    for b, rows in enumerate(blocks):
+        now, ready = ready, scores(blocks[b + 1]) if b + 1 < len(blocks) else None
+        peak = now[0].max(axis=1, keepdims=True)
+        for part in now[1:]:
+            peak = jnp.maximum(peak, part.max(axis=1, keepdims=True))
+        summed = sum(
+            nn(jnp.exp2(part - peak).astype(BF), values[...])
+            for part, (_, values, _) in zip(now, parts)
+        )
+        store(rows, peak, summed)
+
+
+def near_kernel(
+    pick, q_part, l0, l1, l2, l3, con_bias, txt_bias, plane, img_q, im, ims, *refs
+):
+    q_out, cm_out, cs_out, im_out, ims_out = refs[:5]
+    con_q, con_k, con_v, txt_k, txt_v, img_v = refs[5:]
+    n, m = LINE_CON, LINE_TXT
+    line_queries(con_q, (l2, l3))
+    for a, ref in enumerate((l0, l1, l2, l3)):
         con_k[a * n : (a + 1) * n, :] = ref[0:n, 0:HD]
         con_v[a * n : (a + 1) * n, :] = with_ones(ref[0:n, HD:])
         txt_k[a * m : (a + 1) * m, :] = ref[n:LINE, 0:HD]
         txt_v[a * m : (a + 1) * m, :] = with_ones(ref[n:LINE, HD:])
-    images = plane_part(plane)
-    q_out[...] = nn(pick[...], con_q[...]).astype(BF)
-    for b in range(q_out.shape[0] // 256):
-        rows = slice(b * 256, (b + 1) * 256)
-        parts = (images, (con_k[...], con_v[...], con_bias[...]))
-        cm_out[rows, :], cs_out[rows, :] = weigh(q_out[rows, :], parts, None)
+    n_img = plane.shape[0] // 2
+    img_v[...] = with_ones(plane[n_img:, :])
+    rest = nn(pick[:, 2 * n :], con_q[...])
+    q_out[...] = (rest + q_part[...].astype(F32)).astype(BF)
+
+    def store(rows, peak, summed):
+        cm_out[rows, :] = peak
+        cs_out[rows, :] = summed
+
+    parts = ((plane.at[0:n_img, :], img_v, None), (con_k, con_v, con_bias))
+    weigh_blocks(q_out, parts, store)
     text = weigh(img_q[...], ((txt_k[...], txt_v[...], txt_bias[...]),), FACTOR)
     im_out[...], ims_out[...] = join(text, (im[...], ims[...]))
 
 
 def far_kernel(plane, con_q, img_q, cm, cs, im, ims, *refs):
-    outs, (con_out,) = refs[:4], refs[4:]
-    images = plane_part(plane)
-    img = merge(weigh(img_q[...], (images,), FACTOR), (im[...], ims[...]))
+    outs, (con_out, img_v) = refs[:4], refs[4:]
+    n_img = plane.shape[0] // 2
+    img_v[...] = with_ones(plane[n_img:, :])
+    part = (plane[0:n_img, :], img_v[...], None)
+    img = merge(weigh(img_q[...], (part,), FACTOR), (im[...], ims[...]))
     n_con = con_out.shape[0]
-    for b in range(n_con // 256):
-        rows = slice(b * 256, (b + 1) * 256)
-        part = weigh(con_q[rows, :], (images,), None)
-        con_out[rows, :] = merge(part, (cm[rows, :], cs[rows, :]))
+
+    def store(rows, peak, summed):
+        con_out[rows, :] = merge((peak, summed), (cm[rows, :], cs[rows, :]))
+
+    weigh_blocks(con_q, ((plane.at[0:n_img, :], img_v, None),), store)
     dots = nt(img, con_out[...]).astype(BF)
     con_f = con_out[...].astype(F32)
-    con_sq = nt(jnp.ones((16, HD), F32), con_f * con_f, precision=lax.Precision.HIGHEST).astype(BF)
+    con_sq = nt(jnp.ones((8, HD), F32), con_f * con_f, precision=lax.Precision.HIGHEST).astype(BF)
     for s, out in enumerate(outs):
         rows = slice(s * 64, (s + 1) * 64)
         out[0:64, 0:n_con] = dots[rows]
         out[0:64, n_con:] = img[rows]
-        out[64:80, 0:n_con] = con_sq
-        out[64:80, n_con:] = jnp.zeros((16, HD), BF)
+        out[64:72, 0:n_con] = con_sq
+        out[64:72, n_con:] = jnp.zeros((8, HD), BF)
 
 
 def head_sum_kernel(at, b0, b1, b2, b3, own, core, out_own):
     n_con = b0.shape[1] - HD
-    total = jnp.zeros((80, n_con), F32)
+    total = jnp.zeros((72, n_con), F32)
     outs = [jnp.zeros((64, HD), BF) for _ in range(3)]
     for s, ref in enumerate((b0, b1, b2, b3)):
         head = at[4] ^ s
@@ -594,13 +640,13 @@
     total = total.astype(BF)
     for ref, row in ((own, 0), (core, 32)):
         ref[0:32, 0:n_con] = total[row : row + 32]
-        ref[32:48, 0:n_con] = total[64:80]
+        ref[32:40, 0:n_con] = total[64:72]
         ref[0:32, n_con : n_con + HD] = image_sq[row : row + 32]
-        ref[32:48, n_con : n_con + HD] = jnp.zeros((16, HD), BF)
+        ref[32:40, n_con : n_con + HD] = jnp.zeros((8, HD), BF)
     for h in range(3):
         lanes = slice(n_con + (1 + h) * HD, n_con + (2 + h) * HD)
         core[0:32, lanes] = outs[h][32:64]
-        core[32:48, lanes] = jnp.zeros((16, HD), BF)
+        core[32:40, lanes] = jnp.zeros((8, HD), BF)
         out_own[:, h * HD : (h + 1) * HD] = outs[h][0:32]
 
 
@@ -642,20 +688,14 @@
     half = txt_qkv.shape[2] // 2
     n_img = img_q.shape[0]
 
-    own_rows, own_both, own_img, plan = call(
-        plan_kernel,
-        (
-            sds((SLOTS, width)),
-            sds((SLOTS + 16, width)),
-            sds((3 * n_img, half)),
-            sds((8, n), jnp.int32),
-        ),
+    own_rows, own_both, own_img = call(
+        plan_kernel, (sds((SLOTS, width)), sds((SLOTS + 16, width)), sds((3 * n_img, half)))
     )(at, con_ids, text_ids, token_table, img_q, img_k, img_v)
     far_rows = send(own_rows, swap_z(2))
     column_rows = [own_rows] + [send(own_rows, swap_z(s)) for s in (1, 3)]
     core_both = send(own_both, swap_core())
 
-    pack, spots, con_bias, txt_bias, con_line, txt_line = call(
+    pack, spots, con_bias, txt_bias, con_line, txt_line, weights = call(
         pack_kernel,
         (
             sds((ROWS, 8 * SLOTS)),
@@ -664,8 +704,13 @@
             sds((1, 4 * LINE_TXT), F32),
             sds((1, 4 * CON), jnp.int32),
             sds((1, 4 * TXT), jnp.int32),
+            sds((3, width, half)),
         ),
-    )(at, con_ids, text_ids, plan)
+        scratch=(pltpu.SemaphoreType.DMA,),
+        limit=24,
+        us=2.0,
+        in_hbm=1,
+    )(at, con_ids, text_ids, jnp.transpose(txt_qkv, (1, 0, 2)))
     shift_scale = lax.dynamic_index_in_dim(modulation, step_index[0], 0, keepdims=False)
     fits = (spots[1, 0] <= 0).astype(jnp.int32)
 
@@ -687,12 +732,10 @@
         scratch=(
             pltpu.VMEM((8 * SLOTS, width), BF),
             pltpu.VMEM((ROWS, width), BF),
-            pltpu.VMEM((3, width, half), BF),
-            pltpu.SemaphoreType.DMA((3,)),
         ),
+        limit=24,
         us=PROJ_US,
-        in_hbm=1,
-    )(at, pack, *column_rows, *other_rows, shift_scale, qk_gain, jnp.transpose(txt_qkv, (1, 0, 2)))
+    )(at, pack, *column_rows, *other_rows, shift_scale, qk_gain, weights)
 
     *image_blocks, first = lax.optimization_barrier((*image_blocks, qkv[0]))
     image_q, image_kv = call(
@@ -718,23 +761,29 @@
     image_stats = (sds((8 * n_img, 1), F32), sds((8 * n_img, 2 * HD), F32))
     stats = (sds((n_con, 1), F32), sds((n_con, 2 * HD), F32)) + image_stats
     image_near = call(image_near_kernel, image_stats, smem=0)(plane, image_q)
+    q_part = call(
+        order_kernel, sds((n_con, HD)), scratch=(pltpu.VMEM((2 * LINE_CON, HD), BF),), smem=0
+    )(pick, lines[0], lines[1])
     con_q, *near = call(
         near_kernel,
         (sds((n_con, HD)),) + stats,
         scratch=(
-            pltpu.VMEM((4 * LINE_CON, HD), BF),
+            pltpu.VMEM((2 * LINE_CON, HD), BF),
             pltpu.VMEM((4 * LINE_CON, HD), BF),
             pltpu.VMEM((4 * LINE_CON, 2 * HD), BF),
             pltpu.VMEM((4 * LINE_TXT, HD), BF),
             pltpu.VMEM((4 * LINE_TXT, 2 * HD), BF),
+            pltpu.VMEM((32 * n_img, 2 * HD), BF),
         ),
+        limit=32,
         us=NEAR_US,
         smem=0,
-    )(pick, *lines, con_bias, txt_bias, plane, image_q, *image_near)
+    )(pick, q_part, *lines, con_bias, txt_bias, plane, image_q, *image_near)
     blocks = call(
         far_kernel,
-        tuple(sds((80, n_con + HD)) for _ in range(4)),
-        scratch=(pltpu.VMEM((n_con, HD), BF),),
+        tuple(sds((72, n_con + HD)) for _ in range(4)),
+        scratch=(pltpu.VMEM((n_con, HD), BF), pltpu.VMEM((32 * n_img, 2 * HD), BF)),
+        limit=24,
         us=FAR_US,
         smem=0,
     )(other_plane, con_q, image_q, *near)
@@ -742,10 +791,10 @@
     blocks = [blocks[0], blocks[2], blocks[1], blocks[3]]
     own, core, out_own = call(
         head_sum_kernel,
-        (sds((48, n_con + HD)), sds((48, n_con + 4 * HD)), sds((32, half))),
+        (sds((40, n_con + HD)), sds((40, n_con + 4 * HD)), sds((32, half))),
     )(at, *blocks)
     core = send(core, swap_core())
-    own = call(core_sum_kernel, sds((48, n_con + HD)), smem=0)(own, core)
+    own = call(core_sum_kernel, sds((40, n_con + HD)), smem=0)(own, core)
     last = (at, own, send(own, swap_z(2)), core, out_own)
     finish = call(finish_kernel, (sds((n_img, 2 * half)), sds((n_img, n_con), F32)))
 

time: 90.1 us -> 81.3 us (0.902)
  waiting for transfers between devices: 21.2 us -> 14.8 us
  Pallas kernels: 23.5 us -> 21.9 us
  other arithmetic: 1.99 us -> 0.49 us
  starting transfers between devices: 38.7 us -> 40.1 us
    ppermute x25, waiting for transfers between devices: 21.2 us -> 14.8 us  [send(): return lax.ppermute(array, ('ctx', 'head'), pairing)]
    pallas_call x13 -> x14, Pallas kernels: 23.5 us -> 21.9 us  [run(): pl.pallas_call(kernel, out_shape=outs, in_specs=[sm] * smem + [vm] * (len...]
    convert_element_type x1, other arithmetic: 1.99 us -> 0.49 us  [packed(): pick = (con_slot[:, None] == jnp.arange(4 * LINE_CON)[None, :]).astype(BF)]
    ppermute x25, starting transfers between devices: 38.7 us -> 40.1 us  [send(): return lax.ppermute(array, ('ctx', 'head'), pairing)]
  transfers between devices with their start and end apart: 25 -> 25, of which waited for: 8 -> 8; matrix products, arithmetic and copies ran while one was open for 4% -> 2% of each run, Pallas kernels for 17% -> 18%
where the time goes in v4:
time: 81.3 us; the launch traced here: 81 us
  starting transfers between devices  40.1 us (49%)
  Pallas kernels  21.9 us (27%)
  waiting for transfers between devices  14.8 us (18%)
  between operations  2.13 us (3%)
  local copies, waits for them, and re-layouts  1.37 us (2%)
    ppermute x25, starting transfers between devices, send(): return lax.ppermute(array, ('ctx', 'head'), pairing)  40.1 us
    pallas_call x14, Pallas kernels, run(): pl.pallas_call(kernel, out_shape=outs, in_specs=[sm] * smem + [vm] * (len...  21.9 us
    ppermute x25, waiting for transfers between devices, send(): return lax.ppermute(array, ('ctx', 'head'), pairing)  14.8 us
  transfers between devices with their start and end apart: 25, of which 8 were waited for; matrix products, arithmetic and copies ran while one was open for 2% of the time, Pallas kernels for 18%

profile of v4, /device:TPU:1, one launch (start us, length us, event | category | flops | bytes accessed | tf_op | source)
XLA Modules:
  0.0 81.0 jit_solution(11795342470192644337)
XLA Ops:
  0.7 2.1 %shard_map.115 = (bf16[32,3072]{1,0:T(8,128)(2,1)S(1)}, bf16[48,3072]{1,0:T(8,128)(2,1)S(1)}, bf16[96,384]{1,0:T(8,128)(2,1)S(1)}) custom-call(s32[6]{0:T(128)S(1)} %stack.45.at, s32[1,1024]{1,0:T(1,128)} %bitcast.134, s32[1,512]{1,0:T(1,128)} %bitcast.138, bf16[256,3072]{1,0:T(8,128)(2,1)} %table_ref.1, bf16[32,768]{1,0:T(8,128)(2,1)} %q_ref.1, ...), custom_call_target="tpu_custom_call" | custom-call | flops 1100000000 | tf_op jit(solution)/shard_map/pallas_call | solution.py:220
  2.9 4.5 %collective-permute-start.1 = (bf16[32,3072]{1,0:T(8,128)(2,1)S(1)}, bf16[32,3072]{1,0:T(8,128)(2,1)S(1)}, u32[]{:S(2)}, u32[]{:S(2)}) collective-permute-start(bf16[32,3072]{1,0:T(8,128)(2,1)S(1)} %get-tuple-element.97.refs_0_), channel_id=1, source_target_pairs={{0,1},{1,0},{2,3},{3,2},{4,5},{5,4},{6,7},{7,6},{8,9},{9,8},{10,11... | collective-permute-start | bytes 589832 | tf_op jit(solution)/shard_map/ppermute | solution.py:205
  8.1 1.2 %collective-permute-start.2 = (bf16[48,3072]{1,0:T(8,128)(2,1)S(1)}, bf16[48,3072]{1,0:T(8,128)(2,1)S(1)}, u32[]{:S(2)}, u32[]{:S(2)}) collective-permute-start(bf16[48,3072]{1,0:T(8,128)(2,1)S(1)} %get-tuple-element.101), channel_id=1, source_target_pairs={{0,2},{1,3},{2,0},{3,1},{4,6},{5,7},{6,4},{7,5},{8,10},{9,11},{10,... | collective-permute-start | bytes 884744 | tf_op jit(solution)/shard_map/ppermute | solution.py:205
  10.0 0.7 dynamic-slice_bitcast_fusion.refs_8_
  11.3 1.4 %collective-permute-start.3 = (bf16[192,128]{1,0:T(8,128)(2,1)S(1)}, bf16[192,128]{1,0:T(8,128)(2,1)S(1)}, u32[]{:S(2)}, u32[]{:S(2)}) collective-permute-start(bf16[192,128]{1,0:T(8,128)(2,1)S(1)} %get-tuple-element.102), channel_id=1, source_target_pairs={{0,32},{1,33},{2,6},{3,7},{4,36},{5,37},{6,2},{7,3},{8,40},{9,41},... | collective-permute-start | bytes 147464 | tf_op jit(solution)/shard_map/ppermute | solution.py:205
  12.7 2.6 %collective-permute-start.5 = (bf16[192,128]{1,0:T(8,128)(2,1)S(1)}, bf16[192,128]{1,0:T(8,128)(2,1)S(1)}, u32[]{:S(2)}, u32[]{:S(2)}) collective-permute-start(bf16[192,128]{1,0:T(8,128)(2,1)S(1)} %get-tuple-element.106), channel_id=1, source_target_pairs={{0,64},{1,65},{2,10},{3,11},{4,68},{5,69},{6,14},{7,15},{8,72},{9,... | collective-permute-start | bytes 147464 | tf_op jit(solution)/shard_map/ppermute | solution.py:205
  15.3 4.0 %shard_map.116 = (bf16[160,256]{1,0:T(8,128)(2,1)S(1)}, s32[8,1536]{1,0:T(8,128)S(1)}, f32[1,1280]{1,0:T(1,128)S(1)}, f32[1,704]{1,0:T(1,128)S(1)}, s32[1,384]{1...) custom-call(s32[6]{0:T(128)S(1)} %stack.45.at, s32[1,1024]{1,0:T(1,128)S(1)} %bitcast.135, ...), custom_call_target="tpu_custom_call" | custom-call | flops 2200000000 | tf_op jit(solution)/shard_map/pallas_call | solution.py:220
  21.7 2.7 %collective-permute-start.6 = (bf16[192,128]{1,0:T(8,128)(2,1)S(1)}, bf16[192,128]{1,0:T(8,128)(2,1)S(1)}, u32[]{:S(2)}, u32[]{:S(2)}) collective-permute-start(bf16[192,128]{1,0:T(8,128)(2,1)S(1)} %get-tuple-element.108), channel_id=1, source_target_pairs={{0,96},{1,97},{2,14},{3,15},{4,100},{5,101},{6,10},{7,11},{8,104},... | collective-permute-start | bytes 147464 | tf_op jit(solution)/shard_map/ppermute | solution.py:205
  24.4 3.7 %shard_map.118 = (bf16[208,256]{1,0:T(8,128)(2,1)S(1)}, bf16[208,256]{1,0:T(8,128)(2,1)S(1)}, bf16[208,256]{1,0:T(8,128)(2,1)S(1)}, bf16[208,256]{1,0:T(8,128)(2,1)S(1)}) custom-call(s32[6]{0:T(128)S(1)} %stack.45.at, bf16[160,256]{1,0:T(8,128)(2,1)S(1)} %get-tuple-element.109.pack_ref, bf16[32,3072]{1,0:T(8,128)(2,1)S(1)} %get-tuple-element.97.refs_0_, ...), custom_call_target="tpu_custom_call" | custom-call | flops 5500000256 | tf_op jit(solution)/shard_map/pallas_call | solution.py:220
  28.2 2.3 %collective-permute-start.16 = (bf16[208,256]{1,0:T(8,128)(2,1)S(1)}, bf16[208,256]{1,0:T(8,128)(2,1)S(1)}, u32[]{:S(2)}, u32[]{:S(2)}) collective-permute-start(bf16[208,256]{1,0:T(8,128)(2,1)S(1)} %get-tuple-element.124), channel_id=1, source_target_pairs={{0,64},{1,65},{2,10},{3,11},{4,68},{5,69},{6,14},{7,15},{8,72},{9,... | collective-permute-start | bytes 319496 | tf_op jit(solution)/shard_map/ppermute | solution.py:205
  30.5 1.5 %collective-permute-start.17 = (bf16[208,256]{1,0:T(8,128)(2,1)S(1)}, bf16[208,256]{1,0:T(8,128)(2,1)S(1)}, u32[]{:S(2)}, u32[]{:S(2)}) collective-permute-start(bf16[208,256]{1,0:T(8,128)(2,1)S(1)} %get-tuple-element.125), channel_id=1, source_target_pairs={{0,96},{1,97},{2,14},{3,15},{4,100},{5,101},{6,10},{7,11},{8,104},... | collective-permute-start | bytes 319496 | tf_op jit(solution)/shard_map/ppermute | solution.py:205
  32.0 1.1 %collective-permute-start.11 = (bf16[512,128]{1,0:T(8,128)(2,1)S(1)}, bf16[512,128]{1,0:T(8,128)(2,1)S(1)}, u32[]{:S(2)}, u32[]{:S(2)}) collective-permute-start(bf16[512,128]{1,0:T(8,128)(2,1)S(1)} %get-tuple-element.119.a), channel_id=1, source_target_pairs={{0,8},{1,9},{2,66},{3,67},{4,12},{5,13},{6,70},{7,71},{8,0},{9,1},... | collective-permute-start | bytes 393224 | tf_op jit(solution)/shard_map/ppermute | solution.py:205
  33.4 2.0 %collective-permute-start.13 = (bf16[512,128]{1,0:T(8,128)(2,1)S(1)}, bf16[512,128]{1,0:T(8,128)(2,1)S(1)}, u32[]{:S(2)}, u32[]{:S(2)}) collective-permute-start(bf16[512,128]{1,0:T(8,128)(2,1)S(1)} %get-tuple-element.119.a), channel_id=1, source_target_pairs={{0,12},{1,13},{2,98},{3,99},{4,8},{5,9},{6,102},{7,103},{8,4},{9,5... | collective-permute-start | bytes 393224 | tf_op jit(solution)/shard_map/ppermute | solution.py:205
  36.0 1.8 %collective-permute-start.19 = (bf16[656,256]{1,0:T(8,128)(2,1)S(1)}, bf16[656,256]{1,0:T(8,128)(2,1)S(1)}, u32[]{:S(2)}, u32[]{:S(2)}) collective-permute-start(bf16[656,256]{1,0:T(8,128)(2,1)S(1)} %shard_map.121.l0), channel_id=1, source_target_pairs={{0,8},{1,9},{2,66},{3,67},{4,12},{5,13},{6,70},{7,71},{8,0},{9,1},... | collective-permute-start | bytes 1007624 | tf_op jit(solution)/shard_map/ppermute | solution.py:205
  37.8 2.1 %collective-permute-start.20 = (bf16[656,256]{1,0:T(8,128)(2,1)S(1)}, bf16[656,256]{1,0:T(8,128)(2,1)S(1)}, u32[]{:S(2)}, u32[]{:S(2)}) collective-permute-start(bf16[656,256]{1,0:T(8,128)(2,1)S(1)} %shard_map.121.l0), channel_id=1, source_target_pairs={{0,12},{1,13},{2,98},{3,99},{4,8},{5,9},{6,102},{7,103},{8,4},{9,5... | collective-permute-start | bytes 1007624 | tf_op jit(solution)/shard_map/ppermute | solution.py:205
  39.9 1.1 %collective-permute-start.14 = (bf16[2048,128]{1,0:T(8,128)(2,1)S(1)}, bf16[2048,128]{1,0:T(8,128)(2,1)S(1)}, u32[]{:S(2)}, u32[]{:S(2)}) collective-permute-start(bf16[2048,128]{1,0:T(8,128)(2,1)S(1)} %shard_map.120.plane), channel_id=1, source_target_pairs={{0,16},{1,17},{2,18},{3,19},{4,20},{5,21},{6,22},{7,23},{8,24},{9,... | collective-permute-start | bytes 1572872 | tf_op jit(solution)/shard_map/ppermute | solution.py:205
  41.5 0.8 %shard_map.123 = (f32[256,1]{1,0:T(8,128)S(1)}, f32[256,256]{1,0:T(8,128)S(1)}) custom-call(bf16[2048,128]{1,0:T(8,128)(2,1)S(1)} %shard_map.120.plane, bf16[256,128]{1,0:T(8,128)(2,1)S(1)} %get-tuple-element.130.q.img_q), custom_call_target="tpu_custom_call" | custom-call | flops 1100000000 | tf_op jit(solution)/shard_map/pallas_call | solution.py:220
  42.9 3.3 %collective-permute-done.19.l2 = bf16[656,256]{1,0:T(8,128)(2,1)S(1)} collective-permute-done((bf16[656,256]{1,0:T(8,128)(2,1)S(1)}, bf16[656,256]{1,0:T(8,128)(2,1)S(1)}, u32[]{:S(2)}, u32[]{:S(2)}) %collective-permute-start.19) | collective-permute-done | bytes 335904 | tf_op jit(solution)/shard_map/ppermute | solution.py:205
  46.1 2.8 %collective-permute-done.20.l3 = bf16[656,256]{1,0:T(8,128)(2,1)S(1)} collective-permute-done((bf16[656,256]{1,0:T(8,128)(2,1)S(1)}, bf16[656,256]{1,0:T(8,128)(2,1)S(1)}, u32[]{:S(2)}, u32[]{:S(2)}) %collective-permute-start.20) | collective-permute-done | bytes 335904 | tf_op jit(solution)/shard_map/ppermute | solution.py:205
  48.9 4.2 %shard_map.124 = (bf16[1024,128]{1,0:T(8,128)(2,1)S(1)}, f32[1024,1]{1,0:T(8,128)S(1)}, f32[1024,256]{1,0:T(8,128)S(1)}, f32[256,1]{1,0:T(8,128)S(1)}, f32[256,256]{1,0:T(8,128)S(1)}) custom-call(bf16[1024,1280]{1,0:T(8,128)(2,1)S(1)} %fusion.81.pick, bf16[1024,128]{1,0:T(8,128)(2,1)S(1)} %shard_map.122.q_part, bf16[656,256]{1,0:T(8,128)(2,1)S(1)} %shard_map.121.l0, ...), custom_call_target="tpu_custom_call" | custom-call | flops 2200000000 | tf_op jit(solution)/shard_map/pallas_call | solution.py:220
  53.2 2.6 %shard_map.125 = (bf16[72,1152]{1,0:T(8,128)(2,1)S(1)}, bf16[72,1152]{1,0:T(8,128)(2,1)S(1)}, bf16[72,1152]{1,0:T(8,128)(2,1)S(1)}, bf16[72,1152]{1,0:T(8,128)(2,1)S(1)}) custom-call(bf16[2048,128]{1,0:T(8,128)(2,1)S(1)} %collective-permute-done.14.plane, bf16[1024,128]{1,0:T(8,128)(2,1)S(1)} %get-tuple-element.133.con_q, ...), custom_call_target="tpu_custom_call" | custom-call | flops 3300000000 | tf_op jit(solution)/shard_map/pallas_call | solution.py:220
  55.8 2.5 %collective-permute-start.22 = (bf16[72,1152]{1,0:T(8,128)(2,1)S(1)}, bf16[72,1152]{1,0:T(8,128)(2,1)S(1)}, u32[]{:S(2)}, u32[]{:S(2)}) collective-permute-start(bf16[72,1152]{1,0:T(8,128)(2,1)S(1)} %get-tuple-element.140), channel_id=1, source_target_pairs={{0,64},{1,65},{2,10},{3,11},{4,68},{5,69},{6,14},{7,15},{8,72},{9,... | collective-permute-start | bytes 497672 | tf_op jit(solution)/shard_map/ppermute | solution.py:205
  58.3 1.4 %collective-permute-start.23 = (bf16[72,1152]{1,0:T(8,128)(2,1)S(1)}, bf16[72,1152]{1,0:T(8,128)(2,1)S(1)}, u32[]{:S(2)}, u32[]{:S(2)}) collective-permute-start(bf16[72,1152]{1,0:T(8,128)(2,1)S(1)} %get-tuple-element.141), channel_id=1, source_target_pairs={{0,96},{1,97},{2,14},{3,15},{4,100},{5,101},{6,10},{7,11},{8,104},... | collective-permute-start | bytes 497672 | tf_op jit(solution)/shard_map/ppermute | solution.py:205
  60.0 2.9 %collective-permute-done.22.b2 = bf16[72,1152]{1,0:T(8,128)(2,1)S(1)} collective-permute-done((bf16[72,1152]{1,0:T(8,128)(2,1)S(1)}, bf16[72,1152]{1,0:T(8,128)(2,1)S(1)}, u32[]{:S(2)}, u32[]{:S(2)}) %collective-permute-start.22) | collective-permute-done | bytes 165920 | tf_op jit(solution)/shard_map/ppermute | solution.py:205
  62.9 1.7 %collective-permute-done.23.b3 = bf16[72,1152]{1,0:T(8,128)(2,1)S(1)} collective-permute-done((bf16[72,1152]{1,0:T(8,128)(2,1)S(1)}, bf16[72,1152]{1,0:T(8,128)(2,1)S(1)}, u32[]{:S(2)}, u32[]{:S(2)}) %collective-permute-start.23) | collective-permute-done | bytes 165920 | tf_op jit(solution)/shard_map/ppermute | solution.py:205
  64.6 1.3 %shard_map.126 = (bf16[40,1152]{1,0:T(8,128)(2,1)S(1)}, bf16[40,1536]{1,0:T(8,128)(2,1)S(1)}, bf16[32,384]{1,0:T(8,128)(2,1)}) custom-call(s32[6]{0:T(128)S(1)} %stack.45.at, bf16[72,1152]{1,0:T(8,128)(2,1)S(1)} %get-tuple-element.138.b0, bf16[72,1152]{1,0:T(8,128)(2,1)S(1)} %collective-permute-done.21.b1, bf16[72,1152]{1,0:T(8,128)(2,1)S(1)} %collective-permute-done.22.b2, ...), custom_call_target="tpu_custom_call" | custom-call | flops 1100000000 | tf_op jit(solution)/shard_map/pallas_call | solution.py:220
  65.9 6.8 %collective-permute-start.24 = (bf16[40,1536]{1,0:T(8,128)(2,1)S(1)}, bf16[40,1536]{1,0:T(8,128)(2,1)S(1)}, u32[]{:S(2)}, u32[]{:S(2)}) collective-permute-start(bf16[40,1536]{1,0:T(8,128)(2,1)S(1)} %get-tuple-element.143), channel_id=1, source_target_pairs={{0,2},{1,3},{2,0},{3,1},{4,6},{5,7},{6,4},{7,5},{8,10},{9,11},{10,... | collective-permute-start | bytes 368648 | tf_op jit(solution)/shard_map/ppermute | solution.py:205
  72.7 1.0 %collective-permute-done.24.core = bf16[40,1536]{1,0:T(8,128)(2,1)S(1)} collective-permute-done((bf16[40,1536]{1,0:T(8,128)(2,1)S(1)}, bf16[40,1536]{1,0:T(8,128)(2,1)S(1)}, u32[]{:S(2)}, u32[]{:S(2)}) %collective-permute-start.24) | collective-permute-done | bytes 122912 | tf_op jit(solution)/shard_map/ppermute | solution.py:205
  73.7 2.9 %collective-permute-start.25 = (bf16[40,1152]{1,0:T(8,128)(2,1)S(1)}, bf16[40,1152]{1,0:T(8,128)(2,1)S(1)}, u32[]{:S(2)}, u32[]{:S(2)}) collective-permute-start(bf16[40,1152]{1,0:T(8,128)(2,1)S(1)} %shard_map.127), channel_id=1, source_target_pairs={{0,1},{1,0},{2,3},{3,2},{4,5},{5,4},{6,7},{7,6},{8,9},{9,8},{10,11... | collective-permute-start | bytes 276488 | tf_op jit(solution)/shard_map/ppermute | solution.py:205
  76.6 2.6 %collective-permute-done.25 = bf16[40,1152]{1,0:T(8,128)(2,1)S(1)} collective-permute-done((bf16[40,1152]{1,0:T(8,128)(2,1)S(1)}, bf16[40,1152]{1,0:T(8,128)(2,1)S(1)}, u32[]{:S(2)}, u32[]{:S(2)}) %collective-permute-start.25) | collective-permute-done | bytes 92192 | tf_op jit(solution)/shard_map/ppermute | solution.py:205
  79.2 1.8 %conditional.1 = (bf16[32,768]{1,0:T(8,128)(2,1)}, f32[1024,32]{0,1:T(8,128)}) conditional(s32[]{:T(128)} %convert_element_type.70, (s32[512]{0:T(512)S(1)}, s32[1024]{0:T(1024)S(1)}, bf16[256,3072]{1,0:T(8,128)(2,1)S(1)}, s32[1]{0:T(128)}, f32[28,2,3072]{2,1,0:T(2,128)}, /*index=5*/bf16[3072,3,768]{2,0,1:T(8,128)(2,1)}, f32[2,128]{1,0:T(2,128)S(1)}, ...), branch_computations={%region_0.15_spmd, %region_15.16_spmd} | conditional | flops 1100000000 | bytes 257951312 | solution.py:810
  79.5 1.5 %branch_1_fun.1 = (bf16[32,768]{1,0:T(8,128)(2,1)}, f32[32,1024]{1,0:T(8,128)}) custom-call(s32[6]{0:T(128)S(1)} %get-tuple-element.40.at, bf16[40,1152]{1,0:T(8,128)(2,1)S(1)} %get-tuple-element.41.own, bf16[40,1152]{1,0:T(8,128)(2,1)S(1)} %get-tuple-element.42.head, bf16[40,1536]{1,0:T(8,128)(2,1)S(1)} %get-tuple-element.43.core, ...), custom_call_target="tpu_custom_call" | custom-call | flops 1100000000 | tf_op jit(solution)/shard_map/cond/branch_1_fun/pallas_call | solution.py:220
  (52 shorter events, 5.5 us)
Async XLA Ops:
  0.7 14.6 %copy-start.8 = (s32[1024]{0:T(1024)S(1)}, s32[1024]{0:T(1024)}, u32[]{:S(2)}) copy-start(s32[1024]{0:T(1024)} %param.16) | copy-start | bytes 12292
  0.7 14.6 %copy-start.9 = (s32[512]{0:T(512)S(1)}, s32[512]{0:T(512)}, u32[]{:S(2)}) copy-start(s32[512]{0:T(512)} %param.15) | copy-start | bytes 6148
  2.9 18.3 %collective-permute-start.1 = (bf16[32,3072]{1,0:T(8,128)(2,1)S(1)}, bf16[32,3072]{1,0:T(8,128)(2,1)S(1)}, u32[]{:S(2)}, u32[]{:S(2)}) collective-permute-start(bf16[32,3072]{1,0:T(8,128)(2,1)S(1)} %get-tuple-element.97.refs_0_), channel_id=1, source_target_pairs={{0,1},{1,0},{2,3},{3,2},{4,5},{5,4},{6,7},{7,6},{8,9},{9,8},{10,11... | collective-permute-start | bytes 589832 | tf_op jit(solution)/shard_map/ppermute | solution.py:205
  7.3 13.9 %collective-permute-start.4 = (bf16[32,3072]{1,0:T(8,128)(2,1)S(1)}, bf16[32,3072]{1,0:T(8,128)(2,1)S(1)}, u32[]{:S(2)}, u32[]{:S(2)}) collective-permute-start(bf16[32,3072]{1,0:T(8,128)(2,1)S(1)} %get-tuple-element.97.refs_0_), channel_id=1, source_target_pairs={{0,16},{1,17},{2,18},{3,19},{4,20},{5,21},{6,22},{7,23},{8,24},{9,... | collective-permute-start | bytes 589832 | tf_op jit(solution)/shard_map/ppermute | solution.py:205
  8.1 12.5 %collective-permute-start.7 = (bf16[32,3072]{1,0:T(8,128)(2,1)S(1)}, bf16[32,3072]{1,0:T(8,128)(2,1)S(1)}, u32[]{:S(2)}, u32[]{:S(2)}) collective-permute-start(bf16[32,3072]{1,0:T(8,128)(2,1)S(1)} %get-tuple-element.97.refs_0_), channel_id=1, source_target_pairs={{0,17},{1,16},{2,19},{3,18},{4,21},{5,20},{6,23},{7,22},{8,25},{9,... | collective-permute-start | bytes 589832 | tf_op jit(solution)/shard_map/ppermute | solution.py:205
  8.1 2.6 %collective-permute-start.2 = (bf16[48,3072]{1,0:T(8,128)(2,1)S(1)}, bf16[48,3072]{1,0:T(8,128)(2,1)S(1)}, u32[]{:S(2)}, u32[]{:S(2)}) collective-permute-start(bf16[48,3072]{1,0:T(8,128)(2,1)S(1)} %get-tuple-element.101), channel_id=1, source_target_pairs={{0,2},{1,3},{2,0},{3,1},{4,6},{5,7},{6,4},{7,5},{8,10},{9,11},{10,... | collective-permute-start | bytes 884744 | tf_op jit(solution)/shard_map/ppermute | solution.py:205
  11.3 9.8 %collective-permute-start.3 = (bf16[192,128]{1,0:T(8,128)(2,1)S(1)}, bf16[192,128]{1,0:T(8,128)(2,1)S(1)}, u32[]{:S(2)}, u32[]{:S(2)}) collective-permute-start(bf16[192,128]{1,0:T(8,128)(2,1)S(1)} %get-tuple-element.102), channel_id=1, source_target_pairs={{0,32},{1,33},{2,6},{3,7},{4,36},{5,37},{6,2},{7,3},{8,40},{9,41},... | collective-permute-start | bytes 147464 | tf_op jit(solution)/shard_map/ppermute | solution.py:205
  12.7 8.5 %collective-permute-start.5 = (bf16[192,128]{1,0:T(8,128)(2,1)S(1)}, bf16[192,128]{1,0:T(8,128)(2,1)S(1)}, u32[]{:S(2)}, u32[]{:S(2)}) collective-permute-start(bf16[192,128]{1,0:T(8,128)(2,1)S(1)} %get-tuple-element.106), channel_id=1, source_target_pairs={{0,64},{1,65},{2,10},{3,11},{4,68},{5,69},{6,14},{7,15},{8,72},{9,... | collective-permute-start | bytes 147464 | tf_op jit(solution)/shard_map/ppermute | solution.py:205
  15.3 9.1 %copy-start.10 = (f32[2,128]{1,0:T(2,128)S(1)}, f32[2,128]{1,0:T(2,128)}, u32[]{:S(2)}) copy-start(f32[2,128]{1,0:T(2,128)} %refs_9_.1) | copy-start | bytes 3076
  20.6 3.8 %collective-permute-start.10 = (bf16[32,3072]{1,0:T(8,128)(2,1)S(1)}, bf16[32,3072]{1,0:T(8,128)(2,1)S(1)}, u32[]{:S(2)}, u32[]{:S(2)}) collective-permute-start(bf16[32,3072]{1,0:T(8,128)(2,1)S(1)} %collective-permute-done.7.refs_3_), channel_id=1, source_target_pairs={{0,2},{1,3},{2,0},{3,1},{4,6},{5,7},{6,4},{7,5},{8,10},{9,11},{10,... | collective-permute-start | bytes 589832 | tf_op jit(solution)/shard_map/ppermute | solution.py:205
  21.1 3.3 %collective-permute-start.9 = (bf16[32,3072]{1,0:T(8,128)(2,1)S(1)}, bf16[32,3072]{1,0:T(8,128)(2,1)S(1)}, u32[]{:S(2)}, u32[]{:S(2)}) collective-permute-start(bf16[32,3072]{1,0:T(8,128)(2,1)S(1)} %collective-permute-done.1.refs_2_), channel_id=1, source_target_pairs={{0,2},{1,3},{2,0},{3,1},{4,6},{5,7},{6,4},{7,5},{8,10},{9,11},{10,... | collective-permute-start | bytes 589832 | tf_op jit(solution)/shard_map/ppermute | solution.py:205
  21.3 3.1 %collective-permute-start.8 = (bf16[32,3072]{1,0:T(8,128)(2,1)S(1)}, bf16[32,3072]{1,0:T(8,128)(2,1)S(1)}, u32[]{:S(2)}, u32[]{:S(2)}) collective-permute-start(bf16[32,3072]{1,0:T(8,128)(2,1)S(1)} %collective-permute-done.4.refs_1_), channel_id=1, source_target_pairs={{0,2},{1,3},{2,0},{3,1},{4,6},{5,7},{6,4},{7,5},{8,10},{9,11},{10,... | collective-permute-start | bytes 589832 | tf_op jit(solution)/shard_map/ppermute | solution.py:205
  21.7 6.5 %collective-permute-start.6 = (bf16[192,128]{1,0:T(8,128)(2,1)S(1)}, bf16[192,128]{1,0:T(8,128)(2,1)S(1)}, u32[]{:S(2)}, u32[]{:S(2)}) collective-permute-start(bf16[192,128]{1,0:T(8,128)(2,1)S(1)} %get-tuple-element.108), channel_id=1, source_target_pairs={{0,96},{1,97},{2,14},{3,15},{4,100},{5,101},{6,10},{7,11},{8,104},... | collective-permute-start | bytes 147464 | tf_op jit(solution)/shard_map/ppermute | solution.py:205
  28.1 5.3 %collective-permute-start.15 = (bf16[208,256]{1,0:T(8,128)(2,1)S(1)}, bf16[208,256]{1,0:T(8,128)(2,1)S(1)}, u32[]{:S(2)}, u32[]{:S(2)}) collective-permute-start(bf16[208,256]{1,0:T(8,128)(2,1)S(1)} %get-tuple-element.123), channel_id=1, source_target_pairs={{0,32},{1,33},{2,6},{3,7},{4,36},{5,37},{6,2},{7,3},{8,40},{9,41},... | collective-permute-start | bytes 319496 | tf_op jit(solution)/shard_map/ppermute | solution.py:205
  28.2 7.2 %collective-permute-start.16 = (bf16[208,256]{1,0:T(8,128)(2,1)S(1)}, bf16[208,256]{1,0:T(8,128)(2,1)S(1)}, u32[]{:S(2)}, u32[]{:S(2)}) collective-permute-start(bf16[208,256]{1,0:T(8,128)(2,1)S(1)} %get-tuple-element.124), channel_id=1, source_target_pairs={{0,64},{1,65},{2,10},{3,11},{4,68},{5,69},{6,14},{7,15},{8,72},{9,... | collective-permute-start | bytes 319496 | tf_op jit(solution)/shard_map/ppermute | solution.py:205
  30.5 5.1 %collective-permute-start.17 = (bf16[208,256]{1,0:T(8,128)(2,1)S(1)}, bf16[208,256]{1,0:T(8,128)(2,1)S(1)}, u32[]{:S(2)}, u32[]{:S(2)}) collective-permute-start(bf16[208,256]{1,0:T(8,128)(2,1)S(1)} %get-tuple-element.125), channel_id=1, source_target_pairs={{0,96},{1,97},{2,14},{3,15},{4,100},{5,101},{6,10},{7,11},{8,104},... | collective-permute-start | bytes 319496 | tf_op jit(solution)/shard_map/ppermute | solution.py:205
  32.0 5.8 %collective-permute-start.11 = (bf16[512,128]{1,0:T(8,128)(2,1)S(1)}, bf16[512,128]{1,0:T(8,128)(2,1)S(1)}, u32[]{:S(2)}, u32[]{:S(2)}) collective-permute-start(bf16[512,128]{1,0:T(8,128)(2,1)S(1)} %get-tuple-element.119.a), channel_id=1, source_target_pairs={{0,8},{1,9},{2,66},{3,67},{4,12},{5,13},{6,70},{7,71},{8,0},{9,1},... | collective-permute-start | bytes 393224 | tf_op jit(solution)/shard_map/ppermute | solution.py:205
  33.1 6.8 %collective-permute-start.12 = (bf16[512,128]{1,0:T(8,128)(2,1)S(1)}, bf16[512,128]{1,0:T(8,128)(2,1)S(1)}, u32[]{:S(2)}, u32[]{:S(2)}) collective-permute-start(bf16[512,128]{1,0:T(8,128)(2,1)S(1)} %get-tuple-element.119.a), channel_id=1, source_target_pairs={{0,4},{1,5},{2,34},{3,35},{4,0},{5,1},{6,38},{7,39},{8,12},{9,13},... | collective-permute-start | bytes 393224 | tf_op jit(solution)/shard_map/ppermute | solution.py:205
  33.4 6.5 %collective-permute-start.13 = (bf16[512,128]{1,0:T(8,128)(2,1)S(1)}, bf16[512,128]{1,0:T(8,128)(2,1)S(1)}, u32[]{:S(2)}, u32[]{:S(2)}) collective-permute-start(bf16[512,128]{1,0:T(8,128)(2,1)S(1)} %get-tuple-element.119.a), channel_id=1, source_target_pairs={{0,12},{1,13},{2,98},{3,99},{4,8},{5,9},{6,102},{7,103},{8,4},{9,5... | collective-permute-start | bytes 393224 | tf_op jit(solution)/shard_map/ppermute | solution.py:205
  35.9 6.4 %collective-permute-start.18 = (bf16[656,256]{1,0:T(8,128)(2,1)S(1)}, bf16[656,256]{1,0:T(8,128)(2,1)S(1)}, u32[]{:S(2)}, u32[]{:S(2)}) collective-permute-start(bf16[656,256]{1,0:T(8,128)(2,1)S(1)} %shard_map.121.l0), channel_id=1, source_target_pairs={{0,4},{1,5},{2,34},{3,35},{4,0},{5,1},{6,38},{7,39},{8,12},{9,13},... | collective-permute-start | bytes 1007624 | tf_op jit(solution)/shard_map/ppermute | solution.py:205
  36.0 10.1 %collective-permute-start.19 = (bf16[656,256]{1,0:T(8,128)(2,1)S(1)}, bf16[656,256]{1,0:T(8,128)(2,1)S(1)}, u32[]{:S(2)}, u32[]{:S(2)}) collective-permute-start(bf16[656,256]{1,0:T(8,128)(2,1)S(1)} %shard_map.121.l0), channel_id=1, source_target_pairs={{0,8},{1,9},{2,66},{3,67},{4,12},{5,13},{6,70},{7,71},{8,0},{9,1},... | collective-permute-start | bytes 1007624 | tf_op jit(solution)/shard_map/ppermute | solution.py:205
  37.8 11.1 %collective-permute-start.20 = (bf16[656,256]{1,0:T(8,128)(2,1)S(1)}, bf16[656,256]{1,0:T(8,128)(2,1)S(1)}, u32[]{:S(2)}, u32[]{:S(2)}) collective-permute-start(bf16[656,256]{1,0:T(8,128)(2,1)S(1)} %shard_map.121.l0), channel_id=1, source_target_pairs={{0,12},{1,13},{2,98},{3,99},{4,8},{5,9},{6,102},{7,103},{8,4},{9,5... | collective-permute-start | bytes 1007624 | tf_op jit(solution)/shard_map/ppermute | solution.py:205
  39.9 13.2 %collective-permute-start.14 = (bf16[2048,128]{1,0:T(8,128)(2,1)S(1)}, bf16[2048,128]{1,0:T(8,128)(2,1)S(1)}, u32[]{:S(2)}, u32[]{:S(2)}) collective-permute-start(bf16[2048,128]{1,0:T(8,128)(2,1)S(1)} %shard_map.120.plane), channel_id=1, source_target_pairs={{0,16},{1,17},{2,18},{3,19},{4,20},{5,21},{6,22},{7,23},{8,24},{9,... | collective-permute-start | bytes 1572872 | tf_op jit(solution)/shard_map/ppermute | solution.py:205
  55.8 4.2 %collective-permute-start.21 = (bf16[72,1152]{1,0:T(8,128)(2,1)S(1)}, bf16[72,1152]{1,0:T(8,128)(2,1)S(1)}, u32[]{:S(2)}, u32[]{:S(2)}) collective-permute-start(bf16[72,1152]{1,0:T(8,128)(2,1)S(1)} %get-tuple-element.139), channel_id=1, source_target_pairs={{0,32},{1,33},{2,6},{3,7},{4,36},{5,37},{6,2},{7,3},{8,40},{9,41},... | collective-permute-start | bytes 497672 | tf_op jit(solution)/shard_map/ppermute | solution.py:205
  55.8 7.1 %collective-permute-start.22 = (bf16[72,1152]{1,0:T(8,128)(2,1)S(1)}, bf16[72,1152]{1,0:T(8,128)(2,1)S(1)}, u32[]{:S(2)}, u32[]{:S(2)}) collective-permute-start(bf16[72,1152]{1,0:T(8,128)(2,1)S(1)} %get-tuple-element.140), channel_id=1, source_target_pairs={{0,64},{1,65},{2,10},{3,11},{4,68},{5,69},{6,14},{7,15},{8,72},{9,... | collective-permute-start | bytes 497672 | tf_op jit(solution)/shard_map/ppermute | solution.py:205
  58.3 6.3 %collective-permute-start.23 = (bf16[72,1152]{1,0:T(8,128)(2,1)S(1)}, bf16[72,1152]{1,0:T(8,128)(2,1)S(1)}, u32[]{:S(2)}, u32[]{:S(2)}) collective-permute-start(bf16[72,1152]{1,0:T(8,128)(2,1)S(1)} %get-tuple-element.141), channel_id=1, source_target_pairs={{0,96},{1,97},{2,14},{3,15},{4,100},{5,101},{6,10},{7,11},{8,104},... | collective-permute-start | bytes 497672 | tf_op jit(solution)/shard_map/ppermute | solution.py:205
  64.6 14.6 %copy-start = (bf16[256,3072]{1,0:T(8,128)(2,1)S(1)}, bf16[256,3072]{1,0:T(8,128)(2,1)}, u32[]{:S(2)}) copy-start(bf16[256,3072]{1,0:T(8,128)(2,1)} %table_ref.1) | copy-start | bytes 4718596
  64.6 14.6 %copy-start.3 = (bf16[32,768]{1,0:T(8,128)(2,1)S(1)}, bf16[32,768]{1,0:T(8,128)(2,1)}, u32[]{:S(2)}) copy-start(bf16[32,768]{1,0:T(8,128)(2,1)} %q_ref.1) | copy-start | bytes 147460
  64.6 14.6 %copy-start.6 = (bf16[32,768]{1,0:T(8,128)(2,1)S(1)}, bf16[32,768]{1,0:T(8,128)(2,1)}, u32[]{:S(2)}) copy-start(bf16[32,768]{1,0:T(8,128)(2,1)} %k_ref.1) | copy-start | bytes 147460
  64.6 14.6 %copy-start.7 = (bf16[32,768]{1,0:T(8,128)(2,1)S(1)}, bf16[32,768]{1,0:T(8,128)(2,1)}, u32[]{:S(2)}) copy-start(bf16[32,768]{1,0:T(8,128)(2,1)} %v_ref.1) | copy-start | bytes 147460
  65.9 7.8 %collective-permute-start.24 = (bf16[40,1536]{1,0:T(8,128)(2,1)S(1)}, bf16[40,1536]{1,0:T(8,128)(2,1)S(1)}, u32[]{:S(2)}, u32[]{:S(2)}) collective-permute-start(bf16[40,1536]{1,0:T(8,128)(2,1)S(1)} %get-tuple-element.143), channel_id=1, source_target_pairs={{0,2},{1,3},{2,0},{3,1},{4,6},{5,7},{6,4},{7,5},{8,10},{9,11},{10,... | collective-permute-start | bytes 368648 | tf_op jit(solution)/shard_map/ppermute | solution.py:205
  73.7 5.5 %collective-permute-start.25 = (bf16[40,1152]{1,0:T(8,128)(2,1)S(1)}, bf16[40,1152]{1,0:T(8,128)(2,1)S(1)}, u32[]{:S(2)}, u32[]{:S(2)}) collective-permute-start(bf16[40,1152]{1,0:T(8,128)(2,1)S(1)} %shard_map.127), channel_id=1, source_target_pairs={{0,1},{1,0},{2,3},{3,2},{4,5},{5,4},{6,7},{7,6},{8,9},{9,8},{10,11... | collective-permute-start | bytes 276488 | tf_op jit(solution)/shard_map/ppermute | solution.py:205

commit v5 on v4

--- a/solution.py
+++ b/solution.py
@@ -182,15 +182,11 @@
 
 
 def swap_u(s):
-    return pairs(
-        lambda x, zl, y, c, g: (x, zl, y ^ s, c, g) if c else (x ^ s, zl, y, c, g)
-    )
+    return pairs(lambda x, zl, y, c, g: (x ^ s, zl, y, c, g))
 
 
 def swap_v(s):
-    return pairs(
-        lambda x, zl, y, c, g: (x ^ s, zl, y, c, g) if c else (x, zl, y ^ s, c, g)
-    )
+    return pairs(lambda x, zl, y, c, g: (x, zl, y ^ s, c, g))
 
 
 def swap_plane():
@@ -313,21 +309,15 @@
     return jnp.sum(jnp.where(diagonal, column, 0.0), axis=0, keepdims=True)
 
 
-def line_of(at, column):
-    first, second = column >> 2, column & 3
-    return jnp.where(at[2] == 0, first, second), jnp.where(at[2] == 0, second, first)
-
-
 def line_plan(at, counts):
-    u, v = line_of(at, lax.broadcasted_iota(jnp.int32, (16, 16), 0))
-    u2, v2 = line_of(at, lax.broadcasted_iota(jnp.int32, (16, 16), 1))
+    column = lax.broadcasted_iota(jnp.int32, (16, 16), 0)
+    other = lax.broadcasted_iota(jnp.int32, (16, 16), 1)
     row = to_row(counts)
-    same = v == v2
-    before = same & ((u2 ^ at[4]) < (u ^ at[4]))
+    same = (column & 3) == (other & 3)
+    before = same & (((other >> 2) ^ at[4]) < ((column >> 2) ^ at[4]))
     skipped = jnp.sum(jnp.where(before, row, 0.0), axis=1, keepdims=True)
     total = jnp.sum(jnp.where(same, row, 0.0), axis=1, keepdims=True)
-    other = jnp.sum(jnp.where(u == u2, row, 0.0), axis=1, keepdims=True)
-    return skipped, total, jnp.max(jnp.maximum(total, other), axis=0, keepdims=True)
+    return skipped, total, jnp.max(total, axis=0, keepdims=True)
 
 
 def per_lane(values, column):
@@ -343,20 +333,16 @@
     return block, (lane - block * size).astype(F32)
 
 
-def column_at(at, u, v):
-    return jnp.where(at[2] == 0, u * 4 + v, v * 4 + u)
-
-
 def line_targets(at, counts, skipped, slots):
     block, slot = blocks_of(4 * slots, slots, 4)
-    column = column_at(at, block ^ at[4], jnp.zeros_like(block) + at[5])
+    column = ((block ^ at[4]) << 2) | at[5]
     target = per_lane(skipped, column) + slot
     return jnp.where(slot < per_lane(counts, column), target, -1.0).astype(jnp.int32)
 
 
 def line_bias(at, total, rows):
     block, slot = blocks_of(4 * rows, rows, 4)
-    column = column_at(at, jnp.zeros_like(block) + at[4], block ^ at[5])
+    column = (at[4] << 2) | (block ^ at[5])
     return jnp.where(slot < per_lane(total, column), 0.0, -1e30)
 
 
@@ -365,7 +351,7 @@
 ):
     half = w_ref.shape[2]
     lanes = pl.ds(pl.multiple_of(at[2] * half, half), half)
-    weights = pltpu.make_async_copy(w_hbm.at[:, :, lanes], w_ref, sem)
+    weights = pltpu.make_async_copy(w_hbm.at[0:2, :, lanes], w_ref, sem)
     weights.start()
     ids = jnp.concatenate([con_ref[...], txt_ref[...]], axis=1)
     n = ids.shape[1]
@@ -384,9 +370,8 @@
     txt_bias[...] = line_bias(at, txt_total, LINE_TXT)
     con_line[...] = line_targets(at, con_counts, con_skip, CON)
     txt_line[...] = line_targets(at, txt_counts, txt_skip, TXT)
-    _, item_v = line_of(at, column)
     spot_ref[0:1, :] = (
-        (item_v ^ at[5]) * LINE_CON + per_lane(con_skip, column).astype(jnp.int32) + spot
+        ((column & 3) ^ at[5]) * LINE_CON + per_lane(con_skip, column).astype(jnp.int32) + spot
     )
     wanted = (lax.broadcasted_iota(jnp.int32, (128, n), 0) == owner).astype(F32)
     over = jnp.maximum(
@@ -413,9 +398,13 @@
 
 
 def project_kernel(at, pack_ref, *refs):
-    rows, (mod_ref, gain_ref, w_ref), outs, (raw_ref, x_ref) = (
-        refs[:8], refs[8:11], refs[11:15], refs[15:]
-    )
+    rows, (mod_ref, gain_ref, w_ref, w_hbm), outs, (raw_ref, x_ref, w_last, sem) = (
+        refs[:8], refs[8:12], refs[12:16], refs[16:]
+    )
+    half = w_ref.shape[2]
+    lanes = pl.ds(pl.multiple_of(at[2] * half, half), half)
+    weights = pltpu.make_async_copy(w_hbm.at[2, :, lanes], w_last, sem)
+    weights.start()
     for i, ref in enumerate(rows):
         raw_ref[i * SLOTS : (i + 1) * SLOTS, :] = ref[0:SLOTS, :]
     shift = mod_ref[0:1, :]
@@ -434,7 +423,8 @@
 
     q = nn(x_ref[0:CON, :], w_ref[0])
     k = nn(x_ref[...], w_ref[1])
-    v = nn(x_ref[...], w_ref[2])
+    weights.wait()
+    v = nn(x_ref[...], w_last[...])
     heads = []
     for h in range(3):
         cols = slice(h * HD, (h + 1) * HD)
@@ -601,7 +591,7 @@
 
 
 def far_kernel(plane, con_q, img_q, cm, cs, im, ims, *refs):
-    outs, (con_out, img_v) = refs[:4], refs[4:]
+    outs, (con_out, img_v) = refs[:2], refs[2:]
     n_img = plane.shape[0] // 2
     img_v[...] = with_ones(plane[n_img:, :])
     part = (plane[0:n_img, :], img_v[...], None)
@@ -614,59 +604,63 @@
     weigh_blocks(con_q, ((plane.at[0:n_img, :], img_v, None),), store)
     dots = nt(img, con_out[...]).astype(BF)
     con_f = con_out[...].astype(F32)
-    con_sq = nt(jnp.ones((8, HD), F32), con_f * con_f, precision=lax.Precision.HIGHEST).astype(BF)
+    squares = con_f * con_f
+    high = squares.astype(BF)
+    ones = jnp.ones((8, HD), BF)
+    con_sq = (nt(ones, high) + nt(ones, (squares - high.astype(F32)).astype(BF))).astype(BF)
+    for j, out in enumerate(outs):
+        for s in range(4):
+            rows = slice(s * 64 + j * 32, s * 64 + (j + 1) * 32)
+            out[s * 32 : (s + 1) * 32, 0:n_con] = dots[rows]
+            out[s * 32 : (s + 1) * 32, n_con:] = img[rows]
+        out[128:136, 0:n_con] = con_sq
+        out[128:136, n_con:] = jnp.zeros((8, HD), BF)
+
+
+def core_sum_kernel(at, own, core, *outs):
+    n_con = own.shape[1] - HD
+    con_sq = (own[128:136, 0:n_con].astype(F32) + core[128:136, 0:n_con].astype(F32)).astype(BF)
+    mine = pl.ds(pl.multiple_of(n_con + at[2] * HD, HD), HD)
+    theirs = pl.ds(pl.multiple_of(n_con + (1 - at[2]) * HD, HD), HD)
     for s, out in enumerate(outs):
-        rows = slice(s * 64, (s + 1) * 64)
-        out[0:64, 0:n_con] = dots[rows]
-        out[0:64, n_con:] = img[rows]
-        out[64:72, 0:n_con] = con_sq
-        out[64:72, n_con:] = jnp.zeros((8, HD), BF)
-
-
-def head_sum_kernel(at, b0, b1, b2, b3, own, core, out_own):
-    n_con = b0.shape[1] - HD
-    total = jnp.zeros((72, n_con), F32)
-    outs = [jnp.zeros((64, HD), BF) for _ in range(3)]
+        rows = slice(s * 32, (s + 1) * 32)
+        out[0:32, 0:n_con] = (
+            own[rows, 0:n_con].astype(F32) + core[rows, 0:n_con].astype(F32)
+        ).astype(BF)
+        out[0:32, mine] = own[rows, n_con:]
+        out[0:32, theirs] = core[rows, n_con:]
+        out[32:40, 0:n_con] = con_sq
+        out[32:40, n_con:] = jnp.zeros((8, 2 * HD), BF)
+
+
+def head_sum_kernel(at, b0, b1, b2, b3, sums, img):
+    n_con = b0.shape[1] - 2 * HD
+    total = jnp.zeros((40, n_con), F32)
+    outs = [jnp.zeros((32, HD), BF) for _ in range(6)]
     for s, ref in enumerate((b0, b1, b2, b3)):
         head = at[4] ^ s
         total = total + jnp.where(head < 3, ref[:, 0:n_con].astype(F32), 0.0)
-        for h in range(3):
-            outs[h] = jnp.where(head == h, ref[0:64, n_con:], outs[h])
-    image_sq = jnp.zeros((64, 1), F32)
-    for h in range(3):
+        for h in range(6):
+            lanes = slice(n_con + (h // 3) * HD, n_con + (h // 3 + 1) * HD)
+            outs[h] = jnp.where(head == h % 3, ref[0:32, lanes], outs[h])
+    image_sq = jnp.zeros((32, 1), F32)
+    for h in range(6):
         out_f = outs[h].astype(F32)
         image_sq = image_sq + jnp.sum(out_f * out_f, axis=1, keepdims=True)
-    image_sq = jnp.broadcast_to(image_sq, (64, HD)).astype(BF)
-    total = total.astype(BF)
-    for ref, row in ((own, 0), (core, 32)):
-        ref[0:32, 0:n_con] = total[row : row + 32]
-        ref[32:40, 0:n_con] = total[64:72]
-        ref[0:32, n_con : n_con + HD] = image_sq[row : row + 32]
-        ref[32:40, n_con : n_con + HD] = jnp.zeros((8, HD), BF)
-    for h in range(3):
-        lanes = slice(n_con + (1 + h) * HD, n_con + (2 + h) * HD)
-        core[0:32, lanes] = outs[h][32:64]
-        core[32:40, lanes] = jnp.zeros((8, HD), BF)
-        out_own[:, h * HD : (h + 1) * HD] = outs[h][0:32]
-
-
-def core_sum_kernel(own, core, out):
-    cols = own.shape[1]
-    out[...] = (own[...].astype(F32) + core[:, 0:cols].astype(F32)).astype(BF)
-
-
-def finish_kernel(at, own, head, core, out_own, img_ref, sal_ref):
+        img[:, h * HD : (h + 1) * HD] = outs[h]
+    sums[:, 0:n_con] = total.astype(BF)
+    sums[0:32, n_con:] = jnp.broadcast_to(image_sq, (32, HD)).astype(BF)
+    sums[32:40, n_con:] = jnp.zeros((8, HD), BF)
+
+
+def finish_kernel(own, head, img, img_ref, sal_ref):
     n_con = own.shape[1] - HD
     width = 12 * HD
     total = own[...].astype(F32) + head[...].astype(F32)
     con_rms = jnp.sqrt(total[32:33, 0:n_con] / width + 1e-06)
     img_rms = jnp.sqrt(total[0:32, n_con : n_con + 1] / width + 1e-06)
     sal_ref[...] = total[0:32, 0:n_con] / (math.sqrt(width) * con_rms * img_rms)
-    half = 3 * HD
-    mine = pl.ds(pl.multiple_of(at[2] * half, half), half)
-    theirs = pl.ds(pl.multiple_of((1 - at[2]) * half, half), half)
-    img_ref[:, mine] = out_own[...]
-    img_ref[:, theirs] = core[0:32, n_con + HD :]
+    img_ref[...] = img[...]
 
 
 def packed(
@@ -679,9 +673,7 @@
     y = (ctx >> 1) & 3
     zl = (ctx >> 3) & 1
     x = ctx >> 4
-    u = jnp.where(c == 0, x, y)
-    v = jnp.where(c == 0, y, x)
-    at = jnp.stack([ctx * 2 + g, x * 4 + y, c, 2 * g + zl, u, v]).astype(jnp.int32)
+    at = jnp.stack([ctx * 2 + g, x * 4 + y, c, 2 * g + zl, x, y]).astype(jnp.int32)
     con_ids, text_ids = concept_ids[None, :], txt_ids[None, :]
     n = n_con + n_txt
     width = token_table.shape[1]
@@ -695,6 +687,7 @@
     column_rows = [own_rows] + [send(own_rows, swap_z(s)) for s in (1, 3)]
     core_both = send(own_both, swap_core())
 
+    all_weights = jnp.transpose(txt_qkv, (1, 0, 2))
     pack, spots, con_bias, txt_bias, con_line, txt_line, weights = call(
         pack_kernel,
         (
@@ -704,15 +697,14 @@
             sds((1, 4 * LINE_TXT), F32),
             sds((1, 4 * CON), jnp.int32),
             sds((1, 4 * TXT), jnp.int32),
-            sds((3, width, half)),
+            sds((2, width, half)),
         ),
         scratch=(pltpu.SemaphoreType.DMA,),
         limit=24,
         us=2.0,
         in_hbm=1,
-    )(at, con_ids, text_ids, jnp.transpose(txt_qkv, (1, 0, 2)))
+    )(at, con_ids, text_ids, all_weights)
     shift_scale = lax.dynamic_index_in_dim(modulation, step_index[0], 0, keepdims=False)
-    fits = (spots[1, 0] <= 0).astype(jnp.int32)
 
     image_blocks = call(
         image_heads_kernel, tuple(sds((6 * n_img, HD)) for _ in range(4))
@@ -720,8 +712,8 @@
     image_blocks = [image_blocks[0]] + [send(image_blocks[s], swap_u(s)) for s in (2, 1, 3)]
     image_blocks = [image_blocks[0], image_blocks[2], image_blocks[1], image_blocks[3]]
     column_rows[1], image_blocks[2] = lax.optimization_barrier((column_rows[1], image_blocks[2]))
-    far_rows, pack, shift_scale, fits, image_blocks[1] = lax.optimization_barrier(
-        (far_rows, pack, shift_scale, fits, image_blocks[1])
+    far_rows, pack, shift_scale, image_blocks[1] = lax.optimization_barrier(
+        (far_rows, pack, shift_scale, image_blocks[1])
     )
     column_rows.insert(2, far_rows)
     other_rows = [core_both] + [send(r, swap_core()) for r in column_rows[1:]]
@@ -732,10 +724,13 @@
         scratch=(
             pltpu.VMEM((8 * SLOTS, width), BF),
             pltpu.VMEM((ROWS, width), BF),
+            pltpu.VMEM((width, half), BF),
+            pltpu.SemaphoreType.DMA,
         ),
         limit=24,
         us=PROJ_US,
-    )(at, pack, *column_rows, *other_rows, shift_scale, qk_gain, weights)
+        in_hbm=1,
+    )(at, pack, *column_rows, *other_rows, shift_scale, qk_gain, weights, all_weights)
 
     *image_blocks, first = lax.optimization_barrier((*image_blocks, qkv[0]))
     image_q, image_kv = call(
@@ -754,7 +749,7 @@
     lines = [line] + [send(line, swap_v(s)) for s in (2, 1, 3)]
     lines = [lines[0], lines[2], lines[1], lines[3]]
     plane = call(plane_kernel, sds((64 * n_img, HD)), smem=0)(*image_kvs)
-    con_slot, plane = lax.optimization_barrier((spots[0, :n_con], plane))
+    con_slot, over, plane = lax.optimization_barrier((spots[0, :n_con], spots[1, 0], plane))
     other_plane = send(plane, swap_plane())
     pick = (con_slot[:, None] == jnp.arange(4 * LINE_CON)[None, :]).astype(BF)
 
@@ -779,30 +774,27 @@
         us=NEAR_US,
         smem=0,
     )(pick, q_part, *lines, con_bias, txt_bias, plane, image_q, *image_near)
-    blocks = call(
+    own, core = call(
         far_kernel,
-        tuple(sds((72, n_con + HD)) for _ in range(4)),
+        tuple(sds((136, n_con + HD)) for _ in range(2)),
         scratch=(pltpu.VMEM((n_con, HD), BF), pltpu.VMEM((32 * n_img, 2 * HD), BF)),
         limit=24,
         us=FAR_US,
         smem=0,
     )(other_plane, con_q, image_q, *near)
-    blocks = [blocks[0]] + [send(blocks[s], swap_u(s)) for s in (2, 1, 3)]
-    blocks = [blocks[0], blocks[2], blocks[1], blocks[3]]
-    own, core, out_own = call(
-        head_sum_kernel,
-        (sds((40, n_con + HD)), sds((40, n_con + 4 * HD)), sds((32, half))),
-    )(at, *blocks)
-    core = send(core, swap_core())
-    own = call(core_sum_kernel, sds((40, n_con + HD)), smem=0)(own, core)
-    last = (at, own, send(own, swap_z(2)), core, out_own)
-    finish = call(finish_kernel, (sds((n_img, 2 * half)), sds((n_img, n_con), F32)))
+    blocks = call(core_sum_kernel, tuple(sds((40, n_con + 2 * HD)) for _ in range(4)))(
+        at, own, send(core, swap_core())
+    )
+    blocks = [blocks[0]] + [send(blocks[s], swap_u(s)) for s in (1, 2, 3)]
+    sums, img = call(head_sum_kernel, (sds((40, n_con + HD)), sds((n_img, 2 * half))))(at, *blocks)
+    last = (sums, send(sums, swap_z(2)), img)
+    finish = call(finish_kernel, (sds((n_img, 2 * half)), sds((n_img, n_con), F32)), smem=0)
 
     def finished():
         img_out, saliency = finish(*last)
         return img_out, jnp.transpose(saliency)
 
-    return fits > 0, finished
+    return over <= 0, finished
 
 
 def on_device(*args):

time: 81.3 us -> 85.7 us (1.054)
  waiting for transfers between devices: 14.8 us -> 24.5 us
  starting transfers between devices: 40.1 us -> 33.8 us
    ppermute x25, waiting for transfers between devices: 14.8 us -> 24.5 us  [send(): return lax.ppermute(array, ('ctx', 'head'), pairing)]
    ppermute x25, starting transfers between devices: 40.1 us -> 33.8 us  [send(): return lax.ppermute(array, ('ctx', 'head'), pairing)]
  transfers between devices with their start and end apart: 25 -> 25, of which waited for: 8 -> 12; matrix products, arithmetic and copies ran while one was open for 2% -> 2% of each run, Pallas kernels for 18% -> 17%
where the time goes in v5:
time: 85.7 us; the launch traced here: 85 us
  starting transfers between devices  33.8 us (39%)
  waiting for transfers between devices  24.5 us (29%)
  Pallas kernels  22.5 us (26%)
  between operations  2.12 us (2%)
  local copies, waits for them, and re-layouts  1.45 us (2%)
    ppermute x25, starting transfers between devices, send(): return lax.ppermute(array, ('ctx', 'head'), pairing)  33.8 us
    ppermute x25, waiting for transfers between devices, send(): return lax.ppermute(array, ('ctx', 'head'), pairing)  24.5 us
    pallas_call x14, Pallas kernels, run(): pl.pallas_call(kernel, out_shape=outs, in_specs=[sm] * smem + [vm] * (len...  22.5 us
  transfers between devices with their start and end apart: 25, of which 12 were waited for; matrix products, arithmetic and copies ran while one was open for 2% of the time, Pallas kernels for 17%

profile of v5, /device:TPU:1, one launch (start us, length us, event | category | flops | bytes accessed | tf_op | source)
XLA Modules:
  0.0 85.0 jit_solution(11709874290254880956)
XLA Ops:
  0.7 2.1 %shard_map.116 = (bf16[32,3072]{1,0:T(8,128)(2,1)S(1)}, bf16[48,3072]{1,0:T(8,128)(2,1)S(1)}, bf16[96,384]{1,0:T(8,128)(2,1)S(1)}) custom-call(s32[6]{0:T(128)S(1)} %stack.45.at, s32[1,1024]{1,0:T(1,128)} %bitcast.135, s32[1,512]{1,0:T(1,128)} %bitcast.139, bf16[256,3072]{1,0:T(8,128)(2,1)} %table_ref.1, bf16[32,768]{1,0:T(8,128)(2,1)} %q_ref.1, ...), custom_call_target="tpu_custom_call" | custom-call | flops 1100000000 | tf_op jit(solution)/shard_map/pallas_call | solution.py:216
  2.8 4.5 %collective-permute-start.2 = (bf16[32,3072]{1,0:T(8,128)(2,1)S(1)}, bf16[32,3072]{1,0:T(8,128)(2,1)S(1)}, u32[]{:S(2)}, u32[]{:S(2)}) collective-permute-start(bf16[32,3072]{1,0:T(8,128)(2,1)S(1)} %get-tuple-element.96.refs_0_), channel_id=1, source_target_pairs={{0,1},{1,0},{2,3},{3,2},{4,5},{5,4},{6,7},{7,6},{8,9},{9,8},{10,11... | collective-permute-start | bytes 589832 | tf_op jit(solution)/shard_map/ppermute | solution.py:201
  8.1 1.2 %collective-permute-start.1 = (bf16[48,3072]{1,0:T(8,128)(2,1)S(1)}, bf16[48,3072]{1,0:T(8,128)(2,1)S(1)}, u32[]{:S(2)}, u32[]{:S(2)}) collective-permute-start(bf16[48,3072]{1,0:T(8,128)(2,1)S(1)} %get-tuple-element.94), channel_id=1, source_target_pairs={{0,2},{1,3},{2,0},{3,1},{4,6},{5,7},{6,4},{7,5},{8,10},{9,11},{10,... | collective-permute-start | bytes 884744 | tf_op jit(solution)/shard_map/ppermute | solution.py:201
  11.3 1.3 %collective-permute-start.3 = (bf16[192,128]{1,0:T(8,128)(2,1)S(1)}, bf16[192,128]{1,0:T(8,128)(2,1)S(1)}, u32[]{:S(2)}, u32[]{:S(2)}) collective-permute-start(bf16[192,128]{1,0:T(8,128)(2,1)S(1)} %get-tuple-element.98), channel_id=1, source_target_pairs={{0,32},{1,33},{2,34},{3,35},{4,36},{5,37},{6,38},{7,39},{8,40},{9,... | collective-permute-start | bytes 147464 | tf_op jit(solution)/shard_map/ppermute | solution.py:201
  12.6 2.5 %collective-permute-start.5 = (bf16[192,128]{1,0:T(8,128)(2,1)S(1)}, bf16[192,128]{1,0:T(8,128)(2,1)S(1)}, u32[]{:S(2)}, u32[]{:S(2)}) collective-permute-start(bf16[192,128]{1,0:T(8,128)(2,1)S(1)} %get-tuple-element.100), channel_id=1, source_target_pairs={{0,64},{1,65},{2,66},{3,67},{4,68},{5,69},{6,70},{7,71},{8,72},{9,... | collective-permute-start | bytes 147464 | tf_op jit(solution)/shard_map/ppermute | solution.py:201
  15.1 3.8 %shard_map.115 = (bf16[160,256]{1,0:T(8,128)(2,1)S(1)}, s32[8,1536]{1,0:T(8,128)S(1)}, f32[1,1280]{1,0:T(1,128)S(1)}, f32[1,704]{1,0:T(1,128)S(1)}, s32[1,384]{1...) custom-call(s32[6]{0:T(128)S(1)} %stack.45.at, s32[1,1024]{1,0:T(1,128)S(1)} %bitcast.136, ...), custom_call_target="tpu_custom_call" | custom-call | flops 2200000000 | tf_op jit(solution)/shard_map/pallas_call | solution.py:216
  18.9 0.8 collective-permute-start.10
  21.5 4.1 %shard_map.118 = (bf16[208,256]{1,0:T(8,128)(2,1)S(1)}, bf16[208,256]{1,0:T(8,128)(2,1)S(1)}, bf16[208,256]{1,0:T(8,128)(2,1)S(1)}, bf16[208,256]{1,0:T(8,128)(2,1)S(1)}) custom-call(s32[6]{0:T(128)S(1)} %stack.45.at, bf16[160,256]{1,0:T(8,128)(2,1)S(1)} %get-tuple-element.103.pack_ref, bf16[32,3072]{1,0:T(8,128)(2,1)S(1)} %get-tuple-element.96.refs_0_, ...), custom_call_target="tpu_custom_call" | custom-call | flops 5500000256 | tf_op jit(solution)/shard_map/pallas_call | solution.py:216
  25.7 2.6 %collective-permute-start.16 = (bf16[208,256]{1,0:T(8,128)(2,1)S(1)}, bf16[208,256]{1,0:T(8,128)(2,1)S(1)}, u32[]{:S(2)}, u32[]{:S(2)}) collective-permute-start(bf16[208,256]{1,0:T(8,128)(2,1)S(1)} %get-tuple-element.119), channel_id=1, source_target_pairs={{0,64},{1,65},{2,66},{3,67},{4,68},{5,69},{6,70},{7,71},{8,72},{9,... | collective-permute-start | bytes 319496 | tf_op jit(solution)/shard_map/ppermute | solution.py:201
  28.3 1.3 %collective-permute-start.17 = (bf16[208,256]{1,0:T(8,128)(2,1)S(1)}, bf16[208,256]{1,0:T(8,128)(2,1)S(1)}, u32[]{:S(2)}, u32[]{:S(2)}) collective-permute-start(bf16[208,256]{1,0:T(8,128)(2,1)S(1)} %get-tuple-element.120), channel_id=1, source_target_pairs={{0,96},{1,97},{2,98},{3,99},{4,100},{5,101},{6,102},{7,103},{8,104... | collective-permute-start | bytes 319496 | tf_op jit(solution)/shard_map/ppermute | solution.py:201
  29.6 3.0 %collective-permute-start.11 = (bf16[512,128]{1,0:T(8,128)(2,1)S(1)}, bf16[512,128]{1,0:T(8,128)(2,1)S(1)}, u32[]{:S(2)}, u32[]{:S(2)}) collective-permute-start(bf16[512,128]{1,0:T(8,128)(2,1)S(1)} %get-tuple-element.113.a), channel_id=1, source_target_pairs={{0,8},{1,9},{2,10},{3,11},{4,12},{5,13},{6,14},{7,15},{8,0},{9,1},... | collective-permute-start | bytes 393224 | tf_op jit(solution)/shard_map/ppermute | solution.py:201
  33.9 1.9 %collective-permute-done.17.d = bf16[208,256]{1,0:T(8,128)(2,1)S(1)} collective-permute-done((bf16[208,256]{1,0:T(8,128)(2,1)S(1)}, bf16[208,256]{1,0:T(8,128)(2,1)S(1)}, u32[]{:S(2)}, u32[]{:S(2)}) %collective-permute-start.17) | collective-permute-done | bytes 106528 | tf_op jit(solution)/shard_map/ppermute | solution.py:201
  36.2 1.4 %collective-permute-start.18 = (bf16[656,256]{1,0:T(8,128)(2,1)S(1)}, bf16[656,256]{1,0:T(8,128)(2,1)S(1)}, u32[]{:S(2)}, u32[]{:S(2)}) collective-permute-start(bf16[656,256]{1,0:T(8,128)(2,1)S(1)} %shard_map.121.l0), channel_id=1, source_target_pairs={{0,4},{1,5},{2,6},{3,7},{4,0},{5,1},{6,2},{7,3},{8,12},{9,13},{10,... | collective-permute-start | bytes 1007624 | tf_op jit(solution)/shard_map/ppermute | solution.py:201
  37.6 2.6 %collective-permute-start.19 = (bf16[656,256]{1,0:T(8,128)(2,1)S(1)}, bf16[656,256]{1,0:T(8,128)(2,1)S(1)}, u32[]{:S(2)}, u32[]{:S(2)}) collective-permute-start(bf16[656,256]{1,0:T(8,128)(2,1)S(1)} %shard_map.121.l0), channel_id=1, source_target_pairs={{0,8},{1,9},{2,10},{3,11},{4,12},{5,13},{6,14},{7,15},{8,0},{9,1},... | collective-permute-start | bytes 1007624 | tf_op jit(solution)/shard_map/ppermute | solution.py:201
  40.2 1.1 %collective-permute-start.14 = (bf16[2048,128]{1,0:T(8,128)(2,1)S(1)}, bf16[2048,128]{1,0:T(8,128)(2,1)S(1)}, u32[]{:S(2)}, u32[]{:S(2)}) collective-permute-start(bf16[2048,128]{1,0:T(8,128)(2,1)S(1)} %shard_map.120.plane), channel_id=1, source_target_pairs={{0,16},{1,17},{2,18},{3,19},{4,20},{5,21},{6,22},{7,23},{8,24},{9,... | collective-permute-start | bytes 1572872 | tf_op jit(solution)/shard_map/ppermute | solution.py:201
  41.8 0.8 shard_map.123
  42.7 3.6 %collective-permute-done.18.l1 = bf16[656,256]{1,0:T(8,128)(2,1)S(1)} collective-permute-done((bf16[656,256]{1,0:T(8,128)(2,1)S(1)}, bf16[656,256]{1,0:T(8,128)(2,1)S(1)}, u32[]{:S(2)}, u32[]{:S(2)}) %collective-permute-start.18) | collective-permute-done | bytes 335904 | tf_op jit(solution)/shard_map/ppermute | solution.py:201
  46.7 7.9 %collective-permute-done.19.l2 = bf16[656,256]{1,0:T(8,128)(2,1)S(1)} collective-permute-done((bf16[656,256]{1,0:T(8,128)(2,1)S(1)}, bf16[656,256]{1,0:T(8,128)(2,1)S(1)}, u32[]{:S(2)}, u32[]{:S(2)}) %collective-permute-start.19) | collective-permute-done | bytes 335904 | tf_op jit(solution)/shard_map/ppermute | solution.py:201
  54.6 2.0 %collective-permute-done.20.l3 = bf16[656,256]{1,0:T(8,128)(2,1)S(1)} collective-permute-done((bf16[656,256]{1,0:T(8,128)(2,1)S(1)}, bf16[656,256]{1,0:T(8,128)(2,1)S(1)}, u32[]{:S(2)}, u32[]{:S(2)}) %collective-permute-start.20) | collective-permute-done | bytes 335904 | tf_op jit(solution)/shard_map/ppermute | solution.py:201
  56.7 4.2 %shard_map.124 = (bf16[1024,128]{1,0:T(8,128)(2,1)S(1)}, f32[1024,1]{1,0:T(8,128)S(1)}, f32[1024,256]{1,0:T(8,128)S(1)}, f32[256,1]{1,0:T(8,128)S(1)}, f32[256,256]{1,0:T(8,128)S(1)}) custom-call(bf16[1024,1280]{1,0:T(8,128)(2,1)S(1)} %fusion.81.pick, bf16[1024,128]{1,0:T(8,128)(2,1)S(1)} %shard_map.122.q_part, bf16[656,256]{1,0:T(8,128)(2,1)S(1)} %shard_map.121.l0, ...), custom_call_target="tpu_custom_call" | custom-call | flops 2200000000 | tf_op jit(solution)/shard_map/pallas_call | solution.py:216
  60.9 2.5 %shard_map.125 = (bf16[136,1152]{1,0:T(8,128)(2,1)S(1)}, bf16[136,1152]{1,0:T(8,128)(2,1)S(1)}) custom-call(bf16[2048,128]{1,0:T(8,128)(2,1)S(1)} %collective-permute-done.14.plane, bf16[1024,128]{1,0:T(8,128)(2,1)S(1)} %get-tuple-element.128.con_q, bf16[256,128]{1,0:T(8,128)(2,1)S(1)} %get-tuple-element.125.q.img_q, f32[1024,1]{1,0:T(8,128)S(1)} %get-tuple-element.129.cm, ...), custom_call_target="tpu_custom_call" | custom-call | flops 3300000000 | tf_op jit(solution)/shard_map/pallas_call | solution.py:216
  63.4 2.3 %collective-permute-start.21 = (bf16[136,1152]{1,0:T(8,128)(2,1)S(1)}, bf16[136,1152]{1,0:T(8,128)(2,1)S(1)}, u32[]{:S(2)}, u32[]{:S(2)}) collective-permute-start(bf16[136,1152]{1,0:T(8,128)(2,1)S(1)} %get-tuple-element.134), channel_id=1, source_target_pairs={{0,2},{1,3},{2,0},{3,1},{4,6},{5,7},{6,4},{7,5},{8,10},{9,11},{10,... | collective-permute-start | bytes 940040 | tf_op jit(solution)/shard_map/ppermute | solution.py:201
  65.7 1.2 %collective-permute-done.21.core = bf16[136,1152]{1,0:T(8,128)(2,1)S(1)} collective-permute-done((bf16[136,1152]{1,0:T(8,128)(2,1)S(1)}, bf16[136,1152]{1,0:T(8,128)(2,1)S(1)}, u32[]{:S(2)}, u32[]{:S(2)}) %collective-permute-start.21) | collective-permute-done | bytes 313376 | tf_op jit(solution)/shard_map/ppermute | solution.py:201
  67.6 2.0 %collective-permute-start.23 = (bf16[40,1280]{1,0:T(8,128)(2,1)S(1)}, bf16[40,1280]{1,0:T(8,128)(2,1)S(1)}, u32[]{:S(2)}, u32[]{:S(2)}) collective-permute-start(bf16[40,1280]{1,0:T(8,128)(2,1)S(1)} %get-tuple-element.137), channel_id=1, source_target_pairs={{0,64},{1,65},{2,66},{3,67},{4,68},{5,69},{6,70},{7,71},{8,72},{9,... | collective-permute-start | bytes 307208 | tf_op jit(solution)/shard_map/ppermute | solution.py:201
  69.6 1.9 %collective-permute-start.24 = (bf16[40,1280]{1,0:T(8,128)(2,1)S(1)}, bf16[40,1280]{1,0:T(8,128)(2,1)S(1)}, u32[]{:S(2)}, u32[]{:S(2)}) collective-permute-start(bf16[40,1280]{1,0:T(8,128)(2,1)S(1)} %get-tuple-element.138), channel_id=1, source_target_pairs={{0,96},{1,97},{2,98},{3,99},{4,100},{5,101},{6,102},{7,103},{8,104... | collective-permute-start | bytes 307208 | tf_op jit(solution)/shard_map/ppermute | solution.py:201
  71.7 2.7 %collective-permute-done.23.b2 = bf16[40,1280]{1,0:T(8,128)(2,1)S(1)} collective-permute-done((bf16[40,1280]{1,0:T(8,128)(2,1)S(1)}, bf16[40,1280]{1,0:T(8,128)(2,1)S(1)}, u32[]{:S(2)}, u32[]{:S(2)}) %collective-permute-start.23) | collective-permute-done | bytes 102432 | tf_op jit(solution)/shard_map/ppermute | solution.py:201
  74.4 2.6 %collective-permute-done.24.b3 = bf16[40,1280]{1,0:T(8,128)(2,1)S(1)} collective-permute-done((bf16[40,1280]{1,0:T(8,128)(2,1)S(1)}, bf16[40,1280]{1,0:T(8,128)(2,1)S(1)}, u32[]{:S(2)}, u32[]{:S(2)}) %collective-permute-start.24) | collective-permute-done | bytes 102432 | tf_op jit(solution)/shard_map/ppermute | solution.py:201
  77.0 1.3 %shard_map.127 = (bf16[40,1152]{1,0:T(8,128)(2,1)S(1)}, bf16[32,768]{1,0:T(8,128)(2,1)}) custom-call(s32[6]{0:T(128)S(1)} %stack.45.at, bf16[40,1280]{1,0:T(8,128)(2,1)S(1)} %get-tuple-element.135.b0, bf16[40,1280]{1,0:T(8,128)(2,1)S(1)} %collective-permute-done.22.b1, bf16[40,1280]{1,0:T(8,128)(2,1)S(1)} %collective-permute-done.23.b2, ...), custom_call_target="tpu_custom_call" | custom-call | flops 1100000000 | tf_op jit(solution)/shard_map/pallas_call | solution.py:216
  78.3 2.8 %collective-permute-start.25 = (bf16[40,1152]{1,0:T(8,128)(2,1)S(1)}, bf16[40,1152]{1,0:T(8,128)(2,1)S(1)}, u32[]{:S(2)}, u32[]{:S(2)}) collective-permute-start(bf16[40,1152]{1,0:T(8,128)(2,1)S(1)} %get-tuple-element.139), channel_id=1, source_target_pairs={{0,1},{1,0},{2,3},{3,2},{4,5},{5,4},{6,7},{7,6},{8,9},{9,8},{10,11... | collective-permute-start | bytes 276488 | tf_op jit(solution)/shard_map/ppermute | solution.py:201
  81.7 1.5 %collective-permute-done.25 = bf16[40,1152]{1,0:T(8,128)(2,1)S(1)} collective-permute-done((bf16[40,1152]{1,0:T(8,128)(2,1)S(1)}, bf16[40,1152]{1,0:T(8,128)(2,1)S(1)}, u32[]{:S(2)}, u32[]{:S(2)}) %collective-permute-start.25) | collective-permute-done | bytes 92192 | tf_op jit(solution)/shard_map/ppermute | solution.py:201
  83.2 1.8 %conditional.1 = (bf16[32,768]{1,0:T(8,128)(2,1)}, f32[1024,32]{0,1:T(8,128)}) conditional(s32[]{:T(128)} %convert_element_type.62, (s32[512]{0:T(512)S(1)}, s32[1024]{0:T(1024)S(1)}, bf16[256,3072]{1,0:T(8,128)(2,1)S(1)}, s32[1]{0:T(128)}, f32[28,2,3072]{2,1,0:T(2,128)}, /*index=5*/bf16[3072,3,768]{2,0,1:T(8,128)(2,1)}, f32[2,128]{1,0:T(2,128)S(1)}, ...), branch_computations={%region_0.15_spmd, %region_15.16_spmd} | conditional | flops 1100000000 | bytes 257951312 | solution.py:802
  83.5 1.6 %branch_1_fun.1 = (bf16[32,768]{1,0:T(8,128)(2,1)}, f32[32,1024]{1,0:T(8,128)}) custom-call(bf16[40,1152]{1,0:T(8,128)(2,1)S(1)} %get-tuple-element.36.own, bf16[40,1152]{1,0:T(8,128)(2,1)S(1)} %get-tuple-element.37.head, bf16[32,768]{1,0:T(8,128)(2,1)} %get-tuple-element.38.img), custom_call_target="tpu_custom_call" | custom-call | flops 1100000000 | tf_op jit(solution)/shard_map/cond/branch_1_fun/pallas_call | solution.py:216
  (54 shorter events, 7.7 us)
Async XLA Ops:
  0.7 14.3 %copy-start.9 = (s32[1024]{0:T(1024)S(1)}, s32[1024]{0:T(1024)}, u32[]{:S(2)}) copy-start(s32[1024]{0:T(1024)} %param.16) | copy-start | bytes 12292
  0.7 14.3 %copy-start.10 = (s32[512]{0:T(512)S(1)}, s32[512]{0:T(512)}, u32[]{:S(2)}) copy-start(s32[512]{0:T(512)} %param.15) | copy-start | bytes 6148
  2.8 16.9 %collective-permute-start.2 = (bf16[32,3072]{1,0:T(8,128)(2,1)S(1)}, bf16[32,3072]{1,0:T(8,128)(2,1)S(1)}, u32[]{:S(2)}, u32[]{:S(2)}) collective-permute-start(bf16[32,3072]{1,0:T(8,128)(2,1)S(1)} %get-tuple-element.96.refs_0_), channel_id=1, source_target_pairs={{0,1},{1,0},{2,3},{3,2},{4,5},{5,4},{6,7},{7,6},{8,9},{9,8},{10,11... | collective-permute-start | bytes 589832 | tf_op jit(solution)/shard_map/ppermute | solution.py:201
  7.3 12.5 %collective-permute-start.4 = (bf16[32,3072]{1,0:T(8,128)(2,1)S(1)}, bf16[32,3072]{1,0:T(8,128)(2,1)S(1)}, u32[]{:S(2)}, u32[]{:S(2)}) collective-permute-start(bf16[32,3072]{1,0:T(8,128)(2,1)S(1)} %get-tuple-element.96.refs_0_), channel_id=1, source_target_pairs={{0,16},{1,17},{2,18},{3,19},{4,20},{5,21},{6,22},{7,23},{8,24},{9,... | collective-permute-start | bytes 589832 | tf_op jit(solution)/shard_map/ppermute | solution.py:201
  8.1 10.8 %collective-permute-start.7 = (bf16[32,3072]{1,0:T(8,128)(2,1)S(1)}, bf16[32,3072]{1,0:T(8,128)(2,1)S(1)}, u32[]{:S(2)}, u32[]{:S(2)}) collective-permute-start(bf16[32,3072]{1,0:T(8,128)(2,1)S(1)} %get-tuple-element.96.refs_0_), channel_id=1, source_target_pairs={{0,17},{1,16},{2,19},{3,18},{4,21},{5,20},{6,23},{7,22},{8,25},{9,... | collective-permute-start | bytes 589832 | tf_op jit(solution)/shard_map/ppermute | solution.py:201
  8.1 2.6 %collective-permute-start.1 = (bf16[48,3072]{1,0:T(8,128)(2,1)S(1)}, bf16[48,3072]{1,0:T(8,128)(2,1)S(1)}, u32[]{:S(2)}, u32[]{:S(2)}) collective-permute-start(bf16[48,3072]{1,0:T(8,128)(2,1)S(1)} %get-tuple-element.94), channel_id=1, source_target_pairs={{0,2},{1,3},{2,0},{3,1},{4,6},{5,7},{6,4},{7,5},{8,10},{9,11},{10,... | collective-permute-start | bytes 884744 | tf_op jit(solution)/shard_map/ppermute | solution.py:201
  11.3 8.4 %collective-permute-start.3 = (bf16[192,128]{1,0:T(8,128)(2,1)S(1)}, bf16[192,128]{1,0:T(8,128)(2,1)S(1)}, u32[]{:S(2)}, u32[]{:S(2)}) collective-permute-start(bf16[192,128]{1,0:T(8,128)(2,1)S(1)} %get-tuple-element.98), channel_id=1, source_target_pairs={{0,32},{1,33},{2,34},{3,35},{4,36},{5,37},{6,38},{7,39},{8,40},{9,... | collective-permute-start | bytes 147464 | tf_op jit(solution)/shard_map/ppermute | solution.py:201
  12.6 7.2 %collective-permute-start.5 = (bf16[192,128]{1,0:T(8,128)(2,1)S(1)}, bf16[192,128]{1,0:T(8,128)(2,1)S(1)}, u32[]{:S(2)}, u32[]{:S(2)}) collective-permute-start(bf16[192,128]{1,0:T(8,128)(2,1)S(1)} %get-tuple-element.100), channel_id=1, source_target_pairs={{0,64},{1,65},{2,66},{3,67},{4,68},{5,69},{6,70},{7,71},{8,72},{9,... | collective-permute-start | bytes 147464 | tf_op jit(solution)/shard_map/ppermute | solution.py:201
  15.1 6.4 %copy-start.11 = (f32[2,128]{1,0:T(2,128)S(1)}, f32[2,128]{1,0:T(2,128)}, u32[]{:S(2)}) copy-start(f32[2,128]{1,0:T(2,128)} %refs_9_.1) | copy-start | bytes 3076
  18.9 1.9 %collective-permute-start.10 = (bf16[32,3072]{1,0:T(8,128)(2,1)S(1)}, bf16[32,3072]{1,0:T(8,128)(2,1)S(1)}, u32[]{:S(2)}, u32[]{:S(2)}) collective-permute-start(bf16[32,3072]{1,0:T(8,128)(2,1)S(1)} %collective-permute-done.7.refs_3_), channel_id=1, source_target_pairs={{0,2},{1,3},{2,0},{3,1},{4,6},{5,7},{6,4},{7,5},{8,10},{9,11},{10,... | collective-permute-start | bytes 589832 | tf_op jit(solution)/shard_map/ppermute | solution.py:201
  19.7 1.4 %collective-permute-start.9 = (bf16[32,3072]{1,0:T(8,128)(2,1)S(1)}, bf16[32,3072]{1,0:T(8,128)(2,1)S(1)}, u32[]{:S(2)}, u32[]{:S(2)}) collective-permute-start(bf16[32,3072]{1,0:T(8,128)(2,1)S(1)} %collective-permute-done.2.refs_2_), channel_id=1, source_target_pairs={{0,2},{1,3},{2,0},{3,1},{4,6},{5,7},{6,4},{7,5},{8,10},{9,11},{10,... | collective-permute-start | bytes 589832 | tf_op jit(solution)/shard_map/ppermute | solution.py:201
  19.8 1.6 %collective-permute-start.8 = (bf16[32,3072]{1,0:T(8,128)(2,1)S(1)}, bf16[32,3072]{1,0:T(8,128)(2,1)S(1)}, u32[]{:S(2)}, u32[]{:S(2)}) collective-permute-start(bf16[32,3072]{1,0:T(8,128)(2,1)S(1)} %collective-permute-done.4.refs_1_), channel_id=1, source_target_pairs={{0,2},{1,3},{2,0},{3,1},{4,6},{5,7},{6,4},{7,5},{8,10},{9,11},{10,... | collective-permute-start | bytes 589832 | tf_op jit(solution)/shard_map/ppermute | solution.py:201
  20.2 5.5 %collective-permute-start.6 = (bf16[192,128]{1,0:T(8,128)(2,1)S(1)}, bf16[192,128]{1,0:T(8,128)(2,1)S(1)}, u32[]{:S(2)}, u32[]{:S(2)}) collective-permute-start(bf16[192,128]{1,0:T(8,128)(2,1)S(1)} %get-tuple-element.102), channel_id=1, source_target_pairs={{0,96},{1,97},{2,98},{3,99},{4,100},{5,101},{6,102},{7,103},{8,104... | collective-permute-start | bytes 147464 | tf_op jit(solution)/shard_map/ppermute | solution.py:201
  25.6 7.4 %collective-permute-start.15 = (bf16[208,256]{1,0:T(8,128)(2,1)S(1)}, bf16[208,256]{1,0:T(8,128)(2,1)S(1)}, u32[]{:S(2)}, u32[]{:S(2)}) collective-permute-start(bf16[208,256]{1,0:T(8,128)(2,1)S(1)} %get-tuple-element.118), channel_id=1, source_target_pairs={{0,32},{1,33},{2,34},{3,35},{4,36},{5,37},{6,38},{7,39},{8,40},{9,... | collective-permute-start | bytes 319496 | tf_op jit(solution)/shard_map/ppermute | solution.py:201
  25.7 8.2 %collective-permute-start.16 = (bf16[208,256]{1,0:T(8,128)(2,1)S(1)}, bf16[208,256]{1,0:T(8,128)(2,1)S(1)}, u32[]{:S(2)}, u32[]{:S(2)}) collective-permute-start(bf16[208,256]{1,0:T(8,128)(2,1)S(1)} %get-tuple-element.119), channel_id=1, source_target_pairs={{0,64},{1,65},{2,66},{3,67},{4,68},{5,69},{6,70},{7,71},{8,72},{9,... | collective-permute-start | bytes 319496 | tf_op jit(solution)/shard_map/ppermute | solution.py:201
  28.3 7.5 %collective-permute-start.17 = (bf16[208,256]{1,0:T(8,128)(2,1)S(1)}, bf16[208,256]{1,0:T(8,128)(2,1)S(1)}, u32[]{:S(2)}, u32[]{:S(2)}) collective-permute-start(bf16[208,256]{1,0:T(8,128)(2,1)S(1)} %get-tuple-element.120), channel_id=1, source_target_pairs={{0,96},{1,97},{2,98},{3,99},{4,100},{5,101},{6,102},{7,103},{8,104... | collective-permute-start | bytes 319496 | tf_op jit(solution)/shard_map/ppermute | solution.py:201
  29.6 10.6 %collective-permute-start.11 = (bf16[512,128]{1,0:T(8,128)(2,1)S(1)}, bf16[512,128]{1,0:T(8,128)(2,1)S(1)}, u32[]{:S(2)}, u32[]{:S(2)}) collective-permute-start(bf16[512,128]{1,0:T(8,128)(2,1)S(1)} %get-tuple-element.113.a), channel_id=1, source_target_pairs={{0,8},{1,9},{2,10},{3,11},{4,12},{5,13},{6,14},{7,15},{8,0},{9,1},... | collective-permute-start | bytes 393224 | tf_op jit(solution)/shard_map/ppermute | solution.py:201
  32.6 7.6 %collective-permute-start.12 = (bf16[512,128]{1,0:T(8,128)(2,1)S(1)}, bf16[512,128]{1,0:T(8,128)(2,1)S(1)}, u32[]{:S(2)}, u32[]{:S(2)}) collective-permute-start(bf16[512,128]{1,0:T(8,128)(2,1)S(1)} %get-tuple-element.113.a), channel_id=1, source_target_pairs={{0,4},{1,5},{2,6},{3,7},{4,0},{5,1},{6,2},{7,3},{8,12},{9,13},{10,... | collective-permute-start | bytes 393224 | tf_op jit(solution)/shard_map/ppermute | solution.py:201
  33.0 7.2 %collective-permute-start.13 = (bf16[512,128]{1,0:T(8,128)(2,1)S(1)}, bf16[512,128]{1,0:T(8,128)(2,1)S(1)}, u32[]{:S(2)}, u32[]{:S(2)}) collective-permute-start(bf16[512,128]{1,0:T(8,128)(2,1)S(1)} %get-tuple-element.113.a), channel_id=1, source_target_pairs={{0,12},{1,13},{2,14},{3,15},{4,8},{5,9},{6,10},{7,11},{8,4},{9,5},... | collective-permute-start | bytes 393224 | tf_op jit(solution)/shard_map/ppermute | solution.py:201
  36.2 10.1 %collective-permute-start.18 = (bf16[656,256]{1,0:T(8,128)(2,1)S(1)}, bf16[656,256]{1,0:T(8,128)(2,1)S(1)}, u32[]{:S(2)}, u32[]{:S(2)}) collective-permute-start(bf16[656,256]{1,0:T(8,128)(2,1)S(1)} %shard_map.121.l0), channel_id=1, source_target_pairs={{0,4},{1,5},{2,6},{3,7},{4,0},{5,1},{6,2},{7,3},{8,12},{9,13},{10,... | collective-permute-start | bytes 1007624 | tf_op jit(solution)/shard_map/ppermute | solution.py:201
  37.6 17.1 %collective-permute-start.19 = (bf16[656,256]{1,0:T(8,128)(2,1)S(1)}, bf16[656,256]{1,0:T(8,128)(2,1)S(1)}, u32[]{:S(2)}, u32[]{:S(2)}) collective-permute-start(bf16[656,256]{1,0:T(8,128)(2,1)S(1)} %shard_map.121.l0), channel_id=1, source_target_pairs={{0,8},{1,9},{2,10},{3,11},{4,12},{5,13},{6,14},{7,15},{8,0},{9,1},... | collective-permute-start | bytes 1007624 | tf_op jit(solution)/shard_map/ppermute | solution.py:201
  40.2 16.5 %collective-permute-start.20 = (bf16[656,256]{1,0:T(8,128)(2,1)S(1)}, bf16[656,256]{1,0:T(8,128)(2,1)S(1)}, u32[]{:S(2)}, u32[]{:S(2)}) collective-permute-start(bf16[656,256]{1,0:T(8,128)(2,1)S(1)} %shard_map.121.l0), channel_id=1, source_target_pairs={{0,12},{1,13},{2,14},{3,15},{4,8},{5,9},{6,10},{7,11},{8,4},{9,5},... | collective-permute-start | bytes 1007624 | tf_op jit(solution)/shard_map/ppermute | solution.py:201
  40.2 20.7 %collective-permute-start.14 = (bf16[2048,128]{1,0:T(8,128)(2,1)S(1)}, bf16[2048,128]{1,0:T(8,128)(2,1)S(1)}, u32[]{:S(2)}, u32[]{:S(2)}) collective-permute-start(bf16[2048,128]{1,0:T(8,128)(2,1)S(1)} %shard_map.120.plane), channel_id=1, source_target_pairs={{0,16},{1,17},{2,18},{3,19},{4,20},{5,21},{6,22},{7,23},{8,24},{9,... | collective-permute-start | bytes 1572872 | tf_op jit(solution)/shard_map/ppermute | solution.py:201
  63.4 3.5 %collective-permute-start.21 = (bf16[136,1152]{1,0:T(8,128)(2,1)S(1)}, bf16[136,1152]{1,0:T(8,128)(2,1)S(1)}, u32[]{:S(2)}, u32[]{:S(2)}) collective-permute-start(bf16[136,1152]{1,0:T(8,128)(2,1)S(1)} %get-tuple-element.134), channel_id=1, source_target_pairs={{0,2},{1,3},{2,0},{3,1},{4,6},{5,7},{6,4},{7,5},{8,10},{9,11},{10,... | collective-permute-start | bytes 940040 | tf_op jit(solution)/shard_map/ppermute | solution.py:201
  66.9 16.3 %copy-start = (bf16[256,3072]{1,0:T(8,128)(2,1)S(1)}, bf16[256,3072]{1,0:T(8,128)(2,1)}, u32[]{:S(2)}) copy-start(bf16[256,3072]{1,0:T(8,128)(2,1)} %table_ref.1) | copy-start | bytes 4718596
  66.9 16.3 %copy-start.4 = (bf16[32,768]{1,0:T(8,128)(2,1)S(1)}, bf16[32,768]{1,0:T(8,128)(2,1)}, u32[]{:S(2)}) copy-start(bf16[32,768]{1,0:T(8,128)(2,1)} %q_ref.1) | copy-start | bytes 147460
  66.9 16.3 %copy-start.7 = (bf16[32,768]{1,0:T(8,128)(2,1)S(1)}, bf16[32,768]{1,0:T(8,128)(2,1)}, u32[]{:S(2)}) copy-start(bf16[32,768]{1,0:T(8,128)(2,1)} %k_ref.1) | copy-start | bytes 147460
  66.9 16.3 %copy-start.8 = (bf16[32,768]{1,0:T(8,128)(2,1)S(1)}, bf16[32,768]{1,0:T(8,128)(2,1)}, u32[]{:S(2)}) copy-start(bf16[32,768]{1,0:T(8,128)(2,1)} %v_ref.1) | copy-start | bytes 147460
  67.5 4.2 %collective-permute-start.22 = (bf16[40,1280]{1,0:T(8,128)(2,1)S(1)}, bf16[40,1280]{1,0:T(8,128)(2,1)S(1)}, u32[]{:S(2)}, u32[]{:S(2)}) collective-permute-start(bf16[40,1280]{1,0:T(8,128)(2,1)S(1)} %get-tuple-element.136), channel_id=1, source_target_pairs={{0,32},{1,33},{2,34},{3,35},{4,36},{5,37},{6,38},{7,39},{8,40},{9,... | collective-permute-start | bytes 307208 | tf_op jit(solution)/shard_map/ppermute | solution.py:201
  67.6 6.8 %collective-permute-start.23 = (bf16[40,1280]{1,0:T(8,128)(2,1)S(1)}, bf16[40,1280]{1,0:T(8,128)(2,1)S(1)}, u32[]{:S(2)}, u32[]{:S(2)}) collective-permute-start(bf16[40,1280]{1,0:T(8,128)(2,1)S(1)} %get-tuple-element.137), channel_id=1, source_target_pairs={{0,64},{1,65},{2,66},{3,67},{4,68},{5,69},{6,70},{7,71},{8,72},{9,... | collective-permute-start | bytes 307208 | tf_op jit(solution)/shard_map/ppermute | solution.py:201
  69.6 7.4 %collective-permute-start.24 = (bf16[40,1280]{1,0:T(8,128)(2,1)S(1)}, bf16[40,1280]{1,0:T(8,128)(2,1)S(1)}, u32[]{:S(2)}, u32[]{:S(2)}) collective-permute-start(bf16[40,1280]{1,0:T(8,128)(2,1)S(1)} %get-tuple-element.138), channel_id=1, source_target_pairs={{0,96},{1,97},{2,98},{3,99},{4,100},{5,101},{6,102},{7,103},{8,104... | collective-permute-start | bytes 307208 | tf_op jit(solution)/shard_map/ppermute | solution.py:201
  78.3 4.9 %collective-permute-start.25 = (bf16[40,1152]{1,0:T(8,128)(2,1)S(1)}, bf16[40,1152]{1,0:T(8,128)(2,1)S(1)}, u32[]{:S(2)}, u32[]{:S(2)}) collective-permute-start(bf16[40,1152]{1,0:T(8,128)(2,1)S(1)} %get-tuple-element.139), channel_id=1, source_target_pairs={{0,1},{1,0},{2,3},{3,2},{4,5},{5,4},{6,7},{7,6},{8,9},{9,8},{10,11... | collective-permute-start | bytes 276488 | tf_op jit(solution)/shard_map/ppermute | solution.py:201
  (1 other events, 6.4 us)

commit v6 on v4

--- a/solution.py
+++ b/solution.py
@@ -365,7 +365,7 @@
 ):
     half = w_ref.shape[2]
     lanes = pl.ds(pl.multiple_of(at[2] * half, half), half)
-    weights = pltpu.make_async_copy(w_hbm.at[:, :, lanes], w_ref, sem)
+    weights = pltpu.make_async_copy(w_hbm.at[0:2, :, lanes], w_ref, sem)
     weights.start()
     ids = jnp.concatenate([con_ref[...], txt_ref[...]], axis=1)
     n = ids.shape[1]
@@ -413,9 +413,13 @@
 
 
 def project_kernel(at, pack_ref, *refs):
-    rows, (mod_ref, gain_ref, w_ref), outs, (raw_ref, x_ref) = (
-        refs[:8], refs[8:11], refs[11:15], refs[15:]
-    )
+    rows, (mod_ref, gain_ref, w_ref, w_hbm), outs, (raw_ref, x_ref, w_last, sem) = (
+        refs[:8], refs[8:12], refs[12:16], refs[16:]
+    )
+    half = w_ref.shape[2]
+    lanes = pl.ds(pl.multiple_of(at[2] * half, half), half)
+    weights = pltpu.make_async_copy(w_hbm.at[2, :, lanes], w_last, sem)
+    weights.start()
     for i, ref in enumerate(rows):
         raw_ref[i * SLOTS : (i + 1) * SLOTS, :] = ref[0:SLOTS, :]
     shift = mod_ref[0:1, :]
@@ -434,7 +438,8 @@
 
     q = nn(x_ref[0:CON, :], w_ref[0])
     k = nn(x_ref[...], w_ref[1])
-    v = nn(x_ref[...], w_ref[2])
+    weights.wait()
+    v = nn(x_ref[...], w_last[...])
     heads = []
     for h in range(3):
         cols = slice(h * HD, (h + 1) * HD)
@@ -614,7 +619,10 @@
     weigh_blocks(con_q, ((plane.at[0:n_img, :], img_v, None),), store)
     dots = nt(img, con_out[...]).astype(BF)
     con_f = con_out[...].astype(F32)
-    con_sq = nt(jnp.ones((8, HD), F32), con_f * con_f, precision=lax.Precision.HIGHEST).astype(BF)
+    squares = con_f * con_f
+    high = squares.astype(BF)
+    ones = jnp.ones((8, HD), BF)
+    con_sq = (nt(ones, high) + nt(ones, (squares - high.astype(F32)).astype(BF))).astype(BF)
     for s, out in enumerate(outs):
         rows = slice(s * 64, (s + 1) * 64)
         out[0:64, 0:n_con] = dots[rows]
@@ -623,7 +631,7 @@
         out[64:72, n_con:] = jnp.zeros((8, HD), BF)
 
 
-def head_sum_kernel(at, b0, b1, b2, b3, own, core, out_own):
+def head_sum_kernel(at, b0, b1, b2, b3, own, core):
     n_con = b0.shape[1] - HD
     total = jnp.zeros((72, n_con), F32)
     outs = [jnp.zeros((64, HD), BF) for _ in range(3)]
@@ -645,28 +653,27 @@
         ref[32:40, n_con : n_con + HD] = jnp.zeros((8, HD), BF)
     for h in range(3):
         lanes = slice(n_con + (1 + h) * HD, n_con + (2 + h) * HD)
-        core[0:32, lanes] = outs[h][32:64]
-        core[32:40, lanes] = jnp.zeros((8, HD), BF)
-        out_own[:, h * HD : (h + 1) * HD] = outs[h][0:32]
+        for ref, row in ((own, 0), (core, 32)):
+            ref[0:32, lanes] = outs[h][row : row + 32]
+            ref[32:40, lanes] = jnp.zeros((8, HD), BF)
 
 
 def core_sum_kernel(own, core, out):
-    cols = own.shape[1]
-    out[...] = (own[...].astype(F32) + core[:, 0:cols].astype(F32)).astype(BF)
-
-
-def finish_kernel(at, own, head, core, out_own, img_ref, sal_ref):
-    n_con = own.shape[1] - HD
+    cols = out.shape[1]
+    out[...] = (own[:, 0:cols].astype(F32) + core[:, 0:cols].astype(F32)).astype(BF)
+
+
+def finish_kernel(at, sums, head, own, core, img_ref, sal_ref):
+    n_con = sums.shape[1] - HD
     width = 12 * HD
-    total = own[...].astype(F32) + head[...].astype(F32)
+    total = sums[...].astype(F32) + head[...].astype(F32)
     con_rms = jnp.sqrt(total[32:33, 0:n_con] / width + 1e-06)
     img_rms = jnp.sqrt(total[0:32, n_con : n_con + 1] / width + 1e-06)
     sal_ref[...] = total[0:32, 0:n_con] / (math.sqrt(width) * con_rms * img_rms)
     half = 3 * HD
-    mine = pl.ds(pl.multiple_of(at[2] * half, half), half)
-    theirs = pl.ds(pl.multiple_of((1 - at[2]) * half, half), half)
-    img_ref[:, mine] = out_own[...]
-    img_ref[:, theirs] = core[0:32, n_con + HD :]
+    for ref, core_of in ((own, at[2]), (core, 1 - at[2])):
+        lanes = pl.ds(pl.multiple_of(core_of * half, half), half)
+        img_ref[:, lanes] = ref[0:32, n_con + HD :]
 
 
 def packed(
@@ -695,6 +702,7 @@
     column_rows = [own_rows] + [send(own_rows, swap_z(s)) for s in (1, 3)]
     core_both = send(own_both, swap_core())
 
+    all_weights = jnp.transpose(txt_qkv, (1, 0, 2))
     pack, spots, con_bias, txt_bias, con_line, txt_line, weights = call(
         pack_kernel,
         (
@@ -704,15 +712,14 @@
             sds((1, 4 * LINE_TXT), F32),
             sds((1, 4 * CON), jnp.int32),
             sds((1, 4 * TXT), jnp.int32),
-            sds((3, width, half)),
+            sds((2, width, half)),
         ),
         scratch=(pltpu.SemaphoreType.DMA,),
         limit=24,
         us=2.0,
         in_hbm=1,
-    )(at, con_ids, text_ids, jnp.transpose(txt_qkv, (1, 0, 2)))
+    )(at, con_ids, text_ids, all_weights)
     shift_scale = lax.dynamic_index_in_dim(modulation, step_index[0], 0, keepdims=False)
-    fits = (spots[1, 0] <= 0).astype(jnp.int32)
 
     image_blocks = call(
         image_heads_kernel, tuple(sds((6 * n_img, HD)) for _ in range(4))
@@ -720,8 +727,8 @@
     image_blocks = [image_blocks[0]] + [send(image_blocks[s], swap_u(s)) for s in (2, 1, 3)]
     image_blocks = [image_blocks[0], image_blocks[2], image_blocks[1], image_blocks[3]]
     column_rows[1], image_blocks[2] = lax.optimization_barrier((column_rows[1], image_blocks[2]))
-    far_rows, pack, shift_scale, fits, image_blocks[1] = lax.optimization_barrier(
-        (far_rows, pack, shift_scale, fits, image_blocks[1])
+    far_rows, pack, shift_scale, image_blocks[1] = lax.optimization_barrier(
+        (far_rows, pack, shift_scale, image_blocks[1])
     )
     column_rows.insert(2, far_rows)
     other_rows = [core_both] + [send(r, swap_core()) for r in column_rows[1:]]
@@ -732,10 +739,13 @@
         scratch=(
             pltpu.VMEM((8 * SLOTS, width), BF),
             pltpu.VMEM((ROWS, width), BF),
+            pltpu.VMEM((width, half), BF),
+            pltpu.SemaphoreType.DMA,
         ),
         limit=24,
         us=PROJ_US,
-    )(at, pack, *column_rows, *other_rows, shift_scale, qk_gain, weights)
+        in_hbm=1,
+    )(at, pack, *column_rows, *other_rows, shift_scale, qk_gain, weights, all_weights)
 
     *image_blocks, first = lax.optimization_barrier((*image_blocks, qkv[0]))
     image_q, image_kv = call(
@@ -754,7 +764,7 @@
     lines = [line] + [send(line, swap_v(s)) for s in (2, 1, 3)]
     lines = [lines[0], lines[2], lines[1], lines[3]]
     plane = call(plane_kernel, sds((64 * n_img, HD)), smem=0)(*image_kvs)
-    con_slot, plane = lax.optimization_barrier((spots[0, :n_con], plane))
+    con_slot, over, plane = lax.optimization_barrier((spots[0, :n_con], spots[1, 0], plane))
     other_plane = send(plane, swap_plane())
     pick = (con_slot[:, None] == jnp.arange(4 * LINE_CON)[None, :]).astype(BF)
 
@@ -789,20 +799,19 @@
     )(other_plane, con_q, image_q, *near)
     blocks = [blocks[0]] + [send(blocks[s], swap_u(s)) for s in (2, 1, 3)]
     blocks = [blocks[0], blocks[2], blocks[1], blocks[3]]
-    own, core, out_own = call(
-        head_sum_kernel,
-        (sds((40, n_con + HD)), sds((40, n_con + 4 * HD)), sds((32, half))),
-    )(at, *blocks)
+    own, core = call(head_sum_kernel, tuple(sds((40, n_con + 4 * HD)) for _ in range(2)))(
+        at, *blocks
+    )
     core = send(core, swap_core())
-    own = call(core_sum_kernel, sds((40, n_con + HD)), smem=0)(own, core)
-    last = (at, own, send(own, swap_z(2)), core, out_own)
+    sums = call(core_sum_kernel, sds((40, n_con + HD)), smem=0)(own, core)
+    last = (at, sums, send(sums, swap_z(2)), own, core)
     finish = call(finish_kernel, (sds((n_img, 2 * half)), sds((n_img, n_con), F32)))
 
     def finished():
         img_out, saliency = finish(*last)
         return img_out, jnp.transpose(saliency)
 
-    return fits > 0, finished
+    return over <= 0, finished
 
 
 def on_device(*args):

time: 81.3 us -> 79.9 us (0.983)
  transfers between devices with their start and end apart: 25 -> 25, of which waited for: 8 -> 7; matrix products, arithmetic and copies ran while one was open for 2% -> 2% of each run, Pallas kernels for 18% -> 18%
where the time goes in v6:
time: 79.9 us; the launch traced here: 79.7 us
  starting transfers between devices  39.7 us (50%)
  Pallas kernels  21.6 us (27%)
  waiting for transfers between devices  14.1 us (18%)
  between operations  2.17 us (3%)
  local copies, waits for them, and re-layouts  1.38 us (2%)
    ppermute x25, starting transfers between devices, send(): return lax.ppermute(array, ('ctx', 'head'), pairing)  39.7 us
    pallas_call x14, Pallas kernels, run(): pl.pallas_call(kernel, out_shape=outs, in_specs=[sm] * smem + [vm] * (len...  21.6 us
    ppermute x25, waiting for transfers between devices, send(): return lax.ppermute(array, ('ctx', 'head'), pairing)  14.1 us
  transfers between devices with their start and end apart: 25, of which 7 were waited for; matrix products, arithmetic and copies ran while one was open for 2% of the time, Pallas kernels for 18%

profile of v6, /device:TPU:1, one launch (start us, length us, event | category | flops | bytes accessed | tf_op | source)
XLA Modules:
  0.0 79.7 jit_solution(7590204110568602602)
XLA Ops:
  0.7 2.1 %shard_map.116 = (bf16[32,3072]{1,0:T(8,128)(2,1)S(1)}, bf16[48,3072]{1,0:T(8,128)(2,1)S(1)}, bf16[96,384]{1,0:T(8,128)(2,1)S(1)}) custom-call(s32[6]{0:T(128)S(1)} %stack.45.at, s32[1,1024]{1,0:T(1,128)} %bitcast.135, s32[1,512]{1,0:T(1,128)} %bitcast.139, bf16[256,3072]{1,0:T(8,128)(2,1)} %table_ref.1, bf16[32,768]{1,0:T(8,128)(2,1)} %q_ref.1, ...), custom_call_target="tpu_custom_call" | custom-call | flops 1100000000 | tf_op jit(solution)/shard_map/pallas_call | solution.py:220
  2.9 4.5 %collective-permute-start.2 = (bf16[32,3072]{1,0:T(8,128)(2,1)S(1)}, bf16[32,3072]{1,0:T(8,128)(2,1)S(1)}, u32[]{:S(2)}, u32[]{:S(2)}) collective-permute-start(bf16[32,3072]{1,0:T(8,128)(2,1)S(1)} %get-tuple-element.100.refs_0_), channel_id=1, source_target_pairs={{0,1},{1,0},{2,3},{3,2},{4,5},{5,4},{6,7},{7,6},{8,9},{9,8},{10,11... | collective-permute-start | bytes 589832 | tf_op jit(solution)/shard_map/ppermute | solution.py:205
  8.1 1.2 %collective-permute-start.1 = (bf16[48,3072]{1,0:T(8,128)(2,1)S(1)}, bf16[48,3072]{1,0:T(8,128)(2,1)S(1)}, u32[]{:S(2)}, u32[]{:S(2)}) collective-permute-start(bf16[48,3072]{1,0:T(8,128)(2,1)S(1)} %get-tuple-element.98), channel_id=1, source_target_pairs={{0,2},{1,3},{2,0},{3,1},{4,6},{5,7},{6,4},{7,5},{8,10},{9,11},{10,... | collective-permute-start | bytes 884744 | tf_op jit(solution)/shard_map/ppermute | solution.py:205
  10.0 0.7 dynamic-slice_bitcast_fusion.refs_8_
  11.3 1.4 %collective-permute-start.3 = (bf16[192,128]{1,0:T(8,128)(2,1)S(1)}, bf16[192,128]{1,0:T(8,128)(2,1)S(1)}, u32[]{:S(2)}, u32[]{:S(2)}) collective-permute-start(bf16[192,128]{1,0:T(8,128)(2,1)S(1)} %get-tuple-element.102), channel_id=1, source_target_pairs={{0,32},{1,33},{2,6},{3,7},{4,36},{5,37},{6,2},{7,3},{8,40},{9,41},... | collective-permute-start | bytes 147464 | tf_op jit(solution)/shard_map/ppermute | solution.py:205
  12.7 2.6 %collective-permute-start.5 = (bf16[192,128]{1,0:T(8,128)(2,1)S(1)}, bf16[192,128]{1,0:T(8,128)(2,1)S(1)}, u32[]{:S(2)}, u32[]{:S(2)}) collective-permute-start(bf16[192,128]{1,0:T(8,128)(2,1)S(1)} %get-tuple-element.104), channel_id=1, source_target_pairs={{0,64},{1,65},{2,10},{3,11},{4,68},{5,69},{6,14},{7,15},{8,72},{9,... | collective-permute-start | bytes 147464 | tf_op jit(solution)/shard_map/ppermute | solution.py:205
  15.3 3.8 %shard_map.115 = (bf16[160,256]{1,0:T(8,128)(2,1)S(1)}, s32[8,1536]{1,0:T(8,128)S(1)}, f32[1,1280]{1,0:T(1,128)S(1)}, f32[1,704]{1,0:T(1,128)S(1)}, s32[1,384]{1...) custom-call(s32[6]{0:T(128)S(1)} %stack.45.at, s32[1,1024]{1,0:T(1,128)S(1)} %bitcast.136, ...), custom_call_target="tpu_custom_call" | custom-call | flops 2200000000 | tf_op jit(solution)/shard_map/pallas_call | solution.py:220
  20.3 2.7 %collective-permute-start.6 = (bf16[192,128]{1,0:T(8,128)(2,1)S(1)}, bf16[192,128]{1,0:T(8,128)(2,1)S(1)}, u32[]{:S(2)}, u32[]{:S(2)}) collective-permute-start(bf16[192,128]{1,0:T(8,128)(2,1)S(1)} %get-tuple-element.106), channel_id=1, source_target_pairs={{0,96},{1,97},{2,14},{3,15},{4,100},{5,101},{6,10},{7,11},{8,104},... | collective-permute-start | bytes 147464 | tf_op jit(solution)/shard_map/ppermute | solution.py:205
  23.0 4.1 %shard_map.118 = (bf16[208,256]{1,0:T(8,128)(2,1)S(1)}, bf16[208,256]{1,0:T(8,128)(2,1)S(1)}, bf16[208,256]{1,0:T(8,128)(2,1)S(1)}, bf16[208,256]{1,0:T(8,128)(2,1)S(1)}) custom-call(s32[6]{0:T(128)S(1)} %stack.45.at, bf16[160,256]{1,0:T(8,128)(2,1)S(1)} %get-tuple-element.107.pack_ref, bf16[32,3072]{1,0:T(8,128)(2,1)S(1)} %get-tuple-element.100.refs_0_, ...), custom_call_target="tpu_custom_call" | custom-call | flops 5500000256 | tf_op jit(solution)/shard_map/pallas_call | solution.py:220
  27.2 2.3 %collective-permute-start.16 = (bf16[208,256]{1,0:T(8,128)(2,1)S(1)}, bf16[208,256]{1,0:T(8,128)(2,1)S(1)}, u32[]{:S(2)}, u32[]{:S(2)}) collective-permute-start(bf16[208,256]{1,0:T(8,128)(2,1)S(1)} %get-tuple-element.123), channel_id=1, source_target_pairs={{0,64},{1,65},{2,10},{3,11},{4,68},{5,69},{6,14},{7,15},{8,72},{9,... | collective-permute-start | bytes 319496 | tf_op jit(solution)/shard_map/ppermute | solution.py:205
  29.6 1.5 %collective-permute-start.17 = (bf16[208,256]{1,0:T(8,128)(2,1)S(1)}, bf16[208,256]{1,0:T(8,128)(2,1)S(1)}, u32[]{:S(2)}, u32[]{:S(2)}) collective-permute-start(bf16[208,256]{1,0:T(8,128)(2,1)S(1)} %get-tuple-element.124), channel_id=1, source_target_pairs={{0,96},{1,97},{2,14},{3,15},{4,100},{5,101},{6,10},{7,11},{8,104},... | collective-permute-start | bytes 319496 | tf_op jit(solution)/shard_map/ppermute | solution.py:205
  31.1 1.6 %collective-permute-start.11 = (bf16[512,128]{1,0:T(8,128)(2,1)S(1)}, bf16[512,128]{1,0:T(8,128)(2,1)S(1)}, u32[]{:S(2)}, u32[]{:S(2)}) collective-permute-start(bf16[512,128]{1,0:T(8,128)(2,1)S(1)} %get-tuple-element.117.a), channel_id=1, source_target_pairs={{0,8},{1,9},{2,66},{3,67},{4,12},{5,13},{6,70},{7,71},{8,0},{9,1},... | collective-permute-start | bytes 393224 | tf_op jit(solution)/shard_map/ppermute | solution.py:205
  33.0 1.4 %collective-permute-start.13 = (bf16[512,128]{1,0:T(8,128)(2,1)S(1)}, bf16[512,128]{1,0:T(8,128)(2,1)S(1)}, u32[]{:S(2)}, u32[]{:S(2)}) collective-permute-start(bf16[512,128]{1,0:T(8,128)(2,1)S(1)} %get-tuple-element.117.a), channel_id=1, source_target_pairs={{0,12},{1,13},{2,98},{3,99},{4,8},{5,9},{6,102},{7,103},{8,4},{9,5... | collective-permute-start | bytes 393224 | tf_op jit(solution)/shard_map/ppermute | solution.py:205
  35.4 2.4 %collective-permute-start.19 = (bf16[656,256]{1,0:T(8,128)(2,1)S(1)}, bf16[656,256]{1,0:T(8,128)(2,1)S(1)}, u32[]{:S(2)}, u32[]{:S(2)}) collective-permute-start(bf16[656,256]{1,0:T(8,128)(2,1)S(1)} %shard_map.121.l0), channel_id=1, source_target_pairs={{0,8},{1,9},{2,66},{3,67},{4,12},{5,13},{6,70},{7,71},{8,0},{9,1},... | collective-permute-start | bytes 1007624 | tf_op jit(solution)/shard_map/ppermute | solution.py:205
  37.8 1.4 %collective-permute-start.20 = (bf16[656,256]{1,0:T(8,128)(2,1)S(1)}, bf16[656,256]{1,0:T(8,128)(2,1)S(1)}, u32[]{:S(2)}, u32[]{:S(2)}) collective-permute-start(bf16[656,256]{1,0:T(8,128)(2,1)S(1)} %shard_map.121.l0), channel_id=1, source_target_pairs={{0,12},{1,13},{2,98},{3,99},{4,8},{5,9},{6,102},{7,103},{8,4},{9,5... | collective-permute-start | bytes 1007624 | tf_op jit(solution)/shard_map/ppermute | solution.py:205
  39.3 1.1 %collective-permute-start.14 = (bf16[2048,128]{1,0:T(8,128)(2,1)S(1)}, bf16[2048,128]{1,0:T(8,128)(2,1)S(1)}, u32[]{:S(2)}, u32[]{:S(2)}) collective-permute-start(bf16[2048,128]{1,0:T(8,128)(2,1)S(1)} %shard_map.120.plane), channel_id=1, source_target_pairs={{0,16},{1,17},{2,18},{3,19},{4,20},{5,21},{6,22},{7,23},{8,24},{9,... | collective-permute-start | bytes 1572872 | tf_op jit(solution)/shard_map/ppermute | solution.py:205
  40.9 0.8 %shard_map.123 = (f32[256,1]{1,0:T(8,128)S(1)}, f32[256,256]{1,0:T(8,128)S(1)}) custom-call(bf16[2048,128]{1,0:T(8,128)(2,1)S(1)} %shard_map.120.plane, bf16[256,128]{1,0:T(8,128)(2,1)S(1)} %get-tuple-element.129.q.img_q), custom_call_target="tpu_custom_call" | custom-call | flops 1100000000 | tf_op jit(solution)/shard_map/pallas_call | solution.py:220
  42.3 3.8 %collective-permute-done.19.l2 = bf16[656,256]{1,0:T(8,128)(2,1)S(1)} collective-permute-done((bf16[656,256]{1,0:T(8,128)(2,1)S(1)}, bf16[656,256]{1,0:T(8,128)(2,1)S(1)}, u32[]{:S(2)}, u32[]{:S(2)}) %collective-permute-start.19) | collective-permute-done | bytes 335904 | tf_op jit(solution)/shard_map/ppermute | solution.py:205
  46.0 2.9 %collective-permute-done.20.l3 = bf16[656,256]{1,0:T(8,128)(2,1)S(1)} collective-permute-done((bf16[656,256]{1,0:T(8,128)(2,1)S(1)}, bf16[656,256]{1,0:T(8,128)(2,1)S(1)}, u32[]{:S(2)}, u32[]{:S(2)}) %collective-permute-start.20) | collective-permute-done | bytes 335904 | tf_op jit(solution)/shard_map/ppermute | solution.py:205
  48.9 4.2 %shard_map.124 = (bf16[1024,128]{1,0:T(8,128)(2,1)S(1)}, f32[1024,1]{1,0:T(8,128)S(1)}, f32[1024,256]{1,0:T(8,128)S(1)}, f32[256,1]{1,0:T(8,128)S(1)}, f32[256,256]{1,0:T(8,128)S(1)}) custom-call(bf16[1024,1280]{1,0:T(8,128)(2,1)S(1)} %fusion.81.pick, bf16[1024,128]{1,0:T(8,128)(2,1)S(1)} %shard_map.122.q_part, bf16[656,256]{1,0:T(8,128)(2,1)S(1)} %shard_map.121.l0, ...), custom_call_target="tpu_custom_call" | custom-call | flops 2200000000 | tf_op jit(solution)/shard_map/pallas_call | solution.py:220
  53.2 2.5 %shard_map.125 = (bf16[72,1152]{1,0:T(8,128)(2,1)S(1)}, bf16[72,1152]{1,0:T(8,128)(2,1)S(1)}, bf16[72,1152]{1,0:T(8,128)(2,1)S(1)}, bf16[72,1152]{1,0:T(8,128)(2,1)S(1)}) custom-call(bf16[2048,128]{1,0:T(8,128)(2,1)S(1)} %collective-permute-done.14.plane, bf16[1024,128]{1,0:T(8,128)(2,1)S(1)} %get-tuple-element.132.con_q, ...), custom_call_target="tpu_custom_call" | custom-call | flops 3300000000 | tf_op jit(solution)/shard_map/pallas_call | solution.py:220
  55.7 2.1 %collective-permute-start.22 = (bf16[72,1152]{1,0:T(8,128)(2,1)S(1)}, bf16[72,1152]{1,0:T(8,128)(2,1)S(1)}, u32[]{:S(2)}, u32[]{:S(2)}) collective-permute-start(bf16[72,1152]{1,0:T(8,128)(2,1)S(1)} %get-tuple-element.139), channel_id=1, source_target_pairs={{0,64},{1,65},{2,10},{3,11},{4,68},{5,69},{6,14},{7,15},{8,72},{9,... | collective-permute-start | bytes 497672 | tf_op jit(solution)/shard_map/ppermute | solution.py:205
  57.8 1.8 %collective-permute-start.23 = (bf16[72,1152]{1,0:T(8,128)(2,1)S(1)}, bf16[72,1152]{1,0:T(8,128)(2,1)S(1)}, u32[]{:S(2)}, u32[]{:S(2)}) collective-permute-start(bf16[72,1152]{1,0:T(8,128)(2,1)S(1)} %get-tuple-element.140), channel_id=1, source_target_pairs={{0,96},{1,97},{2,14},{3,15},{4,100},{5,101},{6,10},{7,11},{8,104},... | collective-permute-start | bytes 497672 | tf_op jit(solution)/shard_map/ppermute | solution.py:205
  59.9 2.5 %collective-permute-done.22.b2 = bf16[72,1152]{1,0:T(8,128)(2,1)S(1)} collective-permute-done((bf16[72,1152]{1,0:T(8,128)(2,1)S(1)}, bf16[72,1152]{1,0:T(8,128)(2,1)S(1)}, u32[]{:S(2)}, u32[]{:S(2)}) %collective-permute-start.22) | collective-permute-done | bytes 165920 | tf_op jit(solution)/shard_map/ppermute | solution.py:205
  62.4 1.7 %collective-permute-done.23.b3 = bf16[72,1152]{1,0:T(8,128)(2,1)S(1)} collective-permute-done((bf16[72,1152]{1,0:T(8,128)(2,1)S(1)}, bf16[72,1152]{1,0:T(8,128)(2,1)S(1)}, u32[]{:S(2)}, u32[]{:S(2)}) %collective-permute-start.23) | collective-permute-done | bytes 165920 | tf_op jit(solution)/shard_map/ppermute | solution.py:205
  64.0 0.8 %shard_map.126 = (bf16[40,1536]{1,0:T(8,128)(2,1)S(1)}, bf16[40,1536]{1,0:T(8,128)(2,1)S(1)}) custom-call(s32[6]{0:T(128)S(1)} %stack.45.at, bf16[72,1152]{1,0:T(8,128)(2,1)S(1)} %get-tuple-element.137.b0, bf16[72,1152]{1,0:T(8,128)(2,1)S(1)} %collective-permute-done.21.b1, bf16[72,1152]{1,0:T(8,128)(2,1)S(1)} %collective-permute-done.22.b2, ...), custom_call_target="tpu_custom_call" | custom-call | flops 1100000000 | tf_op jit(solution)/shard_map/pallas_call | solution.py:220
  64.9 6.4 %collective-permute-start.24 = (bf16[40,1536]{1,0:T(8,128)(2,1)S(1)}, bf16[40,1536]{1,0:T(8,128)(2,1)S(1)}, u32[]{:S(2)}, u32[]{:S(2)}) collective-permute-start(bf16[40,1536]{1,0:T(8,128)(2,1)S(1)} %get-tuple-element.142), channel_id=1, source_target_pairs={{0,2},{1,3},{2,0},{3,1},{4,6},{5,7},{6,4},{7,5},{8,10},{9,11},{10,... | collective-permute-start | bytes 368648 | tf_op jit(solution)/shard_map/ppermute | solution.py:205
  71.2 1.0 %collective-permute-done.24.core = bf16[40,1536]{1,0:T(8,128)(2,1)S(1)} collective-permute-done((bf16[40,1536]{1,0:T(8,128)(2,1)S(1)}, bf16[40,1536]{1,0:T(8,128)(2,1)S(1)}, u32[]{:S(2)}, u32[]{:S(2)}) %collective-permute-start.24) | collective-permute-done | bytes 122912 | tf_op jit(solution)/shard_map/ppermute | solution.py:205
  72.2 2.9 %collective-permute-start.25 = (bf16[40,1152]{1,0:T(8,128)(2,1)S(1)}, bf16[40,1152]{1,0:T(8,128)(2,1)S(1)}, u32[]{:S(2)}, u32[]{:S(2)}) collective-permute-start(bf16[40,1152]{1,0:T(8,128)(2,1)S(1)} %shard_map.127), channel_id=1, source_target_pairs={{0,1},{1,0},{2,3},{3,2},{4,5},{5,4},{6,7},{7,6},{8,9},{9,8},{10,11... | collective-permute-start | bytes 276488 | tf_op jit(solution)/shard_map/ppermute | solution.py:205
  75.8 1.9 %collective-permute-done.25 = bf16[40,1152]{1,0:T(8,128)(2,1)S(1)} collective-permute-done((bf16[40,1152]{1,0:T(8,128)(2,1)S(1)}, bf16[40,1152]{1,0:T(8,128)(2,1)S(1)}, u32[]{:S(2)}, u32[]{:S(2)}) %collective-permute-start.25) | collective-permute-done | bytes 92192 | tf_op jit(solution)/shard_map/ppermute | solution.py:205
  77.7 2.0 %conditional.1 = (bf16[32,768]{1,0:T(8,128)(2,1)}, f32[1024,32]{0,1:T(8,128)}) conditional(s32[]{:T(128)} %convert_element_type.62, (s32[512]{0:T(512)S(1)}, s32[1024]{0:T(1024)S(1)}, bf16[256,3072]{1,0:T(8,128)(2,1)S(1)}, s32[1]{0:T(128)}, f32[28,2,3072]{2,1,0:T(2,128)}, /*index=5*/bf16[3072,3,768]{2,0,1:T(8,128)(2,1)}, f32[2,128]{1,0:T(2,128)S(1)}, ...), branch_computations={%region_0.15_spmd, %region_15.16_spmd} | conditional | flops 1100000000 | bytes 257951312 | solution.py:819
  78.0 1.7 %branch_1_fun.1 = (bf16[32,768]{1,0:T(8,128)(2,1)}, f32[32,1024]{1,0:T(8,128)}) custom-call(s32[6]{0:T(128)S(1)} %get-tuple-element.40.at, bf16[40,1152]{1,0:T(8,128)(2,1)S(1)} %get-tuple-element.41.sums, bf16[40,1152]{1,0:T(8,128)(2,1)S(1)} %get-tuple-element.42.head, bf16[40,1536]{1,0:T(8,128)(2,1)} %get-tuple-element.43.own, ...), custom_call_target="tpu_custom_call" | custom-call | flops 1100000000 | tf_op jit(solution)/shard_map/cond/branch_1_fun/pallas_call | solution.py:220
  (56 shorter events, 5.4 us)
Async XLA Ops:
  0.7 14.6 %copy-start.9 = (s32[1024]{0:T(1024)S(1)}, s32[1024]{0:T(1024)}, u32[]{:S(2)}) copy-start(s32[1024]{0:T(1024)} %param.16) | copy-start | bytes 12292
  0.7 14.6 %copy-start.10 = (s32[512]{0:T(512)S(1)}, s32[512]{0:T(512)}, u32[]{:S(2)}) copy-start(s32[512]{0:T(512)} %param.15) | copy-start | bytes 6148
  2.9 16.9 %collective-permute-start.2 = (bf16[32,3072]{1,0:T(8,128)(2,1)S(1)}, bf16[32,3072]{1,0:T(8,128)(2,1)S(1)}, u32[]{:S(2)}, u32[]{:S(2)}) collective-permute-start(bf16[32,3072]{1,0:T(8,128)(2,1)S(1)} %get-tuple-element.100.refs_0_), channel_id=1, source_target_pairs={{0,1},{1,0},{2,3},{3,2},{4,5},{5,4},{6,7},{7,6},{8,9},{9,8},{10,11... | collective-permute-start | bytes 589832 | tf_op jit(solution)/shard_map/ppermute | solution.py:205
  7.3 12.5 %collective-permute-start.4 = (bf16[32,3072]{1,0:T(8,128)(2,1)S(1)}, bf16[32,3072]{1,0:T(8,128)(2,1)S(1)}, u32[]{:S(2)}, u32[]{:S(2)}) collective-permute-start(bf16[32,3072]{1,0:T(8,128)(2,1)S(1)} %get-tuple-element.100.refs_0_), channel_id=1, source_target_pairs={{0,16},{1,17},{2,18},{3,19},{4,20},{5,21},{6,22},{7,23},{8,24},{9,... | collective-permute-start | bytes 589832 | tf_op jit(solution)/shard_map/ppermute | solution.py:205
  8.1 11.1 %collective-permute-start.7 = (bf16[32,3072]{1,0:T(8,128)(2,1)S(1)}, bf16[32,3072]{1,0:T(8,128)(2,1)S(1)}, u32[]{:S(2)}, u32[]{:S(2)}) collective-permute-start(bf16[32,3072]{1,0:T(8,128)(2,1)S(1)} %get-tuple-element.100.refs_0_), channel_id=1, source_target_pairs={{0,17},{1,16},{2,19},{3,18},{4,21},{5,20},{6,23},{7,22},{8,25},{9,... | collective-permute-start | bytes 589832 | tf_op jit(solution)/shard_map/ppermute | solution.py:205
  8.1 2.6 %collective-permute-start.1 = (bf16[48,3072]{1,0:T(8,128)(2,1)S(1)}, bf16[48,3072]{1,0:T(8,128)(2,1)S(1)}, u32[]{:S(2)}, u32[]{:S(2)}) collective-permute-start(bf16[48,3072]{1,0:T(8,128)(2,1)S(1)} %get-tuple-element.98), channel_id=1, source_target_pairs={{0,2},{1,3},{2,0},{3,1},{4,6},{5,7},{6,4},{7,5},{8,10},{9,11},{10,... | collective-permute-start | bytes 884744 | tf_op jit(solution)/shard_map/ppermute | solution.py:205
  11.3 8.4 %collective-permute-start.3 = (bf16[192,128]{1,0:T(8,128)(2,1)S(1)}, bf16[192,128]{1,0:T(8,128)(2,1)S(1)}, u32[]{:S(2)}, u32[]{:S(2)}) collective-permute-start(bf16[192,128]{1,0:T(8,128)(2,1)S(1)} %get-tuple-element.102), channel_id=1, source_target_pairs={{0,32},{1,33},{2,6},{3,7},{4,36},{5,37},{6,2},{7,3},{8,40},{9,41},... | collective-permute-start | bytes 147464 | tf_op jit(solution)/shard_map/ppermute | solution.py:205
  12.7 7.1 %collective-permute-start.5 = (bf16[192,128]{1,0:T(8,128)(2,1)S(1)}, bf16[192,128]{1,0:T(8,128)(2,1)S(1)}, u32[]{:S(2)}, u32[]{:S(2)}) collective-permute-start(bf16[192,128]{1,0:T(8,128)(2,1)S(1)} %get-tuple-element.104), channel_id=1, source_target_pairs={{0,64},{1,65},{2,10},{3,11},{4,68},{5,69},{6,14},{7,15},{8,72},{9,... | collective-permute-start | bytes 147464 | tf_op jit(solution)/shard_map/ppermute | solution.py:205
  15.3 7.7 %copy-start.11 = (f32[2,128]{1,0:T(2,128)S(1)}, f32[2,128]{1,0:T(2,128)}, u32[]{:S(2)}) copy-start(f32[2,128]{1,0:T(2,128)} %refs_9_.1) | copy-start | bytes 3076
  19.2 3.8 %collective-permute-start.10 = (bf16[32,3072]{1,0:T(8,128)(2,1)S(1)}, bf16[32,3072]{1,0:T(8,128)(2,1)S(1)}, u32[]{:S(2)}, u32[]{:S(2)}) collective-permute-start(bf16[32,3072]{1,0:T(8,128)(2,1)S(1)} %collective-permute-done.7.refs_3_), channel_id=1, source_target_pairs={{0,2},{1,3},{2,0},{3,1},{4,6},{5,7},{6,4},{7,5},{8,10},{9,11},{10,... | collective-permute-start | bytes 589832 | tf_op jit(solution)/shard_map/ppermute | solution.py:205
  19.7 3.3 %collective-permute-start.9 = (bf16[32,3072]{1,0:T(8,128)(2,1)S(1)}, bf16[32,3072]{1,0:T(8,128)(2,1)S(1)}, u32[]{:S(2)}, u32[]{:S(2)}) collective-permute-start(bf16[32,3072]{1,0:T(8,128)(2,1)S(1)} %collective-permute-done.2.refs_2_), channel_id=1, source_target_pairs={{0,2},{1,3},{2,0},{3,1},{4,6},{5,7},{6,4},{7,5},{8,10},{9,11},{10,... | collective-permute-start | bytes 589832 | tf_op jit(solution)/shard_map/ppermute | solution.py:205
  19.8 3.1 %collective-permute-start.8 = (bf16[32,3072]{1,0:T(8,128)(2,1)S(1)}, bf16[32,3072]{1,0:T(8,128)(2,1)S(1)}, u32[]{:S(2)}, u32[]{:S(2)}) collective-permute-start(bf16[32,3072]{1,0:T(8,128)(2,1)S(1)} %collective-permute-done.4.refs_1_), channel_id=1, source_target_pairs={{0,2},{1,3},{2,0},{3,1},{4,6},{5,7},{6,4},{7,5},{8,10},{9,11},{10,... | collective-permute-start | bytes 589832 | tf_op jit(solution)/shard_map/ppermute | solution.py:205
  20.3 7.0 %collective-permute-start.6 = (bf16[192,128]{1,0:T(8,128)(2,1)S(1)}, bf16[192,128]{1,0:T(8,128)(2,1)S(1)}, u32[]{:S(2)}, u32[]{:S(2)}) collective-permute-start(bf16[192,128]{1,0:T(8,128)(2,1)S(1)} %get-tuple-element.106), channel_id=1, source_target_pairs={{0,96},{1,97},{2,14},{3,15},{4,100},{5,101},{6,10},{7,11},{8,104},... | collective-permute-start | bytes 147464 | tf_op jit(solution)/shard_map/ppermute | solution.py:205
  27.1 5.9 %collective-permute-start.15 = (bf16[208,256]{1,0:T(8,128)(2,1)S(1)}, bf16[208,256]{1,0:T(8,128)(2,1)S(1)}, u32[]{:S(2)}, u32[]{:S(2)}) collective-permute-start(bf16[208,256]{1,0:T(8,128)(2,1)S(1)} %get-tuple-element.122), channel_id=1, source_target_pairs={{0,32},{1,33},{2,6},{3,7},{4,36},{5,37},{6,2},{7,3},{8,40},{9,41},... | collective-permute-start | bytes 319496 | tf_op jit(solution)/shard_map/ppermute | solution.py:205
  27.2 7.7 %collective-permute-start.16 = (bf16[208,256]{1,0:T(8,128)(2,1)S(1)}, bf16[208,256]{1,0:T(8,128)(2,1)S(1)}, u32[]{:S(2)}, u32[]{:S(2)}) collective-permute-start(bf16[208,256]{1,0:T(8,128)(2,1)S(1)} %get-tuple-element.123), channel_id=1, source_target_pairs={{0,64},{1,65},{2,10},{3,11},{4,68},{5,69},{6,14},{7,15},{8,72},{9,... | collective-permute-start | bytes 319496 | tf_op jit(solution)/shard_map/ppermute | solution.py:205
  29.6 5.4 %collective-permute-start.17 = (bf16[208,256]{1,0:T(8,128)(2,1)S(1)}, bf16[208,256]{1,0:T(8,128)(2,1)S(1)}, u32[]{:S(2)}, u32[]{:S(2)}) collective-permute-start(bf16[208,256]{1,0:T(8,128)(2,1)S(1)} %get-tuple-element.124), channel_id=1, source_target_pairs={{0,96},{1,97},{2,14},{3,15},{4,100},{5,101},{6,10},{7,11},{8,104},... | collective-permute-start | bytes 319496 | tf_op jit(solution)/shard_map/ppermute | solution.py:205
  31.1 6.7 %collective-permute-start.11 = (bf16[512,128]{1,0:T(8,128)(2,1)S(1)}, bf16[512,128]{1,0:T(8,128)(2,1)S(1)}, u32[]{:S(2)}, u32[]{:S(2)}) collective-permute-start(bf16[512,128]{1,0:T(8,128)(2,1)S(1)} %get-tuple-element.117.a), channel_id=1, source_target_pairs={{0,8},{1,9},{2,66},{3,67},{4,12},{5,13},{6,70},{7,71},{8,0},{9,1},... | collective-permute-start | bytes 393224 | tf_op jit(solution)/shard_map/ppermute | solution.py:205
  32.7 6.6 %collective-permute-start.12 = (bf16[512,128]{1,0:T(8,128)(2,1)S(1)}, bf16[512,128]{1,0:T(8,128)(2,1)S(1)}, u32[]{:S(2)}, u32[]{:S(2)}) collective-permute-start(bf16[512,128]{1,0:T(8,128)(2,1)S(1)} %get-tuple-element.117.a), channel_id=1, source_target_pairs={{0,4},{1,5},{2,34},{3,35},{4,0},{5,1},{6,38},{7,39},{8,12},{9,13},... | collective-permute-start | bytes 393224 | tf_op jit(solution)/shard_map/ppermute | solution.py:205
  33.0 6.3 %collective-permute-start.13 = (bf16[512,128]{1,0:T(8,128)(2,1)S(1)}, bf16[512,128]{1,0:T(8,128)(2,1)S(1)}, u32[]{:S(2)}, u32[]{:S(2)}) collective-permute-start(bf16[512,128]{1,0:T(8,128)(2,1)S(1)} %get-tuple-element.117.a), channel_id=1, source_target_pairs={{0,12},{1,13},{2,98},{3,99},{4,8},{5,9},{6,102},{7,103},{8,4},{9,5... | collective-permute-start | bytes 393224 | tf_op jit(solution)/shard_map/ppermute | solution.py:205
  35.3 6.4 %collective-permute-start.18 = (bf16[656,256]{1,0:T(8,128)(2,1)S(1)}, bf16[656,256]{1,0:T(8,128)(2,1)S(1)}, u32[]{:S(2)}, u32[]{:S(2)}) collective-permute-start(bf16[656,256]{1,0:T(8,128)(2,1)S(1)} %shard_map.121.l0), channel_id=1, source_target_pairs={{0,4},{1,5},{2,34},{3,35},{4,0},{5,1},{6,38},{7,39},{8,12},{9,13},... | collective-permute-start | bytes 1007624 | tf_op jit(solution)/shard_map/ppermute | solution.py:205
  35.4 10.7 %collective-permute-start.19 = (bf16[656,256]{1,0:T(8,128)(2,1)S(1)}, bf16[656,256]{1,0:T(8,128)(2,1)S(1)}, u32[]{:S(2)}, u32[]{:S(2)}) collective-permute-start(bf16[656,256]{1,0:T(8,128)(2,1)S(1)} %shard_map.121.l0), channel_id=1, source_target_pairs={{0,8},{1,9},{2,66},{3,67},{4,12},{5,13},{6,70},{7,71},{8,0},{9,1},... | collective-permute-start | bytes 1007624 | tf_op jit(solution)/shard_map/ppermute | solution.py:205
  37.8 11.1 %collective-permute-start.20 = (bf16[656,256]{1,0:T(8,128)(2,1)S(1)}, bf16[656,256]{1,0:T(8,128)(2,1)S(1)}, u32[]{:S(2)}, u32[]{:S(2)}) collective-permute-start(bf16[656,256]{1,0:T(8,128)(2,1)S(1)} %shard_map.121.l0), channel_id=1, source_target_pairs={{0,12},{1,13},{2,98},{3,99},{4,8},{5,9},{6,102},{7,103},{8,4},{9,5... | collective-permute-start | bytes 1007624 | tf_op jit(solution)/shard_map/ppermute | solution.py:205
  39.3 13.9 %collective-permute-start.14 = (bf16[2048,128]{1,0:T(8,128)(2,1)S(1)}, bf16[2048,128]{1,0:T(8,128)(2,1)S(1)}, u32[]{:S(2)}, u32[]{:S(2)}) collective-permute-start(bf16[2048,128]{1,0:T(8,128)(2,1)S(1)} %shard_map.120.plane), channel_id=1, source_target_pairs={{0,16},{1,17},{2,18},{3,19},{4,20},{5,21},{6,22},{7,23},{8,24},{9,... | collective-permute-start | bytes 1572872 | tf_op jit(solution)/shard_map/ppermute | solution.py:205
  55.6 4.3 %collective-permute-start.21 = (bf16[72,1152]{1,0:T(8,128)(2,1)S(1)}, bf16[72,1152]{1,0:T(8,128)(2,1)S(1)}, u32[]{:S(2)}, u32[]{:S(2)}) collective-permute-start(bf16[72,1152]{1,0:T(8,128)(2,1)S(1)} %get-tuple-element.138), channel_id=1, source_target_pairs={{0,32},{1,33},{2,6},{3,7},{4,36},{5,37},{6,2},{7,3},{8,40},{9,41},... | collective-permute-start | bytes 497672 | tf_op jit(solution)/shard_map/ppermute | solution.py:205
  55.7 6.6 %collective-permute-start.22 = (bf16[72,1152]{1,0:T(8,128)(2,1)S(1)}, bf16[72,1152]{1,0:T(8,128)(2,1)S(1)}, u32[]{:S(2)}, u32[]{:S(2)}) collective-permute-start(bf16[72,1152]{1,0:T(8,128)(2,1)S(1)} %get-tuple-element.139), channel_id=1, source_target_pairs={{0,64},{1,65},{2,10},{3,11},{4,68},{5,69},{6,14},{7,15},{8,72},{9,... | collective-permute-start | bytes 497672 | tf_op jit(solution)/shard_map/ppermute | solution.py:205
  57.8 6.3 %collective-permute-start.23 = (bf16[72,1152]{1,0:T(8,128)(2,1)S(1)}, bf16[72,1152]{1,0:T(8,128)(2,1)S(1)}, u32[]{:S(2)}, u32[]{:S(2)}) collective-permute-start(bf16[72,1152]{1,0:T(8,128)(2,1)S(1)} %get-tuple-element.140), channel_id=1, source_target_pairs={{0,96},{1,97},{2,14},{3,15},{4,100},{5,101},{6,10},{7,11},{8,104},... | collective-permute-start | bytes 497672 | tf_op jit(solution)/shard_map/ppermute | solution.py:205
  64.0 13.7 %copy-start = (bf16[256,3072]{1,0:T(8,128)(2,1)S(1)}, bf16[256,3072]{1,0:T(8,128)(2,1)}, u32[]{:S(2)}) copy-start(bf16[256,3072]{1,0:T(8,128)(2,1)} %table_ref.1) | copy-start | bytes 4718596
  64.0 13.7 %copy-start.4 = (bf16[32,768]{1,0:T(8,128)(2,1)S(1)}, bf16[32,768]{1,0:T(8,128)(2,1)}, u32[]{:S(2)}) copy-start(bf16[32,768]{1,0:T(8,128)(2,1)} %q_ref.1) | copy-start | bytes 147460
  64.0 13.7 %copy-start.7 = (bf16[32,768]{1,0:T(8,128)(2,1)S(1)}, bf16[32,768]{1,0:T(8,128)(2,1)}, u32[]{:S(2)}) copy-start(bf16[32,768]{1,0:T(8,128)(2,1)} %k_ref.1) | copy-start | bytes 147460
  64.0 13.7 %copy-start.8 = (bf16[32,768]{1,0:T(8,128)(2,1)S(1)}, bf16[32,768]{1,0:T(8,128)(2,1)}, u32[]{:S(2)}) copy-start(bf16[32,768]{1,0:T(8,128)(2,1)} %v_ref.1) | copy-start | bytes 147460
  64.9 7.3 %collective-permute-start.24 = (bf16[40,1536]{1,0:T(8,128)(2,1)S(1)}, bf16[40,1536]{1,0:T(8,128)(2,1)S(1)}, u32[]{:S(2)}, u32[]{:S(2)}) collective-permute-start(bf16[40,1536]{1,0:T(8,128)(2,1)S(1)} %get-tuple-element.142), channel_id=1, source_target_pairs={{0,2},{1,3},{2,0},{3,1},{4,6},{5,7},{6,4},{7,5},{8,10},{9,11},{10,... | collective-permute-start | bytes 368648 | tf_op jit(solution)/shard_map/ppermute | solution.py:205
  72.2 5.5 %collective-permute-start.25 = (bf16[40,1152]{1,0:T(8,128)(2,1)S(1)}, bf16[40,1152]{1,0:T(8,128)(2,1)S(1)}, u32[]{:S(2)}, u32[]{:S(2)}) collective-permute-start(bf16[40,1152]{1,0:T(8,128)(2,1)S(1)} %shard_map.127), channel_id=1, source_target_pairs={{0,1},{1,0},{2,3},{3,2},{4,5},{5,4},{6,7},{7,6},{8,9},{9,8},{10,11... | collective-permute-start | bytes 276488 | tf_op jit(solution)/shard_map/ppermute | solution.py:205
  (2 other events, 15.0 us)

commit v7 on v6

--- a/solution.py
+++ b/solution.py
@@ -243,25 +243,31 @@
     return ((ctx >> 4) << 2) | ((ctx >> 1) & 3)
 
 
-def ranks(keys, classes, resets):
-    n = keys.shape[1]
+def ranks(columns, pieces, reset):
+    n = columns.shape[1]
     blk = 256
     row = lax.broadcasted_iota(jnp.int32, (blk, blk), 0)
     col = lax.broadcasted_iota(jnp.int32, (blk, blk), 1)
     earlier = (row < col).astype(F32).astype(BF)
-    label = lax.broadcasted_iota(jnp.int32, (classes, blk), 0)
-    carry = jnp.zeros((classes, 1), F32)
-    found, counts = [], []
+    label = lax.broadcasted_iota(jnp.int32, (16, blk), 0)
+    label_piece = lax.broadcasted_iota(jnp.int32, (8, blk), 0)
+    carry, carry_piece = jnp.zeros((16, 1), F32), jnp.zeros((8, 1), F32)
+    spots, found, counts = [], [], []
     for b in range(n // blk):
-        if b in resets:
+        if b == reset:
             counts.append(carry)
-            carry = jnp.zeros((classes, 1), F32)
-        hot = (label == keys[:, b * blk : (b + 1) * blk]).astype(F32)
-        before = nn(hot.astype(BF), earlier) + carry
-        found.append(jnp.sum(hot * before, axis=0, keepdims=True))
+            carry = jnp.zeros((16, 1), F32)
+        lanes = slice(b * blk, (b + 1) * blk)
+        hot = (label == columns[:, lanes]).astype(F32)
+        hot_piece = (label_piece == pieces[:, lanes]).astype(F32)
+        before = nn(jnp.concatenate([hot, hot_piece], axis=0).astype(BF), earlier)
+        spots.append(jnp.sum(hot * (before[0:16] + carry), axis=0, keepdims=True))
+        found.append(jnp.sum(hot_piece * (before[16:24] + carry_piece), axis=0, keepdims=True))
         carry = carry + jnp.sum(hot, axis=1, keepdims=True)
+        carry_piece = carry_piece + jnp.sum(hot_piece, axis=1, keepdims=True)
     counts.append(carry)
-    return jnp.concatenate(found, axis=1).astype(jnp.int32), counts
+    spots, found = (jnp.concatenate(r, axis=1).astype(jnp.int32) for r in (spots, found))
+    return spots, found, counts
 
 
 def plan_kernel(
@@ -360,13 +366,7 @@
     return jnp.where(slot < per_lane(total, column), 0.0, -1e30)
 
 
-def pack_kernel(
-    at, con_ref, txt_ref, w_hbm, out_ref, spot_ref, con_bias, txt_bias, con_line, txt_line, w_ref, sem
-):
-    half = w_ref.shape[2]
-    lanes = pl.ds(pl.multiple_of(at[2] * half, half), half)
-    weights = pltpu.make_async_copy(w_hbm.at[0:2, :, lanes], w_ref, sem)
-    weights.start()
+def pack_kernel(at, con_ref, txt_ref, out_ref, spot_ref, con_bias, txt_bias, con_line, txt_line):
     ids = jnp.concatenate([con_ref[...], txt_ref[...]], axis=1)
     n = ids.shape[1]
     n_con = con_ref.shape[1]
@@ -376,8 +376,7 @@
     z = ((owner & 1) << 1) | ((owner >> 4) & 1)
     core = (owner >> 1) & 1
     piece = jnp.where(here, jnp.where(core == at[2], 0, 4) + (at[3] ^ z), -1)
-    rank, _ = ranks(piece, 8, ())
-    spot, (con_counts, txt_counts) = ranks(column, 16, (n_con // 256,))
+    spot, rank, (con_counts, txt_counts) = ranks(column, piece, n_con // 256)
     con_skip, con_total, con_most = line_plan(at, con_counts)
     txt_skip, txt_total, txt_most = line_plan(at, txt_counts)
     con_bias[...] = line_bias(at, con_total, LINE_CON)
@@ -405,21 +404,20 @@
         concept, jnp.where(spot < CON, spot, -1), jnp.where(spot < TXT, spot + CON, -1)
     )
     source = jnp.where(here & (rank < SLOTS), piece * SLOTS + rank, -1)
-    target = jnp.where(here, target, -1)
-    hot_t = (lax.broadcasted_iota(jnp.int32, (ROWS, n), 0) == target).astype(F32).astype(BF)
-    hot_s = (lax.broadcasted_iota(jnp.int32, (8 * SLOTS, n), 0) == source).astype(F32).astype(BF)
-    out_ref[...] = nt(hot_t, hot_s).astype(BF)
-    weights.wait()
+    label = lax.broadcasted_iota(jnp.int32, (8 * SLOTS, n), 0)
+    found = jnp.sum(
+        jnp.where(label == source, (target + 1).astype(F32), 0.0), axis=1, keepdims=True
+    )
+    hot = lax.broadcasted_iota(jnp.int32, (8 * SLOTS, 256), 1) == found.astype(jnp.int32) - 1
+    out_ref[...] = jnp.transpose(hot.astype(F32))[0:ROWS].astype(BF)
 
 
 def project_kernel(at, pack_ref, *refs):
-    rows, (mod_ref, gain_ref, w_ref, w_hbm), outs, (raw_ref, x_ref, w_last, sem) = (
-        refs[:8], refs[8:12], refs[12:16], refs[16:]
-    )
-    half = w_ref.shape[2]
+    rows, (mod_ref, gain_ref, w_ref), outs, (raw_ref, x_ref) = (
+        refs[:8], refs[8:11], refs[11:15], refs[15:]
+    )
+    half = w_ref.shape[2] // 2
     lanes = pl.ds(pl.multiple_of(at[2] * half, half), half)
-    weights = pltpu.make_async_copy(w_hbm.at[2, :, lanes], w_last, sem)
-    weights.start()
     for i, ref in enumerate(rows):
         raw_ref[i * SLOTS : (i + 1) * SLOTS, :] = ref[0:SLOTS, :]
     shift = mod_ref[0:1, :]
@@ -436,10 +434,9 @@
         meansq = jnp.mean(u * u, axis=1, keepdims=True)
         return u * lax.rsqrt(meansq + 1e-06) * gain
 
-    q = nn(x_ref[0:CON, :], w_ref[0])
-    k = nn(x_ref[...], w_ref[1])
-    weights.wait()
-    v = nn(x_ref[...], w_last[...])
+    q = nn(x_ref[0:CON, :], w_ref[0, :, lanes])
+    k = nn(x_ref[...], w_ref[1, :, lanes])
+    v = nn(x_ref[...], w_ref[2, :, lanes])
     heads = []
     for h in range(3):
         cols = slice(h * HD, (h + 1) * HD)
@@ -703,7 +700,7 @@
     core_both = send(own_both, swap_core())
 
     all_weights = jnp.transpose(txt_qkv, (1, 0, 2))
-    pack, spots, con_bias, txt_bias, con_line, txt_line, weights = call(
+    pack, spots, con_bias, txt_bias, con_line, txt_line = call(
         pack_kernel,
         (
             sds((ROWS, 8 * SLOTS)),
@@ -712,13 +709,9 @@
             sds((1, 4 * LINE_TXT), F32),
             sds((1, 4 * CON), jnp.int32),
             sds((1, 4 * TXT), jnp.int32),
-            sds((2, width, half)),
         ),
-        scratch=(pltpu.SemaphoreType.DMA,),
-        limit=24,
         us=2.0,
-        in_hbm=1,
-    )(at, con_ids, text_ids, all_weights)
+    )(at, con_ids, text_ids)
     shift_scale = lax.dynamic_index_in_dim(modulation, step_index[0], 0, keepdims=False)
 
     image_blocks = call(
@@ -739,13 +732,10 @@
         scratch=(
             pltpu.VMEM((8 * SLOTS, width), BF),
             pltpu.VMEM((ROWS, width), BF),
-            pltpu.VMEM((width, half), BF),
-            pltpu.SemaphoreType.DMA,
         ),
-        limit=24,
+        limit=28,
         us=PROJ_US,
-        in_hbm=1,
-    )(at, pack, *column_rows, *other_rows, shift_scale, qk_gain, weights, all_weights)
+    )(at, pack, *column_rows, *other_rows, shift_scale, qk_gain, all_weights)
 
     *image_blocks, first = lax.optimization_barrier((*image_blocks, qkv[0]))
     image_q, image_kv = call(

time: 79.9 us -> 88.2 us (1.10)
  waiting for transfers between devices: 14.1 us -> 22 us
  starting transfers between devices: 39.7 us -> 37.8 us
  Pallas kernels: 21.6 us -> 23.3 us
    ppermute x25, waiting for transfers between devices: 14.1 us -> 22 us  [send(): return lax.ppermute(array, ('ctx', 'head'), pairing)]
    ppermute x25, starting transfers between devices: 39.7 us -> 37.8 us  [send(): return lax.ppermute(array, ('ctx', 'head'), pairing)]
    pallas_call x14, Pallas kernels: 21.6 us -> 23.3 us  [run(): pl.pallas_call(kernel, out_shape=outs, in_specs=[sm] * smem + [vm] * (len...]
  transfers between devices with their start and end apart: 25 -> 25, of which waited for: 7 -> 9; matrix products, arithmetic and copies ran while one was open for 2% -> 2% of each run, Pallas kernels for 18% -> 18%
where the time goes in v7:
time: 88.2 us; the launch traced here: 87.9 us
  starting transfers between devices  37.8 us (43%)
  Pallas kernels  23.3 us (26%)
  waiting for transfers between devices  22 us (25%)
  between operations  2.14 us (2%)
  local copies, waits for them, and re-layouts  2.03 us (2%)
    ppermute x25, starting transfers between devices, send(): return lax.ppermute(array, ('ctx', 'head'), pairing)  37.8 us
    pallas_call x14, Pallas kernels, run(): pl.pallas_call(kernel, out_shape=outs, in_specs=[sm] * smem + [vm] * (len...  23.3 us
    ppermute x25, waiting for transfers between devices, send(): return lax.ppermute(array, ('ctx', 'head'), pairing)  22 us
  transfers between devices with their start and end apart: 25, of which 9 were waited for; matrix products, arithmetic and copies ran while one was open for 2% of the time, Pallas kernels for 18%

profile of v7, /device:TPU:1, one launch (start us, length us, event | category | flops | bytes accessed | tf_op | source)
XLA Modules:
  0.0 87.9 jit_solution(3367250205173165525)
XLA Ops:
  0.7 2.1 %shard_map.116 = (bf16[32,3072]{1,0:T(8,128)(2,1)S(1)}, bf16[48,3072]{1,0:T(8,128)(2,1)S(1)}, bf16[96,384]{1,0:T(8,128)(2,1)S(1)}) custom-call(s32[6]{0:T(128)S(1)} %stack.45.at, s32[1,1024]{1,0:T(1,128)} %bitcast.136, s32[1,512]{1,0:T(1,128)} %bitcast.138, bf16[256,3072]{1,0:T(8,128)(2,1)} %table_ref.1, bf16[32,768]{1,0:T(8,128)(2,1)} %q_ref.1, ...), custom_call_target="tpu_custom_call" | custom-call | flops 1100000000 | tf_op jit(solution)/shard_map/pallas_call | solution.py:220
  2.9 2.5 %collective-permute-start.4 = (bf16[32,3072]{1,0:T(8,128)(2,1)S(1)}, bf16[32,3072]{1,0:T(8,128)(2,1)S(1)}, u32[]{:S(2)}, u32[]{:S(2)}) collective-permute-start(bf16[32,3072]{1,0:T(8,128)(2,1)S(1)} %get-tuple-element.99.refs_0_), channel_id=1, source_target_pairs={{0,16},{1,17},{2,18},{3,19},{4,20},{5,21},{6,22},{7,23},{8,24},{9,... | collective-permute-start | bytes 589832 | tf_op jit(solution)/shard_map/ppermute | solution.py:205
  5.4 3.3 %collective-permute-start.2 = (bf16[32,3072]{1,0:T(8,128)(2,1)S(1)}, bf16[32,3072]{1,0:T(8,128)(2,1)S(1)}, u32[]{:S(2)}, u32[]{:S(2)}) collective-permute-start(bf16[32,3072]{1,0:T(8,128)(2,1)S(1)} %get-tuple-element.99.refs_0_), channel_id=1, source_target_pairs={{0,1},{1,0},{2,3},{3,2},{4,5},{5,4},{6,7},{7,6},{8,9},{9,8},{10,11... | collective-permute-start | bytes 589832 | tf_op jit(solution)/shard_map/ppermute | solution.py:205
  8.7 1.2 %collective-permute-start.1 = (bf16[48,3072]{1,0:T(8,128)(2,1)S(1)}, bf16[48,3072]{1,0:T(8,128)(2,1)S(1)}, u32[]{:S(2)}, u32[]{:S(2)}) collective-permute-start(bf16[48,3072]{1,0:T(8,128)(2,1)S(1)} %get-tuple-element.97), channel_id=1, source_target_pairs={{0,2},{1,3},{2,0},{3,1},{4,6},{5,7},{6,4},{7,5},{8,10},{9,11},{10,... | collective-permute-start | bytes 884744 | tf_op jit(solution)/shard_map/ppermute | solution.py:205
  10.6 0.7 dynamic-slice_bitcast_fusion.refs_8_
  11.9 3.0 %collective-permute-start.5 = (bf16[192,128]{1,0:T(8,128)(2,1)S(1)}, bf16[192,128]{1,0:T(8,128)(2,1)S(1)}, u32[]{:S(2)}, u32[]{:S(2)}) collective-permute-start(bf16[192,128]{1,0:T(8,128)(2,1)S(1)} %get-tuple-element.103), channel_id=1, source_target_pairs={{0,64},{1,65},{2,10},{3,11},{4,68},{5,69},{6,14},{7,15},{8,72},{9,... | collective-permute-start | bytes 147464 | tf_op jit(solution)/shard_map/ppermute | solution.py:205
  15.3 1.3 %shard_map.115 = (bf16[160,256]{1,0:T(8,128)(2,1)S(1)}, s32[8,1536]{1,0:T(8,128)S(1)}, f32[1,1280]{1,0:T(1,128)S(1)}, f32[1,704]{1,0:T(1,128)S(1)}, s32[1,384]{1,0:T(1,128)S(1)}, /*index=5*/s32[1,256]{1,0:T(1,128)S(1)}) custom-call(s32[6]{0:T(128)S(1)} %stack.45.at, s32[1,1024]{1,0:T(1,128)S(1)} %bitcast.137, s32[1,512]{1,0:T(1,128)S(1)} %bitcast.139), custom_call_target="tpu_custom_call" | custom-call | flops 2200000000 | tf_op jit(solution)/shard_map/pallas_call | solution.py:220
  16.6 3.3 %collective-permute-done.7.refs_3_ = bf16[32,3072]{1,0:T(8,128)(2,1)S(1)} collective-permute-done((bf16[32,3072]{1,0:T(8,128)(2,1)S(1)}, bf16[32,3072]{1,0:T(8,128)(2,1)S(1)}, u32[]{:S(2)}, u32[]{:S(2)}) %collective-permute-start.7) | collective-permute-done | bytes 196640 | tf_op jit(solution)/shard_map/ppermute | solution.py:205
  19.9 1.5 %collective-permute-start.10 = (bf16[32,3072]{1,0:T(8,128)(2,1)S(1)}, bf16[32,3072]{1,0:T(8,128)(2,1)S(1)}, u32[]{:S(2)}, u32[]{:S(2)}) collective-permute-start(bf16[32,3072]{1,0:T(8,128)(2,1)S(1)} %collective-permute-done.7.refs_3_), channel_id=1, source_target_pairs={{0,2},{1,3},{2,0},{3,1},{4,6},{5,7},{6,4},{7,5},{8,10},{9,11},{10,... | collective-permute-start | bytes 589832 | tf_op jit(solution)/shard_map/ppermute | solution.py:205
  22.0 2.7 %collective-permute-start.6 = (bf16[192,128]{1,0:T(8,128)(2,1)S(1)}, bf16[192,128]{1,0:T(8,128)(2,1)S(1)}, u32[]{:S(2)}, u32[]{:S(2)}) collective-permute-start(bf16[192,128]{1,0:T(8,128)(2,1)S(1)} %get-tuple-element.105), channel_id=1, source_target_pairs={{0,96},{1,97},{2,14},{3,15},{4,100},{5,101},{6,10},{7,11},{8,104},... | collective-permute-start | bytes 147464 | tf_op jit(solution)/shard_map/ppermute | solution.py:205
  24.7 8.3 %shard_map.118 = (bf16[208,256]{1,0:T(8,128)(2,1)S(1)}, bf16[208,256]{1,0:T(8,128)(2,1)S(1)}, bf16[208,256]{1,0:T(8,128)(2,1)S(1)}, bf16[208,256]{1,0:T(8,128)(2,1)S(1)}) custom-call(s32[6]{0:T(128)S(1)} %stack.45.at, bf16[160,256]{1,0:T(8,128)(2,1)S(1)} %get-tuple-element.106.pack_ref, bf16[32,3072]{1,0:T(8,128)(2,1)S(1)} %get-tuple-element.99.refs_0_, ...), custom_call_target="tpu_custom_call" | custom-call | flops 5500000256 | tf_op jit(solution)/shard_map/pallas_call | solution.py:220
  33.1 2.3 %collective-permute-start.16 = (bf16[208,256]{1,0:T(8,128)(2,1)S(1)}, bf16[208,256]{1,0:T(8,128)(2,1)S(1)}, u32[]{:S(2)}, u32[]{:S(2)}) collective-permute-start(bf16[208,256]{1,0:T(8,128)(2,1)S(1)} %get-tuple-element.121), channel_id=1, source_target_pairs={{0,64},{1,65},{2,10},{3,11},{4,68},{5,69},{6,14},{7,15},{8,72},{9,... | collective-permute-start | bytes 319496 | tf_op jit(solution)/shard_map/ppermute | solution.py:205
  35.4 1.5 %collective-permute-start.17 = (bf16[208,256]{1,0:T(8,128)(2,1)S(1)}, bf16[208,256]{1,0:T(8,128)(2,1)S(1)}, u32[]{:S(2)}, u32[]{:S(2)}) collective-permute-start(bf16[208,256]{1,0:T(8,128)(2,1)S(1)} %get-tuple-element.122), channel_id=1, source_target_pairs={{0,96},{1,97},{2,14},{3,15},{4,100},{5,101},{6,10},{7,11},{8,104},... | collective-permute-start | bytes 319496 | tf_op jit(solution)/shard_map/ppermute | solution.py:205
  37.0 2.8 %collective-permute-start.11 = (bf16[512,128]{1,0:T(8,128)(2,1)S(1)}, bf16[512,128]{1,0:T(8,128)(2,1)S(1)}, u32[]{:S(2)}, u32[]{:S(2)}) collective-permute-start(bf16[512,128]{1,0:T(8,128)(2,1)S(1)} %get-tuple-element.115.a), channel_id=1, source_target_pairs={{0,8},{1,9},{2,66},{3,67},{4,12},{5,13},{6,70},{7,71},{8,0},{9,1},... | collective-permute-start | bytes 393224 | tf_op jit(solution)/shard_map/ppermute | solution.py:205
  41.5 1.7 %collective-permute-start.18 = (bf16[656,256]{1,0:T(8,128)(2,1)S(1)}, bf16[656,256]{1,0:T(8,128)(2,1)S(1)}, u32[]{:S(2)}, u32[]{:S(2)}) collective-permute-start(bf16[656,256]{1,0:T(8,128)(2,1)S(1)} %shard_map.121.l0), channel_id=1, source_target_pairs={{0,4},{1,5},{2,34},{3,35},{4,0},{5,1},{6,38},{7,39},{8,12},{9,13},... | collective-permute-start | bytes 1007624 | tf_op jit(solution)/shard_map/ppermute | solution.py:205
  43.3 1.7 %collective-permute-start.19 = (bf16[656,256]{1,0:T(8,128)(2,1)S(1)}, bf16[656,256]{1,0:T(8,128)(2,1)S(1)}, u32[]{:S(2)}, u32[]{:S(2)}) collective-permute-start(bf16[656,256]{1,0:T(8,128)(2,1)S(1)} %shard_map.121.l0), channel_id=1, source_target_pairs={{0,8},{1,9},{2,66},{3,67},{4,12},{5,13},{6,70},{7,71},{8,0},{9,1},... | collective-permute-start | bytes 1007624 | tf_op jit(solution)/shard_map/ppermute | solution.py:205
  44.9 0.8 collective-permute-start.20
  46.6 0.8 shard_map.123
  48.6 4.8 %collective-permute-done.19.l2 = bf16[656,256]{1,0:T(8,128)(2,1)S(1)} collective-permute-done((bf16[656,256]{1,0:T(8,128)(2,1)S(1)}, bf16[656,256]{1,0:T(8,128)(2,1)S(1)}, u32[]{:S(2)}, u32[]{:S(2)}) %collective-permute-start.19) | collective-permute-done | bytes 335904 | tf_op jit(solution)/shard_map/ppermute | solution.py:205
  53.4 2.6 %collective-permute-done.20.l3 = bf16[656,256]{1,0:T(8,128)(2,1)S(1)} collective-permute-done((bf16[656,256]{1,0:T(8,128)(2,1)S(1)}, bf16[656,256]{1,0:T(8,128)(2,1)S(1)}, u32[]{:S(2)}, u32[]{:S(2)}) %collective-permute-start.20) | collective-permute-done | bytes 335904 | tf_op jit(solution)/shard_map/ppermute | solution.py:205
  56.0 4.2 %shard_map.124 = (bf16[1024,128]{1,0:T(8,128)(2,1)S(1)}, f32[1024,1]{1,0:T(8,128)S(1)}, f32[1024,256]{1,0:T(8,128)S(1)}, f32[256,1]{1,0:T(8,128)S(1)}, f32[256,256]{1,0:T(8,128)S(1)}) custom-call(bf16[1024,1280]{1,0:T(8,128)(2,1)S(1)} %fusion.81.pick, bf16[1024,128]{1,0:T(8,128)(2,1)S(1)} %shard_map.122.q_part, bf16[656,256]{1,0:T(8,128)(2,1)S(1)} %shard_map.121.l0, ...), custom_call_target="tpu_custom_call" | custom-call | flops 2200000000 | tf_op jit(solution)/shard_map/pallas_call | solution.py:220
  60.3 2.5 %shard_map.125 = (bf16[72,1152]{1,0:T(8,128)(2,1)S(1)}, bf16[72,1152]{1,0:T(8,128)(2,1)S(1)}, bf16[72,1152]{1,0:T(8,128)(2,1)S(1)}, bf16[72,1152]{1,0:T(8,128)(2,1)S(1)}) custom-call(bf16[2048,128]{1,0:T(8,128)(2,1)S(1)} %collective-permute-done.14.plane, bf16[1024,128]{1,0:T(8,128)(2,1)S(1)} %get-tuple-element.130.con_q, ...), custom_call_target="tpu_custom_call" | custom-call | flops 3300000000 | tf_op jit(solution)/shard_map/pallas_call | solution.py:220
  62.8 2.3 %collective-permute-start.22 = (bf16[72,1152]{1,0:T(8,128)(2,1)S(1)}, bf16[72,1152]{1,0:T(8,128)(2,1)S(1)}, u32[]{:S(2)}, u32[]{:S(2)}) collective-permute-start(bf16[72,1152]{1,0:T(8,128)(2,1)S(1)} %get-tuple-element.137), channel_id=1, source_target_pairs={{0,64},{1,65},{2,10},{3,11},{4,68},{5,69},{6,14},{7,15},{8,72},{9,... | collective-permute-start | bytes 497672 | tf_op jit(solution)/shard_map/ppermute | solution.py:205
  65.2 1.5 %collective-permute-start.23 = (bf16[72,1152]{1,0:T(8,128)(2,1)S(1)}, bf16[72,1152]{1,0:T(8,128)(2,1)S(1)}, u32[]{:S(2)}, u32[]{:S(2)}) collective-permute-start(bf16[72,1152]{1,0:T(8,128)(2,1)S(1)} %get-tuple-element.138), channel_id=1, source_target_pairs={{0,96},{1,97},{2,14},{3,15},{4,100},{5,101},{6,10},{7,11},{8,104},... | collective-permute-start | bytes 497672 | tf_op jit(solution)/shard_map/ppermute | solution.py:205
  67.0 2.8 %collective-permute-done.22.b2 = bf16[72,1152]{1,0:T(8,128)(2,1)S(1)} collective-permute-done((bf16[72,1152]{1,0:T(8,128)(2,1)S(1)}, bf16[72,1152]{1,0:T(8,128)(2,1)S(1)}, u32[]{:S(2)}, u32[]{:S(2)}) %collective-permute-start.22) | collective-permute-done | bytes 165920 | tf_op jit(solution)/shard_map/ppermute | solution.py:205
  69.8 1.7 %collective-permute-done.23.b3 = bf16[72,1152]{1,0:T(8,128)(2,1)S(1)} collective-permute-done((bf16[72,1152]{1,0:T(8,128)(2,1)S(1)}, bf16[72,1152]{1,0:T(8,128)(2,1)S(1)}, u32[]{:S(2)}, u32[]{:S(2)}) %collective-permute-start.23) | collective-permute-done | bytes 165920 | tf_op jit(solution)/shard_map/ppermute | solution.py:205
  71.5 0.8 shard_map.126
  72.3 6.4 %collective-permute-start.24 = (bf16[40,1536]{1,0:T(8,128)(2,1)S(1)}, bf16[40,1536]{1,0:T(8,128)(2,1)S(1)}, u32[]{:S(2)}, u32[]{:S(2)}) collective-permute-start(bf16[40,1536]{1,0:T(8,128)(2,1)S(1)} %get-tuple-element.140), channel_id=1, source_target_pairs={{0,2},{1,3},{2,0},{3,1},{4,6},{5,7},{6,4},{7,5},{8,10},{9,11},{10,... | collective-permute-start | bytes 368648 | tf_op jit(solution)/shard_map/ppermute | solution.py:205
  78.7 1.0 %collective-permute-done.24.core = bf16[40,1536]{1,0:T(8,128)(2,1)S(1)} collective-permute-done((bf16[40,1536]{1,0:T(8,128)(2,1)S(1)}, bf16[40,1536]{1,0:T(8,128)(2,1)S(1)}, u32[]{:S(2)}, u32[]{:S(2)}) %collective-permute-start.24) | collective-permute-done | bytes 122912 | tf_op jit(solution)/shard_map/ppermute | solution.py:205
  81.1 4.7 %collective-permute-done.25 = bf16[40,1152]{1,0:T(8,128)(2,1)S(1)} collective-permute-done((bf16[40,1152]{1,0:T(8,128)(2,1)S(1)}, bf16[40,1152]{1,0:T(8,128)(2,1)S(1)}, u32[]{:S(2)}, u32[]{:S(2)}) %collective-permute-start.25) | collective-permute-done | bytes 92192 | tf_op jit(solution)/shard_map/ppermute | solution.py:205
  85.9 2.0 %conditional.1 = (bf16[32,768]{1,0:T(8,128)(2,1)}, f32[1024,32]{0,1:T(8,128)}) conditional(s32[]{:T(128)} %convert_element_type.62, (s32[512]{0:T(512)S(1)}, s32[1024]{0:T(1024)S(1)}, bf16[256,3072]{1,0:T(8,128)(2,1)S(1)}, s32[1]{0:T(128)}, f32[28,2,3072]{2,1,0:T(2,128)}, /*index=5*/bf16[3072,3,768]{2,0,1:T(8,128)(2,1)}, f32[2,128]{1,0:T(2,128)S(1)}, ...), branch_computations={%region_0.15_spmd, %region_15.16_spmd} | conditional | flops 1100000000 | bytes 257951312 | solution.py:809
  86.2 1.7 %branch_1_fun.1 = (bf16[32,768]{1,0:T(8,128)(2,1)}, f32[32,1024]{1,0:T(8,128)}) custom-call(s32[6]{0:T(128)S(1)} %get-tuple-element.40.at, bf16[40,1152]{1,0:T(8,128)(2,1)S(1)} %get-tuple-element.41.sums, bf16[40,1152]{1,0:T(8,128)(2,1)S(1)} %get-tuple-element.42.head, bf16[40,1536]{1,0:T(8,128)(2,1)} %get-tuple-element.43.own, ...), custom_call_target="tpu_custom_call" | custom-call | flops 1100000000 | tf_op jit(solution)/shard_map/cond/branch_1_fun/pallas_call | solution.py:220
  (56 shorter events, 6.7 us)
Async XLA Ops:
  0.7 14.6 %copy-start.8 = (s32[1024]{0:T(1024)S(1)}, s32[1024]{0:T(1024)}, u32[]{:S(2)}) copy-start(s32[1024]{0:T(1024)} %param.16) | copy-start | bytes 12292
  0.7 14.6 %copy-start.9 = (s32[512]{0:T(512)S(1)}, s32[512]{0:T(512)}, u32[]{:S(2)}) copy-start(s32[512]{0:T(512)} %param.15) | copy-start | bytes 6148
  2.9 18.6 %collective-permute-start.4 = (bf16[32,3072]{1,0:T(8,128)(2,1)S(1)}, bf16[32,3072]{1,0:T(8,128)(2,1)S(1)}, u32[]{:S(2)}, u32[]{:S(2)}) collective-permute-start(bf16[32,3072]{1,0:T(8,128)(2,1)S(1)} %get-tuple-element.99.refs_0_), channel_id=1, source_target_pairs={{0,16},{1,17},{2,18},{3,19},{4,20},{5,21},{6,22},{7,23},{8,24},{9,... | collective-permute-start | bytes 589832 | tf_op jit(solution)/shard_map/ppermute | solution.py:205
  5.4 16.1 %collective-permute-start.2 = (bf16[32,3072]{1,0:T(8,128)(2,1)S(1)}, bf16[32,3072]{1,0:T(8,128)(2,1)S(1)}, u32[]{:S(2)}, u32[]{:S(2)}) collective-permute-start(bf16[32,3072]{1,0:T(8,128)(2,1)S(1)} %get-tuple-element.99.refs_0_), channel_id=1, source_target_pairs={{0,1},{1,0},{2,3},{3,2},{4,5},{5,4},{6,7},{7,6},{8,9},{9,8},{10,11... | collective-permute-start | bytes 589832 | tf_op jit(solution)/shard_map/ppermute | solution.py:205
  8.7 11.2 %collective-permute-start.7 = (bf16[32,3072]{1,0:T(8,128)(2,1)S(1)}, bf16[32,3072]{1,0:T(8,128)(2,1)S(1)}, u32[]{:S(2)}, u32[]{:S(2)}) collective-permute-start(bf16[32,3072]{1,0:T(8,128)(2,1)S(1)} %get-tuple-element.99.refs_0_), channel_id=1, source_target_pairs={{0,17},{1,16},{2,19},{3,18},{4,21},{5,20},{6,23},{7,22},{8,25},{9,... | collective-permute-start | bytes 589832 | tf_op jit(solution)/shard_map/ppermute | solution.py:205
  8.7 2.6 %collective-permute-start.1 = (bf16[48,3072]{1,0:T(8,128)(2,1)S(1)}, bf16[48,3072]{1,0:T(8,128)(2,1)S(1)}, u32[]{:S(2)}, u32[]{:S(2)}) collective-permute-start(bf16[48,3072]{1,0:T(8,128)(2,1)S(1)} %get-tuple-element.97), channel_id=1, source_target_pairs={{0,2},{1,3},{2,0},{3,1},{4,6},{5,7},{6,4},{7,5},{8,10},{9,11},{10,... | collective-permute-start | bytes 884744 | tf_op jit(solution)/shard_map/ppermute | solution.py:205
  11.9 9.5 %collective-permute-start.5 = (bf16[192,128]{1,0:T(8,128)(2,1)S(1)}, bf16[192,128]{1,0:T(8,128)(2,1)S(1)}, u32[]{:S(2)}, u32[]{:S(2)}) collective-permute-start(bf16[192,128]{1,0:T(8,128)(2,1)S(1)} %get-tuple-element.103), channel_id=1, source_target_pairs={{0,64},{1,65},{2,10},{3,11},{4,68},{5,69},{6,14},{7,15},{8,72},{9,... | collective-permute-start | bytes 147464 | tf_op jit(solution)/shard_map/ppermute | solution.py:205
  14.9 9.8 %copy-start.10 = (f32[2,128]{1,0:T(2,128)S(1)}, f32[2,128]{1,0:T(2,128)}, u32[]{:S(2)}) copy-start(f32[2,128]{1,0:T(2,128)} %refs_9_.1) | copy-start | bytes 3076
  14.9 6.6 %collective-permute-start.3 = (bf16[192,128]{1,0:T(8,128)(2,1)S(1)}, bf16[192,128]{1,0:T(8,128)(2,1)S(1)}, u32[]{:S(2)}, u32[]{:S(2)}) collective-permute-start(bf16[192,128]{1,0:T(8,128)(2,1)S(1)} %get-tuple-element.101), channel_id=1, source_target_pairs={{0,32},{1,33},{2,6},{3,7},{4,36},{5,37},{6,2},{7,3},{8,40},{9,41},... | collective-permute-start | bytes 147464 | tf_op jit(solution)/shard_map/ppermute | solution.py:205
  19.9 4.8 %collective-permute-start.10 = (bf16[32,3072]{1,0:T(8,128)(2,1)S(1)}, bf16[32,3072]{1,0:T(8,128)(2,1)S(1)}, u32[]{:S(2)}, u32[]{:S(2)}) collective-permute-start(bf16[32,3072]{1,0:T(8,128)(2,1)S(1)} %collective-permute-done.7.refs_3_), channel_id=1, source_target_pairs={{0,2},{1,3},{2,0},{3,1},{4,6},{5,7},{6,4},{7,5},{8,10},{9,11},{10,... | collective-permute-start | bytes 589832 | tf_op jit(solution)/shard_map/ppermute | solution.py:205
  21.4 3.3 %collective-permute-start.8 = (bf16[32,3072]{1,0:T(8,128)(2,1)S(1)}, bf16[32,3072]{1,0:T(8,128)(2,1)S(1)}, u32[]{:S(2)}, u32[]{:S(2)}) collective-permute-start(bf16[32,3072]{1,0:T(8,128)(2,1)S(1)} %collective-permute-done.4.refs_1_), channel_id=1, source_target_pairs={{0,2},{1,3},{2,0},{3,1},{4,6},{5,7},{6,4},{7,5},{8,10},{9,11},{10,... | collective-permute-start | bytes 589832 | tf_op jit(solution)/shard_map/ppermute | solution.py:205
  21.5 3.2 %collective-permute-start.9 = (bf16[32,3072]{1,0:T(8,128)(2,1)S(1)}, bf16[32,3072]{1,0:T(8,128)(2,1)S(1)}, u32[]{:S(2)}, u32[]{:S(2)}) collective-permute-start(bf16[32,3072]{1,0:T(8,128)(2,1)S(1)} %collective-permute-done.2.refs_2_), channel_id=1, source_target_pairs={{0,2},{1,3},{2,0},{3,1},{4,6},{5,7},{6,4},{7,5},{8,10},{9,11},{10,... | collective-permute-start | bytes 589832 | tf_op jit(solution)/shard_map/ppermute | solution.py:205
  22.0 15.0 %collective-permute-start.6 = (bf16[192,128]{1,0:T(8,128)(2,1)S(1)}, bf16[192,128]{1,0:T(8,128)(2,1)S(1)}, u32[]{:S(2)}, u32[]{:S(2)}) collective-permute-start(bf16[192,128]{1,0:T(8,128)(2,1)S(1)} %get-tuple-element.105), channel_id=1, source_target_pairs={{0,96},{1,97},{2,14},{3,15},{4,100},{5,101},{6,10},{7,11},{8,104},... | collective-permute-start | bytes 147464 | tf_op jit(solution)/shard_map/ppermute | solution.py:205
  33.0 7.1 %collective-permute-start.15 = (bf16[208,256]{1,0:T(8,128)(2,1)S(1)}, bf16[208,256]{1,0:T(8,128)(2,1)S(1)}, u32[]{:S(2)}, u32[]{:S(2)}) collective-permute-start(bf16[208,256]{1,0:T(8,128)(2,1)S(1)} %get-tuple-element.120), channel_id=1, source_target_pairs={{0,32},{1,33},{2,6},{3,7},{4,36},{5,37},{6,2},{7,3},{8,40},{9,41},... | collective-permute-start | bytes 319496 | tf_op jit(solution)/shard_map/ppermute | solution.py:205
  33.1 8.1 %collective-permute-start.16 = (bf16[208,256]{1,0:T(8,128)(2,1)S(1)}, bf16[208,256]{1,0:T(8,128)(2,1)S(1)}, u32[]{:S(2)}, u32[]{:S(2)}) collective-permute-start(bf16[208,256]{1,0:T(8,128)(2,1)S(1)} %get-tuple-element.121), channel_id=1, source_target_pairs={{0,64},{1,65},{2,10},{3,11},{4,68},{5,69},{6,14},{7,15},{8,72},{9,... | collective-permute-start | bytes 319496 | tf_op jit(solution)/shard_map/ppermute | solution.py:205
  35.4 5.7 %collective-permute-start.17 = (bf16[208,256]{1,0:T(8,128)(2,1)S(1)}, bf16[208,256]{1,0:T(8,128)(2,1)S(1)}, u32[]{:S(2)}, u32[]{:S(2)}) collective-permute-start(bf16[208,256]{1,0:T(8,128)(2,1)S(1)} %get-tuple-element.122), channel_id=1, source_target_pairs={{0,96},{1,97},{2,14},{3,15},{4,100},{5,101},{6,10},{7,11},{8,104},... | collective-permute-start | bytes 319496 | tf_op jit(solution)/shard_map/ppermute | solution.py:205
  37.0 8.0 %collective-permute-start.11 = (bf16[512,128]{1,0:T(8,128)(2,1)S(1)}, bf16[512,128]{1,0:T(8,128)(2,1)S(1)}, u32[]{:S(2)}, u32[]{:S(2)}) collective-permute-start(bf16[512,128]{1,0:T(8,128)(2,1)S(1)} %get-tuple-element.115.a), channel_id=1, source_target_pairs={{0,8},{1,9},{2,66},{3,67},{4,12},{5,13},{6,70},{7,71},{8,0},{9,1},... | collective-permute-start | bytes 393224 | tf_op jit(solution)/shard_map/ppermute | solution.py:205
  39.8 6.0 %collective-permute-start.12 = (bf16[512,128]{1,0:T(8,128)(2,1)S(1)}, bf16[512,128]{1,0:T(8,128)(2,1)S(1)}, u32[]{:S(2)}, u32[]{:S(2)}) collective-permute-start(bf16[512,128]{1,0:T(8,128)(2,1)S(1)} %get-tuple-element.115.a), channel_id=1, source_target_pairs={{0,4},{1,5},{2,34},{3,35},{4,0},{5,1},{6,38},{7,39},{8,12},{9,13},... | collective-permute-start | bytes 393224 | tf_op jit(solution)/shard_map/ppermute | solution.py:205
  40.1 5.7 %collective-permute-start.13 = (bf16[512,128]{1,0:T(8,128)(2,1)S(1)}, bf16[512,128]{1,0:T(8,128)(2,1)S(1)}, u32[]{:S(2)}, u32[]{:S(2)}) collective-permute-start(bf16[512,128]{1,0:T(8,128)(2,1)S(1)} %get-tuple-element.115.a), channel_id=1, source_target_pairs={{0,12},{1,13},{2,98},{3,99},{4,8},{5,9},{6,102},{7,103},{8,4},{9,5... | collective-permute-start | bytes 393224 | tf_op jit(solution)/shard_map/ppermute | solution.py:205
  41.5 6.6 %collective-permute-start.18 = (bf16[656,256]{1,0:T(8,128)(2,1)S(1)}, bf16[656,256]{1,0:T(8,128)(2,1)S(1)}, u32[]{:S(2)}, u32[]{:S(2)}) collective-permute-start(bf16[656,256]{1,0:T(8,128)(2,1)S(1)} %shard_map.121.l0), channel_id=1, source_target_pairs={{0,4},{1,5},{2,34},{3,35},{4,0},{5,1},{6,38},{7,39},{8,12},{9,13},... | collective-permute-start | bytes 1007624 | tf_op jit(solution)/shard_map/ppermute | solution.py:205
  43.3 10.1 %collective-permute-start.19 = (bf16[656,256]{1,0:T(8,128)(2,1)S(1)}, bf16[656,256]{1,0:T(8,128)(2,1)S(1)}, u32[]{:S(2)}, u32[]{:S(2)}) collective-permute-start(bf16[656,256]{1,0:T(8,128)(2,1)S(1)} %shard_map.121.l0), channel_id=1, source_target_pairs={{0,8},{1,9},{2,66},{3,67},{4,12},{5,13},{6,70},{7,71},{8,0},{9,1},... | collective-permute-start | bytes 1007624 | tf_op jit(solution)/shard_map/ppermute | solution.py:205
  44.9 11.1 %collective-permute-start.20 = (bf16[656,256]{1,0:T(8,128)(2,1)S(1)}, bf16[656,256]{1,0:T(8,128)(2,1)S(1)}, u32[]{:S(2)}, u32[]{:S(2)}) collective-permute-start(bf16[656,256]{1,0:T(8,128)(2,1)S(1)} %shard_map.121.l0), channel_id=1, source_target_pairs={{0,12},{1,13},{2,98},{3,99},{4,8},{5,9},{6,102},{7,103},{8,4},{9,5... | collective-permute-start | bytes 1007624 | tf_op jit(solution)/shard_map/ppermute | solution.py:205
  45.8 14.5 %collective-permute-start.14 = (bf16[2048,128]{1,0:T(8,128)(2,1)S(1)}, bf16[2048,128]{1,0:T(8,128)(2,1)S(1)}, u32[]{:S(2)}, u32[]{:S(2)}) collective-permute-start(bf16[2048,128]{1,0:T(8,128)(2,1)S(1)} %shard_map.120.plane), channel_id=1, source_target_pairs={{0,16},{1,17},{2,18},{3,19},{4,20},{5,21},{6,22},{7,23},{8,24},{9,... | collective-permute-start | bytes 1572872 | tf_op jit(solution)/shard_map/ppermute | solution.py:205
  62.8 4.3 %collective-permute-start.21 = (bf16[72,1152]{1,0:T(8,128)(2,1)S(1)}, bf16[72,1152]{1,0:T(8,128)(2,1)S(1)}, u32[]{:S(2)}, u32[]{:S(2)}) collective-permute-start(bf16[72,1152]{1,0:T(8,128)(2,1)S(1)} %get-tuple-element.136), channel_id=1, source_target_pairs={{0,32},{1,33},{2,6},{3,7},{4,36},{5,37},{6,2},{7,3},{8,40},{9,41},... | collective-permute-start | bytes 497672 | tf_op jit(solution)/shard_map/ppermute | solution.py:205
  62.8 6.9 %collective-permute-start.22 = (bf16[72,1152]{1,0:T(8,128)(2,1)S(1)}, bf16[72,1152]{1,0:T(8,128)(2,1)S(1)}, u32[]{:S(2)}, u32[]{:S(2)}) collective-permute-start(bf16[72,1152]{1,0:T(8,128)(2,1)S(1)} %get-tuple-element.137), channel_id=1, source_target_pairs={{0,64},{1,65},{2,10},{3,11},{4,68},{5,69},{6,14},{7,15},{8,72},{9,... | collective-permute-start | bytes 497672 | tf_op jit(solution)/shard_map/ppermute | solution.py:205
  65.2 6.3 %collective-permute-start.23 = (bf16[72,1152]{1,0:T(8,128)(2,1)S(1)}, bf16[72,1152]{1,0:T(8,128)(2,1)S(1)}, u32[]{:S(2)}, u32[]{:S(2)}) collective-permute-start(bf16[72,1152]{1,0:T(8,128)(2,1)S(1)} %get-tuple-element.138), channel_id=1, source_target_pairs={{0,96},{1,97},{2,14},{3,15},{4,100},{5,101},{6,10},{7,11},{8,104},... | collective-permute-start | bytes 497672 | tf_op jit(solution)/shard_map/ppermute | solution.py:205
  71.5 14.4 %copy-start = (bf16[256,3072]{1,0:T(8,128)(2,1)S(1)}, bf16[256,3072]{1,0:T(8,128)(2,1)}, u32[]{:S(2)}) copy-start(bf16[256,3072]{1,0:T(8,128)(2,1)} %table_ref.1) | copy-start | bytes 4718596
  71.5 14.4 %copy-start.3 = (bf16[32,768]{1,0:T(8,128)(2,1)S(1)}, bf16[32,768]{1,0:T(8,128)(2,1)}, u32[]{:S(2)}) copy-start(bf16[32,768]{1,0:T(8,128)(2,1)} %q_ref.1) | copy-start | bytes 147460
  71.5 14.4 %copy-start.6 = (bf16[32,768]{1,0:T(8,128)(2,1)S(1)}, bf16[32,768]{1,0:T(8,128)(2,1)}, u32[]{:S(2)}) copy-start(bf16[32,768]{1,0:T(8,128)(2,1)} %k_ref.1) | copy-start | bytes 147460
  71.5 14.4 %copy-start.7 = (bf16[32,768]{1,0:T(8,128)(2,1)S(1)}, bf16[32,768]{1,0:T(8,128)(2,1)}, u32[]{:S(2)}) copy-start(bf16[32,768]{1,0:T(8,128)(2,1)} %v_ref.1) | copy-start | bytes 147460
  72.3 7.4 %collective-permute-start.24 = (bf16[40,1536]{1,0:T(8,128)(2,1)S(1)}, bf16[40,1536]{1,0:T(8,128)(2,1)S(1)}, u32[]{:S(2)}, u32[]{:S(2)}) collective-permute-start(bf16[40,1536]{1,0:T(8,128)(2,1)S(1)} %get-tuple-element.140), channel_id=1, source_target_pairs={{0,2},{1,3},{2,0},{3,1},{4,6},{5,7},{6,4},{7,5},{8,10},{9,11},{10,... | collective-permute-start | bytes 368648 | tf_op jit(solution)/shard_map/ppermute | solution.py:205
  80.4 5.5 %collective-permute-start.25 = (bf16[40,1152]{1,0:T(8,128)(2,1)S(1)}, bf16[40,1152]{1,0:T(8,128)(2,1)S(1)}, u32[]{:S(2)}, u32[]{:S(2)}) collective-permute-start(bf16[40,1152]{1,0:T(8,128)(2,1)S(1)} %shard_map.127), channel_id=1, source_target_pairs={{0,1},{1,0},{2,3},{3,2},{4,5},{5,4},{6,7},{7,6},{8,9},{9,8},{10,11... | collective-permute-start | bytes 276488 | tf_op jit(solution)/shard_map/ppermute | solution.py:205
  (2 other events, 8.8 us)

commit v8 on v7

--- a/solution.py
+++ b/solution.py
@@ -366,7 +366,13 @@
     return jnp.where(slot < per_lane(total, column), 0.0, -1e30)
 
 
-def pack_kernel(at, con_ref, txt_ref, out_ref, spot_ref, con_bias, txt_bias, con_line, txt_line):
+def pack_kernel(
+    at, con_ref, txt_ref, w_hbm, out_ref, spot_ref, con_bias, txt_bias, con_line, txt_line, w_ref, sem
+):
+    half = w_ref.shape[2]
+    lanes = pl.ds(pl.multiple_of(at[2] * half, half), half)
+    weights = pltpu.make_async_copy(w_hbm.at[:, :, lanes], w_ref, sem)
+    weights.start()
     ids = jnp.concatenate([con_ref[...], txt_ref[...]], axis=1)
     n = ids.shape[1]
     n_con = con_ref.shape[1]
@@ -410,14 +416,13 @@
     )
     hot = lax.broadcasted_iota(jnp.int32, (8 * SLOTS, 256), 1) == found.astype(jnp.int32) - 1
     out_ref[...] = jnp.transpose(hot.astype(F32))[0:ROWS].astype(BF)
+    weights.wait()
 
 
 def project_kernel(at, pack_ref, *refs):
     rows, (mod_ref, gain_ref, w_ref), outs, (raw_ref, x_ref) = (
         refs[:8], refs[8:11], refs[11:15], refs[15:]
     )
-    half = w_ref.shape[2] // 2
-    lanes = pl.ds(pl.multiple_of(at[2] * half, half), half)
     for i, ref in enumerate(rows):
         raw_ref[i * SLOTS : (i + 1) * SLOTS, :] = ref[0:SLOTS, :]
     shift = mod_ref[0:1, :]
@@ -434,9 +439,9 @@
         meansq = jnp.mean(u * u, axis=1, keepdims=True)
         return u * lax.rsqrt(meansq + 1e-06) * gain
 
-    q = nn(x_ref[0:CON, :], w_ref[0, :, lanes])
-    k = nn(x_ref[...], w_ref[1, :, lanes])
-    v = nn(x_ref[...], w_ref[2, :, lanes])
+    q = nn(x_ref[0:CON, :], w_ref[0])
+    k = nn(x_ref[...], w_ref[1])
+    v = nn(x_ref[...], w_ref[2])
     heads = []
     for h in range(3):
         cols = slice(h * HD, (h + 1) * HD)
@@ -460,7 +465,7 @@
 
 
 def join_kernel(a, b, c, d, con_line, txt_line, out, con, txt):
-    for i, ref in enumerate((a, b, c, d)):
+    for i, ref in zip((0, 1, 3, 2), (a, b, c, d)):
         con[i * CON : (i + 1) * CON, 0 : 2 * HD] = ref[0:CON, :]
         con[i * CON : i * CON + CON // 2, 2 * HD :] = ref[ROWS:, 0:HD]
         con[i * CON + CON // 2 : (i + 1) * CON, 2 * HD :] = ref[ROWS:, HD:]
@@ -576,7 +581,7 @@
 
 
 def near_kernel(
-    pick, q_part, l0, l1, l2, l3, con_bias, txt_bias, plane, img_q, im, ims, *refs
+    pick, q_part, l0, l1, l3, l2, con_bias, txt_bias, plane, img_q, im, ims, *refs
 ):
     q_out, cm_out, cs_out, im_out, ims_out = refs[:5]
     con_q, con_k, con_v, txt_k, txt_v, img_v = refs[5:]
@@ -632,7 +637,7 @@
     n_con = b0.shape[1] - HD
     total = jnp.zeros((72, n_con), F32)
     outs = [jnp.zeros((64, HD), BF) for _ in range(3)]
-    for s, ref in enumerate((b0, b1, b2, b3)):
+    for s, ref in zip((0, 1, 3, 2), (b0, b1, b2, b3)):
         head = at[4] ^ s
         total = total + jnp.where(head < 3, ref[:, 0:n_con].astype(F32), 0.0)
         for h in range(3):
@@ -700,7 +705,7 @@
     core_both = send(own_both, swap_core())
 
     all_weights = jnp.transpose(txt_qkv, (1, 0, 2))
-    pack, spots, con_bias, txt_bias, con_line, txt_line = call(
+    pack, spots, con_bias, txt_bias, con_line, txt_line, weights = call(
         pack_kernel,
         (
             sds((ROWS, 8 * SLOTS)),
@@ -709,9 +714,13 @@
             sds((1, 4 * LINE_TXT), F32),
             sds((1, 4 * CON), jnp.int32),
             sds((1, 4 * TXT), jnp.int32),
+            sds((3, width, half)),
         ),
+        scratch=(pltpu.SemaphoreType.DMA,),
+        limit=24,
         us=2.0,
-    )(at, con_ids, text_ids)
+        in_hbm=1,
+    )(at, con_ids, text_ids, all_weights)
     shift_scale = lax.dynamic_index_in_dim(modulation, step_index[0], 0, keepdims=False)
 
     image_blocks = call(
@@ -733,26 +742,24 @@
             pltpu.VMEM((8 * SLOTS, width), BF),
             pltpu.VMEM((ROWS, width), BF),
         ),
-        limit=28,
+        limit=24,
         us=PROJ_US,
-    )(at, pack, *column_rows, *other_rows, shift_scale, qk_gain, all_weights)
+    )(at, pack, *column_rows, *other_rows, shift_scale, qk_gain, weights)
 
     *image_blocks, first = lax.optimization_barrier((*image_blocks, qkv[0]))
     image_q, image_kv = call(
         image_join_kernel, (sds((8 * n_img, HD)), sds((16 * n_img, HD))), smem=0
     )(*image_blocks)
-    image_kvs = [image_kv] + [send(image_kv, swap_v(s)) for s in (2, 1, 3)]
-
-    qkv = [first] + [send(qkv[s], swap_u(s)) for s in (2, 1, 3)]
-    qkv = [qkv[0], qkv[2], qkv[1], qkv[3]]
+    image_kvs = [image_kv] + [send(image_kv, swap_v(s)) for s in (1, 3, 2)]
+
+    qkv = [first] + [send(qkv[s], swap_u(s)) for s in (1, 3, 2)]
     line = call(
         join_kernel,
         sds((LINE + LINE_CON // 2, 2 * HD)),
         scratch=(pltpu.VMEM((4 * CON, 3 * HD), BF), pltpu.VMEM((4 * TXT, 2 * HD), BF)),
         smem=0,
     )(*qkv, con_line, txt_line)
-    lines = [line] + [send(line, swap_v(s)) for s in (2, 1, 3)]
-    lines = [lines[0], lines[2], lines[1], lines[3]]
+    lines = [line] + [send(line, swap_v(s)) for s in (1, 3, 2)]
     plane = call(plane_kernel, sds((64 * n_img, HD)), smem=0)(*image_kvs)
     con_slot, over, plane = lax.optimization_barrier((spots[0, :n_con], spots[1, 0], plane))
     other_plane = send(plane, swap_plane())
@@ -787,8 +794,7 @@
         us=FAR_US,
         smem=0,
     )(other_plane, con_q, image_q, *near)
-    blocks = [blocks[0]] + [send(blocks[s], swap_u(s)) for s in (2, 1, 3)]
-    blocks = [blocks[0], blocks[2], blocks[1], blocks[3]]
+    blocks = [blocks[0]] + [send(blocks[s], swap_u(s)) for s in (1, 3, 2)]
     own, core = call(head_sum_kernel, tuple(sds((40, n_con + 4 * HD)) for _ in range(2)))(
         at, *blocks
     )

time: 88.2 us -> 74.4 us (0.84)
  waiting for transfers between devices: 22 us -> 12 us
  Pallas kernels: 23.3 us -> 21.3 us
  starting transfers between devices: 37.8 us -> 36.6 us
    ppermute x25, waiting for transfers between devices: 22 us -> 12 us  [send(): return lax.ppermute(array, ('ctx', 'head'), pairing)]
    pallas_call x14, Pallas kernels: 23.3 us -> 21.3 us  [run(): pl.pallas_call(kernel, out_shape=outs, in_specs=[sm] * smem + [vm] * (len...]
    ppermute x25, starting transfers between devices: 37.8 us -> 36.6 us  [send(): return lax.ppermute(array, ('ctx', 'head'), pairing)]
  transfers between devices with their start and end apart: 25 -> 25, of which waited for: 9 -> 7; matrix products, arithmetic and copies ran while one was open for 2% -> 2% of each run, Pallas kernels for 18% -> 19%
where the time goes in v8:
time: 74.4 us; the launch traced here: 74.1 us
  starting transfers between devices  36.6 us (49%)
  Pallas kernels  21.3 us (29%)
  waiting for transfers between devices  12 us (16%)
  between operations  2.14 us (3%)
  local copies, waits for them, and re-layouts  1.37 us (2%)
    ppermute x25, starting transfers between devices, send(): return lax.ppermute(array, ('ctx', 'head'), pairing)  36.6 us
    pallas_call x14, Pallas kernels, run(): pl.pallas_call(kernel, out_shape=outs, in_specs=[sm] * smem + [vm] * (len...  21.3 us
    ppermute x25, waiting for transfers between devices, send(): return lax.ppermute(array, ('ctx', 'head'), pairing)  12 us
  transfers between devices with their start and end apart: 25, of which 7 were waited for; matrix products, arithmetic and copies ran while one was open for 2% of the time, Pallas kernels for 19%

profile of v8, /device:TPU:1, one launch (start us, length us, event | category | flops | bytes accessed | tf_op | source)
XLA Modules:
  0.0 74.1 jit_solution(7624896921053062970)
XLA Ops:
  0.7 2.1 %shard_map.116 = (bf16[32,3072]{1,0:T(8,128)(2,1)S(1)}, bf16[48,3072]{1,0:T(8,128)(2,1)S(1)}, bf16[96,384]{1,0:T(8,128)(2,1)S(1)}) custom-call(s32[6]{0:T(128)S(1)} %stack.45.at, s32[1,1024]{1,0:T(1,128)} %bitcast.134, s32[1,512]{1,0:T(1,128)} %bitcast.138, bf16[256,3072]{1,0:T(8,128)(2,1)} %table_ref.1, bf16[32,768]{1,0:T(8,128)(2,1)} %q_ref.1, ...), custom_call_target="tpu_custom_call" | custom-call | flops 1100000000 | tf_op jit(solution)/shard_map/pallas_call | solution.py:220
  2.9 4.5 %collective-permute-start.2 = (bf16[32,3072]{1,0:T(8,128)(2,1)S(1)}, bf16[32,3072]{1,0:T(8,128)(2,1)S(1)}, u32[]{:S(2)}, u32[]{:S(2)}) collective-permute-start(bf16[32,3072]{1,0:T(8,128)(2,1)S(1)} %get-tuple-element.100.refs_0_), channel_id=1, source_target_pairs={{0,1},{1,0},{2,3},{3,2},{4,5},{5,4},{6,7},{7,6},{8,9},{9,8},{10,11... | collective-permute-start | bytes 589832 | tf_op jit(solution)/shard_map/ppermute | solution.py:205
  8.1 1.2 %collective-permute-start.1 = (bf16[48,3072]{1,0:T(8,128)(2,1)S(1)}, bf16[48,3072]{1,0:T(8,128)(2,1)S(1)}, u32[]{:S(2)}, u32[]{:S(2)}) collective-permute-start(bf16[48,3072]{1,0:T(8,128)(2,1)S(1)} %get-tuple-element.98), channel_id=1, source_target_pairs={{0,2},{1,3},{2,0},{3,1},{4,6},{5,7},{6,4},{7,5},{8,10},{9,11},{10,... | collective-permute-start | bytes 884744 | tf_op jit(solution)/shard_map/ppermute | solution.py:205
  10.0 0.7 %dynamic-slice_bitcast_fusion.refs_8_ = f32[2,3072]{1,0:T(2,128)S(1)} fusion(f32[28,2,3072]{2,1,0:T(2,128)} %param.19, s32[]{:T(128)S(6)} %select_n.43), kind=kLoop, calls=%fused_computation.116 | loop fusion | bytes 49156 | tf_op jit(solution)/shard_map/jit(dynamic_index_in_dim)/squeeze | solution.py:724
  11.3 1.4 %collective-permute-start.3 = (bf16[192,128]{1,0:T(8,128)(2,1)S(1)}, bf16[192,128]{1,0:T(8,128)(2,1)S(1)}, u32[]{:S(2)}, u32[]{:S(2)}) collective-permute-start(bf16[192,128]{1,0:T(8,128)(2,1)S(1)} %get-tuple-element.102), channel_id=1, source_target_pairs={{0,32},{1,33},{2,6},{3,7},{4,36},{5,37},{6,2},{7,3},{8,40},{9,41},... | collective-permute-start | bytes 147464 | tf_op jit(solution)/shard_map/ppermute | solution.py:205
  12.7 2.6 %collective-permute-start.5 = (bf16[192,128]{1,0:T(8,128)(2,1)S(1)}, bf16[192,128]{1,0:T(8,128)(2,1)S(1)}, u32[]{:S(2)}, u32[]{:S(2)}) collective-permute-start(bf16[192,128]{1,0:T(8,128)(2,1)S(1)} %get-tuple-element.104), channel_id=1, source_target_pairs={{0,64},{1,65},{2,10},{3,11},{4,68},{5,69},{6,14},{7,15},{8,72},{9,... | collective-permute-start | bytes 147464 | tf_op jit(solution)/shard_map/ppermute | solution.py:205
  15.3 4.0 %shard_map.115 = (bf16[160,256]{1,0:T(8,128)(2,1)S(1)}, s32[8,1536]{1,0:T(8,128)S(1)}, f32[1,1280]{1,0:T(1,128)S(1)}, f32[1,704]{1,0:T(1,128)S(1)}, s32[1,384]{1...) custom-call(s32[6]{0:T(128)S(1)} %stack.45.at, s32[1,1024]{1,0:T(1,128)S(1)} %bitcast.135, ...), custom_call_target="tpu_custom_call" | custom-call | flops 2200000000 | tf_op jit(solution)/shard_map/pallas_call | solution.py:220
  20.4 2.7 %collective-permute-start.6 = (bf16[192,128]{1,0:T(8,128)(2,1)S(1)}, bf16[192,128]{1,0:T(8,128)(2,1)S(1)}, u32[]{:S(2)}, u32[]{:S(2)}) collective-permute-start(bf16[192,128]{1,0:T(8,128)(2,1)S(1)} %get-tuple-element.106), channel_id=1, source_target_pairs={{0,96},{1,97},{2,14},{3,15},{4,100},{5,101},{6,10},{7,11},{8,104},... | collective-permute-start | bytes 147464 | tf_op jit(solution)/shard_map/ppermute | solution.py:205
  23.1 3.7 %shard_map.118 = (bf16[208,256]{1,0:T(8,128)(2,1)S(1)}, bf16[208,256]{1,0:T(8,128)(2,1)S(1)}, bf16[208,256]{1,0:T(8,128)(2,1)S(1)}, bf16[208,256]{1,0:T(8,128)(2,1)S(1)}) custom-call(s32[6]{0:T(128)S(1)} %stack.45.at, bf16[160,256]{1,0:T(8,128)(2,1)S(1)} %get-tuple-element.107.pack_ref, bf16[32,3072]{1,0:T(8,128)(2,1)S(1)} %get-tuple-element.100.refs_0_, ...), custom_call_target="tpu_custom_call" | custom-call | flops 5500000256 | tf_op jit(solution)/shard_map/pallas_call | solution.py:220
  26.9 1.6 %collective-permute-start.16 = (bf16[208,256]{1,0:T(8,128)(2,1)S(1)}, bf16[208,256]{1,0:T(8,128)(2,1)S(1)}, u32[]{:S(2)}, u32[]{:S(2)}) collective-permute-start(bf16[208,256]{1,0:T(8,128)(2,1)S(1)} %get-tuple-element.123), channel_id=1, source_target_pairs={{0,96},{1,97},{2,14},{3,15},{4,100},{5,101},{6,10},{7,11},{8,104},... | collective-permute-start | bytes 319496 | tf_op jit(solution)/shard_map/ppermute | solution.py:205
  28.5 1.6 %collective-permute-start.17 = (bf16[208,256]{1,0:T(8,128)(2,1)S(1)}, bf16[208,256]{1,0:T(8,128)(2,1)S(1)}, u32[]{:S(2)}, u32[]{:S(2)}) collective-permute-start(bf16[208,256]{1,0:T(8,128)(2,1)S(1)} %get-tuple-element.124), channel_id=1, source_target_pairs={{0,64},{1,65},{2,10},{3,11},{4,68},{5,69},{6,14},{7,15},{8,72},{9,... | collective-permute-start | bytes 319496 | tf_op jit(solution)/shard_map/ppermute | solution.py:205
  30.3 1.2 %collective-permute-start.12 = (bf16[512,128]{1,0:T(8,128)(2,1)S(1)}, bf16[512,128]{1,0:T(8,128)(2,1)S(1)}, u32[]{:S(2)}, u32[]{:S(2)}) collective-permute-start(bf16[512,128]{1,0:T(8,128)(2,1)S(1)} %get-tuple-element.117.a), channel_id=1, source_target_pairs={{0,12},{1,13},{2,98},{3,99},{4,8},{5,9},{6,102},{7,103},{8,4},{9,5... | collective-permute-start | bytes 393224 | tf_op jit(solution)/shard_map/ppermute | solution.py:205
  31.5 2.0 %collective-permute-start.13 = (bf16[512,128]{1,0:T(8,128)(2,1)S(1)}, bf16[512,128]{1,0:T(8,128)(2,1)S(1)}, u32[]{:S(2)}, u32[]{:S(2)}) collective-permute-start(bf16[512,128]{1,0:T(8,128)(2,1)S(1)} %get-tuple-element.117.a), channel_id=1, source_target_pairs={{0,8},{1,9},{2,66},{3,67},{4,12},{5,13},{6,70},{7,71},{8,0},{9,1},... | collective-permute-start | bytes 393224 | tf_op jit(solution)/shard_map/ppermute | solution.py:205
  34.6 1.2 %collective-permute-start.19 = (bf16[656,256]{1,0:T(8,128)(2,1)S(1)}, bf16[656,256]{1,0:T(8,128)(2,1)S(1)}, u32[]{:S(2)}, u32[]{:S(2)}) collective-permute-start(bf16[656,256]{1,0:T(8,128)(2,1)S(1)} %shard_map.121.l0), channel_id=1, source_target_pairs={{0,12},{1,13},{2,98},{3,99},{4,8},{5,9},{6,102},{7,103},{8,4},{9,5... | collective-permute-start | bytes 1007624 | tf_op jit(solution)/shard_map/ppermute | solution.py:205
  35.7 2.0 %collective-permute-start.20 = (bf16[656,256]{1,0:T(8,128)(2,1)S(1)}, bf16[656,256]{1,0:T(8,128)(2,1)S(1)}, u32[]{:S(2)}, u32[]{:S(2)}) collective-permute-start(bf16[656,256]{1,0:T(8,128)(2,1)S(1)} %shard_map.121.l0), channel_id=1, source_target_pairs={{0,8},{1,9},{2,66},{3,67},{4,12},{5,13},{6,70},{7,71},{8,0},{9,1},... | collective-permute-start | bytes 1007624 | tf_op jit(solution)/shard_map/ppermute | solution.py:205
  37.8 1.1 %collective-permute-start.14 = (bf16[2048,128]{1,0:T(8,128)(2,1)S(1)}, bf16[2048,128]{1,0:T(8,128)(2,1)S(1)}, u32[]{:S(2)}, u32[]{:S(2)}) collective-permute-start(bf16[2048,128]{1,0:T(8,128)(2,1)S(1)} %shard_map.120.plane), channel_id=1, source_target_pairs={{0,16},{1,17},{2,18},{3,19},{4,20},{5,21},{6,22},{7,23},{8,24},{9,... | collective-permute-start | bytes 1572872 | tf_op jit(solution)/shard_map/ppermute | solution.py:205
  39.4 0.8 %shard_map.123 = (f32[256,1]{1,0:T(8,128)S(1)}, f32[256,256]{1,0:T(8,128)S(1)}) custom-call(bf16[2048,128]{1,0:T(8,128)(2,1)S(1)} %shard_map.120.plane, bf16[256,128]{1,0:T(8,128)(2,1)S(1)} %get-tuple-element.129.q.img_q), custom_call_target="tpu_custom_call" | custom-call | flops 1100000000 | tf_op jit(solution)/shard_map/pallas_call | solution.py:220
  41.3 4.4 %collective-permute-done.19.l3 = bf16[656,256]{1,0:T(8,128)(2,1)S(1)} collective-permute-done((bf16[656,256]{1,0:T(8,128)(2,1)S(1)}, bf16[656,256]{1,0:T(8,128)(2,1)S(1)}, u32[]{:S(2)}, u32[]{:S(2)}) %collective-permute-start.19) | collective-permute-done | bytes 335904 | tf_op jit(solution)/shard_map/ppermute | solution.py:205
  45.7 4.2 %shard_map.124 = (bf16[1024,128]{1,0:T(8,128)(2,1)S(1)}, f32[1024,1]{1,0:T(8,128)S(1)}, f32[1024,256]{1,0:T(8,128)S(1)}, f32[256,1]{1,0:T(8,128)S(1)}, f32[256,256]{1,0:T(8,128)S(1)}) custom-call(bf16[1024,1280]{1,0:T(8,128)(2,1)S(1)} %fusion.81.pick, bf16[1024,128]{1,0:T(8,128)(2,1)S(1)} %shard_map.122.q_part, bf16[656,256]{1,0:T(8,128)(2,1)S(1)} %shard_map.121.l0, ...), custom_call_target="tpu_custom_call" | custom-call | flops 2200000000 | tf_op jit(solution)/shard_map/pallas_call | solution.py:220
  49.9 2.5 %shard_map.125 = (bf16[72,1152]{1,0:T(8,128)(2,1)S(1)}, bf16[72,1152]{1,0:T(8,128)(2,1)S(1)}, bf16[72,1152]{1,0:T(8,128)(2,1)S(1)}, bf16[72,1152]{1,0:T(8,128)(2,1)S(1)}) custom-call(bf16[2048,128]{1,0:T(8,128)(2,1)S(1)} %collective-permute-done.14.plane, bf16[1024,128]{1,0:T(8,128)(2,1)S(1)} %get-tuple-element.132.con_q, ...), custom_call_target="tpu_custom_call" | custom-call | flops 3300000000 | tf_op jit(solution)/shard_map/pallas_call | solution.py:220
  52.6 1.5 %collective-permute-start.22 = (bf16[72,1152]{1,0:T(8,128)(2,1)S(1)}, bf16[72,1152]{1,0:T(8,128)(2,1)S(1)}, u32[]{:S(2)}, u32[]{:S(2)}) collective-permute-start(bf16[72,1152]{1,0:T(8,128)(2,1)S(1)} %get-tuple-element.139), channel_id=1, source_target_pairs={{0,96},{1,97},{2,14},{3,15},{4,100},{5,101},{6,10},{7,11},{8,104},... | collective-permute-start | bytes 497672 | tf_op jit(solution)/shard_map/ppermute | solution.py:205
  54.1 1.7 %collective-permute-start.23 = (bf16[72,1152]{1,0:T(8,128)(2,1)S(1)}, bf16[72,1152]{1,0:T(8,128)(2,1)S(1)}, u32[]{:S(2)}, u32[]{:S(2)}) collective-permute-start(bf16[72,1152]{1,0:T(8,128)(2,1)S(1)} %get-tuple-element.140), channel_id=1, source_target_pairs={{0,64},{1,65},{2,10},{3,11},{4,68},{5,69},{6,14},{7,15},{8,72},{9,... | collective-permute-start | bytes 497672 | tf_op jit(solution)/shard_map/ppermute | solution.py:205
  55.7 0.9 %collective-permute-done.21.b1 = bf16[72,1152]{1,0:T(8,128)(2,1)S(1)} collective-permute-done((bf16[72,1152]{1,0:T(8,128)(2,1)S(1)}, bf16[72,1152]{1,0:T(8,128)(2,1)S(1)}, u32[]{:S(2)}, u32[]{:S(2)}) %collective-permute-start.21) | collective-permute-done | bytes 165920 | tf_op jit(solution)/shard_map/ppermute | solution.py:205
  56.6 1.3 %collective-permute-done.22.b2 = bf16[72,1152]{1,0:T(8,128)(2,1)S(1)} collective-permute-done((bf16[72,1152]{1,0:T(8,128)(2,1)S(1)}, bf16[72,1152]{1,0:T(8,128)(2,1)S(1)}, u32[]{:S(2)}, u32[]{:S(2)}) %collective-permute-start.22) | collective-permute-done | bytes 165920 | tf_op jit(solution)/shard_map/ppermute | solution.py:205
  58.0 1.8 %collective-permute-done.23.b3 = bf16[72,1152]{1,0:T(8,128)(2,1)S(1)} collective-permute-done((bf16[72,1152]{1,0:T(8,128)(2,1)S(1)}, bf16[72,1152]{1,0:T(8,128)(2,1)S(1)}, u32[]{:S(2)}, u32[]{:S(2)}) %collective-permute-start.23) | collective-permute-done | bytes 165920 | tf_op jit(solution)/shard_map/ppermute | solution.py:205
  59.8 0.8 %shard_map.126 = (bf16[40,1536]{1,0:T(8,128)(2,1)S(1)}, bf16[40,1536]{1,0:T(8,128)(2,1)S(1)}) custom-call(s32[6]{0:T(128)S(1)} %stack.45.at, bf16[72,1152]{1,0:T(8,128)(2,1)S(1)} %get-tuple-element.137.b0, bf16[72,1152]{1,0:T(8,128)(2,1)S(1)} %collective-permute-done.21.b1, bf16[72,1152]{1,0:T(8,128)(2,1)S(1)} %collective-permute-done.22.b2, ...), custom_call_target="tpu_custom_call" | custom-call | flops 1100000000 | tf_op jit(solution)/shard_map/pallas_call | solution.py:220
  60.6 5.1 %collective-permute-start.24 = (bf16[40,1536]{1,0:T(8,128)(2,1)S(1)}, bf16[40,1536]{1,0:T(8,128)(2,1)S(1)}, u32[]{:S(2)}, u32[]{:S(2)}) collective-permute-start(bf16[40,1536]{1,0:T(8,128)(2,1)S(1)} %get-tuple-element.142), channel_id=1, source_target_pairs={{0,2},{1,3},{2,0},{3,1},{4,6},{5,7},{6,4},{7,5},{8,10},{9,11},{10,... | collective-permute-start | bytes 368648 | tf_op jit(solution)/shard_map/ppermute | solution.py:205
  65.6 1.0 %collective-permute-done.24.core = bf16[40,1536]{1,0:T(8,128)(2,1)S(1)} collective-permute-done((bf16[40,1536]{1,0:T(8,128)(2,1)S(1)}, bf16[40,1536]{1,0:T(8,128)(2,1)S(1)}, u32[]{:S(2)}, u32[]{:S(2)}) %collective-permute-start.24) | collective-permute-done | bytes 122912 | tf_op jit(solution)/shard_map/ppermute | solution.py:205
  66.6 2.9 %collective-permute-start.25 = (bf16[40,1152]{1,0:T(8,128)(2,1)S(1)}, bf16[40,1152]{1,0:T(8,128)(2,1)S(1)}, u32[]{:S(2)}, u32[]{:S(2)}) collective-permute-start(bf16[40,1152]{1,0:T(8,128)(2,1)S(1)} %shard_map.127), channel_id=1, source_target_pairs={{0,1},{1,0},{2,3},{3,2},{4,5},{5,4},{6,7},{7,6},{8,9},{9,8},{10,11... | collective-permute-start | bytes 276488 | tf_op jit(solution)/shard_map/ppermute | solution.py:205
  70.2 1.9 %collective-permute-done.25 = bf16[40,1152]{1,0:T(8,128)(2,1)S(1)} collective-permute-done((bf16[40,1152]{1,0:T(8,128)(2,1)S(1)}, bf16[40,1152]{1,0:T(8,128)(2,1)S(1)}, u32[]{:S(2)}, u32[]{:S(2)}) %collective-permute-start.25) | collective-permute-done | bytes 92192 | tf_op jit(solution)/shard_map/ppermute | solution.py:205
  72.1 2.0 %conditional.1 = (bf16[32,768]{1,0:T(8,128)(2,1)}, f32[1024,32]{0,1:T(8,128)}) conditional(s32[]{:T(128)} %convert_element_type.62, (s32[512]{0:T(512)S(1)}, s32[1024]{0:T(1024)S(1)}, bf16[256,3072]{1,0:T(8,128)(2,1)S(1)}, s32[1]{0:T(128)}, f32[28,2,3072]{2,1,0:T(2,128)}, /*index=5*/bf16[3072,3,768]{2,0,1:T(8,128)(2,1)}, f32[2,128]{1,0:T(2,128)S(1)}, ...), branch_computations={%region_0.15_spmd, %region_15.16_spmd} | conditional | flops 1100000000 | bytes 257951312 | solution.py:815
  72.4 1.7 %branch_1_fun.1 = (bf16[32,768]{1,0:T(8,128)(2,1)}, f32[32,1024]{1,0:T(8,128)}) custom-call(s32[6]{0:T(128)S(1)} %get-tuple-element.40.at, bf16[40,1152]{1,0:T(8,128)(2,1)S(1)} %get-tuple-element.41.sums, bf16[40,1152]{1,0:T(8,128)(2,1)S(1)} %get-tuple-element.42.head, bf16[40,1536]{1,0:T(8,128)(2,1)} %get-tuple-element.43.own, ...), custom_call_target="tpu_custom_call" | custom-call | flops 1100000000 | tf_op jit(solution)/shard_map/cond/branch_1_fun/pallas_call | solution.py:220
  (54 shorter events, 5.6 us)
Async XLA Ops:
  0.7 14.6 %copy-start.8 = (s32[1024]{0:T(1024)S(1)}, s32[1024]{0:T(1024)}, u32[]{:S(2)}) copy-start(s32[1024]{0:T(1024)} %param.16) | copy-start | bytes 12292
  0.7 14.6 %copy-start.9 = (s32[512]{0:T(512)S(1)}, s32[512]{0:T(512)}, u32[]{:S(2)}) copy-start(s32[512]{0:T(512)} %param.15) | copy-start | bytes 6148
  2.9 17.0 %collective-permute-start.2 = (bf16[32,3072]{1,0:T(8,128)(2,1)S(1)}, bf16[32,3072]{1,0:T(8,128)(2,1)S(1)}, u32[]{:S(2)}, u32[]{:S(2)}) collective-permute-start(bf16[32,3072]{1,0:T(8,128)(2,1)S(1)} %get-tuple-element.100.refs_0_), channel_id=1, source_target_pairs={{0,1},{1,0},{2,3},{3,2},{4,5},{5,4},{6,7},{7,6},{8,9},{9,8},{10,11... | collective-permute-start | bytes 589832 | tf_op jit(solution)/shard_map/ppermute | solution.py:205
  7.3 12.6 %collective-permute-start.4 = (bf16[32,3072]{1,0:T(8,128)(2,1)S(1)}, bf16[32,3072]{1,0:T(8,128)(2,1)S(1)}, u32[]{:S(2)}, u32[]{:S(2)}) collective-permute-start(bf16[32,3072]{1,0:T(8,128)(2,1)S(1)} %get-tuple-element.100.refs_0_), channel_id=1, source_target_pairs={{0,16},{1,17},{2,18},{3,19},{4,20},{5,21},{6,22},{7,23},{8,24},{9,... | collective-permute-start | bytes 589832 | tf_op jit(solution)/shard_map/ppermute | solution.py:205
  8.1 11.2 %collective-permute-start.7 = (bf16[32,3072]{1,0:T(8,128)(2,1)S(1)}, bf16[32,3072]{1,0:T(8,128)(2,1)S(1)}, u32[]{:S(2)}, u32[]{:S(2)}) collective-permute-start(bf16[32,3072]{1,0:T(8,128)(2,1)S(1)} %get-tuple-element.100.refs_0_), channel_id=1, source_target_pairs={{0,17},{1,16},{2,19},{3,18},{4,21},{5,20},{6,23},{7,22},{8,25},{9,... | collective-permute-start | bytes 589832 | tf_op jit(solution)/shard_map/ppermute | solution.py:205
  8.1 2.6 %collective-permute-start.1 = (bf16[48,3072]{1,0:T(8,128)(2,1)S(1)}, bf16[48,3072]{1,0:T(8,128)(2,1)S(1)}, u32[]{:S(2)}, u32[]{:S(2)}) collective-permute-start(bf16[48,3072]{1,0:T(8,128)(2,1)S(1)} %get-tuple-element.98), channel_id=1, source_target_pairs={{0,2},{1,3},{2,0},{3,1},{4,6},{5,7},{6,4},{7,5},{8,10},{9,11},{10,... | collective-permute-start | bytes 884744 | tf_op jit(solution)/shard_map/ppermute | solution.py:205
  11.3 8.5 %collective-permute-start.3 = (bf16[192,128]{1,0:T(8,128)(2,1)S(1)}, bf16[192,128]{1,0:T(8,128)(2,1)S(1)}, u32[]{:S(2)}, u32[]{:S(2)}) collective-permute-start(bf16[192,128]{1,0:T(8,128)(2,1)S(1)} %get-tuple-element.102), channel_id=1, source_target_pairs={{0,32},{1,33},{2,6},{3,7},{4,36},{5,37},{6,2},{7,3},{8,40},{9,41},... | collective-permute-start | bytes 147464 | tf_op jit(solution)/shard_map/ppermute | solution.py:205
  12.7 7.3 %collective-permute-start.5 = (bf16[192,128]{1,0:T(8,128)(2,1)S(1)}, bf16[192,128]{1,0:T(8,128)(2,1)S(1)}, u32[]{:S(2)}, u32[]{:S(2)}) collective-permute-start(bf16[192,128]{1,0:T(8,128)(2,1)S(1)} %get-tuple-element.104), channel_id=1, source_target_pairs={{0,64},{1,65},{2,10},{3,11},{4,68},{5,69},{6,14},{7,15},{8,72},{9,... | collective-permute-start | bytes 147464 | tf_op jit(solution)/shard_map/ppermute | solution.py:205
  15.3 7.8 %copy-start.10 = (f32[2,128]{1,0:T(2,128)S(1)}, f32[2,128]{1,0:T(2,128)}, u32[]{:S(2)}) copy-start(f32[2,128]{1,0:T(2,128)} %refs_9_.1) | copy-start | bytes 3076
  19.3 3.8 %collective-permute-start.10 = (bf16[32,3072]{1,0:T(8,128)(2,1)S(1)}, bf16[32,3072]{1,0:T(8,128)(2,1)S(1)}, u32[]{:S(2)}, u32[]{:S(2)}) collective-permute-start(bf16[32,3072]{1,0:T(8,128)(2,1)S(1)} %collective-permute-done.7.refs_3_), channel_id=1, source_target_pairs={{0,2},{1,3},{2,0},{3,1},{4,6},{5,7},{6,4},{7,5},{8,10},{9,11},{10,... | collective-permute-start | bytes 589832 | tf_op jit(solution)/shard_map/ppermute | solution.py:205
  19.9 3.3 %collective-permute-start.9 = (bf16[32,3072]{1,0:T(8,128)(2,1)S(1)}, bf16[32,3072]{1,0:T(8,128)(2,1)S(1)}, u32[]{:S(2)}, u32[]{:S(2)}) collective-permute-start(bf16[32,3072]{1,0:T(8,128)(2,1)S(1)} %collective-permute-done.2.refs_2_), channel_id=1, source_target_pairs={{0,2},{1,3},{2,0},{3,1},{4,6},{5,7},{6,4},{7,5},{8,10},{9,11},{10,... | collective-permute-start | bytes 589832 | tf_op jit(solution)/shard_map/ppermute | solution.py:205
  20.0 3.1 %collective-permute-start.8 = (bf16[32,3072]{1,0:T(8,128)(2,1)S(1)}, bf16[32,3072]{1,0:T(8,128)(2,1)S(1)}, u32[]{:S(2)}, u32[]{:S(2)}) collective-permute-start(bf16[32,3072]{1,0:T(8,128)(2,1)S(1)} %collective-permute-done.4.refs_1_), channel_id=1, source_target_pairs={{0,2},{1,3},{2,0},{3,1},{4,6},{5,7},{6,4},{7,5},{8,10},{9,11},{10,... | collective-permute-start | bytes 589832 | tf_op jit(solution)/shard_map/ppermute | solution.py:205
  20.4 6.5 %collective-permute-start.6 = (bf16[192,128]{1,0:T(8,128)(2,1)S(1)}, bf16[192,128]{1,0:T(8,128)(2,1)S(1)}, u32[]{:S(2)}, u32[]{:S(2)}) collective-permute-start(bf16[192,128]{1,0:T(8,128)(2,1)S(1)} %get-tuple-element.106), channel_id=1, source_target_pairs={{0,96},{1,97},{2,14},{3,15},{4,100},{5,101},{6,10},{7,11},{8,104},... | collective-permute-start | bytes 147464 | tf_op jit(solution)/shard_map/ppermute | solution.py:205
  26.8 4.7 %collective-permute-start.15 = (bf16[208,256]{1,0:T(8,128)(2,1)S(1)}, bf16[208,256]{1,0:T(8,128)(2,1)S(1)}, u32[]{:S(2)}, u32[]{:S(2)}) collective-permute-start(bf16[208,256]{1,0:T(8,128)(2,1)S(1)} %get-tuple-element.122), channel_id=1, source_target_pairs={{0,32},{1,33},{2,6},{3,7},{4,36},{5,37},{6,2},{7,3},{8,40},{9,41},... | collective-permute-start | bytes 319496 | tf_op jit(solution)/shard_map/ppermute | solution.py:205
  26.9 7.1 %collective-permute-start.16 = (bf16[208,256]{1,0:T(8,128)(2,1)S(1)}, bf16[208,256]{1,0:T(8,128)(2,1)S(1)}, u32[]{:S(2)}, u32[]{:S(2)}) collective-permute-start(bf16[208,256]{1,0:T(8,128)(2,1)S(1)} %get-tuple-element.123), channel_id=1, source_target_pairs={{0,96},{1,97},{2,14},{3,15},{4,100},{5,101},{6,10},{7,11},{8,104},... | collective-permute-start | bytes 319496 | tf_op jit(solution)/shard_map/ppermute | solution.py:205
  28.5 5.5 %collective-permute-start.17 = (bf16[208,256]{1,0:T(8,128)(2,1)S(1)}, bf16[208,256]{1,0:T(8,128)(2,1)S(1)}, u32[]{:S(2)}, u32[]{:S(2)}) collective-permute-start(bf16[208,256]{1,0:T(8,128)(2,1)S(1)} %get-tuple-element.124), channel_id=1, source_target_pairs={{0,64},{1,65},{2,10},{3,11},{4,68},{5,69},{6,14},{7,15},{8,72},{9,... | collective-permute-start | bytes 319496 | tf_op jit(solution)/shard_map/ppermute | solution.py:205
  30.2 5.5 %collective-permute-start.11 = (bf16[512,128]{1,0:T(8,128)(2,1)S(1)}, bf16[512,128]{1,0:T(8,128)(2,1)S(1)}, u32[]{:S(2)}, u32[]{:S(2)}) collective-permute-start(bf16[512,128]{1,0:T(8,128)(2,1)S(1)} %get-tuple-element.117.a), channel_id=1, source_target_pairs={{0,4},{1,5},{2,34},{3,35},{4,0},{5,1},{6,38},{7,39},{8,12},{9,13},... | collective-permute-start | bytes 393224 | tf_op jit(solution)/shard_map/ppermute | solution.py:205
  30.3 7.5 %collective-permute-start.12 = (bf16[512,128]{1,0:T(8,128)(2,1)S(1)}, bf16[512,128]{1,0:T(8,128)(2,1)S(1)}, u32[]{:S(2)}, u32[]{:S(2)}) collective-permute-start(bf16[512,128]{1,0:T(8,128)(2,1)S(1)} %get-tuple-element.117.a), channel_id=1, source_target_pairs={{0,12},{1,13},{2,98},{3,99},{4,8},{5,9},{6,102},{7,103},{8,4},{9,5... | collective-permute-start | bytes 393224 | tf_op jit(solution)/shard_map/ppermute | solution.py:205
  31.5 6.2 %collective-permute-start.13 = (bf16[512,128]{1,0:T(8,128)(2,1)S(1)}, bf16[512,128]{1,0:T(8,128)(2,1)S(1)}, u32[]{:S(2)}, u32[]{:S(2)}) collective-permute-start(bf16[512,128]{1,0:T(8,128)(2,1)S(1)} %get-tuple-element.117.a), channel_id=1, source_target_pairs={{0,8},{1,9},{2,66},{3,67},{4,12},{5,13},{6,70},{7,71},{8,0},{9,1},... | collective-permute-start | bytes 393224 | tf_op jit(solution)/shard_map/ppermute | solution.py:205
  34.4 6.4 %collective-permute-start.18 = (bf16[656,256]{1,0:T(8,128)(2,1)S(1)}, bf16[656,256]{1,0:T(8,128)(2,1)S(1)}, u32[]{:S(2)}, u32[]{:S(2)}) collective-permute-start(bf16[656,256]{1,0:T(8,128)(2,1)S(1)} %shard_map.121.l0), channel_id=1, source_target_pairs={{0,4},{1,5},{2,34},{3,35},{4,0},{5,1},{6,38},{7,39},{8,12},{9,13},... | collective-permute-start | bytes 1007624 | tf_op jit(solution)/shard_map/ppermute | solution.py:205
  34.6 11.1 %collective-permute-start.19 = (bf16[656,256]{1,0:T(8,128)(2,1)S(1)}, bf16[656,256]{1,0:T(8,128)(2,1)S(1)}, u32[]{:S(2)}, u32[]{:S(2)}) collective-permute-start(bf16[656,256]{1,0:T(8,128)(2,1)S(1)} %shard_map.121.l0), channel_id=1, source_target_pairs={{0,12},{1,13},{2,98},{3,99},{4,8},{5,9},{6,102},{7,103},{8,4},{9,5... | collective-permute-start | bytes 1007624 | tf_op jit(solution)/shard_map/ppermute | solution.py:205
  35.7 10.0 %collective-permute-start.20 = (bf16[656,256]{1,0:T(8,128)(2,1)S(1)}, bf16[656,256]{1,0:T(8,128)(2,1)S(1)}, u32[]{:S(2)}, u32[]{:S(2)}) collective-permute-start(bf16[656,256]{1,0:T(8,128)(2,1)S(1)} %shard_map.121.l0), channel_id=1, source_target_pairs={{0,8},{1,9},{2,66},{3,67},{4,12},{5,13},{6,70},{7,71},{8,0},{9,1},... | collective-permute-start | bytes 1007624 | tf_op jit(solution)/shard_map/ppermute | solution.py:205
  37.8 12.2 %collective-permute-start.14 = (bf16[2048,128]{1,0:T(8,128)(2,1)S(1)}, bf16[2048,128]{1,0:T(8,128)(2,1)S(1)}, u32[]{:S(2)}, u32[]{:S(2)}) collective-permute-start(bf16[2048,128]{1,0:T(8,128)(2,1)S(1)} %shard_map.120.plane), channel_id=1, source_target_pairs={{0,16},{1,17},{2,18},{3,19},{4,20},{5,21},{6,22},{7,23},{8,24},{9,... | collective-permute-start | bytes 1572872 | tf_op jit(solution)/shard_map/ppermute | solution.py:205
  52.4 4.3 %collective-permute-start.21 = (bf16[72,1152]{1,0:T(8,128)(2,1)S(1)}, bf16[72,1152]{1,0:T(8,128)(2,1)S(1)}, u32[]{:S(2)}, u32[]{:S(2)}) collective-permute-start(bf16[72,1152]{1,0:T(8,128)(2,1)S(1)} %get-tuple-element.138), channel_id=1, source_target_pairs={{0,32},{1,33},{2,6},{3,7},{4,36},{5,37},{6,2},{7,3},{8,40},{9,41},... | collective-permute-start | bytes 497672 | tf_op jit(solution)/shard_map/ppermute | solution.py:205
  52.6 5.4 %collective-permute-start.22 = (bf16[72,1152]{1,0:T(8,128)(2,1)S(1)}, bf16[72,1152]{1,0:T(8,128)(2,1)S(1)}, u32[]{:S(2)}, u32[]{:S(2)}) collective-permute-start(bf16[72,1152]{1,0:T(8,128)(2,1)S(1)} %get-tuple-element.139), channel_id=1, source_target_pairs={{0,96},{1,97},{2,14},{3,15},{4,100},{5,101},{6,10},{7,11},{8,104},... | collective-permute-start | bytes 497672 | tf_op jit(solution)/shard_map/ppermute | solution.py:205
  54.1 5.7 %collective-permute-start.23 = (bf16[72,1152]{1,0:T(8,128)(2,1)S(1)}, bf16[72,1152]{1,0:T(8,128)(2,1)S(1)}, u32[]{:S(2)}, u32[]{:S(2)}) collective-permute-start(bf16[72,1152]{1,0:T(8,128)(2,1)S(1)} %get-tuple-element.140), channel_id=1, source_target_pairs={{0,64},{1,65},{2,10},{3,11},{4,68},{5,69},{6,14},{7,15},{8,72},{9,... | collective-permute-start | bytes 497672 | tf_op jit(solution)/shard_map/ppermute | solution.py:205
  59.8 12.4 %copy-start = (bf16[256,3072]{1,0:T(8,128)(2,1)S(1)}, bf16[256,3072]{1,0:T(8,128)(2,1)}, u32[]{:S(2)}) copy-start(bf16[256,3072]{1,0:T(8,128)(2,1)} %table_ref.1) | copy-start | bytes 4718596
  59.8 12.4 %copy-start.3 = (bf16[32,768]{1,0:T(8,128)(2,1)S(1)}, bf16[32,768]{1,0:T(8,128)(2,1)}, u32[]{:S(2)}) copy-start(bf16[32,768]{1,0:T(8,128)(2,1)} %q_ref.1) | copy-start | bytes 147460
  59.8 12.4 %copy-start.6 = (bf16[32,768]{1,0:T(8,128)(2,1)S(1)}, bf16[32,768]{1,0:T(8,128)(2,1)}, u32[]{:S(2)}) copy-start(bf16[32,768]{1,0:T(8,128)(2,1)} %k_ref.1) | copy-start | bytes 147460
  59.8 12.4 %copy-start.7 = (bf16[32,768]{1,0:T(8,128)(2,1)S(1)}, bf16[32,768]{1,0:T(8,128)(2,1)}, u32[]{:S(2)}) copy-start(bf16[32,768]{1,0:T(8,128)(2,1)} %v_ref.1) | copy-start | bytes 147460
  60.6 6.0 %collective-permute-start.24 = (bf16[40,1536]{1,0:T(8,128)(2,1)S(1)}, bf16[40,1536]{1,0:T(8,128)(2,1)S(1)}, u32[]{:S(2)}, u32[]{:S(2)}) collective-permute-start(bf16[40,1536]{1,0:T(8,128)(2,1)S(1)} %get-tuple-element.142), channel_id=1, source_target_pairs={{0,2},{1,3},{2,0},{3,1},{4,6},{5,7},{6,4},{7,5},{8,10},{9,11},{10,... | collective-permute-start | bytes 368648 | tf_op jit(solution)/shard_map/ppermute | solution.py:205
  66.6 5.5 %collective-permute-start.25 = (bf16[40,1152]{1,0:T(8,128)(2,1)S(1)}, bf16[40,1152]{1,0:T(8,128)(2,1)S(1)}, u32[]{:S(2)}, u32[]{:S(2)}) collective-permute-start(bf16[40,1152]{1,0:T(8,128)(2,1)S(1)} %shard_map.127), channel_id=1, source_target_pairs={{0,1},{1,0},{2,3},{3,2},{4,5},{5,4},{6,7},{7,6},{8,9},{9,8},{10,11... | collective-permute-start | bytes 276488 | tf_op jit(solution)/shard_map/ppermute | solution.py:205
  (1 other events, 6.0 us)

commit v9 on v8

--- a/solution.py
+++ b/solution.py
@@ -551,9 +551,20 @@
         con_q[a * n + n // 2 : (a + 1) * n, :] = ref[LINE:, HD:]
 
 
-def order_kernel(pick, l0, l1, q_out, con_q):
+def line_texts(txt_k, txt_v, refs):
+    m = LINE_TXT
+    for a, ref in enumerate(refs):
+        txt_k[a * m : (a + 1) * m, :] = ref[LINE_CON:LINE, 0:HD]
+        txt_v[a * m : (a + 1) * m, :] = with_ones(ref[LINE_CON:LINE, HD:])
+
+
+def order_kernel(pick, l0, l1, txt_bias, img_q, im, ims, *refs):
+    (q_out, im_out, ims_out), (con_q, txt_k, txt_v) = refs[:3], refs[3:]
     line_queries(con_q, (l0, l1))
     q_out[...] = nn(pick[:, : 2 * LINE_CON], con_q[...]).astype(BF)
+    line_texts(txt_k, txt_v, (l0, l1))
+    part = (txt_k[...], txt_v[...], txt_bias[:, 0 : 2 * LINE_TXT])
+    im_out[...], ims_out[...] = join(weigh(img_q[...], (part,), FACTOR), (im[...], ims[...]))
 
 
 def weigh_blocks(q, parts, store):
@@ -585,13 +596,12 @@
 ):
     q_out, cm_out, cs_out, im_out, ims_out = refs[:5]
     con_q, con_k, con_v, txt_k, txt_v, img_v = refs[5:]
-    n, m = LINE_CON, LINE_TXT
+    n = LINE_CON
     line_queries(con_q, (l2, l3))
     for a, ref in enumerate((l0, l1, l2, l3)):
         con_k[a * n : (a + 1) * n, :] = ref[0:n, 0:HD]
         con_v[a * n : (a + 1) * n, :] = with_ones(ref[0:n, HD:])
-        txt_k[a * m : (a + 1) * m, :] = ref[n:LINE, 0:HD]
-        txt_v[a * m : (a + 1) * m, :] = with_ones(ref[n:LINE, HD:])
+    line_texts(txt_k, txt_v, (l2, l3))
     n_img = plane.shape[0] // 2
     img_v[...] = with_ones(plane[n_img:, :])
     rest = nn(pick[:, 2 * n :], con_q[...])
@@ -603,7 +613,7 @@
 
     parts = ((plane.at[0:n_img, :], img_v, None), (con_k, con_v, con_bias))
     weigh_blocks(q_out, parts, store)
-    text = weigh(img_q[...], ((txt_k[...], txt_v[...], txt_bias[...]),), FACTOR)
+    text = weigh(img_q[...], ((txt_k[...], txt_v[...], txt_bias[:, 2 * LINE_TXT :]),), FACTOR)
     im_out[...], ims_out[...] = join(text, (im[...], ims[...]))
 
 
@@ -768,9 +778,16 @@
     image_stats = (sds((8 * n_img, 1), F32), sds((8 * n_img, 2 * HD), F32))
     stats = (sds((n_con, 1), F32), sds((n_con, 2 * HD), F32)) + image_stats
     image_near = call(image_near_kernel, image_stats, smem=0)(plane, image_q)
-    q_part = call(
-        order_kernel, sds((n_con, HD)), scratch=(pltpu.VMEM((2 * LINE_CON, HD), BF),), smem=0
-    )(pick, lines[0], lines[1])
+    q_part, *image_near = call(
+        order_kernel,
+        (sds((n_con, HD)),) + image_stats,
+        scratch=(
+            pltpu.VMEM((2 * LINE_CON, HD), BF),
+            pltpu.VMEM((2 * LINE_TXT, HD), BF),
+            pltpu.VMEM((2 * LINE_TXT, 2 * HD), BF),
+        ),
+        smem=0,
+    )(pick, lines[0], lines[1], txt_bias, image_q, *image_near)
     con_q, *near = call(
         near_kernel,
         (sds((n_con, HD)),) + stats,
@@ -778,8 +795,8 @@
             pltpu.VMEM((2 * LINE_CON, HD), BF),
             pltpu.VMEM((4 * LINE_CON, HD), BF),
             pltpu.VMEM((4 * LINE_CON, 2 * HD), BF),
-            pltpu.VMEM((4 * LINE_TXT, HD), BF),
-            pltpu.VMEM((4 * LINE_TXT, 2 * HD), BF),
+            pltpu.VMEM((2 * LINE_TXT, HD), BF),
+            pltpu.VMEM((2 * LINE_TXT, 2 * HD), BF),
             pltpu.VMEM((32 * n_img, 2 * HD), BF),
         ),
         limit=32,

time: 74.4 us -> 74.3 us (level)
  transfers between devices with their start and end apart: 25 -> 25, of which waited for: 7 -> 7; matrix products, arithmetic and copies ran while one was open for 2% -> 2% of each run, Pallas kernels for 19% -> 20%
where the time goes in v9:
time: 74.3 us; the launch traced here: 74 us
  starting transfers between devices  36.6 us (49%)
  Pallas kernels  21.6 us (29%)
  waiting for transfers between devices  11.6 us (16%)
  between operations  2.14 us (3%)
  local copies, waits for them, and re-layouts  1.37 us (2%)
    ppermute x25, starting transfers between devices, send(): return lax.ppermute(array, ('ctx', 'head'), pairing)  36.6 us
    pallas_call x14, Pallas kernels, run(): pl.pallas_call(kernel, out_shape=outs, in_specs=[sm] * smem + [vm] * (len...  21.6 us
    ppermute x25, waiting for transfers between devices, send(): return lax.ppermute(array, ('ctx', 'head'), pairing)  11.6 us
  transfers between devices with their start and end apart: 25, of which 7 were waited for; matrix products, arithmetic and copies ran while one was open for 2% of the time, Pallas kernels for 20%

profile of v9, /device:TPU:1, one launch (start us, length us, event | category | flops | bytes accessed | tf_op | source)
XLA Modules:
  0.0 74.0 jit_solution(542281068220376427)
XLA Ops:
  0.7 2.1 %shard_map.116 = (bf16[32,3072]{1,0:T(8,128)(2,1)S(1)}, bf16[48,3072]{1,0:T(8,128)(2,1)S(1)}, bf16[96,384]{1,0:T(8,128)(2,1)S(1)}) custom-call(s32[6]{0:T(128)S(1)} %stack.45.at, s32[1,1024]{1,0:T(1,128)} %bitcast.134, s32[1,512]{1,0:T(1,128)} %bitcast.138, bf16[256,3072]{1,0:T(8,128)(2,1)} %table_ref.1, bf16[32,768]{1,0:T(8,128)(2,1)} %q_ref.1, ...), custom_call_target="tpu_custom_call" | custom-call | flops 1100000000 | tf_op jit(solution)/shard_map/pallas_call | solution.py:220
  2.9 4.5 %collective-permute-start.2 = (bf16[32,3072]{1,0:T(8,128)(2,1)S(1)}, bf16[32,3072]{1,0:T(8,128)(2,1)S(1)}, u32[]{:S(2)}, u32[]{:S(2)}) collective-permute-start(bf16[32,3072]{1,0:T(8,128)(2,1)S(1)} %get-tuple-element.103.refs_0_), channel_id=1, source_target_pairs={{0,1},{1,0},{2,3},{3,2},{4,5},{5,4},{6,7},{7,6},{8,9},{9,8},{10,11... | collective-permute-start | bytes 589832 | tf_op jit(solution)/shard_map/ppermute | solution.py:205
  8.1 1.2 %collective-permute-start.1 = (bf16[48,3072]{1,0:T(8,128)(2,1)S(1)}, bf16[48,3072]{1,0:T(8,128)(2,1)S(1)}, u32[]{:S(2)}, u32[]{:S(2)}) collective-permute-start(bf16[48,3072]{1,0:T(8,128)(2,1)S(1)} %get-tuple-element.101), channel_id=1, source_target_pairs={{0,2},{1,3},{2,0},{3,1},{4,6},{5,7},{6,4},{7,5},{8,10},{9,11},{10,... | collective-permute-start | bytes 884744 | tf_op jit(solution)/shard_map/ppermute | solution.py:205
  11.3 1.4 %collective-permute-start.3 = (bf16[192,128]{1,0:T(8,128)(2,1)S(1)}, bf16[192,128]{1,0:T(8,128)(2,1)S(1)}, u32[]{:S(2)}, u32[]{:S(2)}) collective-permute-start(bf16[192,128]{1,0:T(8,128)(2,1)S(1)} %get-tuple-element.105), channel_id=1, source_target_pairs={{0,32},{1,33},{2,6},{3,7},{4,36},{5,37},{6,2},{7,3},{8,40},{9,41},... | collective-permute-start | bytes 147464 | tf_op jit(solution)/shard_map/ppermute | solution.py:205
  12.7 2.6 %collective-permute-start.5 = (bf16[192,128]{1,0:T(8,128)(2,1)S(1)}, bf16[192,128]{1,0:T(8,128)(2,1)S(1)}, u32[]{:S(2)}, u32[]{:S(2)}) collective-permute-start(bf16[192,128]{1,0:T(8,128)(2,1)S(1)} %get-tuple-element.107), channel_id=1, source_target_pairs={{0,64},{1,65},{2,10},{3,11},{4,68},{5,69},{6,14},{7,15},{8,72},{9,... | collective-permute-start | bytes 147464 | tf_op jit(solution)/shard_map/ppermute | solution.py:205
  15.3 4.0 %shard_map.115 = (bf16[160,256]{1,0:T(8,128)(2,1)S(1)}, s32[8,1536]{1,0:T(8,128)S(1)}, f32[1,1280]{1,0:T(1,128)S(1)}, f32[1,704]{1,0:T(1,128)S(1)}, s32[1,384]{1...) custom-call(s32[6]{0:T(128)S(1)} %stack.45.at, s32[1,1024]{1,0:T(1,128)S(1)} %bitcast.135, ...), custom_call_target="tpu_custom_call" | custom-call | flops 2200000000 | tf_op jit(solution)/shard_map/pallas_call | solution.py:220
  20.4 2.7 %collective-permute-start.6 = (bf16[192,128]{1,0:T(8,128)(2,1)S(1)}, bf16[192,128]{1,0:T(8,128)(2,1)S(1)}, u32[]{:S(2)}, u32[]{:S(2)}) collective-permute-start(bf16[192,128]{1,0:T(8,128)(2,1)S(1)} %get-tuple-element.109), channel_id=1, source_target_pairs={{0,96},{1,97},{2,14},{3,15},{4,100},{5,101},{6,10},{7,11},{8,104},... | collective-permute-start | bytes 147464 | tf_op jit(solution)/shard_map/ppermute | solution.py:205
  23.1 3.8 %shard_map.118 = (bf16[208,256]{1,0:T(8,128)(2,1)S(1)}, bf16[208,256]{1,0:T(8,128)(2,1)S(1)}, bf16[208,256]{1,0:T(8,128)(2,1)S(1)}, bf16[208,256]{1,0:T(8,128)(2,1)S(1)}) custom-call(s32[6]{0:T(128)S(1)} %stack.45.at, bf16[160,256]{1,0:T(8,128)(2,1)S(1)} %get-tuple-element.110.pack_ref, bf16[32,3072]{1,0:T(8,128)(2,1)S(1)} %get-tuple-element.103.refs_0_, ...), custom_call_target="tpu_custom_call" | custom-call | flops 5500000256 | tf_op jit(solution)/shard_map/pallas_call | solution.py:220
  27.1 1.6 %collective-permute-start.16 = (bf16[208,256]{1,0:T(8,128)(2,1)S(1)}, bf16[208,256]{1,0:T(8,128)(2,1)S(1)}, u32[]{:S(2)}, u32[]{:S(2)}) collective-permute-start(bf16[208,256]{1,0:T(8,128)(2,1)S(1)} %get-tuple-element.126), channel_id=1, source_target_pairs={{0,96},{1,97},{2,14},{3,15},{4,100},{5,101},{6,10},{7,11},{8,104},... | collective-permute-start | bytes 319496 | tf_op jit(solution)/shard_map/ppermute | solution.py:205
  28.7 1.6 %collective-permute-start.17 = (bf16[208,256]{1,0:T(8,128)(2,1)S(1)}, bf16[208,256]{1,0:T(8,128)(2,1)S(1)}, u32[]{:S(2)}, u32[]{:S(2)}) collective-permute-start(bf16[208,256]{1,0:T(8,128)(2,1)S(1)} %get-tuple-element.127), channel_id=1, source_target_pairs={{0,64},{1,65},{2,10},{3,11},{4,68},{5,69},{6,14},{7,15},{8,72},{9,... | collective-permute-start | bytes 319496 | tf_op jit(solution)/shard_map/ppermute | solution.py:205
  30.4 1.2 %collective-permute-start.12 = (bf16[512,128]{1,0:T(8,128)(2,1)S(1)}, bf16[512,128]{1,0:T(8,128)(2,1)S(1)}, u32[]{:S(2)}, u32[]{:S(2)}) collective-permute-start(bf16[512,128]{1,0:T(8,128)(2,1)S(1)} %get-tuple-element.120.a), channel_id=1, source_target_pairs={{0,12},{1,13},{2,98},{3,99},{4,8},{5,9},{6,102},{7,103},{8,4},{9,5... | collective-permute-start | bytes 393224 | tf_op jit(solution)/shard_map/ppermute | solution.py:205
  31.6 2.0 %collective-permute-start.13 = (bf16[512,128]{1,0:T(8,128)(2,1)S(1)}, bf16[512,128]{1,0:T(8,128)(2,1)S(1)}, u32[]{:S(2)}, u32[]{:S(2)}) collective-permute-start(bf16[512,128]{1,0:T(8,128)(2,1)S(1)} %get-tuple-element.120.a), channel_id=1, source_target_pairs={{0,8},{1,9},{2,66},{3,67},{4,12},{5,13},{6,70},{7,71},{8,0},{9,1},... | collective-permute-start | bytes 393224 | tf_op jit(solution)/shard_map/ppermute | solution.py:205
  34.7 1.2 %collective-permute-start.19 = (bf16[656,256]{1,0:T(8,128)(2,1)S(1)}, bf16[656,256]{1,0:T(8,128)(2,1)S(1)}, u32[]{:S(2)}, u32[]{:S(2)}) collective-permute-start(bf16[656,256]{1,0:T(8,128)(2,1)S(1)} %shard_map.121.l0), channel_id=1, source_target_pairs={{0,12},{1,13},{2,98},{3,99},{4,8},{5,9},{6,102},{7,103},{8,4},{9,5... | collective-permute-start | bytes 1007624 | tf_op jit(solution)/shard_map/ppermute | solution.py:205
  35.9 2.0 %collective-permute-start.20 = (bf16[656,256]{1,0:T(8,128)(2,1)S(1)}, bf16[656,256]{1,0:T(8,128)(2,1)S(1)}, u32[]{:S(2)}, u32[]{:S(2)}) collective-permute-start(bf16[656,256]{1,0:T(8,128)(2,1)S(1)} %shard_map.121.l0), channel_id=1, source_target_pairs={{0,8},{1,9},{2,66},{3,67},{4,12},{5,13},{6,70},{7,71},{8,0},{9,1},... | collective-permute-start | bytes 1007624 | tf_op jit(solution)/shard_map/ppermute | solution.py:205
  37.9 1.1 %collective-permute-start.14 = (bf16[2048,128]{1,0:T(8,128)(2,1)S(1)}, bf16[2048,128]{1,0:T(8,128)(2,1)S(1)}, u32[]{:S(2)}, u32[]{:S(2)}) collective-permute-start(bf16[2048,128]{1,0:T(8,128)(2,1)S(1)} %shard_map.120.plane), channel_id=1, source_target_pairs={{0,16},{1,17},{2,18},{3,19},{4,20},{5,21},{6,22},{7,23},{8,24},{9,... | collective-permute-start | bytes 1572872 | tf_op jit(solution)/shard_map/ppermute | solution.py:205
  39.5 0.8 %shard_map.122 = (f32[256,1]{1,0:T(8,128)S(1)}, f32[256,256]{1,0:T(8,128)S(1)}) custom-call(bf16[2048,128]{1,0:T(8,128)(2,1)S(1)} %shard_map.120.plane, bf16[256,128]{1,0:T(8,128)(2,1)S(1)} %get-tuple-element.131.q.img_q), custom_call_target="tpu_custom_call" | custom-call | flops 1100000000 | tf_op jit(solution)/shard_map/pallas_call | solution.py:220
  40.9 0.9 %shard_map.123 = (bf16[1024,128]{1,0:T(8,128)(2,1)S(1)}, f32[256,1]{1,0:T(8,128)S(1)}, f32[256,256]{1,0:T(8,128)S(1)}) custom-call(bf16[1024,1280]{1,0:T(8,128)(2,1)S(1)} %fusion.81.pick, bf16[656,256]{1,0:T(8,128)(2,1)S(1)} %shard_map.121.l0, bf16[656,256]{1,0:T(8,128)(2,1)S(1)} %collective-permute-done.18.l1, f32[1,704]{1,0:T(1,128)S(1)} %get-tuple-element.130.txt_bias, ...), custom_call_target="tpu_custom_call" | custom-call | flops 1100000000 | tf_op jit(solution)/shard_map/pallas_call | solution.py:220
  41.8 4.0 %collective-permute-done.19.l3 = bf16[656,256]{1,0:T(8,128)(2,1)S(1)} collective-permute-done((bf16[656,256]{1,0:T(8,128)(2,1)S(1)}, bf16[656,256]{1,0:T(8,128)(2,1)S(1)}, u32[]{:S(2)}, u32[]{:S(2)}) %collective-permute-start.19) | collective-permute-done | bytes 335904 | tf_op jit(solution)/shard_map/ppermute | solution.py:205
  45.8 4.1 %shard_map.124 = (bf16[1024,128]{1,0:T(8,128)(2,1)S(1)}, f32[1024,1]{1,0:T(8,128)S(1)}, f32[1024,256]{1,0:T(8,128)S(1)}, f32[256,1]{1,0:T(8,128)S(1)}, f32[256,256]{1,0:T(8,128)S(1)}) custom-call(bf16[1024,1280]{1,0:T(8,128)(2,1)S(1)} %fusion.81.pick, bf16[1024,128]{1,0:T(8,128)(2,1)S(1)} %get-tuple-element.134.q_part, bf16[656,256]{1,0:T(8,128)(2,1)S(1)} %shard_map.121.l0, ...), custom_call_target="tpu_custom_call" | custom-call | flops 2200000000 | tf_op jit(solution)/shard_map/pallas_call | solution.py:220
  49.9 2.5 %shard_map.125 = (bf16[72,1152]{1,0:T(8,128)(2,1)S(1)}, bf16[72,1152]{1,0:T(8,128)(2,1)S(1)}, bf16[72,1152]{1,0:T(8,128)(2,1)S(1)}, bf16[72,1152]{1,0:T(8,128)(2,1)S(1)}) custom-call(bf16[2048,128]{1,0:T(8,128)(2,1)S(1)} %collective-permute-done.14.plane, bf16[1024,128]{1,0:T(8,128)(2,1)S(1)} %get-tuple-element.138.con_q, ...), custom_call_target="tpu_custom_call" | custom-call | flops 3300000000 | tf_op jit(solution)/shard_map/pallas_call | solution.py:220
  52.5 1.5 %collective-permute-start.22 = (bf16[72,1152]{1,0:T(8,128)(2,1)S(1)}, bf16[72,1152]{1,0:T(8,128)(2,1)S(1)}, u32[]{:S(2)}, u32[]{:S(2)}) collective-permute-start(bf16[72,1152]{1,0:T(8,128)(2,1)S(1)} %get-tuple-element.145), channel_id=1, source_target_pairs={{0,96},{1,97},{2,14},{3,15},{4,100},{5,101},{6,10},{7,11},{8,104},... | collective-permute-start | bytes 497672 | tf_op jit(solution)/shard_map/ppermute | solution.py:205
  54.0 1.6 %collective-permute-start.23 = (bf16[72,1152]{1,0:T(8,128)(2,1)S(1)}, bf16[72,1152]{1,0:T(8,128)(2,1)S(1)}, u32[]{:S(2)}, u32[]{:S(2)}) collective-permute-start(bf16[72,1152]{1,0:T(8,128)(2,1)S(1)} %get-tuple-element.146), channel_id=1, source_target_pairs={{0,64},{1,65},{2,10},{3,11},{4,68},{5,69},{6,14},{7,15},{8,72},{9,... | collective-permute-start | bytes 497672 | tf_op jit(solution)/shard_map/ppermute | solution.py:205
  55.7 0.9 %collective-permute-done.21.b1 = bf16[72,1152]{1,0:T(8,128)(2,1)S(1)} collective-permute-done((bf16[72,1152]{1,0:T(8,128)(2,1)S(1)}, bf16[72,1152]{1,0:T(8,128)(2,1)S(1)}, u32[]{:S(2)}, u32[]{:S(2)}) %collective-permute-start.21) | collective-permute-done | bytes 165920 | tf_op jit(solution)/shard_map/ppermute | solution.py:205
  56.6 1.3 %collective-permute-done.22.b2 = bf16[72,1152]{1,0:T(8,128)(2,1)S(1)} collective-permute-done((bf16[72,1152]{1,0:T(8,128)(2,1)S(1)}, bf16[72,1152]{1,0:T(8,128)(2,1)S(1)}, u32[]{:S(2)}, u32[]{:S(2)}) %collective-permute-start.22) | collective-permute-done | bytes 165920 | tf_op jit(solution)/shard_map/ppermute | solution.py:205
  57.9 1.8 %collective-permute-done.23.b3 = bf16[72,1152]{1,0:T(8,128)(2,1)S(1)} collective-permute-done((bf16[72,1152]{1,0:T(8,128)(2,1)S(1)}, bf16[72,1152]{1,0:T(8,128)(2,1)S(1)}, u32[]{:S(2)}, u32[]{:S(2)}) %collective-permute-start.23) | collective-permute-done | bytes 165920 | tf_op jit(solution)/shard_map/ppermute | solution.py:205
  59.7 0.8 %shard_map.126 = (bf16[40,1536]{1,0:T(8,128)(2,1)S(1)}, bf16[40,1536]{1,0:T(8,128)(2,1)S(1)}) custom-call(s32[6]{0:T(128)S(1)} %stack.45.at, bf16[72,1152]{1,0:T(8,128)(2,1)S(1)} %get-tuple-element.143.b0, bf16[72,1152]{1,0:T(8,128)(2,1)S(1)} %collective-permute-done.21.b1, bf16[72,1152]{1,0:T(8,128)(2,1)S(1)} %collective-permute-done.22.b2, ...), custom_call_target="tpu_custom_call" | custom-call | flops 1100000000 | tf_op jit(solution)/shard_map/pallas_call | solution.py:220
  60.5 5.0 %collective-permute-start.24 = (bf16[40,1536]{1,0:T(8,128)(2,1)S(1)}, bf16[40,1536]{1,0:T(8,128)(2,1)S(1)}, u32[]{:S(2)}, u32[]{:S(2)}) collective-permute-start(bf16[40,1536]{1,0:T(8,128)(2,1)S(1)} %get-tuple-element.148), channel_id=1, source_target_pairs={{0,2},{1,3},{2,0},{3,1},{4,6},{5,7},{6,4},{7,5},{8,10},{9,11},{10,... | collective-permute-start | bytes 368648 | tf_op jit(solution)/shard_map/ppermute | solution.py:205
  65.6 1.0 %collective-permute-done.24.core = bf16[40,1536]{1,0:T(8,128)(2,1)S(1)} collective-permute-done((bf16[40,1536]{1,0:T(8,128)(2,1)S(1)}, bf16[40,1536]{1,0:T(8,128)(2,1)S(1)}, u32[]{:S(2)}, u32[]{:S(2)}) %collective-permute-start.24) | collective-permute-done | bytes 122912 | tf_op jit(solution)/shard_map/ppermute | solution.py:205
  66.6 2.9 %collective-permute-start.25 = (bf16[40,1152]{1,0:T(8,128)(2,1)S(1)}, bf16[40,1152]{1,0:T(8,128)(2,1)S(1)}, u32[]{:S(2)}, u32[]{:S(2)}) collective-permute-start(bf16[40,1152]{1,0:T(8,128)(2,1)S(1)} %shard_map.127), channel_id=1, source_target_pairs={{0,1},{1,0},{2,3},{3,2},{4,5},{5,4},{6,7},{7,6},{8,9},{9,8},{10,11... | collective-permute-start | bytes 276488 | tf_op jit(solution)/shard_map/ppermute | solution.py:205
  70.1 1.9 %collective-permute-done.25 = bf16[40,1152]{1,0:T(8,128)(2,1)S(1)} collective-permute-done((bf16[40,1152]{1,0:T(8,128)(2,1)S(1)}, bf16[40,1152]{1,0:T(8,128)(2,1)S(1)}, u32[]{:S(2)}, u32[]{:S(2)}) %collective-permute-start.25) | collective-permute-done | bytes 92192 | tf_op jit(solution)/shard_map/ppermute | solution.py:205
  72.1 2.0 %conditional.1 = (bf16[32,768]{1,0:T(8,128)(2,1)}, f32[1024,32]{0,1:T(8,128)}) conditional(s32[]{:T(128)} %convert_element_type.62, (s32[512]{0:T(512)S(1)}, s32[1024]{0:T(1024)S(1)}, bf16[256,3072]{1,0:T(8,128)(2,1)S(1)}, s32[1]{0:T(128)}, f32[28,2,3072]{2,1,0:T(2,128)}, /*index=5*/bf16[3072,3,768]{2,0,1:T(8,128)(2,1)}, f32[2,128]{1,0:T(2,128)S(1)}, ...), branch_computations={%region_0.15_spmd, %region_15.16_spmd} | conditional | flops 1100000000 | bytes 257951312 | solution.py:832
  72.4 1.7 %branch_1_fun.1 = (bf16[32,768]{1,0:T(8,128)(2,1)}, f32[32,1024]{1,0:T(8,128)}) custom-call(s32[6]{0:T(128)S(1)} %get-tuple-element.40.at, bf16[40,1152]{1,0:T(8,128)(2,1)S(1)} %get-tuple-element.41.sums, bf16[40,1152]{1,0:T(8,128)(2,1)S(1)} %get-tuple-element.42.head, bf16[40,1536]{1,0:T(8,128)(2,1)} %get-tuple-element.43.own, ...), custom_call_target="tpu_custom_call" | custom-call | flops 1100000000 | tf_op jit(solution)/shard_map/cond/branch_1_fun/pallas_call | solution.py:220
  (54 shorter events, 5.8 us)
Async XLA Ops:
  0.7 14.6 %copy-start.8 = (s32[1024]{0:T(1024)S(1)}, s32[1024]{0:T(1024)}, u32[]{:S(2)}) copy-start(s32[1024]{0:T(1024)} %param.16) | copy-start | bytes 12292
  0.7 14.6 %copy-start.9 = (s32[512]{0:T(512)S(1)}, s32[512]{0:T(512)}, u32[]{:S(2)}) copy-start(s32[512]{0:T(512)} %param.15) | copy-start | bytes 6148
  2.9 17.0 %collective-permute-start.2 = (bf16[32,3072]{1,0:T(8,128)(2,1)S(1)}, bf16[32,3072]{1,0:T(8,128)(2,1)S(1)}, u32[]{:S(2)}, u32[]{:S(2)}) collective-permute-start(bf16[32,3072]{1,0:T(8,128)(2,1)S(1)} %get-tuple-element.103.refs_0_), channel_id=1, source_target_pairs={{0,1},{1,0},{2,3},{3,2},{4,5},{5,4},{6,7},{7,6},{8,9},{9,8},{10,11... | collective-permute-start | bytes 589832 | tf_op jit(solution)/shard_map/ppermute | solution.py:205
  7.3 12.6 %collective-permute-start.4 = (bf16[32,3072]{1,0:T(8,128)(2,1)S(1)}, bf16[32,3072]{1,0:T(8,128)(2,1)S(1)}, u32[]{:S(2)}, u32[]{:S(2)}) collective-permute-start(bf16[32,3072]{1,0:T(8,128)(2,1)S(1)} %get-tuple-element.103.refs_0_), channel_id=1, source_target_pairs={{0,16},{1,17},{2,18},{3,19},{4,20},{5,21},{6,22},{7,23},{8,24},{9,... | collective-permute-start | bytes 589832 | tf_op jit(solution)/shard_map/ppermute | solution.py:205
  8.1 11.2 %collective-permute-start.7 = (bf16[32,3072]{1,0:T(8,128)(2,1)S(1)}, bf16[32,3072]{1,0:T(8,128)(2,1)S(1)}, u32[]{:S(2)}, u32[]{:S(2)}) collective-permute-start(bf16[32,3072]{1,0:T(8,128)(2,1)S(1)} %get-tuple-element.103.refs_0_), channel_id=1, source_target_pairs={{0,17},{1,16},{2,19},{3,18},{4,21},{5,20},{6,23},{7,22},{8,25},{9,... | collective-permute-start | bytes 589832 | tf_op jit(solution)/shard_map/ppermute | solution.py:205
  8.1 2.6 %collective-permute-start.1 = (bf16[48,3072]{1,0:T(8,128)(2,1)S(1)}, bf16[48,3072]{1,0:T(8,128)(2,1)S(1)}, u32[]{:S(2)}, u32[]{:S(2)}) collective-permute-start(bf16[48,3072]{1,0:T(8,128)(2,1)S(1)} %get-tuple-element.101), channel_id=1, source_target_pairs={{0,2},{1,3},{2,0},{3,1},{4,6},{5,7},{6,4},{7,5},{8,10},{9,11},{10,... | collective-permute-start | bytes 884744 | tf_op jit(solution)/shard_map/ppermute | solution.py:205
  11.3 8.5 %collective-permute-start.3 = (bf16[192,128]{1,0:T(8,128)(2,1)S(1)}, bf16[192,128]{1,0:T(8,128)(2,1)S(1)}, u32[]{:S(2)}, u32[]{:S(2)}) collective-permute-start(bf16[192,128]{1,0:T(8,128)(2,1)S(1)} %get-tuple-element.105), channel_id=1, source_target_pairs={{0,32},{1,33},{2,6},{3,7},{4,36},{5,37},{6,2},{7,3},{8,40},{9,41},... | collective-permute-start | bytes 147464 | tf_op jit(solution)/shard_map/ppermute | solution.py:205
  12.7 7.3 %collective-permute-start.5 = (bf16[192,128]{1,0:T(8,128)(2,1)S(1)}, bf16[192,128]{1,0:T(8,128)(2,1)S(1)}, u32[]{:S(2)}, u32[]{:S(2)}) collective-permute-start(bf16[192,128]{1,0:T(8,128)(2,1)S(1)} %get-tuple-element.107), channel_id=1, source_target_pairs={{0,64},{1,65},{2,10},{3,11},{4,68},{5,69},{6,14},{7,15},{8,72},{9,... | collective-permute-start | bytes 147464 | tf_op jit(solution)/shard_map/ppermute | solution.py:205
  15.3 7.8 %copy-start.10 = (f32[2,128]{1,0:T(2,128)S(1)}, f32[2,128]{1,0:T(2,128)}, u32[]{:S(2)}) copy-start(f32[2,128]{1,0:T(2,128)} %refs_9_.1) | copy-start | bytes 3076
  19.3 3.8 %collective-permute-start.10 = (bf16[32,3072]{1,0:T(8,128)(2,1)S(1)}, bf16[32,3072]{1,0:T(8,128)(2,1)S(1)}, u32[]{:S(2)}, u32[]{:S(2)}) collective-permute-start(bf16[32,3072]{1,0:T(8,128)(2,1)S(1)} %collective-permute-done.7.refs_3_), channel_id=1, source_target_pairs={{0,2},{1,3},{2,0},{3,1},{4,6},{5,7},{6,4},{7,5},{8,10},{9,11},{10,... | collective-permute-start | bytes 589832 | tf_op jit(solution)/shard_map/ppermute | solution.py:205
  19.9 3.3 %collective-permute-start.9 = (bf16[32,3072]{1,0:T(8,128)(2,1)S(1)}, bf16[32,3072]{1,0:T(8,128)(2,1)S(1)}, u32[]{:S(2)}, u32[]{:S(2)}) collective-permute-start(bf16[32,3072]{1,0:T(8,128)(2,1)S(1)} %collective-permute-done.2.refs_2_), channel_id=1, source_target_pairs={{0,2},{1,3},{2,0},{3,1},{4,6},{5,7},{6,4},{7,5},{8,10},{9,11},{10,... | collective-permute-start | bytes 589832 | tf_op jit(solution)/shard_map/ppermute | solution.py:205
  20.0 3.1 %collective-permute-start.8 = (bf16[32,3072]{1,0:T(8,128)(2,1)S(1)}, bf16[32,3072]{1,0:T(8,128)(2,1)S(1)}, u32[]{:S(2)}, u32[]{:S(2)}) collective-permute-start(bf16[32,3072]{1,0:T(8,128)(2,1)S(1)} %collective-permute-done.4.refs_1_), channel_id=1, source_target_pairs={{0,2},{1,3},{2,0},{3,1},{4,6},{5,7},{6,4},{7,5},{8,10},{9,11},{10,... | collective-permute-start | bytes 589832 | tf_op jit(solution)/shard_map/ppermute | solution.py:205
  20.4 6.7 %collective-permute-start.6 = (bf16[192,128]{1,0:T(8,128)(2,1)S(1)}, bf16[192,128]{1,0:T(8,128)(2,1)S(1)}, u32[]{:S(2)}, u32[]{:S(2)}) collective-permute-start(bf16[192,128]{1,0:T(8,128)(2,1)S(1)} %get-tuple-element.109), channel_id=1, source_target_pairs={{0,96},{1,97},{2,14},{3,15},{4,100},{5,101},{6,10},{7,11},{8,104},... | collective-permute-start | bytes 147464 | tf_op jit(solution)/shard_map/ppermute | solution.py:205
  26.9 4.7 %collective-permute-start.15 = (bf16[208,256]{1,0:T(8,128)(2,1)S(1)}, bf16[208,256]{1,0:T(8,128)(2,1)S(1)}, u32[]{:S(2)}, u32[]{:S(2)}) collective-permute-start(bf16[208,256]{1,0:T(8,128)(2,1)S(1)} %get-tuple-element.125), channel_id=1, source_target_pairs={{0,32},{1,33},{2,6},{3,7},{4,36},{5,37},{6,2},{7,3},{8,40},{9,41},... | collective-permute-start | bytes 319496 | tf_op jit(solution)/shard_map/ppermute | solution.py:205
  27.1 7.1 %collective-permute-start.16 = (bf16[208,256]{1,0:T(8,128)(2,1)S(1)}, bf16[208,256]{1,0:T(8,128)(2,1)S(1)}, u32[]{:S(2)}, u32[]{:S(2)}) collective-permute-start(bf16[208,256]{1,0:T(8,128)(2,1)S(1)} %get-tuple-element.126), channel_id=1, source_target_pairs={{0,96},{1,97},{2,14},{3,15},{4,100},{5,101},{6,10},{7,11},{8,104},... | collective-permute-start | bytes 319496 | tf_op jit(solution)/shard_map/ppermute | solution.py:205
  28.7 5.5 %collective-permute-start.17 = (bf16[208,256]{1,0:T(8,128)(2,1)S(1)}, bf16[208,256]{1,0:T(8,128)(2,1)S(1)}, u32[]{:S(2)}, u32[]{:S(2)}) collective-permute-start(bf16[208,256]{1,0:T(8,128)(2,1)S(1)} %get-tuple-element.127), channel_id=1, source_target_pairs={{0,64},{1,65},{2,10},{3,11},{4,68},{5,69},{6,14},{7,15},{8,72},{9,... | collective-permute-start | bytes 319496 | tf_op jit(solution)/shard_map/ppermute | solution.py:205
  30.3 5.6 %collective-permute-start.11 = (bf16[512,128]{1,0:T(8,128)(2,1)S(1)}, bf16[512,128]{1,0:T(8,128)(2,1)S(1)}, u32[]{:S(2)}, u32[]{:S(2)}) collective-permute-start(bf16[512,128]{1,0:T(8,128)(2,1)S(1)} %get-tuple-element.120.a), channel_id=1, source_target_pairs={{0,4},{1,5},{2,34},{3,35},{4,0},{5,1},{6,38},{7,39},{8,12},{9,13},... | collective-permute-start | bytes 393224 | tf_op jit(solution)/shard_map/ppermute | solution.py:205
  30.4 7.5 %collective-permute-start.12 = (bf16[512,128]{1,0:T(8,128)(2,1)S(1)}, bf16[512,128]{1,0:T(8,128)(2,1)S(1)}, u32[]{:S(2)}, u32[]{:S(2)}) collective-permute-start(bf16[512,128]{1,0:T(8,128)(2,1)S(1)} %get-tuple-element.120.a), channel_id=1, source_target_pairs={{0,12},{1,13},{2,98},{3,99},{4,8},{5,9},{6,102},{7,103},{8,4},{9,5... | collective-permute-start | bytes 393224 | tf_op jit(solution)/shard_map/ppermute | solution.py:205
  31.6 6.2 %collective-permute-start.13 = (bf16[512,128]{1,0:T(8,128)(2,1)S(1)}, bf16[512,128]{1,0:T(8,128)(2,1)S(1)}, u32[]{:S(2)}, u32[]{:S(2)}) collective-permute-start(bf16[512,128]{1,0:T(8,128)(2,1)S(1)} %get-tuple-element.120.a), channel_id=1, source_target_pairs={{0,8},{1,9},{2,66},{3,67},{4,12},{5,13},{6,70},{7,71},{8,0},{9,1},... | collective-permute-start | bytes 393224 | tf_op jit(solution)/shard_map/ppermute | solution.py:205
  34.5 6.4 %collective-permute-start.18 = (bf16[656,256]{1,0:T(8,128)(2,1)S(1)}, bf16[656,256]{1,0:T(8,128)(2,1)S(1)}, u32[]{:S(2)}, u32[]{:S(2)}) collective-permute-start(bf16[656,256]{1,0:T(8,128)(2,1)S(1)} %shard_map.121.l0), channel_id=1, source_target_pairs={{0,4},{1,5},{2,34},{3,35},{4,0},{5,1},{6,38},{7,39},{8,12},{9,13},... | collective-permute-start | bytes 1007624 | tf_op jit(solution)/shard_map/ppermute | solution.py:205
  34.7 11.1 %collective-permute-start.19 = (bf16[656,256]{1,0:T(8,128)(2,1)S(1)}, bf16[656,256]{1,0:T(8,128)(2,1)S(1)}, u32[]{:S(2)}, u32[]{:S(2)}) collective-permute-start(bf16[656,256]{1,0:T(8,128)(2,1)S(1)} %shard_map.121.l0), channel_id=1, source_target_pairs={{0,12},{1,13},{2,98},{3,99},{4,8},{5,9},{6,102},{7,103},{8,4},{9,5... | collective-permute-start | bytes 1007624 | tf_op jit(solution)/shard_map/ppermute | solution.py:205
  35.9 10.0 %collective-permute-start.20 = (bf16[656,256]{1,0:T(8,128)(2,1)S(1)}, bf16[656,256]{1,0:T(8,128)(2,1)S(1)}, u32[]{:S(2)}, u32[]{:S(2)}) collective-permute-start(bf16[656,256]{1,0:T(8,128)(2,1)S(1)} %shard_map.121.l0), channel_id=1, source_target_pairs={{0,8},{1,9},{2,66},{3,67},{4,12},{5,13},{6,70},{7,71},{8,0},{9,1},... | collective-permute-start | bytes 1007624 | tf_op jit(solution)/shard_map/ppermute | solution.py:205
  37.9 12.0 %collective-permute-start.14 = (bf16[2048,128]{1,0:T(8,128)(2,1)S(1)}, bf16[2048,128]{1,0:T(8,128)(2,1)S(1)}, u32[]{:S(2)}, u32[]{:S(2)}) collective-permute-start(bf16[2048,128]{1,0:T(8,128)(2,1)S(1)} %shard_map.120.plane), channel_id=1, source_target_pairs={{0,16},{1,17},{2,18},{3,19},{4,20},{5,21},{6,22},{7,23},{8,24},{9,... | collective-permute-start | bytes 1572872 | tf_op jit(solution)/shard_map/ppermute | solution.py:205
  52.3 4.3 %collective-permute-start.21 = (bf16[72,1152]{1,0:T(8,128)(2,1)S(1)}, bf16[72,1152]{1,0:T(8,128)(2,1)S(1)}, u32[]{:S(2)}, u32[]{:S(2)}) collective-permute-start(bf16[72,1152]{1,0:T(8,128)(2,1)S(1)} %get-tuple-element.144), channel_id=1, source_target_pairs={{0,32},{1,33},{2,6},{3,7},{4,36},{5,37},{6,2},{7,3},{8,40},{9,41},... | collective-permute-start | bytes 497672 | tf_op jit(solution)/shard_map/ppermute | solution.py:205
  52.5 5.4 %collective-permute-start.22 = (bf16[72,1152]{1,0:T(8,128)(2,1)S(1)}, bf16[72,1152]{1,0:T(8,128)(2,1)S(1)}, u32[]{:S(2)}, u32[]{:S(2)}) collective-permute-start(bf16[72,1152]{1,0:T(8,128)(2,1)S(1)} %get-tuple-element.145), channel_id=1, source_target_pairs={{0,96},{1,97},{2,14},{3,15},{4,100},{5,101},{6,10},{7,11},{8,104},... | collective-permute-start | bytes 497672 | tf_op jit(solution)/shard_map/ppermute | solution.py:205
  54.0 5.7 %collective-permute-start.23 = (bf16[72,1152]{1,0:T(8,128)(2,1)S(1)}, bf16[72,1152]{1,0:T(8,128)(2,1)S(1)}, u32[]{:S(2)}, u32[]{:S(2)}) collective-permute-start(bf16[72,1152]{1,0:T(8,128)(2,1)S(1)} %get-tuple-element.146), channel_id=1, source_target_pairs={{0,64},{1,65},{2,10},{3,11},{4,68},{5,69},{6,14},{7,15},{8,72},{9,... | collective-permute-start | bytes 497672 | tf_op jit(solution)/shard_map/ppermute | solution.py:205
  59.7 12.4 %copy-start = (bf16[256,3072]{1,0:T(8,128)(2,1)S(1)}, bf16[256,3072]{1,0:T(8,128)(2,1)}, u32[]{:S(2)}) copy-start(bf16[256,3072]{1,0:T(8,128)(2,1)} %table_ref.1) | copy-start | bytes 4718596
  59.7 12.4 %copy-start.3 = (bf16[32,768]{1,0:T(8,128)(2,1)S(1)}, bf16[32,768]{1,0:T(8,128)(2,1)}, u32[]{:S(2)}) copy-start(bf16[32,768]{1,0:T(8,128)(2,1)} %q_ref.1) | copy-start | bytes 147460
  59.7 12.4 %copy-start.6 = (bf16[32,768]{1,0:T(8,128)(2,1)S(1)}, bf16[32,768]{1,0:T(8,128)(2,1)}, u32[]{:S(2)}) copy-start(bf16[32,768]{1,0:T(8,128)(2,1)} %k_ref.1) | copy-start | bytes 147460
  59.7 12.4 %copy-start.7 = (bf16[32,768]{1,0:T(8,128)(2,1)S(1)}, bf16[32,768]{1,0:T(8,128)(2,1)}, u32[]{:S(2)}) copy-start(bf16[32,768]{1,0:T(8,128)(2,1)} %v_ref.1) | copy-start | bytes 147460
  60.5 6.0 %collective-permute-start.24 = (bf16[40,1536]{1,0:T(8,128)(2,1)S(1)}, bf16[40,1536]{1,0:T(8,128)(2,1)S(1)}, u32[]{:S(2)}, u32[]{:S(2)}) collective-permute-start(bf16[40,1536]{1,0:T(8,128)(2,1)S(1)} %get-tuple-element.148), channel_id=1, source_target_pairs={{0,2},{1,3},{2,0},{3,1},{4,6},{5,7},{6,4},{7,5},{8,10},{9,11},{10,... | collective-permute-start | bytes 368648 | tf_op jit(solution)/shard_map/ppermute | solution.py:205
  66.6 5.5 %collective-permute-start.25 = (bf16[40,1152]{1,0:T(8,128)(2,1)S(1)}, bf16[40,1152]{1,0:T(8,128)(2,1)S(1)}, u32[]{:S(2)}, u32[]{:S(2)}) collective-permute-start(bf16[40,1152]{1,0:T(8,128)(2,1)S(1)} %shard_map.127), channel_id=1, source_target_pairs={{0,1},{1,0},{2,3},{3,2},{4,5},{5,4},{6,7},{7,6},{8,9},{9,8},{10,11... | collective-permute-start | bytes 276488 | tf_op jit(solution)/shard_map/ppermute | solution.py:205
  (1 other events, 6.0 us)

commit v10 on v9

--- a/solution.py
+++ b/solution.py
@@ -771,7 +771,8 @@
     )(*qkv, con_line, txt_line)
     lines = [line] + [send(line, swap_v(s)) for s in (1, 3, 2)]
     plane = call(plane_kernel, sds((64 * n_img, HD)), smem=0)(*image_kvs)
-    con_slot, over, plane = lax.optimization_barrier((spots[0, :n_con], spots[1, 0], plane))
+    spots, plane = lax.optimization_barrier((spots, plane))
+    con_slot, over = spots[0, :n_con], spots[1, 0]
     other_plane = send(plane, swap_plane())
     pick = (con_slot[:, None] == jnp.arange(4 * LINE_CON)[None, :]).astype(BF)
 

time: 74.3 us -> 74.3 us (level)
  transfers between devices with their start and end apart: 25 -> 25, of which waited for: 7 -> 8; matrix products, arithmetic and copies ran while one was open for 2% -> 2% of each run, Pallas kernels for 20% -> 20%
where the time goes in v10:
time: 74.3 us; the launch traced here: 74 us
  starting transfers between devices  36.6 us (49%)
  Pallas kernels  21.6 us (29%)
  waiting for transfers between devices  11.6 us (16%)
  between operations  2.15 us (3%)
  local copies, waits for them, and re-layouts  1.38 us (2%)
    ppermute x25, starting transfers between devices, send(): return lax.ppermute(array, ('ctx', 'head'), pairing)  36.6 us
    pallas_call x14, Pallas kernels, run(): pl.pallas_call(kernel, out_shape=outs, in_specs=[sm] * smem + [vm] * (len...  21.6 us
    ppermute x25, waiting for transfers between devices, send(): return lax.ppermute(array, ('ctx', 'head'), pairing)  11.6 us
  transfers between devices with their start and end apart: 25, of which 8 were waited for; matrix products, arithmetic and copies ran while one was open for 2% of the time, Pallas kernels for 20%

profile of v10, /device:TPU:1, one launch (start us, length us, event | category | flops | bytes accessed | tf_op | source)
XLA Modules:
  0.0 74.0 jit_solution(18209261063871880885)
XLA Ops:
  0.7 2.1 %shard_map.116 = (bf16[32,3072]{1,0:T(8,128)(2,1)S(1)}, bf16[48,3072]{1,0:T(8,128)(2,1)S(1)}, bf16[96,384]{1,0:T(8,128)(2,1)S(1)}) custom-call(s32[6]{0:T(128)S(1)} %stack.45.at, s32[1,1024]{1,0:T(1,128)} %bitcast.134, s32[1,512]{1,0:T(1,128)} %bitcast.138, bf16[256,3072]{1,0:T(8,128)(2,1)} %table_ref.1, bf16[32,768]{1,0:T(8,128)(2,1)} %q_ref.1, ...), custom_call_target="tpu_custom_call" | custom-call | flops 1100000000 | tf_op jit(solution)/shard_map/pallas_call | solution.py:220
  2.9 4.5 %collective-permute-start.2 = (bf16[32,3072]{1,0:T(8,128)(2,1)S(1)}, bf16[32,3072]{1,0:T(8,128)(2,1)S(1)}, u32[]{:S(2)}, u32[]{:S(2)}) collective-permute-start(bf16[32,3072]{1,0:T(8,128)(2,1)S(1)} %get-tuple-element.102.refs_0_), channel_id=1, source_target_pairs={{0,1},{1,0},{2,3},{3,2},{4,5},{5,4},{6,7},{7,6},{8,9},{9,8},{10,11... | collective-permute-start | bytes 589832 | tf_op jit(solution)/shard_map/ppermute | solution.py:205
  8.1 1.2 %collective-permute-start.1 = (bf16[48,3072]{1,0:T(8,128)(2,1)S(1)}, bf16[48,3072]{1,0:T(8,128)(2,1)S(1)}, u32[]{:S(2)}, u32[]{:S(2)}) collective-permute-start(bf16[48,3072]{1,0:T(8,128)(2,1)S(1)} %get-tuple-element.100), channel_id=1, source_target_pairs={{0,2},{1,3},{2,0},{3,1},{4,6},{5,7},{6,4},{7,5},{8,10},{9,11},{10,... | collective-permute-start | bytes 884744 | tf_op jit(solution)/shard_map/ppermute | solution.py:205
  11.3 1.4 %collective-permute-start.3 = (bf16[192,128]{1,0:T(8,128)(2,1)S(1)}, bf16[192,128]{1,0:T(8,128)(2,1)S(1)}, u32[]{:S(2)}, u32[]{:S(2)}) collective-permute-start(bf16[192,128]{1,0:T(8,128)(2,1)S(1)} %get-tuple-element.104), channel_id=1, source_target_pairs={{0,32},{1,33},{2,6},{3,7},{4,36},{5,37},{6,2},{7,3},{8,40},{9,41},... | collective-permute-start | bytes 147464 | tf_op jit(solution)/shard_map/ppermute | solution.py:205
  12.7 2.6 %collective-permute-start.5 = (bf16[192,128]{1,0:T(8,128)(2,1)S(1)}, bf16[192,128]{1,0:T(8,128)(2,1)S(1)}, u32[]{:S(2)}, u32[]{:S(2)}) collective-permute-start(bf16[192,128]{1,0:T(8,128)(2,1)S(1)} %get-tuple-element.106), channel_id=1, source_target_pairs={{0,64},{1,65},{2,10},{3,11},{4,68},{5,69},{6,14},{7,15},{8,72},{9,... | collective-permute-start | bytes 147464 | tf_op jit(solution)/shard_map/ppermute | solution.py:205
  15.3 4.0 %shard_map.115 = (bf16[160,256]{1,0:T(8,128)(2,1)S(1)}, s32[8,1536]{1,0:T(8,128)S(1)}, f32[1,1280]{1,0:T(1,128)S(1)}, f32[1,704]{1,0:T(1,128)S(1)}, s32[1,384]{1...) custom-call(s32[6]{0:T(128)S(1)} %stack.45.at, s32[1,1024]{1,0:T(1,128)S(1)} %bitcast.135, ...), custom_call_target="tpu_custom_call" | custom-call | flops 2200000000 | tf_op jit(solution)/shard_map/pallas_call | solution.py:220
  20.4 2.7 %collective-permute-start.6 = (bf16[192,128]{1,0:T(8,128)(2,1)S(1)}, bf16[192,128]{1,0:T(8,128)(2,1)S(1)}, u32[]{:S(2)}, u32[]{:S(2)}) collective-permute-start(bf16[192,128]{1,0:T(8,128)(2,1)S(1)} %get-tuple-element.108), channel_id=1, source_target_pairs={{0,96},{1,97},{2,14},{3,15},{4,100},{5,101},{6,10},{7,11},{8,104},... | collective-permute-start | bytes 147464 | tf_op jit(solution)/shard_map/ppermute | solution.py:205
  23.1 3.8 %shard_map.118 = (bf16[208,256]{1,0:T(8,128)(2,1)S(1)}, bf16[208,256]{1,0:T(8,128)(2,1)S(1)}, bf16[208,256]{1,0:T(8,128)(2,1)S(1)}, bf16[208,256]{1,0:T(8,128)(2,1)S(1)}) custom-call(s32[6]{0:T(128)S(1)} %stack.45.at, bf16[160,256]{1,0:T(8,128)(2,1)S(1)} %get-tuple-element.109.pack_ref, bf16[32,3072]{1,0:T(8,128)(2,1)S(1)} %get-tuple-element.102.refs_0_, ...), custom_call_target="tpu_custom_call" | custom-call | flops 5500000256 | tf_op jit(solution)/shard_map/pallas_call | solution.py:220
  27.1 1.6 %collective-permute-start.16 = (bf16[208,256]{1,0:T(8,128)(2,1)S(1)}, bf16[208,256]{1,0:T(8,128)(2,1)S(1)}, u32[]{:S(2)}, u32[]{:S(2)}) collective-permute-start(bf16[208,256]{1,0:T(8,128)(2,1)S(1)} %get-tuple-element.124), channel_id=1, source_target_pairs={{0,96},{1,97},{2,14},{3,15},{4,100},{5,101},{6,10},{7,11},{8,104},... | collective-permute-start | bytes 319496 | tf_op jit(solution)/shard_map/ppermute | solution.py:205
  28.7 1.6 %collective-permute-start.17 = (bf16[208,256]{1,0:T(8,128)(2,1)S(1)}, bf16[208,256]{1,0:T(8,128)(2,1)S(1)}, u32[]{:S(2)}, u32[]{:S(2)}) collective-permute-start(bf16[208,256]{1,0:T(8,128)(2,1)S(1)} %get-tuple-element.125), channel_id=1, source_target_pairs={{0,64},{1,65},{2,10},{3,11},{4,68},{5,69},{6,14},{7,15},{8,72},{9,... | collective-permute-start | bytes 319496 | tf_op jit(solution)/shard_map/ppermute | solution.py:205
  30.4 1.2 %collective-permute-start.12 = (bf16[512,128]{1,0:T(8,128)(2,1)S(1)}, bf16[512,128]{1,0:T(8,128)(2,1)S(1)}, u32[]{:S(2)}, u32[]{:S(2)}) collective-permute-start(bf16[512,128]{1,0:T(8,128)(2,1)S(1)} %get-tuple-element.119.a), channel_id=1, source_target_pairs={{0,12},{1,13},{2,98},{3,99},{4,8},{5,9},{6,102},{7,103},{8,4},{9,5... | collective-permute-start | bytes 393224 | tf_op jit(solution)/shard_map/ppermute | solution.py:205
  31.6 2.0 %collective-permute-start.13 = (bf16[512,128]{1,0:T(8,128)(2,1)S(1)}, bf16[512,128]{1,0:T(8,128)(2,1)S(1)}, u32[]{:S(2)}, u32[]{:S(2)}) collective-permute-start(bf16[512,128]{1,0:T(8,128)(2,1)S(1)} %get-tuple-element.119.a), channel_id=1, source_target_pairs={{0,8},{1,9},{2,66},{3,67},{4,12},{5,13},{6,70},{7,71},{8,0},{9,1},... | collective-permute-start | bytes 393224 | tf_op jit(solution)/shard_map/ppermute | solution.py:205
  34.5 0.9 %collective-permute-start.19 = (bf16[656,256]{1,0:T(8,128)(2,1)S(1)}, bf16[656,256]{1,0:T(8,128)(2,1)S(1)}, u32[]{:S(2)}, u32[]{:S(2)}) collective-permute-start(bf16[656,256]{1,0:T(8,128)(2,1)S(1)} %shard_map.121.l0), channel_id=1, source_target_pairs={{0,12},{1,13},{2,98},{3,99},{4,8},{5,9},{6,102},{7,103},{8,4},{9,5... | collective-permute-start | bytes 1007624 | tf_op jit(solution)/shard_map/ppermute | solution.py:205
  35.3 2.4 %collective-permute-start.20 = (bf16[656,256]{1,0:T(8,128)(2,1)S(1)}, bf16[656,256]{1,0:T(8,128)(2,1)S(1)}, u32[]{:S(2)}, u32[]{:S(2)}) collective-permute-start(bf16[656,256]{1,0:T(8,128)(2,1)S(1)} %shard_map.121.l0), channel_id=1, source_target_pairs={{0,8},{1,9},{2,66},{3,67},{4,12},{5,13},{6,70},{7,71},{8,0},{9,1},... | collective-permute-start | bytes 1007624 | tf_op jit(solution)/shard_map/ppermute | solution.py:205
  37.8 1.1 %collective-permute-start.14 = (bf16[2048,128]{1,0:T(8,128)(2,1)S(1)}, bf16[2048,128]{1,0:T(8,128)(2,1)S(1)}, u32[]{:S(2)}, u32[]{:S(2)}) collective-permute-start(bf16[2048,128]{1,0:T(8,128)(2,1)S(1)} %shard_map.120.plane), channel_id=1, source_target_pairs={{0,16},{1,17},{2,18},{3,19},{4,20},{5,21},{6,22},{7,23},{8,24},{9,... | collective-permute-start | bytes 1572872 | tf_op jit(solution)/shard_map/ppermute | solution.py:205
  39.4 0.8 %shard_map.122 = (f32[256,1]{1,0:T(8,128)S(1)}, f32[256,256]{1,0:T(8,128)S(1)}) custom-call(bf16[2048,128]{1,0:T(8,128)(2,1)S(1)} %shard_map.120.plane, bf16[256,128]{1,0:T(8,128)(2,1)S(1)} %get-tuple-element.129.q.img_q), custom_call_target="tpu_custom_call" | custom-call | flops 1100000000 | tf_op jit(solution)/shard_map/pallas_call | solution.py:220
  40.8 0.9 %shard_map.123 = (bf16[1024,128]{1,0:T(8,128)(2,1)S(1)}, f32[256,1]{1,0:T(8,128)S(1)}, f32[256,256]{1,0:T(8,128)S(1)}) custom-call(bf16[1024,1280]{1,0:T(8,128)(2,1)S(1)} %fusion.81.pick, bf16[656,256]{1,0:T(8,128)(2,1)S(1)} %shard_map.121.l0, bf16[656,256]{1,0:T(8,128)(2,1)S(1)} %collective-permute-done.18.l1, f32[1,704]{1,0:T(1,128)S(1)} %get-tuple-element.128.txt_bias, ...), custom_call_target="tpu_custom_call" | custom-call | flops 1100000000 | tf_op jit(solution)/shard_map/pallas_call | solution.py:220
  41.6 4.0 %collective-permute-done.19.l3 = bf16[656,256]{1,0:T(8,128)(2,1)S(1)} collective-permute-done((bf16[656,256]{1,0:T(8,128)(2,1)S(1)}, bf16[656,256]{1,0:T(8,128)(2,1)S(1)}, u32[]{:S(2)}, u32[]{:S(2)}) %collective-permute-start.19) | collective-permute-done | bytes 335904 | tf_op jit(solution)/shard_map/ppermute | solution.py:205
  45.7 4.1 %shard_map.124 = (bf16[1024,128]{1,0:T(8,128)(2,1)S(1)}, f32[1024,1]{1,0:T(8,128)S(1)}, f32[1024,256]{1,0:T(8,128)S(1)}, f32[256,1]{1,0:T(8,128)S(1)}, f32[256,256]{1,0:T(8,128)S(1)}) custom-call(bf16[1024,1280]{1,0:T(8,128)(2,1)S(1)} %fusion.81.pick, bf16[1024,128]{1,0:T(8,128)(2,1)S(1)} %get-tuple-element.132.q_part, bf16[656,256]{1,0:T(8,128)(2,1)S(1)} %shard_map.121.l0, ...), custom_call_target="tpu_custom_call" | custom-call | flops 2200000000 | tf_op jit(solution)/shard_map/pallas_call | solution.py:220
  49.7 2.5 %shard_map.125 = (bf16[72,1152]{1,0:T(8,128)(2,1)S(1)}, bf16[72,1152]{1,0:T(8,128)(2,1)S(1)}, bf16[72,1152]{1,0:T(8,128)(2,1)S(1)}, bf16[72,1152]{1,0:T(8,128)(2,1)S(1)}) custom-call(bf16[2048,128]{1,0:T(8,128)(2,1)S(1)} %collective-permute-done.14.plane, bf16[1024,128]{1,0:T(8,128)(2,1)S(1)} %get-tuple-element.136.con_q, ...), custom_call_target="tpu_custom_call" | custom-call | flops 3300000000 | tf_op jit(solution)/shard_map/pallas_call | solution.py:220
  52.5 1.5 %collective-permute-start.22 = (bf16[72,1152]{1,0:T(8,128)(2,1)S(1)}, bf16[72,1152]{1,0:T(8,128)(2,1)S(1)}, u32[]{:S(2)}, u32[]{:S(2)}) collective-permute-start(bf16[72,1152]{1,0:T(8,128)(2,1)S(1)} %get-tuple-element.143), channel_id=1, source_target_pairs={{0,96},{1,97},{2,14},{3,15},{4,100},{5,101},{6,10},{7,11},{8,104},... | collective-permute-start | bytes 497672 | tf_op jit(solution)/shard_map/ppermute | solution.py:205
  54.0 1.5 %collective-permute-start.23 = (bf16[72,1152]{1,0:T(8,128)(2,1)S(1)}, bf16[72,1152]{1,0:T(8,128)(2,1)S(1)}, u32[]{:S(2)}, u32[]{:S(2)}) collective-permute-start(bf16[72,1152]{1,0:T(8,128)(2,1)S(1)} %get-tuple-element.144), channel_id=1, source_target_pairs={{0,64},{1,65},{2,10},{3,11},{4,68},{5,69},{6,14},{7,15},{8,72},{9,... | collective-permute-start | bytes 497672 | tf_op jit(solution)/shard_map/ppermute | solution.py:205
  55.5 0.9 %collective-permute-done.21.b1 = bf16[72,1152]{1,0:T(8,128)(2,1)S(1)} collective-permute-done((bf16[72,1152]{1,0:T(8,128)(2,1)S(1)}, bf16[72,1152]{1,0:T(8,128)(2,1)S(1)}, u32[]{:S(2)}, u32[]{:S(2)}) %collective-permute-start.21) | collective-permute-done | bytes 165920 | tf_op jit(solution)/shard_map/ppermute | solution.py:205
  56.5 1.5 %collective-permute-done.22.b2 = bf16[72,1152]{1,0:T(8,128)(2,1)S(1)} collective-permute-done((bf16[72,1152]{1,0:T(8,128)(2,1)S(1)}, bf16[72,1152]{1,0:T(8,128)(2,1)S(1)}, u32[]{:S(2)}, u32[]{:S(2)}) %collective-permute-start.22) | collective-permute-done | bytes 165920 | tf_op jit(solution)/shard_map/ppermute | solution.py:205
  57.9 1.8 %collective-permute-done.23.b3 = bf16[72,1152]{1,0:T(8,128)(2,1)S(1)} collective-permute-done((bf16[72,1152]{1,0:T(8,128)(2,1)S(1)}, bf16[72,1152]{1,0:T(8,128)(2,1)S(1)}, u32[]{:S(2)}, u32[]{:S(2)}) %collective-permute-start.23) | collective-permute-done | bytes 165920 | tf_op jit(solution)/shard_map/ppermute | solution.py:205
  59.7 0.8 %shard_map.126 = (bf16[40,1536]{1,0:T(8,128)(2,1)S(1)}, bf16[40,1536]{1,0:T(8,128)(2,1)S(1)}) custom-call(s32[6]{0:T(128)S(1)} %stack.45.at, bf16[72,1152]{1,0:T(8,128)(2,1)S(1)} %get-tuple-element.141.b0, bf16[72,1152]{1,0:T(8,128)(2,1)S(1)} %collective-permute-done.21.b1, bf16[72,1152]{1,0:T(8,128)(2,1)S(1)} %collective-permute-done.22.b2, ...), custom_call_target="tpu_custom_call" | custom-call | flops 1100000000 | tf_op jit(solution)/shard_map/pallas_call | solution.py:220
  60.5 5.0 %collective-permute-start.24 = (bf16[40,1536]{1,0:T(8,128)(2,1)S(1)}, bf16[40,1536]{1,0:T(8,128)(2,1)S(1)}, u32[]{:S(2)}, u32[]{:S(2)}) collective-permute-start(bf16[40,1536]{1,0:T(8,128)(2,1)S(1)} %get-tuple-element.146), channel_id=1, source_target_pairs={{0,2},{1,3},{2,0},{3,1},{4,6},{5,7},{6,4},{7,5},{8,10},{9,11},{10,... | collective-permute-start | bytes 368648 | tf_op jit(solution)/shard_map/ppermute | solution.py:205
  65.6 1.0 %collective-permute-done.24.core = bf16[40,1536]{1,0:T(8,128)(2,1)S(1)} collective-permute-done((bf16[40,1536]{1,0:T(8,128)(2,1)S(1)}, bf16[40,1536]{1,0:T(8,128)(2,1)S(1)}, u32[]{:S(2)}, u32[]{:S(2)}) %collective-permute-start.24) | collective-permute-done | bytes 122912 | tf_op jit(solution)/shard_map/ppermute | solution.py:205
  66.6 2.9 %collective-permute-start.25 = (bf16[40,1152]{1,0:T(8,128)(2,1)S(1)}, bf16[40,1152]{1,0:T(8,128)(2,1)S(1)}, u32[]{:S(2)}, u32[]{:S(2)}) collective-permute-start(bf16[40,1152]{1,0:T(8,128)(2,1)S(1)} %shard_map.127), channel_id=1, source_target_pairs={{0,1},{1,0},{2,3},{3,2},{4,5},{5,4},{6,7},{7,6},{8,9},{9,8},{10,11... | collective-permute-start | bytes 276488 | tf_op jit(solution)/shard_map/ppermute | solution.py:205
  70.6 1.4 %collective-permute-done.25 = bf16[40,1152]{1,0:T(8,128)(2,1)S(1)} collective-permute-done((bf16[40,1152]{1,0:T(8,128)(2,1)S(1)}, bf16[40,1152]{1,0:T(8,128)(2,1)S(1)}, u32[]{:S(2)}, u32[]{:S(2)}) %collective-permute-start.25) | collective-permute-done | bytes 92192 | tf_op jit(solution)/shard_map/ppermute | solution.py:205
  72.1 2.0 %conditional.1 = (bf16[32,768]{1,0:T(8,128)(2,1)}, f32[1024,32]{0,1:T(8,128)}) conditional(s32[]{:T(128)} %bitcast.38, (s32[512]{0:T(512)S(1)}, s32[1024]{0:T(1024)S(1)}, bf16[256,3072]{1,0:T(8,128)(2,1)S(1)}, s32[1]{0:T(128)}, f32[28,2,3072]{2,1,0:T(2,128)}, /*index=5*/bf16[3072,3,768]{2,0,1:T(8,128)(2,1)}, f32[2,128]{1,0:T(2,128)S(1)}, ...), branch_computations={%region_0.15_spmd, %region_15.16_spmd} | conditional | flops 1100000000 | bytes 257951312 | solution.py:833
  72.4 1.7 %branch_1_fun.1 = (bf16[32,768]{1,0:T(8,128)(2,1)}, f32[32,1024]{1,0:T(8,128)}) custom-call(s32[6]{0:T(128)S(1)} %get-tuple-element.40.at, bf16[40,1152]{1,0:T(8,128)(2,1)S(1)} %get-tuple-element.41.sums, bf16[40,1152]{1,0:T(8,128)(2,1)S(1)} %get-tuple-element.42.head, bf16[40,1536]{1,0:T(8,128)(2,1)} %get-tuple-element.43.own, ...), custom_call_target="tpu_custom_call" | custom-call | flops 1100000000 | tf_op jit(solution)/shard_map/cond/branch_1_fun/pallas_call | solution.py:220
  (54 shorter events, 6.3 us)
Async XLA Ops:
  0.7 14.6 %copy-start.8 = (s32[1024]{0:T(1024)S(1)}, s32[1024]{0:T(1024)}, u32[]{:S(2)}) copy-start(s32[1024]{0:T(1024)} %param.16) | copy-start | bytes 12292
  0.7 14.6 %copy-start.9 = (s32[512]{0:T(512)S(1)}, s32[512]{0:T(512)}, u32[]{:S(2)}) copy-start(s32[512]{0:T(512)} %param.15) | copy-start | bytes 6148
  2.9 17.0 %collective-permute-start.2 = (bf16[32,3072]{1,0:T(8,128)(2,1)S(1)}, bf16[32,3072]{1,0:T(8,128)(2,1)S(1)}, u32[]{:S(2)}, u32[]{:S(2)}) collective-permute-start(bf16[32,3072]{1,0:T(8,128)(2,1)S(1)} %get-tuple-element.102.refs_0_), channel_id=1, source_target_pairs={{0,1},{1,0},{2,3},{3,2},{4,5},{5,4},{6,7},{7,6},{8,9},{9,8},{10,11... | collective-permute-start | bytes 589832 | tf_op jit(solution)/shard_map/ppermute | solution.py:205
  7.3 12.6 %collective-permute-start.4 = (bf16[32,3072]{1,0:T(8,128)(2,1)S(1)}, bf16[32,3072]{1,0:T(8,128)(2,1)S(1)}, u32[]{:S(2)}, u32[]{:S(2)}) collective-permute-start(bf16[32,3072]{1,0:T(8,128)(2,1)S(1)} %get-tuple-element.102.refs_0_), channel_id=1, source_target_pairs={{0,16},{1,17},{2,18},{3,19},{4,20},{5,21},{6,22},{7,23},{8,24},{9,... | collective-permute-start | bytes 589832 | tf_op jit(solution)/shard_map/ppermute | solution.py:205
  8.1 11.2 %collective-permute-start.7 = (bf16[32,3072]{1,0:T(8,128)(2,1)S(1)}, bf16[32,3072]{1,0:T(8,128)(2,1)S(1)}, u32[]{:S(2)}, u32[]{:S(2)}) collective-permute-start(bf16[32,3072]{1,0:T(8,128)(2,1)S(1)} %get-tuple-element.102.refs_0_), channel_id=1, source_target_pairs={{0,17},{1,16},{2,19},{3,18},{4,21},{5,20},{6,23},{7,22},{8,25},{9,... | collective-permute-start | bytes 589832 | tf_op jit(solution)/shard_map/ppermute | solution.py:205
  8.1 2.6 %collective-permute-start.1 = (bf16[48,3072]{1,0:T(8,128)(2,1)S(1)}, bf16[48,3072]{1,0:T(8,128)(2,1)S(1)}, u32[]{:S(2)}, u32[]{:S(2)}) collective-permute-start(bf16[48,3072]{1,0:T(8,128)(2,1)S(1)} %get-tuple-element.100), channel_id=1, source_target_pairs={{0,2},{1,3},{2,0},{3,1},{4,6},{5,7},{6,4},{7,5},{8,10},{9,11},{10,... | collective-permute-start | bytes 884744 | tf_op jit(solution)/shard_map/ppermute | solution.py:205
  11.3 8.5 %collective-permute-start.3 = (bf16[192,128]{1,0:T(8,128)(2,1)S(1)}, bf16[192,128]{1,0:T(8,128)(2,1)S(1)}, u32[]{:S(2)}, u32[]{:S(2)}) collective-permute-start(bf16[192,128]{1,0:T(8,128)(2,1)S(1)} %get-tuple-element.104), channel_id=1, source_target_pairs={{0,32},{1,33},{2,6},{3,7},{4,36},{5,37},{6,2},{7,3},{8,40},{9,41},... | collective-permute-start | bytes 147464 | tf_op jit(solution)/shard_map/ppermute | solution.py:205
  12.7 7.3 %collective-permute-start.5 = (bf16[192,128]{1,0:T(8,128)(2,1)S(1)}, bf16[192,128]{1,0:T(8,128)(2,1)S(1)}, u32[]{:S(2)}, u32[]{:S(2)}) collective-permute-start(bf16[192,128]{1,0:T(8,128)(2,1)S(1)} %get-tuple-element.106), channel_id=1, source_target_pairs={{0,64},{1,65},{2,10},{3,11},{4,68},{5,69},{6,14},{7,15},{8,72},{9,... | collective-permute-start | bytes 147464 | tf_op jit(solution)/shard_map/ppermute | solution.py:205
  15.3 7.8 %copy-start.10 = (f32[2,128]{1,0:T(2,128)S(1)}, f32[2,128]{1,0:T(2,128)}, u32[]{:S(2)}) copy-start(f32[2,128]{1,0:T(2,128)} %refs_9_.1) | copy-start | bytes 3076
  19.3 3.8 %collective-permute-start.10 = (bf16[32,3072]{1,0:T(8,128)(2,1)S(1)}, bf16[32,3072]{1,0:T(8,128)(2,1)S(1)}, u32[]{:S(2)}, u32[]{:S(2)}) collective-permute-start(bf16[32,3072]{1,0:T(8,128)(2,1)S(1)} %collective-permute-done.7.refs_3_), channel_id=1, source_target_pairs={{0,2},{1,3},{2,0},{3,1},{4,6},{5,7},{6,4},{7,5},{8,10},{9,11},{10,... | collective-permute-start | bytes 589832 | tf_op jit(solution)/shard_map/ppermute | solution.py:205
  19.9 3.3 %collective-permute-start.9 = (bf16[32,3072]{1,0:T(8,128)(2,1)S(1)}, bf16[32,3072]{1,0:T(8,128)(2,1)S(1)}, u32[]{:S(2)}, u32[]{:S(2)}) collective-permute-start(bf16[32,3072]{1,0:T(8,128)(2,1)S(1)} %collective-permute-done.2.refs_2_), channel_id=1, source_target_pairs={{0,2},{1,3},{2,0},{3,1},{4,6},{5,7},{6,4},{7,5},{8,10},{9,11},{10,... | collective-permute-start | bytes 589832 | tf_op jit(solution)/shard_map/ppermute | solution.py:205
  20.0 3.1 %collective-permute-start.8 = (bf16[32,3072]{1,0:T(8,128)(2,1)S(1)}, bf16[32,3072]{1,0:T(8,128)(2,1)S(1)}, u32[]{:S(2)}, u32[]{:S(2)}) collective-permute-start(bf16[32,3072]{1,0:T(8,128)(2,1)S(1)} %collective-permute-done.4.refs_1_), channel_id=1, source_target_pairs={{0,2},{1,3},{2,0},{3,1},{4,6},{5,7},{6,4},{7,5},{8,10},{9,11},{10,... | collective-permute-start | bytes 589832 | tf_op jit(solution)/shard_map/ppermute | solution.py:205
  20.4 6.7 %collective-permute-start.6 = (bf16[192,128]{1,0:T(8,128)(2,1)S(1)}, bf16[192,128]{1,0:T(8,128)(2,1)S(1)}, u32[]{:S(2)}, u32[]{:S(2)}) collective-permute-start(bf16[192,128]{1,0:T(8,128)(2,1)S(1)} %get-tuple-element.108), channel_id=1, source_target_pairs={{0,96},{1,97},{2,14},{3,15},{4,100},{5,101},{6,10},{7,11},{8,104},... | collective-permute-start | bytes 147464 | tf_op jit(solution)/shard_map/ppermute | solution.py:205
  26.9 4.7 %collective-permute-start.15 = (bf16[208,256]{1,0:T(8,128)(2,1)S(1)}, bf16[208,256]{1,0:T(8,128)(2,1)S(1)}, u32[]{:S(2)}, u32[]{:S(2)}) collective-permute-start(bf16[208,256]{1,0:T(8,128)(2,1)S(1)} %get-tuple-element.123), channel_id=1, source_target_pairs={{0,32},{1,33},{2,6},{3,7},{4,36},{5,37},{6,2},{7,3},{8,40},{9,41},... | collective-permute-start | bytes 319496 | tf_op jit(solution)/shard_map/ppermute | solution.py:205
  27.1 6.6 %collective-permute-start.16 = (bf16[208,256]{1,0:T(8,128)(2,1)S(1)}, bf16[208,256]{1,0:T(8,128)(2,1)S(1)}, u32[]{:S(2)}, u32[]{:S(2)}) collective-permute-start(bf16[208,256]{1,0:T(8,128)(2,1)S(1)} %get-tuple-element.124), channel_id=1, source_target_pairs={{0,96},{1,97},{2,14},{3,15},{4,100},{5,101},{6,10},{7,11},{8,104},... | collective-permute-start | bytes 319496 | tf_op jit(solution)/shard_map/ppermute | solution.py:205
  28.7 5.4 %collective-permute-start.17 = (bf16[208,256]{1,0:T(8,128)(2,1)S(1)}, bf16[208,256]{1,0:T(8,128)(2,1)S(1)}, u32[]{:S(2)}, u32[]{:S(2)}) collective-permute-start(bf16[208,256]{1,0:T(8,128)(2,1)S(1)} %get-tuple-element.125), channel_id=1, source_target_pairs={{0,64},{1,65},{2,10},{3,11},{4,68},{5,69},{6,14},{7,15},{8,72},{9,... | collective-permute-start | bytes 319496 | tf_op jit(solution)/shard_map/ppermute | solution.py:205
  30.3 5.0 %collective-permute-start.11 = (bf16[512,128]{1,0:T(8,128)(2,1)S(1)}, bf16[512,128]{1,0:T(8,128)(2,1)S(1)}, u32[]{:S(2)}, u32[]{:S(2)}) collective-permute-start(bf16[512,128]{1,0:T(8,128)(2,1)S(1)} %get-tuple-element.119.a), channel_id=1, source_target_pairs={{0,4},{1,5},{2,34},{3,35},{4,0},{5,1},{6,38},{7,39},{8,12},{9,13},... | collective-permute-start | bytes 393224 | tf_op jit(solution)/shard_map/ppermute | solution.py:205
  30.4 7.3 %collective-permute-start.12 = (bf16[512,128]{1,0:T(8,128)(2,1)S(1)}, bf16[512,128]{1,0:T(8,128)(2,1)S(1)}, u32[]{:S(2)}, u32[]{:S(2)}) collective-permute-start(bf16[512,128]{1,0:T(8,128)(2,1)S(1)} %get-tuple-element.119.a), channel_id=1, source_target_pairs={{0,12},{1,13},{2,98},{3,99},{4,8},{5,9},{6,102},{7,103},{8,4},{9,5... | collective-permute-start | bytes 393224 | tf_op jit(solution)/shard_map/ppermute | solution.py:205
  31.6 6.1 %collective-permute-start.13 = (bf16[512,128]{1,0:T(8,128)(2,1)S(1)}, bf16[512,128]{1,0:T(8,128)(2,1)S(1)}, u32[]{:S(2)}, u32[]{:S(2)}) collective-permute-start(bf16[512,128]{1,0:T(8,128)(2,1)S(1)} %get-tuple-element.119.a), channel_id=1, source_target_pairs={{0,8},{1,9},{2,66},{3,67},{4,12},{5,13},{6,70},{7,71},{8,0},{9,1},... | collective-permute-start | bytes 393224 | tf_op jit(solution)/shard_map/ppermute | solution.py:205
  34.4 6.4 %collective-permute-start.18 = (bf16[656,256]{1,0:T(8,128)(2,1)S(1)}, bf16[656,256]{1,0:T(8,128)(2,1)S(1)}, u32[]{:S(2)}, u32[]{:S(2)}) collective-permute-start(bf16[656,256]{1,0:T(8,128)(2,1)S(1)} %shard_map.121.l0), channel_id=1, source_target_pairs={{0,4},{1,5},{2,34},{3,35},{4,0},{5,1},{6,38},{7,39},{8,12},{9,13},... | collective-permute-start | bytes 1007624 | tf_op jit(solution)/shard_map/ppermute | solution.py:205
  34.5 11.2 %collective-permute-start.19 = (bf16[656,256]{1,0:T(8,128)(2,1)S(1)}, bf16[656,256]{1,0:T(8,128)(2,1)S(1)}, u32[]{:S(2)}, u32[]{:S(2)}) collective-permute-start(bf16[656,256]{1,0:T(8,128)(2,1)S(1)} %shard_map.121.l0), channel_id=1, source_target_pairs={{0,12},{1,13},{2,98},{3,99},{4,8},{5,9},{6,102},{7,103},{8,4},{9,5... | collective-permute-start | bytes 1007624 | tf_op jit(solution)/shard_map/ppermute | solution.py:205
  35.3 10.3 %collective-permute-start.20 = (bf16[656,256]{1,0:T(8,128)(2,1)S(1)}, bf16[656,256]{1,0:T(8,128)(2,1)S(1)}, u32[]{:S(2)}, u32[]{:S(2)}) collective-permute-start(bf16[656,256]{1,0:T(8,128)(2,1)S(1)} %shard_map.121.l0), channel_id=1, source_target_pairs={{0,8},{1,9},{2,66},{3,67},{4,12},{5,13},{6,70},{7,71},{8,0},{9,1},... | collective-permute-start | bytes 1007624 | tf_op jit(solution)/shard_map/ppermute | solution.py:205
  37.8 11.9 %collective-permute-start.14 = (bf16[2048,128]{1,0:T(8,128)(2,1)S(1)}, bf16[2048,128]{1,0:T(8,128)(2,1)S(1)}, u32[]{:S(2)}, u32[]{:S(2)}) collective-permute-start(bf16[2048,128]{1,0:T(8,128)(2,1)S(1)} %shard_map.120.plane), channel_id=1, source_target_pairs={{0,16},{1,17},{2,18},{3,19},{4,20},{5,21},{6,22},{7,23},{8,24},{9,... | collective-permute-start | bytes 1572872 | tf_op jit(solution)/shard_map/ppermute | solution.py:205
  52.2 4.3 %collective-permute-start.21 = (bf16[72,1152]{1,0:T(8,128)(2,1)S(1)}, bf16[72,1152]{1,0:T(8,128)(2,1)S(1)}, u32[]{:S(2)}, u32[]{:S(2)}) collective-permute-start(bf16[72,1152]{1,0:T(8,128)(2,1)S(1)} %get-tuple-element.142), channel_id=1, source_target_pairs={{0,32},{1,33},{2,6},{3,7},{4,36},{5,37},{6,2},{7,3},{8,40},{9,41},... | collective-permute-start | bytes 497672 | tf_op jit(solution)/shard_map/ppermute | solution.py:205
  52.5 5.4 %collective-permute-start.22 = (bf16[72,1152]{1,0:T(8,128)(2,1)S(1)}, bf16[72,1152]{1,0:T(8,128)(2,1)S(1)}, u32[]{:S(2)}, u32[]{:S(2)}) collective-permute-start(bf16[72,1152]{1,0:T(8,128)(2,1)S(1)} %get-tuple-element.143), channel_id=1, source_target_pairs={{0,96},{1,97},{2,14},{3,15},{4,100},{5,101},{6,10},{7,11},{8,104},... | collective-permute-start | bytes 497672 | tf_op jit(solution)/shard_map/ppermute | solution.py:205
  54.0 5.7 %collective-permute-start.23 = (bf16[72,1152]{1,0:T(8,128)(2,1)S(1)}, bf16[72,1152]{1,0:T(8,128)(2,1)S(1)}, u32[]{:S(2)}, u32[]{:S(2)}) collective-permute-start(bf16[72,1152]{1,0:T(8,128)(2,1)S(1)} %get-tuple-element.144), channel_id=1, source_target_pairs={{0,64},{1,65},{2,10},{3,11},{4,68},{5,69},{6,14},{7,15},{8,72},{9,... | collective-permute-start | bytes 497672 | tf_op jit(solution)/shard_map/ppermute | solution.py:205
  59.7 12.4 %copy-start = (bf16[256,3072]{1,0:T(8,128)(2,1)S(1)}, bf16[256,3072]{1,0:T(8,128)(2,1)}, u32[]{:S(2)}) copy-start(bf16[256,3072]{1,0:T(8,128)(2,1)} %table_ref.1) | copy-start | bytes 4718596
  59.7 12.4 %copy-start.3 = (bf16[32,768]{1,0:T(8,128)(2,1)S(1)}, bf16[32,768]{1,0:T(8,128)(2,1)}, u32[]{:S(2)}) copy-start(bf16[32,768]{1,0:T(8,128)(2,1)} %q_ref.1) | copy-start | bytes 147460
  59.7 12.4 %copy-start.6 = (bf16[32,768]{1,0:T(8,128)(2,1)S(1)}, bf16[32,768]{1,0:T(8,128)(2,1)}, u32[]{:S(2)}) copy-start(bf16[32,768]{1,0:T(8,128)(2,1)} %k_ref.1) | copy-start | bytes 147460
  59.7 12.4 %copy-start.7 = (bf16[32,768]{1,0:T(8,128)(2,1)S(1)}, bf16[32,768]{1,0:T(8,128)(2,1)}, u32[]{:S(2)}) copy-start(bf16[32,768]{1,0:T(8,128)(2,1)} %v_ref.1) | copy-start | bytes 147460
  60.5 6.0 %collective-permute-start.24 = (bf16[40,1536]{1,0:T(8,128)(2,1)S(1)}, bf16[40,1536]{1,0:T(8,128)(2,1)S(1)}, u32[]{:S(2)}, u32[]{:S(2)}) collective-permute-start(bf16[40,1536]{1,0:T(8,128)(2,1)S(1)} %get-tuple-element.146), channel_id=1, source_target_pairs={{0,2},{1,3},{2,0},{3,1},{4,6},{5,7},{6,4},{7,5},{8,10},{9,11},{10,... | collective-permute-start | bytes 368648 | tf_op jit(solution)/shard_map/ppermute | solution.py:205
  66.6 5.5 %collective-permute-start.25 = (bf16[40,1152]{1,0:T(8,128)(2,1)S(1)}, bf16[40,1152]{1,0:T(8,128)(2,1)S(1)}, u32[]{:S(2)}, u32[]{:S(2)}) collective-permute-start(bf16[40,1152]{1,0:T(8,128)(2,1)S(1)} %shard_map.127), channel_id=1, source_target_pairs={{0,1},{1,0},{2,3},{3,2},{4,5},{5,4},{6,7},{7,6},{8,9},{9,8},{10,11... | collective-permute-start | bytes 276488 | tf_op jit(solution)/shard_map/ppermute | solution.py:205
  (1 other events, 6.0 us)
